TPU v7x, 32 devices: a whole 2x2x4 slice. The times are simulated.
32 devices in a mesh: dp: 16 (over z, y, x), tensor: 2 (over core).
Axes of the slice: x: 2, y: 2, z: 4, core: 2. Of those that a mesh axis runs over, the one named last changes fastest.
Arguments:
- features: bfloat16 [16384, 4096], P(('dp', 'tensor')), may hold values from -20 to 20
- key_grads: bfloat16 [16384, 256], P('dp', 'tensor'), may hold values from -20 to 20
- error_in: bfloat16 [16, 4096, 256], P('dp', None, 'tensor'), may hold values from -24 to 24
- selected: int32 [16, 2, 32], P('dp', 'tensor'), may hold values from 0 to 4095, as said below
- bin_edges: int32 [17], replicated, may hold values from 0 to 4096, as said below
- threshold: int32 [1], replicated, may hold values from 1 to 15
- moment: float32 [4096, 256], P('dp', 'tensor'), may hold values from -2 to 2
- second: float32 [4096, 256], P('dp', 'tensor'), may hold values from 0.05 to 2
- master: float32 [4096, 256], P('dp', 'tensor'), may hold values from -0.0625 to 0.0625
Outputs:
- keys: bfloat16 [16384, 256], P('dp', 'tensor')
- error_out: bfloat16 [16, 4096, 256], P('dp', None, 'tensor')
- moment_new: float32 [4096, 256], P('dp', 'tensor')
- second_new: float32 [4096, 256], P('dp', 'tensor')
- master_new: float32 [4096, 256], P('dp', 'tensor')
Inputs may be any that keep to these rules, and one draw needn't show every extreme that they name: Each device's 32 rows are distinct; the rows o * 256 to (o + 1) * 256 - 1 form owner o's region, and one device's row of selected names at most 6 rows of one region; there is one region, the same for every row of selected, that receives exactly 6 blocks from each row; every other region receives at most 6 from a row. bin_edges[0] = 0, bin_edges[16] = 4096, strictly increasing.
All inputs are finite; a program needn't handle non-finite values.
Results may differ from a plain program's by a relative error of at most 0.001.
The roundings to bfloat16 on the way count: a program that leaves them out, or rounds other values in their place, can miss the bound.
Values may be sent and summed in bfloat16 or wider, within the bound.
No kernel may reach another device: no remote copies, remote signals or barrier semaphores. Data moves between devices by JAX's collectives and lax.ppermute only.
A program may use at most 64 MiB of HBM per device.

v0:
```python
import functools

import jax
import jax.numpy as jnp
from jax import lax
from jax.experimental import pallas as pl
from jax.experimental.pallas import tpu as pltpu
from jax.sharding import PartitionSpec as P

CAP = 6
SLOTS = 8
LANES = 128

beta_first = 0.9
beta_second = 0.95
learn_rate = 0.001
decay_rate = 0.1
epsilon = 1e-06
adam_epsilon = 1e-08
step_count = 10.0

VMEM = pl.BlockSpec(memory_space=pltpu.VMEM)
SMEM = pl.BlockSpec(memory_space=pltpu.SMEM)
ANY = pl.BlockSpec(memory_space=pl.ANY)


def shift(x, axis, step):
    n = lax.axis_size(axis)
    return lax.ppermute(x, axis, [(i, (i + step) % n) for i in range(n)])


def swap(x, axis, mask):
    return lax.ppermute(x, axis, [(i, i ^ mask) for i in range(lax.axis_size(axis))])


def params(*arrays):
    total = sum(a.size * jnp.dtype(a.dtype).itemsize for a in arrays)
    return pltpu.CompilerParams(vmem_limit_bytes=total + (6 << 20))


def cost(flops, nbytes):
    return pl.CostEstimate(flops=flops, bytes_accessed=nbytes, transcendentals=0)


def load_kernel(pieces, *refs):
    n = len(refs) // 2
    sources, targets, sem = refs[:n], refs[n : 2 * n], refs[2 * n]
    copies = []
    for i in range(n):
        rows = sources[i].shape[0] // pieces
        for j in range(pieces):
            part = pl.ds(j * rows, rows)
            copies.append(
                pltpu.make_async_copy(sources[i].at[part], targets[i].at[part], sem.at[i, j])
            )
            copies[-1].start()
    for copy in copies:
        copy.wait()


def load(arrays):
    pieces = 8
    return pl.pallas_call(
        functools.partial(load_kernel, pieces),
        in_specs=[ANY] * len(arrays),
        out_specs=[VMEM] * len(arrays),
        out_shape=[pltpu.VMEM(a.shape, a.dtype) for a in arrays],
        scratch_shapes=[pltpu.SemaphoreType.DMA((len(arrays), pieces))],
        compiler_params=params(*arrays),
        cost_estimate=cost(0, 4 * sum(a.size for a in arrays)),
    )(*[pltpu.with_memory_space_constraint(a, pltpu.HBM) for a in arrays])


def part_kernel(first, core, f_ref, g_ref, *rest):
    tokens = f_ref.shape[0]
    count = rest[-1].shape[0]
    tile = min(1024, count)
    g = g_ref[pl.ds(pl.multiple_of(core[0] * tokens, tokens), tokens), :]
    for at in range(0, count, tile):
        p = lax.dot_general(
            f_ref[:, first + at : first + at + tile],
            g,
            (((0,), (0,)), ((), ())),
            preferred_element_type=jnp.float32,
        )
        if len(rest) > 1:
            p = p + rest[0][at : at + tile, :].astype(jnp.float32)
        rest[-1][at : at + tile, :] = p


def part_sum(core, features, grads, first, count, *error):
    tokens = features.shape[0]
    width = grads.shape[1]
    part = jax.ShapeDtypeStruct((count, width), jnp.float32)
    return pl.pallas_call(
        functools.partial(part_kernel, first),
        in_specs=[SMEM, VMEM, VMEM] + [VMEM] * len(error),
        out_specs=VMEM,
        out_shape=part,
        compiler_params=params(features, grads, part, *error),
        cost_estimate=cost(2 * tokens * count * width, 2 * tokens * count + 4 * count * width),
    )(core, features, grads, *error)


def collect_kernel(n_chunks, owners, bins, sel, lo_ref, hi_ref, own_ref, *refs):
    parts, (sum_ref, out_ref, count_ref) = refs[:-3], refs[-3:]
    rows, width = sum_ref.shape
    region = rows // owners
    lo, hi = lo_ref[...], hi_ref[...]
    count = rows // n_chunks
    tile = min(1024, count)
    acc = jnp.zeros((8, LANES), jnp.float32)
    for first in range(0, rows, tile):
        s = own_ref[first : first + tile, :]
        for ref in parts[first // count :: n_chunks]:
            s = s + ref[first % count : first % count + tile, :]
        sum_ref[first : first + tile, :] = s
        q = jnp.sum(s * s, axis=1, keepdims=True)
        ids = first + lax.broadcasted_iota(jnp.int32, (tile, LANES), 0)
        hit = (ids >= lo) & (ids < hi)
        acc = acc + jnp.sum(jnp.where(hit, q, 0.0).reshape(tile // 8, 8, LANES), axis=0)
    energy = jnp.sum(acc, axis=0, keepdims=True)
    lane = lax.broadcasted_iota(jnp.int32, (1, LANES), 1)
    out_ref[...] = jnp.zeros_like(out_ref)
    note = jnp.where((lane >= bins) & (lane < bins + CAP), -1.0, energy)
    for o in range(owners):
        out_ref[o * SLOTS + CAP : o * SLOTS + CAP + 1, :] = note
        count_ref[o] = 0

    def take(i, carry):
        r = sel[i]
        o = lax.div(r, region)
        k = count_ref[o]
        count_ref[o] = k + 1
        out_ref[pl.ds(o * SLOTS + k, 1), :] = sum_ref[pl.ds(r, 1), :]
        sum_ref[pl.ds(r, 1), :] = jnp.zeros((1, width), jnp.float32)
        at = pl.ds(o * SLOTS + CAP, 1)
        out_ref[at, :] = jnp.where(
            lane == bins + k, (r - o * region).astype(jnp.float32), out_ref[at, :]
        )
        return carry

    lax.fori_loop(0, sel.shape[0], take, 0, unroll=8)


def collect(selected, lo, hi, own, parts, n_chunks, owners, bins):
    rows, width = own.shape
    return pl.pallas_call(
        functools.partial(collect_kernel, n_chunks, owners, bins),
        in_specs=[SMEM, VMEM, VMEM, VMEM] + [VMEM] * len(parts),
        out_specs=[VMEM, VMEM],
        out_shape=[
            jax.ShapeDtypeStruct((rows, width), jnp.float32),
            jax.ShapeDtypeStruct((owners * SLOTS, width), jnp.float32),
        ],
        scratch_shapes=[pltpu.SMEM((owners,), jnp.int32)],
        compiler_params=params(own, own, own, *parts),
        cost_estimate=cost(8 * rows * width, 4 * rows * width * 3),
    )(selected, lo, hi, own, *parts)


def adam_kernel(bins, info, lo_ref, hi_ref, arr_ref, m_ref, v_ref, w_ref, mo, vo, wo, bo):
    owners, slots, width = arr_ref.shape
    region = m_ref.shape[0]
    lo, hi = lo_ref[...], hi_ref[...]
    lane = lax.broadcasted_iota(jnp.int32, (1, LANES), 1)
    arr = arr_ref[...]
    notes = arr[:, CAP : CAP + 1, :]
    energy = jnp.sum(notes, axis=0)
    widths = jnp.maximum(hi - lo, 1).astype(jnp.float32)
    normal = 1.0 / jnp.sqrt(energy / (owners * width * widths) + epsilon)
    scale = jnp.where((lane >= info[1]) & (lane < bins), normal, 1.0)
    ids = info[0] * region + lax.broadcasted_iota(jnp.int32, (region, LANES), 0)
    row_scale = jnp.sum(
        jnp.where((ids >= lo) & (ids < hi), scale, 0.0), axis=1, keepdims=True
    )
    slot = lax.broadcasted_iota(jnp.int32, (owners, slots, LANES), 1)
    lane3 = lax.broadcasted_iota(jnp.int32, (owners, slots, LANES), 2)
    offset = jnp.sum(
        jnp.where((lane3 == bins + slot) & (slot < CAP), notes, 0.0), axis=2, keepdims=True
    )
    slot1 = lax.broadcasted_iota(jnp.int32, (owners, slots, 1), 1)
    offset = jnp.where(slot1 < CAP, offset, -1.0).reshape(owners * slots, 1)
    row = lax.broadcasted_iota(jnp.int32, (owners * slots, region), 1).astype(jnp.float32)
    place = jnp.where(row == offset, 1.0, 0.0)
    grad = lax.dot_general(
        place,
        arr.reshape(owners * slots, width),
        (((0,), (0,)), ((), ())),
        precision=lax.Precision.HIGHEST,
        preferred_element_type=jnp.float32,
    )
    grad = grad * row_scale
    master = w_ref[...]
    moment_new = beta_first * m_ref[...] + (1.0 - beta_first) * grad
    second_new = beta_second * v_ref[...] + (1.0 - beta_second) * grad * grad
    first_hat = moment_new / (1.0 - beta_first**step_count)
    second_hat = second_new / (1.0 - beta_second**step_count)
    master_new = master - learn_rate * (
        first_hat / (jnp.sqrt(second_hat) + adam_epsilon) + decay_rate * master
    )
    mo[...] = moment_new
    vo[...] = second_new
    wo[...] = master_new
    bo[...] = master_new.astype(jnp.bfloat16)


def adam(info, lo, hi, arrived, moment, second, master, bins):
    f32 = jax.ShapeDtypeStruct(master.shape, jnp.float32)
    return pl.pallas_call(
        functools.partial(adam_kernel, bins),
        in_specs=[SMEM] + [VMEM] * 6,
        out_specs=[VMEM] * 4,
        out_shape=[f32, f32, f32, jax.ShapeDtypeStruct(master.shape, jnp.bfloat16)],
        compiler_params=params(arrived, arrived, *[f32] * 7),
        cost_estimate=cost(2 * 6 * arrived.size * master.shape[0], 30 * master.size),
    )(info, lo, hi, arrived, moment, second, master)


def project_kernel(last, n_f, at, w_ref, *refs):
    feats, old, out_ref = refs[:n_f], refs[n_f:-1], refs[-1]
    count, region, width = w_ref.shape
    tokens = feats[0].shape[0]
    for i, f_ref in enumerate(feats):
        mine = pl.ds(i * tokens, tokens)
        total = old[0][mine, :] if old else None
        for j in range(count):
            cols = pl.ds(pl.multiple_of(at[j] * region, region), region)
            part = jnp.dot(f_ref[:, cols], w_ref[j], preferred_element_type=jnp.float32)
            total = part if total is None else total + part
        if last:
            place = lax.rem(at[count] + i, n_f) * tokens
            mine = pl.ds(pl.multiple_of(place, tokens), tokens)
        out_ref[mine, :] = total.astype(out_ref.dtype)


def project(at, feats, pieces, total, last):
    count, region, width = pieces.shape
    whole = len(feats) * feats[0].shape[0]
    old = [] if total is None else [total]
    out = jax.ShapeDtypeStruct((whole, width), jnp.bfloat16 if last else jnp.float32)
    return pl.pallas_call(
        functools.partial(project_kernel, last, len(feats)),
        in_specs=[SMEM, VMEM] + [VMEM] * (len(feats) + len(old)),
        out_specs=VMEM,
        out_shape=out,
        compiler_params=params(pieces, out, *feats, *old),
        cost_estimate=cost(
            2 * whole * count * region * width, 2 * whole * count * region + 8 * whole * width
        ),
    )(at, pieces, *feats, *old)


def spans(mask_bits):
    masks = [0]
    for b in mask_bits:
        masks = masks + [m | b for m in masks]
    return masks


def shards(features, key_grads, error_in, selected, bin_edges, threshold, moment, second, master):
    cores, owners = lax.axis_size("tensor"), lax.axis_size("dp")
    core, me = lax.axis_index("tensor"), lax.axis_index("dp")
    tokens, rows = features.shape
    width = key_grads.shape[1]
    region = rows // owners
    bins = bin_edges.shape[0] - 1
    pad = (0, LANES - bins)
    lo = jnp.pad(bin_edges[:-1], pad)[None]
    hi = jnp.pad(bin_edges[1:], pad)[None]
    core1 = core.reshape(1).astype(jnp.int32)

    [held] = load([features])
    n_chunks = 4 if cores == 2 else 1
    count = rows // n_chunks
    made, got = [], []
    for s in range(1, cores):
        theirs = shift(key_grads, "tensor", s)
        for j in range(n_chunks):
            made.append(part_sum(core1, held, theirs, j * count, count))
            got.append(shift(made[-1], "tensor", -s))
    mine, _ = lax.optimization_barrier((key_grads, made[-1]))
    own = part_sum(core1, held, mine, 0, rows, error_in[0])
    later, _ = lax.optimization_barrier((features, [own] + got))
    rest, outgoing = collect(selected[0, 0], lo, hi, own, got, n_chunks, owners, bins)
    error_out = rest.astype(jnp.bfloat16)[None]
    feats = [features] + [shift(later, "tensor", -s) for s in range(1, cores)]

    arrived = lax.all_to_all(
        outgoing.reshape(owners, SLOTS, width), "dp", split_axis=0, concat_axis=0, tiled=True
    )
    info = jnp.stack([me.astype(jnp.int32), threshold[0]])
    moment_new, second_new, master_new, weight = adam(
        info, lo, hi, arrived, moment, second, master, bins
    )

    bits = [1 << i for i in range(owners.bit_length() - 1)]
    if 1 << len(bits) == owners and len(bits) > 2 and region % LANES == 0:
        plane, line = spans(bits[:2]), spans(bits[2:])
        mine = jnp.stack([weight if m == 0 else swap(weight, "dp", m) for m in line])
        feats = load(feats)
        total = None
        for j, b in enumerate(plane):
            here = mine if b == 0 else swap(mine, "dp", b)
            at = jnp.stack([me ^ (b ^ m) for m in line] + [core]).astype(jnp.int32)
            total = project(at, feats, here, total, j == len(plane) - 1)
        keys = total
    else:
        whole = jnp.concatenate(feats, axis=0)
        whole = jnp.roll(whole, core * tokens, axis=0)
        keys = jnp.dot(
            whole,
            lax.all_gather(weight, "dp", axis=0, tiled=True),
            preferred_element_type=jnp.float32,
        ).astype(jnp.bfloat16)
    return (keys, error_out, moment_new, second_new, master_new)


def solution(mesh):
    in_specs = (
        P(("dp", "tensor"), None),
        P("dp", "tensor"),
        P("dp", None, "tensor"),
        P("dp", "tensor", None),
        P(),
        P(),
        P("dp", "tensor"),
        P("dp", "tensor"),
        P("dp", "tensor"),
    )
    out_specs = (
        P("dp", "tensor"),
        P("dp", None, "tensor"),
        P("dp", "tensor"),
        P("dp", "tensor"),
        P("dp", "tensor"),
    )
    return jax.shard_map(shards, mesh=mesh, in_specs=in_specs, out_specs=out_specs, check_vma=False)
```

profile of v0, /device:TPU:0, one launch (start us, length us, event | category | flops | bytes accessed | tf_op | source)
XLA Modules:
  0.0 51.4 jit_solution(6674016206939874675)
XLA Ops:
  0.6 0.5 %collective-permute-start = (bf16[1024,128]{1,0:T(8,128)(2,1)}, bf16[1024,128]{1,0:T(8,128)(2,1)S(1)}, u32[]{:S(2)}, u32[]{:S(2)}) collective-permute-start(bf16[1024,128]{1,0:T(8,128)(2,1)} %g_ref), channel_id=1, source_target_pairs={{0,1},{1,0},{2,3},{3,2},{4,5},{5,4},{6,7},{7,6},{8,9},{9,8},{10,11... | collective-permute-start | bytes 786440 | tf_op jit(solution)/shard_map/ppermute | solution.py:29
  1.1 2.2 %shard_map.128.f_ref = bf16[512,4096]{1,0:T(8,128)(2,1)S(1)} custom-call(bf16[512,4096]{1,0:T(8,128)(2,1)} %refs_0_.3), custom_call_target="tpu_custom_call" | custom-call | bytes 8388608 | tf_op jit(solution)/shard_map/pallas_call | solution.py:63
  3.4 0.5 %shard_map.131 = f32[1024,128]{1,0:T(8,128)S(1)} custom-call(s32[1]{0:T(128)} %bitcast.4.core, bf16[512,4096]{1,0:T(8,128)(2,1)S(1)} %shard_map.128.f_ref, bf16[1024,128]{1,0:T(8,128)(2,1)S(1)} %collective-permute-done.g_ref), custom_call_target="tpu_custom_call" | custom-call | flops 134217728 | bytes 1572864 | tf_op jit(solution)/shard_map/pallas_call | solution.py:95
  3.9 0.1 collective-permute-start.1
  4.0 0.5 %shard_map.132 = f32[1024,128]{1,0:T(8,128)S(1)} custom-call(s32[1]{0:T(128)} %bitcast.4.core, bf16[512,4096]{1,0:T(8,128)(2,1)S(1)} %shard_map.128.f_ref, bf16[1024,128]{1,0:T(8,128)(2,1)S(1)} %collective-permute-done.g_ref), custom_call_target="tpu_custom_call" | custom-call | flops 134217728 | bytes 1572864 | tf_op jit(solution)/shard_map/pallas_call | solution.py:95
  4.6 0.5 %collective-permute-start.2 = (f32[1024,128]{1,0:T(8,128)S(1)}, f32[1024,128]{1,0:T(8,128)S(1)}, u32[]{:S(2)}, u32[]{:S(2)}) collective-permute-start(f32[1024,128]{1,0:T(8,128)S(1)} %shard_map.132), channel_id=1, source_target_pairs={{0,1},{1,0},{2,3},{3,2},{4,5},{5,4},{6,7},{7,6},{8,9},{9,8},{10,11... | collective-permute-start | bytes 1572872 | tf_op jit(solution)/shard_map/ppermute | solution.py:29
  5.1 0.5 %shard_map.133 = f32[1024,128]{1,0:T(8,128)S(1)} custom-call(s32[1]{0:T(128)} %bitcast.4.core, bf16[512,4096]{1,0:T(8,128)(2,1)S(1)} %shard_map.128.f_ref, bf16[1024,128]{1,0:T(8,128)(2,1)S(1)} %collective-permute-done.g_ref), custom_call_target="tpu_custom_call" | custom-call | flops 134217728 | bytes 1572864 | tf_op jit(solution)/shard_map/pallas_call | solution.py:95
  5.6 0.1 collective-permute-start.3
  5.8 0.5 %shard_map.129 = f32[1024,128]{1,0:T(8,128)S(1)} custom-call(s32[1]{0:T(128)} %bitcast.4.core, bf16[512,4096]{1,0:T(8,128)(2,1)S(1)} %shard_map.128.f_ref, bf16[1024,128]{1,0:T(8,128)(2,1)S(1)} %collective-permute-done.g_ref), custom_call_target="tpu_custom_call" | custom-call | flops 134217728 | bytes 1572864 | tf_op jit(solution)/shard_map/pallas_call | solution.py:95
  6.3 0.5 %collective-permute-start.4 = (f32[1024,128]{1,0:T(8,128)S(1)}, f32[1024,128]{1,0:T(8,128)S(1)}, u32[]{:S(2)}, u32[]{:S(2)}) collective-permute-start(f32[1024,128]{1,0:T(8,128)S(1)} %shard_map.129), channel_id=1, source_target_pairs={{0,1},{1,0},{2,3},{3,2},{4,5},{5,4},{6,7},{7,6},{8,9},{9,8},{10,11... | collective-permute-start | bytes 1572872 | tf_op jit(solution)/shard_map/ppermute | solution.py:29
  6.9 1.4 %shard_map.130.own_ref = f32[4096,128]{1,0:T(8,128)S(1)} custom-call(s32[1]{0:T(128)} %bitcast.4.core, bf16[512,4096]{1,0:T(8,128)(2,1)S(1)} %shard_map.128.f_ref, bf16[1024,128]{1,0:T(8,128)(2,1)S(1)} %copy-done.1, bf16[4096,128]{1,0:T(8,128)(2,1)S(1)} %bitcast.30), custom_call_target="tpu_custom_call" | custom-call | flops 536870912 | bytes 6291456 | tf_op jit(solution)/shard_map/pallas_call | solution.py:95
  8.4 0.4 collective-permute-start.9
  8.8 2.1 %shard_map.134 = (f32[4096,128]{1,0:T(8,128)S(1)}, f32[128,128]{1,0:T(8,128)}) custom-call(s32[32]{0:T(128)S(1)} %bitcast.32, s32[1,128]{1,0:T(1,128)S(1)} %get-tuple-element.28.lo_ref, s32[1,128]{1,0:T(1,128)S(1)} %get-tuple-element.27.hi_ref, f32[4096,128]{1,0:T(8,128)S(1)} %shard_map.130.own_ref, f32[1024,128]{1,0:T(8,128)S(1)} %collective-permute-done.1.refs_0_, ...), custom_call_target="tpu_custom_call" | custom-call | flops 4194304 | bytes 6291456 | tf_op jit(solution)/shard_map/pallas_call | solution.py:148
  10.9 8.0 %all-to-all-start = ((f32[16,8,128]{2,1,0:T(8,128)}), f32[16,8,128]{2,1,0:T(8,128)S(1)}, u32[]{:S(2)}, u32[]{:S(2)}) async-start(f32[16,8,128]{2,1,0:T(8,128)} %bitcast.10), calls=%async_computation | async-start | bytes 131072 | tf_op jit(solution)/shard_map/all_to_all | solution.py:289
  19.7 6.8 %all-to-all-done.arr_ref = f32[16,8,128]{2,1,0:T(8,128)S(1)} async-done(((f32[16,8,128]{2,1,0:T(8,128)}), f32[16,8,128]{2,1,0:T(8,128)S(1)}, u32[]{:S(2)}, u32[]{:S(2)}) %all-to-all-start) | async-done | bytes 65568 | tf_op jit(solution)/shard_map/all_to_all | solution.py:289
  26.5 1.7 %shard_map.135 = (f32[256,128]{1,0:T(8,128)}, f32[256,128]{1,0:T(8,128)}, f32[256,128]{1,0:T(8,128)}, bf16[256,128]{1,0:T(8,128)(2,1)S(1)}) custom-call(s32[2]{0:T(128)S(1)} %pad_add_fusion.info, s32[1,128]{1,0:T(1,128)S(1)} %get-tuple-element.28.lo_ref, s32[1,128]{1,0:T(1,128)S(1)} %get-tuple-element.27.hi_ref, f32[16,8,128]{2,1,0:T(8,128)S(1)} %all-to-all-done.arr_ref, ...), custom_call_target="tpu_custom_call" | custom-call | flops 50331648 | bytes 983040 | tf_op jit(solution)/shard_map/pallas_call | solution.py:210
  28.2 0.9 %collective-permute-start.7 = (bf16[256,128]{1,0:T(8,128)(2,1)S(1)}, bf16[256,128]{1,0:T(8,128)(2,1)S(1)}, u32[]{:S(2)}, u32[]{:S(2)}) collective-permute-start(bf16[256,128]{1,0:T(8,128)(2,1)S(1)} %get-tuple-element.17), channel_id=1, source_target_pairs={{0,24},{2,26},{4,28},{6,30},{8,16},{10,18},{12,20},{14,22},{16,8},... | collective-permute-start | bytes 196616 | tf_op jit(solution)/shard_map/ppermute | solution.py:33
  29.1 1.2 %collective-permute-start.6 = (bf16[256,128]{1,0:T(8,128)(2,1)S(1)}, bf16[256,128]{1,0:T(8,128)(2,1)S(1)}, u32[]{:S(2)}, u32[]{:S(2)}) collective-permute-start(bf16[256,128]{1,0:T(8,128)(2,1)S(1)} %get-tuple-element.17), channel_id=1, source_target_pairs={{0,16},{2,18},{4,20},{6,22},{8,24},{10,26},{12,28},{14,30},{16,0},... | collective-permute-start | bytes 196616 | tf_op jit(solution)/shard_map/ppermute | solution.py:33
  30.3 2.3 %collective-permute-start.5 = (bf16[256,128]{1,0:T(8,128)(2,1)S(1)}, bf16[256,128]{1,0:T(8,128)(2,1)S(1)}, u32[]{:S(2)}, u32[]{:S(2)}) collective-permute-start(bf16[256,128]{1,0:T(8,128)(2,1)S(1)} %get-tuple-element.17), channel_id=1, source_target_pairs={{0,8},{2,10},{4,12},{6,14},{8,0},{10,2},{12,4},{14,6},{16,24},{18,... | collective-permute-start | bytes 196616 | tf_op jit(solution)/shard_map/ppermute | solution.py:33
  32.7 0.1 stack.90.at
  32.9 1.6 %collective-permute-done.7 = bf16[256,128]{1,0:T(8,128)(2,1)S(1)} collective-permute-done((bf16[256,128]{1,0:T(8,128)(2,1)S(1)}, bf16[256,128]{1,0:T(8,128)(2,1)S(1)}, u32[]{:S(2)}, u32[]{:S(2)}) %collective-permute-start.7) | collective-permute-done | bytes 65568 | tf_op jit(solution)/shard_map/ppermute | solution.py:33
  34.5 1.8 %collective-permute-done.6 = bf16[256,128]{1,0:T(8,128)(2,1)S(1)} collective-permute-done((bf16[256,128]{1,0:T(8,128)(2,1)S(1)}, bf16[256,128]{1,0:T(8,128)(2,1)S(1)}, u32[]{:S(2)}, u32[]{:S(2)}) %collective-permute-start.6) | collective-permute-done | bytes 65568 | tf_op jit(solution)/shard_map/ppermute | solution.py:33
  36.4 0.5 collective-permute-start.11
  36.9 0.9 %collective-permute-start.10 = (bf16[4,256,128]{2,1,0:T(8,128)(2,1)S(1)}, bf16[4,256,128]{2,1,0:T(8,128)(2,1)S(1)}, u32[]{:S(2)}, u32[]{:S(2)}) collective-permute-start(bf16[4,256,128]{2,1,0:T(8,128)(2,1)S(1)} %pad_maximum_fusion.w_ref), channel_id=1, source_target_pairs={{0,4},{2,6},{4,0},{6,2},{8,12},{10,14},{12,8},{14,10},{16,20},{18,... | collective-permute-start | bytes 786440 | tf_op jit(solution)/shard_map/ppermute | solution.py:33
  37.8 2.1 %collective-permute-start.8 = (bf16[4,256,128]{2,1,0:T(8,128)(2,1)S(1)}, bf16[4,256,128]{2,1,0:T(8,128)(2,1)S(1)}, u32[]{:S(2)}, u32[]{:S(2)}) collective-permute-start(bf16[4,256,128]{2,1,0:T(8,128)(2,1)S(1)} %pad_maximum_fusion.w_ref), channel_id=1, source_target_pairs={{0,6},{2,4},{4,2},{6,0},{8,14},{10,12},{12,10},{14,8},{16,22},{18,... | collective-permute-start | bytes 786440 | tf_op jit(solution)/shard_map/ppermute | solution.py:33
  39.9 1.1 %convert_bitcast_fusion = bf16[1,4096,128]{2,1,0:T(8,128)(2,1)} fusion(f32[4096,128]{1,0:T(8,128)S(1)} %get-tuple-element.21), kind=kLoop, calls=%fused_computation | loop fusion | flops 524288 | bytes 3145728 | tf_op jit(solution)/shard_map/broadcast_in_dim | solution.py:286
  41.0 3.5 %shard_map.136 = (bf16[512,4096]{1,0:T(8,128)(2,1)S(1)}, bf16[512,4096]{1,0:T(8,128)(2,1)S(1)}) custom-call(bf16[512,4096]{1,0:T(8,128)(2,1)} %refs_0_.3, bf16[512,4096]{1,0:T(8,128)(2,1)} %collective-permute-done.9.refs_1_), custom_call_target="tpu_custom_call" | custom-call | bytes 16777216 | tf_op jit(solution)/shard_map/pallas_call | solution.py:63
  44.5 1.2 %shard_map.137.refs_2_ = f32[1024,128]{1,0:T(8,128)S(1)} custom-call(s32[5]{0:T(128)S(1)} %stack.111.at, bf16[4,256,128]{2,1,0:T(8,128)(2,1)S(1)} %pad_maximum_fusion.w_ref, bf16[512,4096]{1,0:T(8,128)(2,1)S(1)} %get-tuple-element.19.refs_0_, bf16[512,4096]{1,0:T(8,128)(2,1)S(1)} %get-tuple-element.20.refs_1_), custom_call_target="tpu_custom_call" | custom-call | flops 268435456 | bytes 3145728 | tf_op jit(solution)/shard_map/pallas_call | solution.py:242
  45.8 1.2 %shard_map.138.refs_2_ = f32[1024,128]{1,0:T(8,128)S(1)} custom-call(s32[5]{0:T(128)S(1)} %stack.107.at, bf16[4,256,128]{2,1,0:T(8,128)(2,1)S(1)} %collective-permute-done.11.w_ref, bf16[512,4096]{1,0:T(8,128)(2,1)S(1)} %get-tuple-element.19.refs_0_, bf16[512,4096]{1,0:T(8,128)(2,1)S(1)} %get-tuple-element.20.refs_1_, f32[1024,128]{1,0:T(8,128)S(1)} %shard_map.137.refs_2_), custom_call_target="tpu_custom_call" | custom-call | flops 268435456 | bytes 3145728 | tf_op jit(solution)/shard_map/pallas_call | solution.py:242
  47.1 1.2 %shard_map.139.refs_2_ = f32[1024,128]{1,0:T(8,128)S(1)} custom-call(s32[5]{0:T(128)S(1)} %stack.102.at, bf16[4,256,128]{2,1,0:T(8,128)(2,1)S(1)} %collective-permute-done.10.w_ref, bf16[512,4096]{1,0:T(8,128)(2,1)S(1)} %get-tuple-element.19.refs_0_, bf16[512,4096]{1,0:T(8,128)(2,1)S(1)} %get-tuple-element.20.refs_1_, f32[1024,128]{1,0:T(8,128)S(1)} %shard_map.138.refs_2_), custom_call_target="tpu_custom_call" | custom-call | flops 268435456 | bytes 3145728 | tf_op jit(solution)/shard_map/pallas_call | solution.py:242
  48.3 1.1 %collective-permute-done.8.w_ref = bf16[4,256,128]{2,1,0:T(8,128)(2,1)S(1)} collective-permute-done((bf16[4,256,128]{2,1,0:T(8,128)(2,1)S(1)}, bf16[4,256,128]{2,1,0:T(8,128)(2,1)S(1)}, u32[]{:S(2)}, u32[]{:S(2)}) %collective-permute-start.8) | collective-permute-done | bytes 262176 | tf_op jit(solution)/shard_map/ppermute | solution.py:33
  49.4 2.0 %shard_map.140 = bf16[1024,128]{1,0:T(8,128)(2,1)} custom-call(s32[5]{0:T(128)S(1)} %stack.90.at, bf16[4,256,128]{2,1,0:T(8,128)(2,1)S(1)} %collective-permute-done.8.w_ref, bf16[512,4096]{1,0:T(8,128)(2,1)S(1)} %get-tuple-element.19.refs_0_, bf16[512,4096]{1,0:T(8,128)(2,1)S(1)} %get-tuple-element.20.refs_1_, f32[1024,128]{1,0:T(8,128)S(1)} %shard_map.139.refs_2_), custom_call_target="tpu_custom_call" | custom-call | flops 268435456 | bytes 3145728 | tf_op jit(solution)/shard_map/pallas_call | solution.py:242
  (30 shorter events, 0.6 us)
Async XLA Ops:
  0.6 2.7 %collective-permute-start = (bf16[1024,128]{1,0:T(8,128)(2,1)}, bf16[1024,128]{1,0:T(8,128)(2,1)S(1)}, u32[]{:S(2)}, u32[]{:S(2)}) collective-permute-start(bf16[1024,128]{1,0:T(8,128)(2,1)} %g_ref), channel_id=1, source_target_pairs={{0,1},{1,0},{2,3},{3,2},{4,5},{5,4},{6,7},{7,6},{8,9},{9,8},{10,11... | collective-permute-start | bytes 786440 | tf_op jit(solution)/shard_map/ppermute | solution.py:29
  3.9 4.4 %collective-permute-start.1 = (f32[1024,128]{1,0:T(8,128)S(1)}, f32[1024,128]{1,0:T(8,128)S(1)}, u32[]{:S(2)}, u32[]{:S(2)}) collective-permute-start(f32[1024,128]{1,0:T(8,128)S(1)} %shard_map.131), channel_id=1, source_target_pairs={{0,1},{1,0},{2,3},{3,2},{4,5},{5,4},{6,7},{7,6},{8,9},{9,8},{10,11... | collective-permute-start | bytes 1572872 | tf_op jit(solution)/shard_map/ppermute | solution.py:29
  4.6 2.3 %copy-start = (bf16[1,4096,128]{2,1,0:T(8,128)(2,1)S(1)}, bf16[1,4096,128]{2,1,0:T(8,128)(2,1)}, u32[]{:S(2)}) copy-start(bf16[1,4096,128]{2,1,0:T(8,128)(2,1)} %param.11) | copy-start | bytes 3145732
  4.6 2.3 %copy-start.1 = (bf16[1024,128]{1,0:T(8,128)(2,1)S(1)}, bf16[1024,128]{1,0:T(8,128)(2,1)}, u32[]{:S(2)}) copy-start(bf16[1024,128]{1,0:T(8,128)(2,1)} %g_ref) | copy-start | bytes 786436
  4.6 3.7 %collective-permute-start.2 = (f32[1024,128]{1,0:T(8,128)S(1)}, f32[1024,128]{1,0:T(8,128)S(1)}, u32[]{:S(2)}, u32[]{:S(2)}) collective-permute-start(f32[1024,128]{1,0:T(8,128)S(1)} %shard_map.132), channel_id=1, source_target_pairs={{0,1},{1,0},{2,3},{3,2},{4,5},{5,4},{6,7},{7,6},{8,9},{9,8},{10,11... | collective-permute-start | bytes 1572872 | tf_op jit(solution)/shard_map/ppermute | solution.py:29
  5.6 2.7 %collective-permute-start.3 = (f32[1024,128]{1,0:T(8,128)S(1)}, f32[1024,128]{1,0:T(8,128)S(1)}, u32[]{:S(2)}, u32[]{:S(2)}) collective-permute-start(f32[1024,128]{1,0:T(8,128)S(1)} %shard_map.133), channel_id=1, source_target_pairs={{0,1},{1,0},{2,3},{3,2},{4,5},{5,4},{6,7},{7,6},{8,9},{9,8},{10,11... | collective-permute-start | bytes 1572872 | tf_op jit(solution)/shard_map/ppermute | solution.py:29
  6.3 2.5 %copy-start.6 = (s32[17]{0:T(128)S(1)}, s32[17]{0:T(128)}, u32[]{:S(2)}) copy-start(s32[17]{0:T(128)} %param.13) | copy-start | bytes 208
  6.3 2.5 %copy-start.5 = (s32[1,1,32]{2,1,0:T(1,128)S(1)}, s32[1,1,32]{2,1,0:T(1,128)}, u32[]{:S(2)}) copy-start(s32[1,1,32]{2,1,0:T(1,128)} %param.12) | copy-start | bytes 388
  6.3 2.1 %collective-permute-start.4 = (f32[1024,128]{1,0:T(8,128)S(1)}, f32[1024,128]{1,0:T(8,128)S(1)}, u32[]{:S(2)}, u32[]{:S(2)}) collective-permute-start(f32[1024,128]{1,0:T(8,128)S(1)} %shard_map.129), channel_id=1, source_target_pairs={{0,1},{1,0},{2,3},{3,2},{4,5},{5,4},{6,7},{7,6},{8,9},{9,8},{10,11... | collective-permute-start | bytes 1572872 | tf_op jit(solution)/shard_map/ppermute | solution.py:29
  6.8 19.6 %copy-start.2 = (f32[256,128]{1,0:T(8,128)S(1)}, f32[256,128]{1,0:T(8,128)}, u32[]{:S(2)}) copy-start(f32[256,128]{1,0:T(8,128)} %m_ref.1) | copy-start | bytes 393220
  6.8 19.6 %copy-start.3 = (f32[256,128]{1,0:T(8,128)S(1)}, f32[256,128]{1,0:T(8,128)}, u32[]{:S(2)}) copy-start(f32[256,128]{1,0:T(8,128)} %v_ref.1) | copy-start | bytes 393220
  6.8 19.6 %copy-start.4 = (f32[256,128]{1,0:T(8,128)S(1)}, f32[256,128]{1,0:T(8,128)}, u32[]{:S(2)}) copy-start(f32[256,128]{1,0:T(8,128)} %w_ref.1) | copy-start | bytes 393220
  8.4 32.6 %collective-permute-start.9 = (bf16[512,4096]{1,0:T(8,128)(2,1)}, bf16[512,4096]{1,0:T(8,128)(2,1)}, u32[]{:S(2)}, u32[]{:S(2)}) collective-permute-start(bf16[512,4096]{1,0:T(8,128)(2,1)} %refs_0_.3), channel_id=1, source_target_pairs={{0,1},{1,0},{2,3},{3,2},{4,5},{5,4},{6,7},{7,6},{8,9},{9,8},{10,11... | collective-permute-start | bytes 12582920 | tf_op jit(solution)/shard_map/ppermute | solution.py:29
  10.9 15.6 %all-to-all-start = ((f32[16,8,128]{2,1,0:T(8,128)}), f32[16,8,128]{2,1,0:T(8,128)S(1)}, u32[]{:S(2)}, u32[]{:S(2)}) async-start(f32[16,8,128]{2,1,0:T(8,128)} %bitcast.10), calls=%async_computation | async-start | bytes 131072 | tf_op jit(solution)/shard_map/all_to_all | solution.py:289
  28.2 6.3 %collective-permute-start.7 = (bf16[256,128]{1,0:T(8,128)(2,1)S(1)}, bf16[256,128]{1,0:T(8,128)(2,1)S(1)}, u32[]{:S(2)}, u32[]{:S(2)}) collective-permute-start(bf16[256,128]{1,0:T(8,128)(2,1)S(1)} %get-tuple-element.17), channel_id=1, source_target_pairs={{0,24},{2,26},{4,28},{6,30},{8,16},{10,18},{12,20},{14,22},{16,8},... | collective-permute-start | bytes 196616 | tf_op jit(solution)/shard_map/ppermute | solution.py:33
  29.1 7.2 %collective-permute-start.6 = (bf16[256,128]{1,0:T(8,128)(2,1)S(1)}, bf16[256,128]{1,0:T(8,128)(2,1)S(1)}, u32[]{:S(2)}, u32[]{:S(2)}) collective-permute-start(bf16[256,128]{1,0:T(8,128)(2,1)S(1)} %get-tuple-element.17), channel_id=1, source_target_pairs={{0,16},{2,18},{4,20},{6,22},{8,24},{10,26},{12,28},{14,30},{16,0},... | collective-permute-start | bytes 196616 | tf_op jit(solution)/shard_map/ppermute | solution.py:33
  30.3 6.0 %collective-permute-start.5 = (bf16[256,128]{1,0:T(8,128)(2,1)S(1)}, bf16[256,128]{1,0:T(8,128)(2,1)S(1)}, u32[]{:S(2)}, u32[]{:S(2)}) collective-permute-start(bf16[256,128]{1,0:T(8,128)(2,1)S(1)} %get-tuple-element.17), channel_id=1, source_target_pairs={{0,8},{2,10},{4,12},{6,14},{8,0},{10,2},{12,4},{14,6},{16,24},{18,... | collective-permute-start | bytes 196616 | tf_op jit(solution)/shard_map/ppermute | solution.py:33
  36.4 9.4 %collective-permute-start.11 = (bf16[4,256,128]{2,1,0:T(8,128)(2,1)S(1)}, bf16[4,256,128]{2,1,0:T(8,128)(2,1)S(1)}, u32[]{:S(2)}, u32[]{:S(2)}) collective-permute-start(bf16[4,256,128]{2,1,0:T(8,128)(2,1)S(1)} %pad_maximum_fusion.w_ref), channel_id=1, source_target_pairs={{0,2},{2,0},{4,6},{6,4},{8,10},{10,8},{12,14},{14,12},{16,18},{18,... | collective-permute-start | bytes 786440 | tf_op jit(solution)/shard_map/ppermute | solution.py:33
  36.9 10.2 %collective-permute-start.10 = (bf16[4,256,128]{2,1,0:T(8,128)(2,1)S(1)}, bf16[4,256,128]{2,1,0:T(8,128)(2,1)S(1)}, u32[]{:S(2)}, u32[]{:S(2)}) collective-permute-start(bf16[4,256,128]{2,1,0:T(8,128)(2,1)S(1)} %pad_maximum_fusion.w_ref), channel_id=1, source_target_pairs={{0,4},{2,6},{4,0},{6,2},{8,12},{10,14},{12,8},{14,10},{16,20},{18,... | collective-permute-start | bytes 786440 | tf_op jit(solution)/shard_map/ppermute | solution.py:33
  37.8 11.6 %collective-permute-start.8 = (bf16[4,256,128]{2,1,0:T(8,128)(2,1)S(1)}, bf16[4,256,128]{2,1,0:T(8,128)(2,1)S(1)}, u32[]{:S(2)}, u32[]{:S(2)}) collective-permute-start(bf16[4,256,128]{2,1,0:T(8,128)(2,1)S(1)} %pad_maximum_fusion.w_ref), channel_id=1, source_target_pairs={{0,6},{2,4},{4,2},{6,0},{8,14},{10,12},{12,10},{14,8},{16,22},{18,... | collective-permute-start | bytes 786440 | tf_op jit(solution)/shard_map/ppermute | solution.py:33
where the time goes:
time: 51.6 us; the launch traced here: 51.4 us
  Pallas kernels  18.7 us (36%)
  starting transfers between devices  18.1 us (35%)
  waiting for transfers between devices  11.4 us (22%)
  between operations  1.48 us (3%)
  other arithmetic  1.18 us (2%)
    all_to_all x1, starting transfers between devices, shards(): lax.all_to_all(outgoing.reshape(owners, SLOTS, width), 'dp', split_axis=0...  8.02 us
    ppermute x6, starting transfers between devices, swap(): lax.ppermute(x, axis, [(i, i ^ mask) for i in range(lax.axis_size(axis))])  7.94 us
    all_to_all x1, waiting for transfers between devices, shards(): lax.all_to_all(outgoing.reshape(owners, SLOTS, width), 'dp', split_axis=0...  6.81 us
    pallas_call x2, Pallas kernels, load(): pl.pallas_call(functools.partial(load_kernel, pieces), in_specs=[ANY] * l...  5.72 us
    pallas_call x4, Pallas kernels, project(): pl.pallas_call(functools.partial(project_kernel, last, len(feats)), in_sp...  5.69 us
    ppermute x6, waiting for transfers between devices, swap(): lax.ppermute(x, axis, [(i, i ^ mask) for i in range(lax.axis_size(axis))])  4.53 us
    pallas_call x5, Pallas kernels, part_sum(): pl.pallas_call(functools.partial(part_kernel, first), in_specs=[SMEM, VME...  3.49 us
    ppermute x6, starting transfers between devices, shift(): return lax.ppermute(x, axis, [(i, (i + step) % n) for i in range(n)])  2.17 us
  transfers between devices with their start and end apart: 13, of which 5 were waited for; matrix products, arithmetic and copies ran while one was open for 3% of the time, Pallas kernels for 32%

commit v1 on v0

--- a/solution.py
+++ b/solution.py
@@ -42,33 +42,56 @@
     return pl.CostEstimate(flops=flops, bytes_accessed=nbytes, transcendentals=0)
 
 
-def load_kernel(pieces, *refs):
-    n = len(refs) // 2
-    sources, targets, sem = refs[:n], refs[n : 2 * n], refs[2 * n]
+def load_kernel(pieces, n, *refs):
+    sources, refs = refs[:n], refs[n:]
+    state, refs = (refs[:3], refs[3:]) if len(refs) > n + 1 else ((), refs)
     copies = []
+    if state:
+        held, s_sem, refs = refs[-2], refs[-1], refs[:-2]
+        copies = [
+            pltpu.make_async_copy(ref, held.at[i], s_sem.at[i]) for i, ref in enumerate(state)
+        ]
+        for copy in copies:
+            copy.start()
+        base, refs = refs[0], refs[1:]
+    targets, sem = refs[:n], refs[n]
+    moves = []
     for i in range(n):
         rows = sources[i].shape[0] // pieces
         for j in range(pieces):
             part = pl.ds(j * rows, rows)
-            copies.append(
+            moves.append(
                 pltpu.make_async_copy(sources[i].at[part], targets[i].at[part], sem.at[i, j])
             )
-            copies[-1].start()
+            moves[-1].start()
     for copy in copies:
         copy.wait()
-
-
-def load(arrays):
+    if state:
+        grad = jnp.zeros(base.shape, jnp.float32)
+        base[...] = adam_step(held[0], held[1], held[2], grad)[2].astype(base.dtype)
+    for move in moves:
+        move.wait()
+
+
+def load(arrays, *state):
     pieces = 8
+    base, scratch = [], []
+    if state:
+        base = [jax.ShapeDtypeStruct(state[0].shape, jnp.bfloat16)]
+        scratch = [
+            pltpu.VMEM((len(state), *state[0].shape), jnp.float32),
+            pltpu.SemaphoreType.DMA((len(state),)),
+        ]
+    fixed = [pltpu.with_memory_space_constraint(a, pltpu.HBM) for a in (*arrays, *state)]
     return pl.pallas_call(
-        functools.partial(load_kernel, pieces),
-        in_specs=[ANY] * len(arrays),
-        out_specs=[VMEM] * len(arrays),
-        out_shape=[pltpu.VMEM(a.shape, a.dtype) for a in arrays],
-        scratch_shapes=[pltpu.SemaphoreType.DMA((len(arrays), pieces))],
-        compiler_params=params(*arrays),
+        functools.partial(load_kernel, pieces, len(arrays)),
+        in_specs=[ANY] * len(fixed),
+        out_specs=[VMEM] * (len(base) + len(arrays)),
+        out_shape=base + [pltpu.VMEM(a.shape, a.dtype) for a in arrays],
+        scratch_shapes=[pltpu.SemaphoreType.DMA((len(arrays), pieces))] + scratch,
+        compiler_params=params(*arrays, *state, *base),
         cost_estimate=cost(0, 4 * sum(a.size for a in arrays)),
-    )(*[pltpu.with_memory_space_constraint(a, pltpu.HBM) for a in arrays])
+    )(*fixed)
 
 
 def part_kernel(first, core, f_ref, g_ref, *rest):
@@ -159,6 +182,17 @@
     )(selected, lo, hi, own, *parts)
 
 
+def adam_step(moment, second, master, grad):
+    moment_new = beta_first * moment + (1.0 - beta_first) * grad
+    second_new = beta_second * second + (1.0 - beta_second) * grad * grad
+    first_hat = moment_new / (1.0 - beta_first**step_count)
+    second_hat = second_new / (1.0 - beta_second**step_count)
+    master_new = master - learn_rate * (
+        first_hat / (jnp.sqrt(second_hat) + adam_epsilon) + decay_rate * master
+    )
+    return moment_new, second_new, master_new
+
+
 def adam_kernel(bins, info, lo_ref, hi_ref, arr_ref, m_ref, v_ref, w_ref, mo, vo, wo, bo):
     owners, slots, width = arr_ref.shape
     region = m_ref.shape[0]
@@ -190,43 +224,72 @@
         precision=lax.Precision.HIGHEST,
         preferred_element_type=jnp.float32,
     )
-    grad = grad * row_scale
-    master = w_ref[...]
-    moment_new = beta_first * m_ref[...] + (1.0 - beta_first) * grad
-    second_new = beta_second * v_ref[...] + (1.0 - beta_second) * grad * grad
-    first_hat = moment_new / (1.0 - beta_first**step_count)
-    second_hat = second_new / (1.0 - beta_second**step_count)
-    master_new = master - learn_rate * (
-        first_hat / (jnp.sqrt(second_hat) + adam_epsilon) + decay_rate * master
+    moment_new, second_new, master_new = adam_step(
+        m_ref[...], v_ref[...], w_ref[...], grad * row_scale
     )
     mo[...] = moment_new
     vo[...] = second_new
     wo[...] = master_new
-    bo[...] = master_new.astype(jnp.bfloat16)
-
-
-def adam(info, lo, hi, arrived, moment, second, master, bins):
+    weight = master_new.astype(jnp.bfloat16)
+    if bo.shape[0] == region:
+        bo[...] = weight
+        return
+    sent = bo.shape[0]
+    at = lax.broadcasted_iota(jnp.int32, (owners * slots, sent), 0)
+    dense = (at // slots) * CAP + at % slots
+    to = lax.broadcasted_iota(jnp.int32, (owners * slots, sent), 1)
+    there = (dense == to) & (at % slots < CAP)
+    number = jnp.sum(jnp.where(there, offset + 1.0, 0.0), axis=0, keepdims=True) - 1.0
+    again = (offset == number) & (dense < to) & (at % slots < CAP)
+    number = jnp.where(jnp.sum(jnp.where(again, 1.0, 0.0), axis=0, keepdims=True) > 0, -1.0, number)
+    pick = jnp.where(
+        lax.broadcasted_iota(jnp.int32, (region, sent), 0).astype(jnp.float32) == number, 1.0, 0.0
+    )
+    rows = lax.dot_general(
+        pick.astype(jnp.bfloat16),
+        weight,
+        (((0,), (0,)), ((), ())),
+        preferred_element_type=jnp.float32,
+    )
+    wide = jnp.concatenate([number, jnp.full((1, width - sent), -1.0, jnp.float32)], axis=1)
+    last = lax.broadcasted_iota(jnp.int32, (sent, width), 0) == owners * CAP
+    bo[...] = jnp.where(last, wide, rows).astype(jnp.bfloat16)
+
+
+def adam(info, lo, hi, arrived, moment, second, master, bins, sent):
     f32 = jax.ShapeDtypeStruct(master.shape, jnp.float32)
     return pl.pallas_call(
         functools.partial(adam_kernel, bins),
         in_specs=[SMEM] + [VMEM] * 6,
         out_specs=[VMEM] * 4,
-        out_shape=[f32, f32, f32, jax.ShapeDtypeStruct(master.shape, jnp.bfloat16)],
+        out_shape=[f32, f32, f32, jax.ShapeDtypeStruct((sent, master.shape[1]), jnp.bfloat16)],
         compiler_params=params(arrived, arrived, *[f32] * 7),
         cost_estimate=cost(2 * 6 * arrived.size * master.shape[0], 30 * master.size),
     )(info, lo, hi, arrived, moment, second, master)
 
 
-def project_kernel(last, n_f, at, w_ref, *refs):
+def project_kernel(last, n_slots, n_f, at, base_ref, new_ref, *refs):
     feats, old, out_ref = refs[:n_f], refs[n_f:-1], refs[-1]
-    count, region, width = w_ref.shape
+    count, region, width = base_ref.shape
+    sent = new_ref.shape[1]
     tokens = feats[0].shape[0]
+    ids = lax.broadcasted_iota(jnp.int32, (region, sent), 0).astype(jnp.float32)
+    weights = []
+    for j in range(count):
+        rows = new_ref[j]
+        number = rows[n_slots : n_slots + 1, :sent].astype(jnp.float32)
+        pick = jnp.where(ids == number, 1.0, 0.0)
+        put = jnp.dot(pick.astype(jnp.bfloat16), rows, preferred_element_type=jnp.float32)
+        hit = jnp.max(pick, axis=1, keepdims=True) > 0
+        weights.append(
+            jnp.where(hit, put, base_ref[j].astype(jnp.float32)).astype(jnp.bfloat16)
+        )
     for i, f_ref in enumerate(feats):
         mine = pl.ds(i * tokens, tokens)
         total = old[0][mine, :] if old else None
         for j in range(count):
             cols = pl.ds(pl.multiple_of(at[j] * region, region), region)
-            part = jnp.dot(f_ref[:, cols], w_ref[j], preferred_element_type=jnp.float32)
+            part = jnp.dot(f_ref[:, cols], weights[j], preferred_element_type=jnp.float32)
             total = part if total is None else total + part
         if last:
             place = lax.rem(at[count] + i, n_f) * tokens
@@ -234,21 +297,21 @@
         out_ref[mine, :] = total.astype(out_ref.dtype)
 
 
-def project(at, feats, pieces, total, last):
-    count, region, width = pieces.shape
+def project(at, feats, base, changed, total, last, n_slots):
+    count, region, width = base.shape
     whole = len(feats) * feats[0].shape[0]
     old = [] if total is None else [total]
     out = jax.ShapeDtypeStruct((whole, width), jnp.bfloat16 if last else jnp.float32)
     return pl.pallas_call(
-        functools.partial(project_kernel, last, len(feats)),
-        in_specs=[SMEM, VMEM] + [VMEM] * (len(feats) + len(old)),
+        functools.partial(project_kernel, last, n_slots, len(feats)),
+        in_specs=[SMEM, VMEM, VMEM] + [VMEM] * (len(feats) + len(old)),
         out_specs=VMEM,
         out_shape=out,
-        compiler_params=params(pieces, out, *feats, *old),
+        compiler_params=params(base, changed, out, *feats, *old),
         cost_estimate=cost(
             2 * whole * count * region * width, 2 * whole * count * region + 8 * whole * width
         ),
-    )(at, pieces, *feats, *old)
+    )(at, base, changed, *feats, *old)
 
 
 def spans(mask_bits):
@@ -270,7 +333,13 @@
     hi = jnp.pad(bin_edges[1:], pad)[None]
     core1 = core.reshape(1).astype(jnp.int32)
 
-    [held] = load([features])
+    bits = [1 << i for i in range(owners.bit_length() - 1)]
+    n_slots = owners * CAP
+    sent = (n_slots + 16) // 16 * 16
+    fast = 1 << len(bits) == owners and len(bits) > 2 and region % LANES == 0
+    fast = fast and sent <= LANES and region <= 256
+
+    base, held = load([features], moment, second, master)
     n_chunks = 4 if cores == 2 else 1
     count = rows // n_chunks
     made, got = [], []
@@ -290,27 +359,35 @@
         outgoing.reshape(owners, SLOTS, width), "dp", split_axis=0, concat_axis=0, tiled=True
     )
     info = jnp.stack([me.astype(jnp.int32), threshold[0]])
-    moment_new, second_new, master_new, weight = adam(
-        info, lo, hi, arrived, moment, second, master, bins
-    )
-
-    bits = [1 << i for i in range(owners.bit_length() - 1)]
-    if 1 << len(bits) == owners and len(bits) > 2 and region % LANES == 0:
+    moment_new, second_new, master_new, changed = adam(
+        info, lo, hi, arrived, moment, second, master, bins, sent if fast else region
+    )
+
+    if fast:
         plane, line = spans(bits[:2]), spans(bits[2:])
-        mine = jnp.stack([weight if m == 0 else swap(weight, "dp", m) for m in line])
+
+        def along(x):
+            return jnp.stack([x if m == 0 else swap(x, "dp", m) for m in line])
+
+        def across(x):
+            return [x if b == 0 else swap(x, "dp", b) for b in plane]
+
+        early, _ = lax.optimization_barrier((base, own))
+        bases = across(along(early))
+        changes = across(along(changed))
         feats = load(feats)
         total = None
         for j, b in enumerate(plane):
-            here = mine if b == 0 else swap(mine, "dp", b)
             at = jnp.stack([me ^ (b ^ m) for m in line] + [core]).astype(jnp.int32)
-            total = project(at, feats, here, total, j == len(plane) - 1)
+            final = j == len(plane) - 1
+            total = project(at, feats, bases[j], changes[j], total, final, n_slots)
         keys = total
     else:
         whole = jnp.concatenate(feats, axis=0)
         whole = jnp.roll(whole, core * tokens, axis=0)
         keys = jnp.dot(
             whole,
-            lax.all_gather(weight, "dp", axis=0, tiled=True),
+            lax.all_gather(changed, "dp", axis=0, tiled=True),
             preferred_element_type=jnp.float32,
         ).astype(jnp.bfloat16)
     return (keys, error_out, moment_new, second_new, master_new)

time: 51.6 us -> 57.3 us (1.11)
  starting transfers between devices: 18.1 us -> 26.7 us
  waiting for transfers between devices: 11.4 us -> 7.67 us
  Pallas kernels: 18.7 us -> 19.5 us
    ppermute x6 -> x12, starting transfers between devices: 7.94 us -> 17.4 us  [swap(): lax.ppermute(x, axis, [(i, i ^ mask) for i in range(lax.axis_size(axis))])]
    all_to_all x1, waiting for transfers between devices: 6.81 us -> 4.84 us  [shards(): lax.all_to_all(outgoing.reshape(owners, SLOTS, width), 'dp', split_axis=0...]
    ppermute x6 -> x12, waiting for transfers between devices: 4.53 us -> 2.76 us  [swap(): lax.ppermute(x, axis, [(i, i ^ mask) for i in range(lax.axis_size(axis))])]
    all_to_all x1, starting transfers between devices: 8.02 us -> 7.08 us  [shards(): lax.all_to_all(outgoing.reshape(owners, SLOTS, width), 'dp', split_axis=0...]
    pallas_call x6, Pallas kernels: 11.4 us -> 12.2 us  [the longest x4 6.34 us: project(): pl.pallas_call(functools.partial(project_kernel, last, n_slots, len(feats...]
  transfers between devices with their start and end apart: 13 -> 19, of which waited for: 5 -> 5; matrix products, arithmetic and copies ran while one was open for 3% -> 3% of each run, Pallas kernels for 32% -> 30%
where the time goes in v1:
time: 57.3 us; the launch traced here: 57 us
  starting transfers between devices  26.7 us (47%)
  Pallas kernels  19.5 us (34%)
  waiting for transfers between devices  7.67 us (13%)
  between operations  1.53 us (3%)
  other arithmetic  1.2 us (2%)
    ppermute x12, starting transfers between devices, swap(): lax.ppermute(x, axis, [(i, i ^ mask) for i in range(lax.axis_size(axis))])  17.4 us
    all_to_all x1, starting transfers between devices, shards(): lax.all_to_all(outgoing.reshape(owners, SLOTS, width), 'dp', split_axis=0...  7.08 us
    pallas_call x4, Pallas kernels, project(): pl.pallas_call(functools.partial(project_kernel, last, n_slots, len(feats...  6.34 us
    pallas_call x2, Pallas kernels, load(): pl.pallas_call(functools.partial(load_kernel, pieces, len(arrays)), in_sp...  5.87 us
    all_to_all x1, waiting for transfers between devices, shards(): lax.all_to_all(outgoing.reshape(owners, SLOTS, width), 'dp', split_axis=0...  4.84 us
    pallas_call x5, Pallas kernels, part_sum(): pl.pallas_call(functools.partial(part_kernel, first), in_specs=[SMEM, VME...  3.49 us
    ppermute x12, waiting for transfers between devices, swap(): lax.ppermute(x, axis, [(i, i ^ mask) for i in range(lax.axis_size(axis))])  2.76 us
    ppermute x6, starting transfers between devices, shift(): return lax.ppermute(x, axis, [(i, (i + step) % n) for i in range(n)])  2.17 us
  transfers between devices with their start and end apart: 19, of which 5 were waited for; matrix products, arithmetic and copies ran while one was open for 3% of the time, Pallas kernels for 30%

profile of v1, /device:TPU:0, one launch (start us, length us, event | category | flops | bytes accessed | tf_op | source)
XLA Modules:
  0.0 57.0 jit_solution(12450534648566957145)
XLA Ops:
  0.6 0.5 collective-permute-start
  1.1 2.4 %shard_map.128 = (bf16[256,128]{1,0:T(8,128)(2,1)S(1)}, bf16[512,4096]{1,0:T(8,128)(2,1)S(1)}) custom-call(bf16[512,4096]{1,0:T(8,128)(2,1)} %refs_0_.3, f32[256,128]{1,0:T(8,128)} %m_ref.1, f32[256,128]{1,0:T(8,128)} %v_ref.1, f32[256,128]{1,0:T(8,128)} %w_ref.1), custom_call_target="tpu_custom_call" | custom-call | bytes 8388608 | tf_op jit(solution)/shard_map/pallas_call | solution.py:86
  3.5 0.5 shard_map.129
  4.2 0.5 shard_map.131
  4.7 0.5 collective-permute-start.5
  5.3 0.5 shard_map.132
  5.9 0.5 shard_map.133
  6.5 0.5 collective-permute-start.7
  7.0 1.4 %shard_map.130.own_ref = f32[4096,128]{1,0:T(8,128)S(1)} custom-call(s32[1]{0:T(128)} %bitcast.4.core, bf16[512,4096]{1,0:T(8,128)(2,1)S(1)} %get-tuple-element.19.f_ref, bf16[1024,128]{1,0:T(8,128)(2,1)S(1)} %copy-done.4, bf16[4096,128]{1,0:T(8,128)(2,1)S(1)} %bitcast.34), custom_call_target="tpu_custom_call" | custom-call | flops 536870912 | bytes 6291456 | tf_op jit(solution)/shard_map/pallas_call | solution.py:118
  9.0 2.7 %collective-permute-start.1 = (bf16[256,128]{1,0:T(8,128)(2,1)S(1)}, bf16[256,128]{1,0:T(8,128)(2,1)S(1)}, u32[]{:S(2)}, u32[]{:S(2)}) collective-permute-start(bf16[256,128]{1,0:T(8,128)(2,1)S(1)} %get-tuple-element.21), channel_id=1, source_target_pairs={{0,8},{2,10},{4,12},{6,14},{8,0},{10,2},{12,4},{14,6},{16,24},{18,... | collective-permute-start | bytes 196616 | tf_op jit(solution)/shard_map/ppermute | solution.py:33
  11.7 2.6 %collective-permute-start.2 = (bf16[256,128]{1,0:T(8,128)(2,1)S(1)}, bf16[256,128]{1,0:T(8,128)(2,1)S(1)}, u32[]{:S(2)}, u32[]{:S(2)}) collective-permute-start(bf16[256,128]{1,0:T(8,128)(2,1)S(1)} %get-tuple-element.21), channel_id=1, source_target_pairs={{0,16},{2,18},{4,20},{6,22},{8,24},{10,26},{12,28},{14,30},{16,0},... | collective-permute-start | bytes 196616 | tf_op jit(solution)/shard_map/ppermute | solution.py:33
  14.3 2.1 %shard_map.134 = (f32[4096,128]{1,0:T(8,128)S(1)}, f32[128,128]{1,0:T(8,128)}) custom-call(s32[32]{0:T(128)S(1)} %bitcast.37, s32[1,128]{1,0:T(1,128)S(1)} %get-tuple-element.34.lo_ref, s32[1,128]{1,0:T(1,128)S(1)} %get-tuple-element.33.hi_ref, f32[4096,128]{1,0:T(8,128)S(1)} %shard_map.130.own_ref, f32[1024,128]{1,0:T(8,128)S(1)} %collective-permute-done.5.refs_0_, ...), custom_call_target="tpu_custom_call" | custom-call | flops 4194304 | bytes 6291456 | tf_op jit(solution)/shard_map/pallas_call | solution.py:171
  16.4 7.1 %all-to-all-start = ((f32[16,8,128]{2,1,0:T(8,128)}), f32[16,8,128]{2,1,0:T(8,128)S(1)}, u32[]{:S(2)}, u32[]{:S(2)}) async-start(f32[16,8,128]{2,1,0:T(8,128)} %bitcast.14), calls=%async_computation | async-start | bytes 131072 | tf_op jit(solution)/shard_map/all_to_all | solution.py:358
  23.5 2.0 %collective-permute-start.16 = (bf16[4,256,128]{2,1,0:T(8,128)(2,1)S(1)}, bf16[4,256,128]{2,1,0:T(8,128)(2,1)S(1)}, u32[]{:S(2)}, u32[]{:S(2)}) collective-permute-start(bf16[4,256,128]{2,1,0:T(8,128)(2,1)S(1)} %pad_maximum_fusion.base_ref), channel_id=1, source_target_pairs={{0,2},{2,0},{4,6},{6,4},{8,10},{10,8},{12,14},{14,12},{16,18},{18,... | collective-permute-start | bytes 786440 | tf_op jit(solution)/shard_map/ppermute | solution.py:33
  26.3 4.8 %all-to-all-done.arr_ref = f32[16,8,128]{2,1,0:T(8,128)S(1)} async-done(((f32[16,8,128]{2,1,0:T(8,128)}), f32[16,8,128]{2,1,0:T(8,128)S(1)}, u32[]{:S(2)}, u32[]{:S(2)}) %all-to-all-start) | async-done | bytes 65568 | tf_op jit(solution)/shard_map/all_to_all | solution.py:358
  31.1 1.7 %shard_map.135 = (f32[256,128]{1,0:T(8,128)}, f32[256,128]{1,0:T(8,128)}, f32[256,128]{1,0:T(8,128)}, bf16[112,128]{1,0:T(8,128)(2,1)S(1)}) custom-call(s32[2]{0:T(128)S(1)} %pad_add_fusion.info, s32[1,128]{1,0:T(1,128)S(1)} %get-tuple-element.34.lo_ref, s32[1,128]{1,0:T(1,128)S(1)} %get-tuple-element.33.hi_ref, f32[16,8,128]{2,1,0:T(8,128)S(1)} %all-to-all-done.arr_ref, ...), custom_call_target="tpu_custom_call" | custom-call | flops 50331648 | bytes 983040 | tf_op jit(solution)/shard_map/pallas_call | solution.py:261
  32.8 0.7 %collective-permute-start.9 = (bf16[112,128]{1,0:T(8,128)(2,1)S(1)}, bf16[112,128]{1,0:T(8,128)(2,1)S(1)}, u32[]{:S(2)}, u32[]{:S(2)}) collective-permute-start(bf16[112,128]{1,0:T(8,128)(2,1)S(1)} %get-tuple-element.23), channel_id=1, source_target_pairs={{0,8},{2,10},{4,12},{6,14},{8,0},{10,2},{12,4},{14,6},{16,24},{18,... | collective-permute-start | bytes 86024 | tf_op jit(solution)/shard_map/ppermute | solution.py:33
  33.5 0.7 %collective-permute-start.10 = (bf16[112,128]{1,0:T(8,128)(2,1)S(1)}, bf16[112,128]{1,0:T(8,128)(2,1)S(1)}, u32[]{:S(2)}, u32[]{:S(2)}) collective-permute-start(bf16[112,128]{1,0:T(8,128)(2,1)S(1)} %get-tuple-element.23), channel_id=1, source_target_pairs={{0,16},{2,18},{4,20},{6,22},{8,24},{10,26},{12,28},{14,30},{16,0},... | collective-permute-start | bytes 86024 | tf_op jit(solution)/shard_map/ppermute | solution.py:33
  34.2 3.0 %collective-permute-start.11 = (bf16[112,128]{1,0:T(8,128)(2,1)S(1)}, bf16[112,128]{1,0:T(8,128)(2,1)S(1)}, u32[]{:S(2)}, u32[]{:S(2)}) collective-permute-start(bf16[112,128]{1,0:T(8,128)(2,1)S(1)} %get-tuple-element.23), channel_id=1, source_target_pairs={{0,24},{2,26},{4,28},{6,30},{8,16},{10,18},{12,20},{14,22},{16,8},... | collective-permute-start | bytes 86024 | tf_op jit(solution)/shard_map/ppermute | solution.py:33
  37.6 0.7 %collective-permute-start.14 = (bf16[4,256,128]{2,1,0:T(8,128)(2,1)S(1)}, bf16[4,256,128]{2,1,0:T(8,128)(2,1)S(1)}, u32[]{:S(2)}, u32[]{:S(2)}) collective-permute-start(bf16[4,256,128]{2,1,0:T(8,128)(2,1)S(1)} %pad_maximum_fusion.base_ref), channel_id=1, source_target_pairs={{0,4},{2,6},{4,0},{6,2},{8,12},{10,14},{12,8},{14,10},{16,20},{18,... | collective-permute-start | bytes 786440 | tf_op jit(solution)/shard_map/ppermute | solution.py:33
  38.3 1.5 %collective-permute-start.4 = (bf16[4,256,128]{2,1,0:T(8,128)(2,1)S(1)}, bf16[4,256,128]{2,1,0:T(8,128)(2,1)S(1)}, u32[]{:S(2)}, u32[]{:S(2)}) collective-permute-start(bf16[4,256,128]{2,1,0:T(8,128)(2,1)S(1)} %pad_maximum_fusion.base_ref), channel_id=1, source_target_pairs={{0,6},{2,4},{4,2},{6,0},{8,14},{10,12},{12,10},{14,8},{16,22},{18,... | collective-permute-start | bytes 786440 | tf_op jit(solution)/shard_map/ppermute | solution.py:33
  39.9 1.2 %collective-permute-start.17 = (bf16[4,112,128]{2,1,0:T(8,128)(2,1)S(1)}, bf16[4,112,128]{2,1,0:T(8,128)(2,1)S(1)}, u32[]{:S(2)}, u32[]{:S(2)}) collective-permute-start(bf16[4,112,128]{2,1,0:T(8,128)(2,1)S(1)} %pad_maximum_fusion.1.new_ref), channel_id=1, source_target_pairs={{0,2},{2,0},{4,6},{6,4},{8,10},{10,8},{12,14},{14,12},{16,18},{18,... | collective-permute-start | bytes 344072 | tf_op jit(solution)/shard_map/ppermute | solution.py:33
  41.2 0.7 %collective-permute-start.15 = (bf16[4,112,128]{2,1,0:T(8,128)(2,1)S(1)}, bf16[4,112,128]{2,1,0:T(8,128)(2,1)S(1)}, u32[]{:S(2)}, u32[]{:S(2)}) collective-permute-start(bf16[4,112,128]{2,1,0:T(8,128)(2,1)S(1)} %pad_maximum_fusion.1.new_ref), channel_id=1, source_target_pairs={{0,4},{2,6},{4,0},{6,2},{8,12},{10,14},{12,8},{14,10},{16,20},{18,... | collective-permute-start | bytes 344072 | tf_op jit(solution)/shard_map/ppermute | solution.py:33
  41.9 1.6 %collective-permute-start.12 = (bf16[4,112,128]{2,1,0:T(8,128)(2,1)S(1)}, bf16[4,112,128]{2,1,0:T(8,128)(2,1)S(1)}, u32[]{:S(2)}, u32[]{:S(2)}) collective-permute-start(bf16[4,112,128]{2,1,0:T(8,128)(2,1)S(1)} %pad_maximum_fusion.1.new_ref), channel_id=1, source_target_pairs={{0,6},{2,4},{4,2},{6,0},{8,14},{10,12},{12,10},{14,8},{16,22},{18,... | collective-permute-start | bytes 344072 | tf_op jit(solution)/shard_map/ppermute | solution.py:33
  43.5 1.1 %convert_bitcast_fusion = bf16[1,4096,128]{2,1,0:T(8,128)(2,1)} fusion(f32[4096,128]{1,0:T(8,128)S(1)} %get-tuple-element.27), kind=kLoop, calls=%fused_computation | loop fusion | flops 524288 | bytes 3145728 | tf_op jit(solution)/shard_map/broadcast_in_dim | solution.py:355
  44.6 3.5 %shard_map.136 = (bf16[512,4096]{1,0:T(8,128)(2,1)S(1)}, bf16[512,4096]{1,0:T(8,128)(2,1)S(1)}) custom-call(bf16[512,4096]{1,0:T(8,128)(2,1)} %refs_0_.3, bf16[512,4096]{1,0:T(8,128)(2,1)} %collective-permute-done.13.refs_1_), custom_call_target="tpu_custom_call" | custom-call | bytes 16777216 | tf_op jit(solution)/shard_map/pallas_call | solution.py:86
  48.1 1.4 %shard_map.137.refs_2_ = f32[1024,128]{1,0:T(8,128)S(1)} custom-call(s32[5]{0:T(128)S(1)} %stack.131.at, bf16[4,256,128]{2,1,0:T(8,128)(2,1)S(1)} %pad_maximum_fusion.base_ref, bf16[4,112,128]{2,1,0:T(8,128)(2,1)S(1)} %pad_maximum_fusion.1.new_ref, bf16[512,4096]{1,0:T(8,128)(2,1)S(1)} %get-tuple-element.25.refs_0_, ...), custom_call_target="tpu_custom_call" | custom-call | flops 268435456 | bytes 3145728 | tf_op jit(solution)/shard_map/pallas_call | solution.py:305
  49.5 1.4 %shard_map.138.refs_2_ = f32[1024,128]{1,0:T(8,128)S(1)} custom-call(s32[5]{0:T(128)S(1)} %stack.127.at, bf16[4,256,128]{2,1,0:T(8,128)(2,1)S(1)} %collective-permute-done.16.base_ref, bf16[4,112,128]{2,1,0:T(8,128)(2,1)S(1)} %collective-permute-done.17.new_ref, bf16[512,4096]{1,0:T(8,128)(2,1)S(1)} %get-tuple-element.25.refs_0_, ...), custom_call_target="tpu_custom_call" | custom-call | flops 268435456 | bytes 3145728 | tf_op jit(solution)/shard_map/pallas_call | solution.py:305
  50.9 1.3 %collective-permute-done.14.base_ref = bf16[4,256,128]{2,1,0:T(8,128)(2,1)S(1)} collective-permute-done((bf16[4,256,128]{2,1,0:T(8,128)(2,1)S(1)}, bf16[4,256,128]{2,1,0:T(8,128)(2,1)S(1)}, u32[]{:S(2)}, u32[]{:S(2)}) %collective-permute-start.14) | collective-permute-done | bytes 262176 | tf_op jit(solution)/shard_map/ppermute | solution.py:33
  52.2 1.2 %collective-permute-done.15.new_ref = bf16[4,112,128]{2,1,0:T(8,128)(2,1)S(1)} collective-permute-done((bf16[4,112,128]{2,1,0:T(8,128)(2,1)S(1)}, bf16[4,112,128]{2,1,0:T(8,128)(2,1)S(1)}, u32[]{:S(2)}, u32[]{:S(2)}) %collective-permute-start.15) | collective-permute-done | bytes 114720 | tf_op jit(solution)/shard_map/ppermute | solution.py:33
  53.5 1.4 %shard_map.139.refs_2_ = f32[1024,128]{1,0:T(8,128)S(1)} custom-call(s32[5]{0:T(128)S(1)} %stack.122.at, bf16[4,256,128]{2,1,0:T(8,128)(2,1)S(1)} %collective-permute-done.14.base_ref, bf16[4,112,128]{2,1,0:T(8,128)(2,1)S(1)} %collective-permute-done.15.new_ref, bf16[512,4096]{1,0:T(8,128)(2,1)S(1)} %get-tuple-element.25.refs_0_, ...), custom_call_target="tpu_custom_call" | custom-call | flops 268435456 | bytes 3145728 | tf_op jit(solution)/shard_map/pallas_call | solution.py:305
  54.9 2.1 %shard_map.140 = bf16[1024,128]{1,0:T(8,128)(2,1)} custom-call(s32[5]{0:T(128)S(1)} %stack.105.at, bf16[4,256,128]{2,1,0:T(8,128)(2,1)S(1)} %collective-permute-done.4.base_ref, bf16[4,112,128]{2,1,0:T(8,128)(2,1)S(1)} %collective-permute-done.12.new_ref, bf16[512,4096]{1,0:T(8,128)(2,1)S(1)} %get-tuple-element.25.refs_0_, ...), custom_call_target="tpu_custom_call" | custom-call | flops 268435456 | bytes 3145728 | tf_op jit(solution)/shard_map/pallas_call | solution.py:305
  (43 shorter events, 1.4 us)
Async XLA Ops:
  0.6 2.9 %collective-permute-start = (bf16[1024,128]{1,0:T(8,128)(2,1)}, bf16[1024,128]{1,0:T(8,128)(2,1)S(1)}, u32[]{:S(2)}, u32[]{:S(2)}) collective-permute-start(bf16[1024,128]{1,0:T(8,128)(2,1)} %g_ref), channel_id=1, source_target_pairs={{0,1},{1,0},{2,3},{3,2},{4,5},{5,4},{6,7},{7,6},{8,9},{9,8},{10,11... | collective-permute-start | bytes 786440 | tf_op jit(solution)/shard_map/ppermute | solution.py:29
  4.1 4.4 %collective-permute-start.8 = (f32[1024,128]{1,0:T(8,128)S(1)}, f32[1024,128]{1,0:T(8,128)S(1)}, u32[]{:S(2)}, u32[]{:S(2)}) collective-permute-start(f32[1024,128]{1,0:T(8,128)S(1)} %shard_map.129), channel_id=1, source_target_pairs={{0,1},{1,0},{2,3},{3,2},{4,5},{5,4},{6,7},{7,6},{8,9},{9,8},{10,11... | collective-permute-start | bytes 1572872 | tf_op jit(solution)/shard_map/ppermute | solution.py:29
  4.7 2.3 %copy-start = (bf16[1,4096,128]{2,1,0:T(8,128)(2,1)S(1)}, bf16[1,4096,128]{2,1,0:T(8,128)(2,1)}, u32[]{:S(2)}) copy-start(bf16[1,4096,128]{2,1,0:T(8,128)(2,1)} %param.11) | copy-start | bytes 3145732
  4.7 2.3 %copy-start.4 = (bf16[1024,128]{1,0:T(8,128)(2,1)S(1)}, bf16[1024,128]{1,0:T(8,128)(2,1)}, u32[]{:S(2)}) copy-start(bf16[1024,128]{1,0:T(8,128)(2,1)} %g_ref) | copy-start | bytes 786436
  4.7 3.7 %collective-permute-start.5 = (f32[1024,128]{1,0:T(8,128)S(1)}, f32[1024,128]{1,0:T(8,128)S(1)}, u32[]{:S(2)}, u32[]{:S(2)}) collective-permute-start(f32[1024,128]{1,0:T(8,128)S(1)} %shard_map.131), channel_id=1, source_target_pairs={{0,1},{1,0},{2,3},{3,2},{4,5},{5,4},{6,7},{7,6},{8,9},{9,8},{10,11... | collective-permute-start | bytes 1572872 | tf_op jit(solution)/shard_map/ppermute | solution.py:29
  5.8 2.7 %collective-permute-start.6 = (f32[1024,128]{1,0:T(8,128)S(1)}, f32[1024,128]{1,0:T(8,128)S(1)}, u32[]{:S(2)}, u32[]{:S(2)}) collective-permute-start(f32[1024,128]{1,0:T(8,128)S(1)} %shard_map.132), channel_id=1, source_target_pairs={{0,1},{1,0},{2,3},{3,2},{4,5},{5,4},{6,7},{7,6},{8,9},{9,8},{10,11... | collective-permute-start | bytes 1572872 | tf_op jit(solution)/shard_map/ppermute | solution.py:29
  6.4 2.5 %copy-start.6 = (s32[17]{0:T(128)S(1)}, s32[17]{0:T(128)}, u32[]{:S(2)}) copy-start(s32[17]{0:T(128)} %param.13) | copy-start | bytes 208
  6.4 7.8 %copy-start.5 = (s32[1,1,32]{2,1,0:T(1,128)S(1)}, s32[1,1,32]{2,1,0:T(1,128)}, u32[]{:S(2)}) copy-start(s32[1,1,32]{2,1,0:T(1,128)} %param.12) | copy-start | bytes 388
  6.5 2.1 %collective-permute-start.7 = (f32[1024,128]{1,0:T(8,128)S(1)}, f32[1024,128]{1,0:T(8,128)S(1)}, u32[]{:S(2)}, u32[]{:S(2)}) collective-permute-start(f32[1024,128]{1,0:T(8,128)S(1)} %shard_map.133), channel_id=1, source_target_pairs={{0,1},{1,0},{2,3},{3,2},{4,5},{5,4},{6,7},{7,6},{8,9},{9,8},{10,11... | collective-permute-start | bytes 1572872 | tf_op jit(solution)/shard_map/ppermute | solution.py:29
  8.4 22.7 %copy-start.1 = (f32[256,128]{1,0:T(8,128)S(1)}, f32[256,128]{1,0:T(8,128)}, u32[]{:S(2)}) copy-start(f32[256,128]{1,0:T(8,128)} %m_ref.1) | copy-start | bytes 393220
  8.4 22.7 %copy-start.2 = (f32[256,128]{1,0:T(8,128)S(1)}, f32[256,128]{1,0:T(8,128)}, u32[]{:S(2)}) copy-start(f32[256,128]{1,0:T(8,128)} %v_ref.1) | copy-start | bytes 393220
  8.4 22.7 %copy-start.3 = (f32[256,128]{1,0:T(8,128)S(1)}, f32[256,128]{1,0:T(8,128)}, u32[]{:S(2)}) copy-start(f32[256,128]{1,0:T(8,128)} %w_ref.1) | copy-start | bytes 393220
  8.5 33.3 %collective-permute-start.13 = (bf16[512,4096]{1,0:T(8,128)(2,1)}, bf16[512,4096]{1,0:T(8,128)(2,1)}, u32[]{:S(2)}, u32[]{:S(2)}) collective-permute-start(bf16[512,4096]{1,0:T(8,128)(2,1)} %refs_0_.3), channel_id=1, source_target_pairs={{0,1},{1,0},{2,3},{3,2},{4,5},{5,4},{6,7},{7,6},{8,9},{9,8},{10,11... | collective-permute-start | bytes 12582920 | tf_op jit(solution)/shard_map/ppermute | solution.py:29
  9.0 14.5 %collective-permute-start.1 = (bf16[256,128]{1,0:T(8,128)(2,1)S(1)}, bf16[256,128]{1,0:T(8,128)(2,1)S(1)}, u32[]{:S(2)}, u32[]{:S(2)}) collective-permute-start(bf16[256,128]{1,0:T(8,128)(2,1)S(1)} %get-tuple-element.21), channel_id=1, source_target_pairs={{0,8},{2,10},{4,12},{6,14},{8,0},{10,2},{12,4},{14,6},{16,24},{18,... | collective-permute-start | bytes 196616 | tf_op jit(solution)/shard_map/ppermute | solution.py:33
  11.7 11.8 %collective-permute-start.2 = (bf16[256,128]{1,0:T(8,128)(2,1)S(1)}, bf16[256,128]{1,0:T(8,128)(2,1)S(1)}, u32[]{:S(2)}, u32[]{:S(2)}) collective-permute-start(bf16[256,128]{1,0:T(8,128)(2,1)S(1)} %get-tuple-element.21), channel_id=1, source_target_pairs={{0,16},{2,18},{4,20},{6,22},{8,24},{10,26},{12,28},{14,30},{16,0},... | collective-permute-start | bytes 196616 | tf_op jit(solution)/shard_map/ppermute | solution.py:33
  14.3 9.2 %collective-permute-start.3 = (bf16[256,128]{1,0:T(8,128)(2,1)S(1)}, bf16[256,128]{1,0:T(8,128)(2,1)S(1)}, u32[]{:S(2)}, u32[]{:S(2)}) collective-permute-start(bf16[256,128]{1,0:T(8,128)(2,1)S(1)} %get-tuple-element.21), channel_id=1, source_target_pairs={{0,24},{2,26},{4,28},{6,30},{8,16},{10,18},{12,20},{14,22},{16,8},... | collective-permute-start | bytes 196616 | tf_op jit(solution)/shard_map/ppermute | solution.py:33
  16.4 14.7 %all-to-all-start = ((f32[16,8,128]{2,1,0:T(8,128)}), f32[16,8,128]{2,1,0:T(8,128)S(1)}, u32[]{:S(2)}, u32[]{:S(2)}) async-start(f32[16,8,128]{2,1,0:T(8,128)} %bitcast.14), calls=%async_computation | async-start | bytes 131072 | tf_op jit(solution)/shard_map/all_to_all | solution.py:358
  23.5 17.6 %collective-permute-start.16 = (bf16[4,256,128]{2,1,0:T(8,128)(2,1)S(1)}, bf16[4,256,128]{2,1,0:T(8,128)(2,1)S(1)}, u32[]{:S(2)}, u32[]{:S(2)}) collective-permute-start(bf16[4,256,128]{2,1,0:T(8,128)(2,1)S(1)} %pad_maximum_fusion.base_ref), channel_id=1, source_target_pairs={{0,2},{2,0},{4,6},{6,4},{8,10},{10,8},{12,14},{14,12},{16,18},{18,... | collective-permute-start | bytes 786440 | tf_op jit(solution)/shard_map/ppermute | solution.py:33
  32.8 4.7 %collective-permute-start.9 = (bf16[112,128]{1,0:T(8,128)(2,1)S(1)}, bf16[112,128]{1,0:T(8,128)(2,1)S(1)}, u32[]{:S(2)}, u32[]{:S(2)}) collective-permute-start(bf16[112,128]{1,0:T(8,128)(2,1)S(1)} %get-tuple-element.23), channel_id=1, source_target_pairs={{0,8},{2,10},{4,12},{6,14},{8,0},{10,2},{12,4},{14,6},{16,24},{18,... | collective-permute-start | bytes 86024 | tf_op jit(solution)/shard_map/ppermute | solution.py:33
  33.5 4.8 %collective-permute-start.10 = (bf16[112,128]{1,0:T(8,128)(2,1)S(1)}, bf16[112,128]{1,0:T(8,128)(2,1)S(1)}, u32[]{:S(2)}, u32[]{:S(2)}) collective-permute-start(bf16[112,128]{1,0:T(8,128)(2,1)S(1)} %get-tuple-element.23), channel_id=1, source_target_pairs={{0,16},{2,18},{4,20},{6,22},{8,24},{10,26},{12,28},{14,30},{16,0},... | collective-permute-start | bytes 86024 | tf_op jit(solution)/shard_map/ppermute | solution.py:33
  34.2 5.7 %collective-permute-start.11 = (bf16[112,128]{1,0:T(8,128)(2,1)S(1)}, bf16[112,128]{1,0:T(8,128)(2,1)S(1)}, u32[]{:S(2)}, u32[]{:S(2)}) collective-permute-start(bf16[112,128]{1,0:T(8,128)(2,1)S(1)} %get-tuple-element.23), channel_id=1, source_target_pairs={{0,24},{2,26},{4,28},{6,30},{8,16},{10,18},{12,20},{14,22},{16,8},... | collective-permute-start | bytes 86024 | tf_op jit(solution)/shard_map/ppermute | solution.py:33
  37.6 14.7 %collective-permute-start.14 = (bf16[4,256,128]{2,1,0:T(8,128)(2,1)S(1)}, bf16[4,256,128]{2,1,0:T(8,128)(2,1)S(1)}, u32[]{:S(2)}, u32[]{:S(2)}) collective-permute-start(bf16[4,256,128]{2,1,0:T(8,128)(2,1)S(1)} %pad_maximum_fusion.base_ref), channel_id=1, source_target_pairs={{0,4},{2,6},{4,0},{6,2},{8,12},{10,14},{12,8},{14,10},{16,20},{18,... | collective-permute-start | bytes 786440 | tf_op jit(solution)/shard_map/ppermute | solution.py:33
  38.3 16.6 %collective-permute-start.4 = (bf16[4,256,128]{2,1,0:T(8,128)(2,1)S(1)}, bf16[4,256,128]{2,1,0:T(8,128)(2,1)S(1)}, u32[]{:S(2)}, u32[]{:S(2)}) collective-permute-start(bf16[4,256,128]{2,1,0:T(8,128)(2,1)S(1)} %pad_maximum_fusion.base_ref), channel_id=1, source_target_pairs={{0,6},{2,4},{4,2},{6,0},{8,14},{10,12},{12,10},{14,8},{16,22},{18,... | collective-permute-start | bytes 786440 | tf_op jit(solution)/shard_map/ppermute | solution.py:33
  39.9 9.6 %collective-permute-start.17 = (bf16[4,112,128]{2,1,0:T(8,128)(2,1)S(1)}, bf16[4,112,128]{2,1,0:T(8,128)(2,1)S(1)}, u32[]{:S(2)}, u32[]{:S(2)}) collective-permute-start(bf16[4,112,128]{2,1,0:T(8,128)(2,1)S(1)} %pad_maximum_fusion.1.new_ref), channel_id=1, source_target_pairs={{0,2},{2,0},{4,6},{6,4},{8,10},{10,8},{12,14},{14,12},{16,18},{18,... | collective-permute-start | bytes 344072 | tf_op jit(solution)/shard_map/ppermute | solution.py:33
  41.2 12.3 %collective-permute-start.15 = (bf16[4,112,128]{2,1,0:T(8,128)(2,1)S(1)}, bf16[4,112,128]{2,1,0:T(8,128)(2,1)S(1)}, u32[]{:S(2)}, u32[]{:S(2)}) collective-permute-start(bf16[4,112,128]{2,1,0:T(8,128)(2,1)S(1)} %pad_maximum_fusion.1.new_ref), channel_id=1, source_target_pairs={{0,4},{2,6},{4,0},{6,2},{8,12},{10,14},{12,8},{14,10},{16,20},{18,... | collective-permute-start | bytes 344072 | tf_op jit(solution)/shard_map/ppermute | solution.py:33
  41.9 13.0 %collective-permute-start.12 = (bf16[4,112,128]{2,1,0:T(8,128)(2,1)S(1)}, bf16[4,112,128]{2,1,0:T(8,128)(2,1)S(1)}, u32[]{:S(2)}, u32[]{:S(2)}) collective-permute-start(bf16[4,112,128]{2,1,0:T(8,128)(2,1)S(1)} %pad_maximum_fusion.1.new_ref), channel_id=1, source_target_pairs={{0,6},{2,4},{4,2},{6,0},{8,14},{10,12},{12,10},{14,8},{16,22},{18,... | collective-permute-start | bytes 344072 | tf_op jit(solution)/shard_map/ppermute | solution.py:33

commit v2 on v0

--- a/solution.py
+++ b/solution.py
@@ -159,9 +159,9 @@
     )(selected, lo, hi, own, *parts)
 
 
-def adam_kernel(bins, info, lo_ref, hi_ref, arr_ref, m_ref, v_ref, w_ref, mo, vo, wo, bo):
+def grad_kernel(bins, info, lo_ref, hi_ref, arr_ref, m_ref, v_ref, w_ref, g_ref, b_ref):
     owners, slots, width = arr_ref.shape
-    region = m_ref.shape[0]
+    region = g_ref.shape[0]
     lo, hi = lo_ref[...], hi_ref[...]
     lane = lax.broadcasted_iota(jnp.int32, (1, LANES), 1)
     arr = arr_ref[...]
@@ -191,64 +191,112 @@
         preferred_element_type=jnp.float32,
     )
     grad = grad * row_scale
-    master = w_ref[...]
-    moment_new = beta_first * m_ref[...] + (1.0 - beta_first) * grad
-    second_new = beta_second * v_ref[...] + (1.0 - beta_second) * grad * grad
+    g_ref[...] = grad
+    b_ref[...] = adam_step(m_ref[...], v_ref[...], w_ref[...], grad)[2].astype(b_ref.dtype)
+
+
+def adam_step(moment, second, master, grad):
+    moment_new = beta_first * moment + (1.0 - beta_first) * grad
+    second_new = beta_second * second + (1.0 - beta_second) * grad * grad
     first_hat = moment_new / (1.0 - beta_first**step_count)
     second_hat = second_new / (1.0 - beta_second**step_count)
     master_new = master - learn_rate * (
         first_hat / (jnp.sqrt(second_hat) + adam_epsilon) + decay_rate * master
     )
-    mo[...] = moment_new
-    vo[...] = second_new
-    wo[...] = master_new
-    bo[...] = master_new.astype(jnp.bfloat16)
-
-
-def adam(info, lo, hi, arrived, moment, second, master, bins):
+    return moment_new, second_new, master_new
+
+
+def weigh(info, lo, hi, arrived, moment, second, master, bins):
     f32 = jax.ShapeDtypeStruct(master.shape, jnp.float32)
     return pl.pallas_call(
-        functools.partial(adam_kernel, bins),
+        functools.partial(grad_kernel, bins),
         in_specs=[SMEM] + [VMEM] * 6,
-        out_specs=[VMEM] * 4,
-        out_shape=[f32, f32, f32, jax.ShapeDtypeStruct(master.shape, jnp.bfloat16)],
-        compiler_params=params(arrived, arrived, *[f32] * 7),
+        out_specs=[VMEM] * 2,
+        out_shape=[f32, jax.ShapeDtypeStruct(master.shape, jnp.bfloat16)],
+        compiler_params=params(arrived, arrived, *[f32] * 5),
         cost_estimate=cost(2 * 6 * arrived.size * master.shape[0], 30 * master.size),
     )(info, lo, hi, arrived, moment, second, master)
 
 
-def project_kernel(last, n_f, at, w_ref, *refs):
-    feats, old, out_ref = refs[:n_f], refs[n_f:-1], refs[-1]
-    count, region, width = w_ref.shape
-    tokens = feats[0].shape[0]
+def project_kernel(step, last, n_f, at, *refs):
+    feats, refs = refs[:n_f], refs[n_f:]
+    if step == 0:
+        sources, feats, sem = feats, refs[-n_f - 1 : -1], refs[-1]
+        out_ref, refs = refs[-n_f - 2], refs[: -n_f - 2]
+    else:
+        out_ref, refs = refs[-1], refs[:-1]
+    tokens, rows = feats[0].shape
+    region = refs[0].shape[-2]
+    owners = rows // region
+    weights, old = [], None
+    for ref in refs:
+        if ref.dtype == jnp.float32:
+            old = ref
+        elif len(ref.shape) == 2:
+            weights.append(ref[...])
+        else:
+            weights += [ref[j] for j in range(ref.shape[0])]
+    count = len(weights)
+    here = [
+        pl.ds(pl.multiple_of(at[q] * region, region), region)
+        for q in range(0 if step == 0 else step * count, owners if step == 0 else (step + 1) * count)
+    ]
+    if step == 0:
+        moves = [
+            [
+                pltpu.make_async_copy(sources[i].at[:, c], feats[i].at[:, c], sem.at[i, q])
+                for q, c in enumerate(here)
+            ]
+            for i in range(n_f)
+        ]
+        for q in range(owners):
+            for i in range(n_f):
+                moves[i][q].start()
+    weight = jnp.concatenate(weights, axis=0)
     for i, f_ref in enumerate(feats):
         mine = pl.ds(i * tokens, tokens)
-        total = old[0][mine, :] if old else None
-        for j in range(count):
-            cols = pl.ds(pl.multiple_of(at[j] * region, region), region)
-            part = jnp.dot(f_ref[:, cols], w_ref[j], preferred_element_type=jnp.float32)
-            total = part if total is None else total + part
+        if step == 0:
+            for q in range(count):
+                moves[i][q].wait()
+        part = jnp.concatenate([f_ref[:, c] for c in here[:count]], axis=1)
+        total = jnp.dot(part, weight, preferred_element_type=jnp.float32)
+        if old is not None:
+            total = total + old[mine, :]
         if last:
-            place = lax.rem(at[count] + i, n_f) * tokens
+            place = lax.rem(at[owners] + i, n_f) * tokens
             mine = pl.ds(pl.multiple_of(place, tokens), tokens)
         out_ref[mine, :] = total.astype(out_ref.dtype)
-
-
-def project(at, feats, pieces, total, last):
-    count, region, width = pieces.shape
-    whole = len(feats) * feats[0].shape[0]
+    if step == 0:
+        for i in range(n_f):
+            for q in range(count, owners):
+                moves[i][q].wait()
+
+
+def project(step, at, feats, pieces, total, last):
+    region, width = pieces[0].shape[-2:]
+    tokens, rows = feats[0].shape
+    whole = len(feats) * tokens
     old = [] if total is None else [total]
     out = jax.ShapeDtypeStruct((whole, width), jnp.bfloat16 if last else jnp.float32)
-    return pl.pallas_call(
-        functools.partial(project_kernel, last, len(feats)),
-        in_specs=[SMEM, VMEM] + [VMEM] * (len(feats) + len(old)),
-        out_specs=VMEM,
-        out_shape=out,
-        compiler_params=params(pieces, out, *feats, *old),
+    held, scratch = [], []
+    if step == 0:
+        feats = [pltpu.with_memory_space_constraint(f, pltpu.HBM) for f in feats]
+        held = [pltpu.VMEM(f.shape, f.dtype) for f in feats]
+        scratch = [pltpu.SemaphoreType.DMA((len(feats), rows // region))]
+    weights = sum(p.size for p in pieces)
+    return pl.pallas_call(
+        functools.partial(project_kernel, step, last, len(feats)),
+        in_specs=[SMEM]
+        + [ANY if step == 0 else VMEM] * len(feats)
+        + [VMEM] * (len(pieces) + len(old)),
+        out_specs=[VMEM] * (1 + len(held)),
+        out_shape=[out] + held,
+        scratch_shapes=scratch,
+        compiler_params=params(*pieces, out, *feats, *old),
         cost_estimate=cost(
-            2 * whole * count * region * width, 2 * whole * count * region + 8 * whole * width
+            2 * whole * weights, 2 * whole * (rows if held else weights // width) + 8 * whole * width
         ),
-    )(at, pieces, *feats, *old)
+    )(at, *feats, *pieces, *old)
 
 
 def spans(mask_bits):
@@ -290,21 +338,18 @@
         outgoing.reshape(owners, SLOTS, width), "dp", split_axis=0, concat_axis=0, tiled=True
     )
     info = jnp.stack([me.astype(jnp.int32), threshold[0]])
-    moment_new, second_new, master_new, weight = adam(
-        info, lo, hi, arrived, moment, second, master, bins
-    )
+    grad, weight = weigh(info, lo, hi, arrived, moment, second, master, bins)
 
     bits = [1 << i for i in range(owners.bit_length() - 1)]
     if 1 << len(bits) == owners and len(bits) > 2 and region % LANES == 0:
         plane, line = spans(bits[:2]), spans(bits[2:])
-        mine = jnp.stack([weight if m == 0 else swap(weight, "dp", m) for m in line])
-        feats = load(feats)
-        total = None
-        for j, b in enumerate(plane):
-            here = mine if b == 0 else swap(mine, "dp", b)
-            at = jnp.stack([me ^ (b ^ m) for m in line] + [core]).astype(jnp.int32)
-            total = project(at, feats, here, total, j == len(plane) - 1)
-        keys = total
+        rest = jnp.stack([swap(weight, "dp", m) for m in line[1:]])
+        groups = [[weight, rest]]
+        groups += [[swap(weight, "dp", b), swap(rest, "dp", b)] for b in plane[1:]]
+        at = jnp.stack([me ^ (b ^ m) for b in plane for m in line] + [core]).astype(jnp.int32)
+        keys, *feats = project(0, at, feats, groups[0], None, False)
+        for j in range(1, len(plane)):
+            [keys] = project(j, at, feats, groups[j], keys, j == len(plane) - 1)
     else:
         whole = jnp.concatenate(feats, axis=0)
         whole = jnp.roll(whole, core * tokens, axis=0)
@@ -313,6 +358,7 @@
             lax.all_gather(weight, "dp", axis=0, tiled=True),
             preferred_element_type=jnp.float32,
         ).astype(jnp.bfloat16)
+    moment_new, second_new, master_new = adam_step(moment, second, master, grad)
     return (keys, error_out, moment_new, second_new, master_new)
 
 

time: 51.6 us -> 51.4 us (level)
  starting transfers between devices: 18.1 us -> 20.5 us
  waiting for transfers between devices: 11.4 us -> 9.31 us
  Pallas kernels: 18.7 us -> 17.6 us
  other arithmetic: 1.18 us -> 1.98 us
    pallas_call x2 -> x1, Pallas kernels: 5.72 us -> 2.21 us  [load(): pl.pallas_call(functools.partial(load_kernel, pieces), in_specs=[ANY] * l...]
    ppermute x6 -> x9, starting transfers between devices: 7.94 us -> 10.3 us  [swap(): lax.ppermute(x, axis, [(i, i ^ mask) for i in range(lax.axis_size(axis))])]
    pallas_call x5, Pallas kernels: 7.43 us -> 9.8 us  [the longest x4 8.77 us: project(): pl.pallas_call(functools.partial(project_kernel, step, last, len(feats)),...]
    ppermute x6 -> x9, waiting for transfers between devices: 4.53 us -> 2.53 us  [swap(): lax.ppermute(x, axis, [(i, i ^ mask) for i in range(lax.axis_size(axis))])]
    sub x0 -> x1, other arithmetic: none -> 0.8 us  [adam_step(): master - learn_rate * (first_hat / (jnp.sqrt(second_hat) + adam_epsilon)...]
  transfers between devices with their start and end apart: 13 -> 16, of which waited for: 5 -> 5; matrix products, arithmetic and copies ran while one was open for 3% -> 4% of each run, Pallas kernels for 32% -> 30%
where the time goes in v2:
time: 51.4 us; the launch traced here: 51.1 us
  starting transfers between devices  20.5 us (40%)
  Pallas kernels  17.6 us (34%)
  waiting for transfers between devices  9.31 us (18%)
  other arithmetic  1.98 us (4%)
  between operations  1.51 us (3%)
    ppermute x9, starting transfers between devices, swap(): lax.ppermute(x, axis, [(i, i ^ mask) for i in range(lax.axis_size(axis))])  10.3 us
    pallas_call x4, Pallas kernels, project(): pl.pallas_call(functools.partial(project_kernel, step, last, len(feats)),...  8.77 us
    all_to_all x1, starting transfers between devices, shards(): lax.all_to_all(outgoing.reshape(owners, SLOTS, width), 'dp', split_axis=0...  8.02 us
    all_to_all x1, waiting for transfers between devices, shards(): lax.all_to_all(outgoing.reshape(owners, SLOTS, width), 'dp', split_axis=0...  6.69 us
    pallas_call x5, Pallas kernels, part_sum(): pl.pallas_call(functools.partial(part_kernel, first), in_specs=[SMEM, VME...  3.49 us
    ppermute x9, waiting for transfers between devices, swap(): lax.ppermute(x, axis, [(i, i ^ mask) for i in range(lax.axis_size(axis))])  2.53 us
    pallas_call x1, Pallas kernels, load(): pl.pallas_call(functools.partial(load_kernel, pieces), in_specs=[ANY] * l...  2.21 us
    ppermute x6, starting transfers between devices, shift(): return lax.ppermute(x, axis, [(i, (i + step) % n) for i in range(n)])  2.17 us
  transfers between devices with their start and end apart: 16, of which 5 were waited for; matrix products, arithmetic and copies ran while one was open for 4% of the time, Pallas kernels for 30%

profile of v2, /device:TPU:0, one launch (start us, length us, event | category | flops | bytes accessed | tf_op | source)
XLA Modules:
  0.0 51.1 jit_solution(2158497639339865055)
XLA Ops:
  0.6 0.5 %collective-permute-start = (bf16[1024,128]{1,0:T(8,128)(2,1)}, bf16[1024,128]{1,0:T(8,128)(2,1)S(1)}, u32[]{:S(2)}, u32[]{:S(2)}) collective-permute-start(bf16[1024,128]{1,0:T(8,128)(2,1)} %g_ref), channel_id=1, source_target_pairs={{0,1},{1,0},{2,3},{3,2},{4,5},{5,4},{6,7},{7,6},{8,9},{9,8},{10,11... | collective-permute-start | bytes 786440 | tf_op jit(solution)/shard_map/ppermute | solution.py:29
  1.1 2.2 %shard_map.128.f_ref = bf16[512,4096]{1,0:T(8,128)(2,1)S(1)} custom-call(bf16[512,4096]{1,0:T(8,128)(2,1)} %refs_0_.3), custom_call_target="tpu_custom_call" | custom-call | bytes 8388608 | tf_op jit(solution)/shard_map/pallas_call | solution.py:63
  3.4 0.5 %shard_map.131 = f32[1024,128]{1,0:T(8,128)S(1)} custom-call(s32[1]{0:T(128)} %bitcast.16.core, bf16[512,4096]{1,0:T(8,128)(2,1)S(1)} %shard_map.128.f_ref, bf16[1024,128]{1,0:T(8,128)(2,1)S(1)} %collective-permute-done.g_ref), custom_call_target="tpu_custom_call" | custom-call | flops 134217728 | bytes 1572864 | tf_op jit(solution)/shard_map/pallas_call | solution.py:95
  4.0 0.5 %shard_map.132 = f32[1024,128]{1,0:T(8,128)S(1)} custom-call(s32[1]{0:T(128)} %bitcast.16.core, bf16[512,4096]{1,0:T(8,128)(2,1)S(1)} %shard_map.128.f_ref, bf16[1024,128]{1,0:T(8,128)(2,1)S(1)} %collective-permute-done.g_ref), custom_call_target="tpu_custom_call" | custom-call | flops 134217728 | bytes 1572864 | tf_op jit(solution)/shard_map/pallas_call | solution.py:95
  4.6 0.5 %collective-permute-start.2 = (f32[1024,128]{1,0:T(8,128)S(1)}, f32[1024,128]{1,0:T(8,128)S(1)}, u32[]{:S(2)}, u32[]{:S(2)}) collective-permute-start(f32[1024,128]{1,0:T(8,128)S(1)} %shard_map.132), channel_id=1, source_target_pairs={{0,1},{1,0},{2,3},{3,2},{4,5},{5,4},{6,7},{7,6},{8,9},{9,8},{10,11... | collective-permute-start | bytes 1572872 | tf_op jit(solution)/shard_map/ppermute | solution.py:29
  5.1 0.5 %shard_map.133 = f32[1024,128]{1,0:T(8,128)S(1)} custom-call(s32[1]{0:T(128)} %bitcast.16.core, bf16[512,4096]{1,0:T(8,128)(2,1)S(1)} %shard_map.128.f_ref, bf16[1024,128]{1,0:T(8,128)(2,1)S(1)} %collective-permute-done.g_ref), custom_call_target="tpu_custom_call" | custom-call | flops 134217728 | bytes 1572864 | tf_op jit(solution)/shard_map/pallas_call | solution.py:95
  5.8 0.5 %shard_map.129 = f32[1024,128]{1,0:T(8,128)S(1)} custom-call(s32[1]{0:T(128)} %bitcast.16.core, bf16[512,4096]{1,0:T(8,128)(2,1)S(1)} %shard_map.128.f_ref, bf16[1024,128]{1,0:T(8,128)(2,1)S(1)} %collective-permute-done.g_ref), custom_call_target="tpu_custom_call" | custom-call | flops 134217728 | bytes 1572864 | tf_op jit(solution)/shard_map/pallas_call | solution.py:95
  6.3 0.5 %collective-permute-start.4 = (f32[1024,128]{1,0:T(8,128)S(1)}, f32[1024,128]{1,0:T(8,128)S(1)}, u32[]{:S(2)}, u32[]{:S(2)}) collective-permute-start(f32[1024,128]{1,0:T(8,128)S(1)} %shard_map.129), channel_id=1, source_target_pairs={{0,1},{1,0},{2,3},{3,2},{4,5},{5,4},{6,7},{7,6},{8,9},{9,8},{10,11... | collective-permute-start | bytes 1572872 | tf_op jit(solution)/shard_map/ppermute | solution.py:29
  6.9 1.4 %shard_map.130.own_ref = f32[4096,128]{1,0:T(8,128)S(1)} custom-call(s32[1]{0:T(128)} %bitcast.16.core, bf16[512,4096]{1,0:T(8,128)(2,1)S(1)} %shard_map.128.f_ref, bf16[1024,128]{1,0:T(8,128)(2,1)S(1)} %copy-done.4, bf16[4096,128]{1,0:T(8,128)(2,1)S(1)} %bitcast.29), custom_call_target="tpu_custom_call" | custom-call | flops 536870912 | bytes 6291456 | tf_op jit(solution)/shard_map/pallas_call | solution.py:95
  8.4 0.4 collective-permute-start.5
  8.8 2.1 %shard_map.134 = (f32[4096,128]{1,0:T(8,128)S(1)}, f32[128,128]{1,0:T(8,128)}) custom-call(s32[32]{0:T(128)S(1)} %bitcast.30, s32[1,128]{1,0:T(1,128)S(1)} %get-tuple-element.29.lo_ref, s32[1,128]{1,0:T(1,128)S(1)} %get-tuple-element.28.hi_ref, f32[4096,128]{1,0:T(8,128)S(1)} %shard_map.130.own_ref, f32[1024,128]{1,0:T(8,128)S(1)} %collective-permute-done.1.refs_0_, ...), custom_call_target="tpu_custom_call" | custom-call | flops 4194304 | bytes 6291456 | tf_op jit(solution)/shard_map/pallas_call | solution.py:148
  10.9 8.0 %all-to-all-start = ((f32[16,8,128]{2,1,0:T(8,128)}), f32[16,8,128]{2,1,0:T(8,128)S(1)}, u32[]{:S(2)}, u32[]{:S(2)}) async-start(f32[16,8,128]{2,1,0:T(8,128)} %bitcast.21), calls=%async_computation | async-start | bytes 131072 | tf_op jit(solution)/shard_map/all_to_all | solution.py:337
  19.8 6.7 %all-to-all-done.arr_ref = f32[16,8,128]{2,1,0:T(8,128)S(1)} async-done(((f32[16,8,128]{2,1,0:T(8,128)}), f32[16,8,128]{2,1,0:T(8,128)S(1)}, u32[]{:S(2)}, u32[]{:S(2)}) %all-to-all-start) | async-done | bytes 65568 | tf_op jit(solution)/shard_map/all_to_all | solution.py:337
  26.5 1.0 %shard_map.135 = (f32[256,128]{1,0:T(8,128)S(1)}, bf16[256,128]{1,0:T(8,128)(2,1)S(1)}) custom-call(s32[2]{0:T(128)S(1)} %pad_add_fusion.info, s32[1,128]{1,0:T(1,128)S(1)} %get-tuple-element.29.lo_ref, s32[1,128]{1,0:T(1,128)S(1)} %get-tuple-element.28.hi_ref, f32[16,8,128]{2,1,0:T(8,128)S(1)} %all-to-all-done.arr_ref, f32[256,128]{1,0:T(8,128)S(1)} %copy-done.1, ...), custom_call_target="tpu_custom_call" | custom-call | flops 50331648 | bytes 983040 | tf_op jit(solution)/shard_map/pallas_call | solution.py:211
  27.5 1.0 %collective-permute-start.8 = (bf16[256,128]{1,0:T(8,128)(2,1)S(1)}, bf16[256,128]{1,0:T(8,128)(2,1)S(1)}, u32[]{:S(2)}, u32[]{:S(2)}) collective-permute-start(bf16[256,128]{1,0:T(8,128)(2,1)S(1)} %get-tuple-element.17.refs_2_), channel_id=1, source_target_pairs={{0,24},{2,26},{4,28},{6,30},{8,16},{10,18},{12,20},{14,22},{16,8},... | collective-permute-start | bytes 196616 | tf_op jit(solution)/shard_map/ppermute | solution.py:33
  28.5 1.2 %collective-permute-start.7 = (bf16[256,128]{1,0:T(8,128)(2,1)S(1)}, bf16[256,128]{1,0:T(8,128)(2,1)S(1)}, u32[]{:S(2)}, u32[]{:S(2)}) collective-permute-start(bf16[256,128]{1,0:T(8,128)(2,1)S(1)} %get-tuple-element.17.refs_2_), channel_id=1, source_target_pairs={{0,16},{2,18},{4,20},{6,22},{8,24},{10,26},{12,28},{14,30},{16,0},... | collective-permute-start | bytes 196616 | tf_op jit(solution)/shard_map/ppermute | solution.py:33
  29.7 2.3 %collective-permute-start.6 = (bf16[256,128]{1,0:T(8,128)(2,1)S(1)}, bf16[256,128]{1,0:T(8,128)(2,1)S(1)}, u32[]{:S(2)}, u32[]{:S(2)}) collective-permute-start(bf16[256,128]{1,0:T(8,128)(2,1)S(1)} %get-tuple-element.17.refs_2_), channel_id=1, source_target_pairs={{0,8},{2,10},{4,12},{6,14},{8,0},{10,2},{12,4},{14,6},{16,24},{18,... | collective-permute-start | bytes 196616 | tf_op jit(solution)/shard_map/ppermute | solution.py:33
  32.0 1.1 %convert_bitcast_fusion = bf16[1,4096,128]{2,1,0:T(8,128)(2,1)} fusion(f32[4096,128]{1,0:T(8,128)S(1)} %get-tuple-element.21), kind=kLoop, calls=%fused_computation | loop fusion | flops 524288 | bytes 3145728 | tf_op jit(solution)/shard_map/broadcast_in_dim | solution.py:334
  33.0 0.8 %collective-permute-start.13 = (bf16[256,128]{1,0:T(8,128)(2,1)S(1)}, bf16[256,128]{1,0:T(8,128)(2,1)S(1)}, u32[]{:S(2)}, u32[]{:S(2)}) collective-permute-start(bf16[256,128]{1,0:T(8,128)(2,1)S(1)} %get-tuple-element.17.refs_2_), channel_id=1, source_target_pairs={{0,2},{2,0},{4,6},{6,4},{8,10},{10,8},{12,14},{14,12},{16,18},{18,... | collective-permute-start | bytes 196616 | tf_op jit(solution)/shard_map/ppermute | solution.py:33
  33.9 0.7 %collective-permute-start.11 = (bf16[256,128]{1,0:T(8,128)(2,1)S(1)}, bf16[256,128]{1,0:T(8,128)(2,1)S(1)}, u32[]{:S(2)}, u32[]{:S(2)}) collective-permute-start(bf16[256,128]{1,0:T(8,128)(2,1)S(1)} %get-tuple-element.17.refs_2_), channel_id=1, source_target_pairs={{0,4},{2,6},{4,0},{6,2},{8,12},{10,14},{12,8},{14,10},{16,20},{18,... | collective-permute-start | bytes 196616 | tf_op jit(solution)/shard_map/ppermute | solution.py:33
  34.6 1.1 %collective-permute-done.7 = bf16[256,128]{1,0:T(8,128)(2,1)S(1)} collective-permute-done((bf16[256,128]{1,0:T(8,128)(2,1)S(1)}, bf16[256,128]{1,0:T(8,128)(2,1)S(1)}, u32[]{:S(2)}, u32[]{:S(2)}) %collective-permute-start.7) | collective-permute-done | bytes 65568 | tf_op jit(solution)/shard_map/ppermute | solution.py:33
  35.7 0.5 collective-permute-start.14
  36.2 1.0 %collective-permute-start.12 = (bf16[3,256,128]{2,1,0:T(8,128)(2,1)S(1)}, bf16[3,256,128]{2,1,0:T(8,128)(2,1)S(1)}, u32[]{:S(2)}, u32[]{:S(2)}) collective-permute-start(bf16[3,256,128]{2,1,0:T(8,128)(2,1)S(1)} %pad_maximum_fusion.refs_3_), channel_id=1, source_target_pairs={{0,4},{2,6},{4,0},{6,2},{8,12},{10,14},{12,8},{14,10},{16,20},{18,... | collective-permute-start | bytes 589832 | tf_op jit(solution)/shard_map/ppermute | solution.py:33
  37.2 0.2 collective-permute-done.13.refs_2_
  37.4 1.9 %collective-permute-start.10 = (bf16[3,256,128]{2,1,0:T(8,128)(2,1)S(1)}, bf16[3,256,128]{2,1,0:T(8,128)(2,1)S(1)}, u32[]{:S(2)}, u32[]{:S(2)}) collective-permute-start(bf16[3,256,128]{2,1,0:T(8,128)(2,1)S(1)} %pad_maximum_fusion.refs_3_), channel_id=1, source_target_pairs={{0,6},{2,4},{4,2},{6,0},{8,14},{10,12},{12,10},{14,8},{16,22},{18,... | collective-permute-start | bytes 589832 | tf_op jit(solution)/shard_map/ppermute | solution.py:33
  39.3 0.8 %multiply_subtract_fusion = (f32[256,128]{1,0:T(8,128)}, f32[256,128]{1,0:T(8,128)}, f32[256,128]{1,0:T(8,128)}) fusion(f32[256,128]{1,0:T(8,128)S(1)} %copy-done.3, f32[256,128]{1,0:T(8,128)S(1)} %get-tuple-element.22, f32[256,128]{1,0:T(8,128)S(1)} %copy-done.2, f32[256,128]{1,0:T(8,128)S(1)} %copy-done.1), kind=kLoop, calls=%fused_computation.4 | loop fusion | flops 491520 | bytes 917504 | tf_op jit(solution)/shard_map/sub | solution.py:203
  40.1 1.0 %collective-permute-start.9 = (bf16[256,128]{1,0:T(8,128)(2,1)S(1)}, bf16[256,128]{1,0:T(8,128)(2,1)S(1)}, u32[]{:S(2)}, u32[]{:S(2)}) collective-permute-start(bf16[256,128]{1,0:T(8,128)(2,1)S(1)} %get-tuple-element.17.refs_2_), channel_id=1, source_target_pairs={{0,6},{2,4},{4,2},{6,0},{8,14},{10,12},{12,10},{14,8},{16,22},{18,... | collective-permute-start | bytes 196616 | tf_op jit(solution)/shard_map/ppermute | solution.py:33
  41.1 4.3 %shard_map.136 = (f32[1024,128]{1,0:T(8,128)S(1)}, bf16[512,4096]{1,0:T(8,128)(2,1)S(1)}, bf16[512,4096]{1,0:T(8,128)(2,1)S(1)}) custom-call(s32[17]{0:T(128)S(1)} %stack.87.at, bf16[512,4096]{1,0:T(8,128)(2,1)} %refs_0_.3, bf16[512,4096]{1,0:T(8,128)(2,1)} %collective-permute-done.5.refs_1_, bf16[256,128]{1,0:T(8,128)(2,1)S(1)} %get-tuple-element.17.refs_2_, ...), custom_call_target="tpu_custom_call" | custom-call | flops 268435456 | bytes 9437184 | tf_op jit(solution)/shard_map/pallas_call | solution.py:287
  45.4 1.2 %shard_map.137.refs_4_ = f32[1024,128]{1,0:T(8,128)S(1)} custom-call(s32[17]{0:T(128)S(1)} %stack.87.at, bf16[512,4096]{1,0:T(8,128)(2,1)S(1)} %get-tuple-element.18.refs_0_, bf16[512,4096]{1,0:T(8,128)(2,1)S(1)} %get-tuple-element.19.refs_1_, bf16[256,128]{1,0:T(8,128)(2,1)S(1)} %collective-permute-done.13.refs_2_, ...), custom_call_target="tpu_custom_call" | custom-call | flops 268435456 | bytes 3145728 | tf_op jit(solution)/shard_map/pallas_call | solution.py:287
  46.7 1.2 %collective-permute-done.12.refs_3_ = bf16[3,256,128]{2,1,0:T(8,128)(2,1)S(1)} collective-permute-done((bf16[3,256,128]{2,1,0:T(8,128)(2,1)S(1)}, bf16[3,256,128]{2,1,0:T(8,128)(2,1)S(1)}, u32[]{:S(2)}, u32[]{:S(2)}) %collective-permute-start.12) | collective-permute-done | bytes 196640 | tf_op jit(solution)/shard_map/ppermute | solution.py:33
  47.9 1.2 %shard_map.138.refs_4_ = f32[1024,128]{1,0:T(8,128)S(1)} custom-call(s32[17]{0:T(128)S(1)} %stack.87.at, bf16[512,4096]{1,0:T(8,128)(2,1)S(1)} %get-tuple-element.18.refs_0_, bf16[512,4096]{1,0:T(8,128)(2,1)S(1)} %get-tuple-element.19.refs_1_, bf16[256,128]{1,0:T(8,128)(2,1)S(1)} %collective-permute-done.11.refs_2_, ...), custom_call_target="tpu_custom_call" | custom-call | flops 268435456 | bytes 3145728 | tf_op jit(solution)/shard_map/pallas_call | solution.py:287
  49.2 2.0 %shard_map.139 = bf16[1024,128]{1,0:T(8,128)(2,1)} custom-call(s32[17]{0:T(128)S(1)} %stack.87.at, bf16[512,4096]{1,0:T(8,128)(2,1)S(1)} %get-tuple-element.18.refs_0_, bf16[512,4096]{1,0:T(8,128)(2,1)S(1)} %get-tuple-element.19.refs_1_, bf16[256,128]{1,0:T(8,128)(2,1)S(1)} %collective-permute-done.9.refs_2_, ...), custom_call_target="tpu_custom_call" | custom-call | flops 268435456 | bytes 3145728 | tf_op jit(solution)/shard_map/pallas_call | solution.py:287
  (33 shorter events, 0.7 us)
Async XLA Ops:
  0.6 2.7 %collective-permute-start = (bf16[1024,128]{1,0:T(8,128)(2,1)}, bf16[1024,128]{1,0:T(8,128)(2,1)S(1)}, u32[]{:S(2)}, u32[]{:S(2)}) collective-permute-start(bf16[1024,128]{1,0:T(8,128)(2,1)} %g_ref), channel_id=1, source_target_pairs={{0,1},{1,0},{2,3},{3,2},{4,5},{5,4},{6,7},{7,6},{8,9},{9,8},{10,11... | collective-permute-start | bytes 786440 | tf_op jit(solution)/shard_map/ppermute | solution.py:29
  3.9 4.4 %collective-permute-start.1 = (f32[1024,128]{1,0:T(8,128)S(1)}, f32[1024,128]{1,0:T(8,128)S(1)}, u32[]{:S(2)}, u32[]{:S(2)}) collective-permute-start(f32[1024,128]{1,0:T(8,128)S(1)} %shard_map.131), channel_id=1, source_target_pairs={{0,1},{1,0},{2,3},{3,2},{4,5},{5,4},{6,7},{7,6},{8,9},{9,8},{10,11... | collective-permute-start | bytes 1572872 | tf_op jit(solution)/shard_map/ppermute | solution.py:29
  4.6 2.3 %copy-start = (bf16[1,4096,128]{2,1,0:T(8,128)(2,1)S(1)}, bf16[1,4096,128]{2,1,0:T(8,128)(2,1)}, u32[]{:S(2)}) copy-start(bf16[1,4096,128]{2,1,0:T(8,128)(2,1)} %param.11) | copy-start | bytes 3145732
  4.6 2.3 %copy-start.4 = (bf16[1024,128]{1,0:T(8,128)(2,1)S(1)}, bf16[1024,128]{1,0:T(8,128)(2,1)}, u32[]{:S(2)}) copy-start(bf16[1024,128]{1,0:T(8,128)(2,1)} %g_ref) | copy-start | bytes 786436
  4.6 3.7 %collective-permute-start.2 = (f32[1024,128]{1,0:T(8,128)S(1)}, f32[1024,128]{1,0:T(8,128)S(1)}, u32[]{:S(2)}, u32[]{:S(2)}) collective-permute-start(f32[1024,128]{1,0:T(8,128)S(1)} %shard_map.132), channel_id=1, source_target_pairs={{0,1},{1,0},{2,3},{3,2},{4,5},{5,4},{6,7},{7,6},{8,9},{9,8},{10,11... | collective-permute-start | bytes 1572872 | tf_op jit(solution)/shard_map/ppermute | solution.py:29
  5.6 2.7 %collective-permute-start.3 = (f32[1024,128]{1,0:T(8,128)S(1)}, f32[1024,128]{1,0:T(8,128)S(1)}, u32[]{:S(2)}, u32[]{:S(2)}) collective-permute-start(f32[1024,128]{1,0:T(8,128)S(1)} %shard_map.133), channel_id=1, source_target_pairs={{0,1},{1,0},{2,3},{3,2},{4,5},{5,4},{6,7},{7,6},{8,9},{9,8},{10,11... | collective-permute-start | bytes 1572872 | tf_op jit(solution)/shard_map/ppermute | solution.py:29
  6.3 2.5 %copy-start.6 = (s32[17]{0:T(128)S(1)}, s32[17]{0:T(128)}, u32[]{:S(2)}) copy-start(s32[17]{0:T(128)} %param.13) | copy-start | bytes 208
  6.3 2.5 %copy-start.5 = (s32[1,1,32]{2,1,0:T(1,128)S(1)}, s32[1,1,32]{2,1,0:T(1,128)}, u32[]{:S(2)}) copy-start(s32[1,1,32]{2,1,0:T(1,128)} %param.12) | copy-start | bytes 388
  6.3 2.1 %collective-permute-start.4 = (f32[1024,128]{1,0:T(8,128)S(1)}, f32[1024,128]{1,0:T(8,128)S(1)}, u32[]{:S(2)}, u32[]{:S(2)}) collective-permute-start(f32[1024,128]{1,0:T(8,128)S(1)} %shard_map.129), channel_id=1, source_target_pairs={{0,1},{1,0},{2,3},{3,2},{4,5},{5,4},{6,7},{7,6},{8,9},{9,8},{10,11... | collective-permute-start | bytes 1572872 | tf_op jit(solution)/shard_map/ppermute | solution.py:29
  6.8 19.6 %copy-start.1 = (f32[256,128]{1,0:T(8,128)S(1)}, f32[256,128]{1,0:T(8,128)}, u32[]{:S(2)}) copy-start(f32[256,128]{1,0:T(8,128)} %m_ref.1) | copy-start | bytes 393220
  6.8 19.6 %copy-start.2 = (f32[256,128]{1,0:T(8,128)S(1)}, f32[256,128]{1,0:T(8,128)}, u32[]{:S(2)}) copy-start(f32[256,128]{1,0:T(8,128)} %v_ref.1) | copy-start | bytes 393220
  6.8 19.6 %copy-start.3 = (f32[256,128]{1,0:T(8,128)S(1)}, f32[256,128]{1,0:T(8,128)}, u32[]{:S(2)}) copy-start(f32[256,128]{1,0:T(8,128)} %w_ref.1) | copy-start | bytes 393220
  8.4 31.7 %collective-permute-start.5 = (bf16[512,4096]{1,0:T(8,128)(2,1)}, bf16[512,4096]{1,0:T(8,128)(2,1)}, u32[]{:S(2)}, u32[]{:S(2)}) collective-permute-start(bf16[512,4096]{1,0:T(8,128)(2,1)} %refs_0_.3), channel_id=1, source_target_pairs={{0,1},{1,0},{2,3},{3,2},{4,5},{5,4},{6,7},{7,6},{8,9},{9,8},{10,11... | collective-permute-start | bytes 12582920 | tf_op jit(solution)/shard_map/ppermute | solution.py:29
  10.9 15.6 %all-to-all-start = ((f32[16,8,128]{2,1,0:T(8,128)}), f32[16,8,128]{2,1,0:T(8,128)S(1)}, u32[]{:S(2)}, u32[]{:S(2)}) async-start(f32[16,8,128]{2,1,0:T(8,128)} %bitcast.21), calls=%async_computation | async-start | bytes 131072 | tf_op jit(solution)/shard_map/all_to_all | solution.py:337
  27.5 6.4 %collective-permute-start.8 = (bf16[256,128]{1,0:T(8,128)(2,1)S(1)}, bf16[256,128]{1,0:T(8,128)(2,1)S(1)}, u32[]{:S(2)}, u32[]{:S(2)}) collective-permute-start(bf16[256,128]{1,0:T(8,128)(2,1)S(1)} %get-tuple-element.17.refs_2_), channel_id=1, source_target_pairs={{0,24},{2,26},{4,28},{6,30},{8,16},{10,18},{12,20},{14,22},{16,8},... | collective-permute-start | bytes 196616 | tf_op jit(solution)/shard_map/ppermute | solution.py:33
  28.5 7.2 %collective-permute-start.7 = (bf16[256,128]{1,0:T(8,128)(2,1)S(1)}, bf16[256,128]{1,0:T(8,128)(2,1)S(1)}, u32[]{:S(2)}, u32[]{:S(2)}) collective-permute-start(bf16[256,128]{1,0:T(8,128)(2,1)S(1)} %get-tuple-element.17.refs_2_), channel_id=1, source_target_pairs={{0,16},{2,18},{4,20},{6,22},{8,24},{10,26},{12,28},{14,30},{16,0},... | collective-permute-start | bytes 196616 | tf_op jit(solution)/shard_map/ppermute | solution.py:33
  29.7 6.0 %collective-permute-start.6 = (bf16[256,128]{1,0:T(8,128)(2,1)S(1)}, bf16[256,128]{1,0:T(8,128)(2,1)S(1)}, u32[]{:S(2)}, u32[]{:S(2)}) collective-permute-start(bf16[256,128]{1,0:T(8,128)(2,1)S(1)} %get-tuple-element.17.refs_2_), channel_id=1, source_target_pairs={{0,8},{2,10},{4,12},{6,14},{8,0},{10,2},{12,4},{14,6},{16,24},{18,... | collective-permute-start | bytes 196616 | tf_op jit(solution)/shard_map/ppermute | solution.py:33
  33.0 4.3 %collective-permute-start.13 = (bf16[256,128]{1,0:T(8,128)(2,1)S(1)}, bf16[256,128]{1,0:T(8,128)(2,1)S(1)}, u32[]{:S(2)}, u32[]{:S(2)}) collective-permute-start(bf16[256,128]{1,0:T(8,128)(2,1)S(1)} %get-tuple-element.17.refs_2_), channel_id=1, source_target_pairs={{0,2},{2,0},{4,6},{6,4},{8,10},{10,8},{12,14},{14,12},{16,18},{18,... | collective-permute-start | bytes 196616 | tf_op jit(solution)/shard_map/ppermute | solution.py:33
  33.9 12.8 %collective-permute-start.11 = (bf16[256,128]{1,0:T(8,128)(2,1)S(1)}, bf16[256,128]{1,0:T(8,128)(2,1)S(1)}, u32[]{:S(2)}, u32[]{:S(2)}) collective-permute-start(bf16[256,128]{1,0:T(8,128)(2,1)S(1)} %get-tuple-element.17.refs_2_), channel_id=1, source_target_pairs={{0,4},{2,6},{4,0},{6,2},{8,12},{10,14},{12,8},{14,10},{16,20},{18,... | collective-permute-start | bytes 196616 | tf_op jit(solution)/shard_map/ppermute | solution.py:33
  35.7 9.7 %collective-permute-start.14 = (bf16[3,256,128]{2,1,0:T(8,128)(2,1)S(1)}, bf16[3,256,128]{2,1,0:T(8,128)(2,1)S(1)}, u32[]{:S(2)}, u32[]{:S(2)}) collective-permute-start(bf16[3,256,128]{2,1,0:T(8,128)(2,1)S(1)} %pad_maximum_fusion.refs_3_), channel_id=1, source_target_pairs={{0,2},{2,0},{4,6},{6,4},{8,10},{10,8},{12,14},{14,12},{16,18},{18,... | collective-permute-start | bytes 589832 | tf_op jit(solution)/shard_map/ppermute | solution.py:33
  36.2 11.7 %collective-permute-start.12 = (bf16[3,256,128]{2,1,0:T(8,128)(2,1)S(1)}, bf16[3,256,128]{2,1,0:T(8,128)(2,1)S(1)}, u32[]{:S(2)}, u32[]{:S(2)}) collective-permute-start(bf16[3,256,128]{2,1,0:T(8,128)(2,1)S(1)} %pad_maximum_fusion.refs_3_), channel_id=1, source_target_pairs={{0,4},{2,6},{4,0},{6,2},{8,12},{10,14},{12,8},{14,10},{16,20},{18,... | collective-permute-start | bytes 589832 | tf_op jit(solution)/shard_map/ppermute | solution.py:33
  37.4 11.8 %collective-permute-start.10 = (bf16[3,256,128]{2,1,0:T(8,128)(2,1)S(1)}, bf16[3,256,128]{2,1,0:T(8,128)(2,1)S(1)}, u32[]{:S(2)}, u32[]{:S(2)}) collective-permute-start(bf16[3,256,128]{2,1,0:T(8,128)(2,1)S(1)} %pad_maximum_fusion.refs_3_), channel_id=1, source_target_pairs={{0,6},{2,4},{4,2},{6,0},{8,14},{10,12},{12,10},{14,8},{16,22},{18,... | collective-permute-start | bytes 589832 | tf_op jit(solution)/shard_map/ppermute | solution.py:33
  40.1 9.1 %collective-permute-start.9 = (bf16[256,128]{1,0:T(8,128)(2,1)S(1)}, bf16[256,128]{1,0:T(8,128)(2,1)S(1)}, u32[]{:S(2)}, u32[]{:S(2)}) collective-permute-start(bf16[256,128]{1,0:T(8,128)(2,1)S(1)} %get-tuple-element.17.refs_2_), channel_id=1, source_target_pairs={{0,6},{2,4},{4,2},{6,0},{8,14},{10,12},{12,10},{14,8},{16,22},{18,... | collective-permute-start | bytes 196616 | tf_op jit(solution)/shard_map/ppermute | solution.py:33

commit v3 on v0

--- a/solution.py
+++ b/solution.py
@@ -36,6 +36,15 @@
 def params(*arrays):
     total = sum(a.size * jnp.dtype(a.dtype).itemsize for a in arrays)
     return pltpu.CompilerParams(vmem_limit_bytes=total + (6 << 20))
+
+
+def bounds(edges):
+    lane = lax.broadcasted_iota(jnp.int32, (1, LANES), 1)
+    lo = hi = jnp.zeros((1, LANES), jnp.int32)
+    for b in range(edges.shape[0] - 1):
+        lo = jnp.where(lane == b, edges[b], lo)
+        hi = jnp.where(lane == b, edges[b + 1], hi)
+    return lo, hi
 
 
 def cost(flops, nbytes):
@@ -102,11 +111,11 @@
     )(core, features, grads, *error)
 
 
-def collect_kernel(n_chunks, owners, bins, sel, lo_ref, hi_ref, own_ref, *refs):
+def collect_kernel(n_chunks, owners, bins, sel, edges, own_ref, *refs):
     parts, (sum_ref, out_ref, count_ref) = refs[:-3], refs[-3:]
     rows, width = sum_ref.shape
     region = rows // owners
-    lo, hi = lo_ref[...], hi_ref[...]
+    lo, hi = bounds(edges)
     count = rows // n_chunks
     tile = min(1024, count)
     acc = jnp.zeros((8, LANES), jnp.float32)
@@ -143,11 +152,11 @@
     lax.fori_loop(0, sel.shape[0], take, 0, unroll=8)
 
 
-def collect(selected, lo, hi, own, parts, n_chunks, owners, bins):
+def collect(selected, edges, own, parts, n_chunks, owners, bins):
     rows, width = own.shape
     return pl.pallas_call(
         functools.partial(collect_kernel, n_chunks, owners, bins),
-        in_specs=[SMEM, VMEM, VMEM, VMEM] + [VMEM] * len(parts),
+        in_specs=[SMEM, SMEM, VMEM] + [VMEM] * len(parts),
         out_specs=[VMEM, VMEM],
         out_shape=[
             jax.ShapeDtypeStruct((rows, width), jnp.float32),
@@ -156,21 +165,21 @@
         scratch_shapes=[pltpu.SMEM((owners,), jnp.int32)],
         compiler_params=params(own, own, own, *parts),
         cost_estimate=cost(8 * rows * width, 4 * rows * width * 3),
-    )(selected, lo, hi, own, *parts)
-
-
-def adam_kernel(bins, info, lo_ref, hi_ref, arr_ref, m_ref, v_ref, w_ref, mo, vo, wo, bo):
+    )(selected, edges, own, *parts)
+
+
+def grad_kernel(bins, me, least, edges, arr_ref, m_ref, v_ref, w_ref, g_ref, b_ref):
     owners, slots, width = arr_ref.shape
-    region = m_ref.shape[0]
-    lo, hi = lo_ref[...], hi_ref[...]
+    region = g_ref.shape[0]
+    lo, hi = bounds(edges)
     lane = lax.broadcasted_iota(jnp.int32, (1, LANES), 1)
     arr = arr_ref[...]
     notes = arr[:, CAP : CAP + 1, :]
     energy = jnp.sum(notes, axis=0)
     widths = jnp.maximum(hi - lo, 1).astype(jnp.float32)
     normal = 1.0 / jnp.sqrt(energy / (owners * width * widths) + epsilon)
-    scale = jnp.where((lane >= info[1]) & (lane < bins), normal, 1.0)
-    ids = info[0] * region + lax.broadcasted_iota(jnp.int32, (region, LANES), 0)
+    scale = jnp.where((lane >= least[0]) & (lane < bins), normal, 1.0)
+    ids = me[0] * region + lax.broadcasted_iota(jnp.int32, (region, LANES), 0)
     row_scale = jnp.sum(
         jnp.where((ids >= lo) & (ids < hi), scale, 0.0), axis=1, keepdims=True
     )
@@ -191,64 +200,120 @@
         preferred_element_type=jnp.float32,
     )
     grad = grad * row_scale
-    master = w_ref[...]
-    moment_new = beta_first * m_ref[...] + (1.0 - beta_first) * grad
-    second_new = beta_second * v_ref[...] + (1.0 - beta_second) * grad * grad
+    g_ref[...] = grad
+    b_ref[...] = adam_step(m_ref[...], v_ref[...], w_ref[...], grad)[2].astype(b_ref.dtype)
+
+
+def adam_step(moment, second, master, grad):
+    moment_new = beta_first * moment + (1.0 - beta_first) * grad
+    second_new = beta_second * second + (1.0 - beta_second) * grad * grad
     first_hat = moment_new / (1.0 - beta_first**step_count)
     second_hat = second_new / (1.0 - beta_second**step_count)
     master_new = master - learn_rate * (
         first_hat / (jnp.sqrt(second_hat) + adam_epsilon) + decay_rate * master
     )
-    mo[...] = moment_new
-    vo[...] = second_new
-    wo[...] = master_new
-    bo[...] = master_new.astype(jnp.bfloat16)
-
-
-def adam(info, lo, hi, arrived, moment, second, master, bins):
+    return moment_new, second_new, master_new
+
+
+def weigh(me, least, edges, arrived, moment, second, master):
     f32 = jax.ShapeDtypeStruct(master.shape, jnp.float32)
     return pl.pallas_call(
-        functools.partial(adam_kernel, bins),
-        in_specs=[SMEM] + [VMEM] * 6,
-        out_specs=[VMEM] * 4,
-        out_shape=[f32, f32, f32, jax.ShapeDtypeStruct(master.shape, jnp.bfloat16)],
-        compiler_params=params(arrived, arrived, *[f32] * 7),
+        functools.partial(grad_kernel, edges.shape[0] - 1),
+        in_specs=[SMEM] * 3 + [VMEM] * 4,
+        out_specs=[VMEM] * 2,
+        out_shape=[f32, jax.ShapeDtypeStruct(master.shape, jnp.bfloat16)],
+        compiler_params=params(arrived, arrived, *[f32] * 5),
         cost_estimate=cost(2 * 6 * arrived.size * master.shape[0], 30 * master.size),
-    )(info, lo, hi, arrived, moment, second, master)
-
-
-def project_kernel(last, n_f, at, w_ref, *refs):
-    feats, old, out_ref = refs[:n_f], refs[n_f:-1], refs[-1]
-    count, region, width = w_ref.shape
+    )(me, least, edges, arrived, moment, second, master)
+
+
+def state_kernel(g_ref, m_ref, v_ref, w_ref, *outs):
+    new = adam_step(m_ref[...], v_ref[...], w_ref[...], g_ref[...])
+    for out, value in zip(outs, new):
+        out[...] = value
+
+
+def state(grad, moment, second, master):
+    return pl.pallas_call(
+        state_kernel,
+        in_specs=[VMEM] * 4,
+        out_specs=[VMEM] * 3,
+        out_shape=[jax.ShapeDtypeStruct(grad.shape, jnp.float32)] * 3,
+        compiler_params=params(*[grad] * 7),
+        cost_estimate=cost(20 * grad.size, 28 * grad.size),
+    )(grad, moment, second, master)
+
+
+def round_kernel(x_ref, o_ref):
+    o_ref[...] = x_ref[...].astype(o_ref.dtype)
+
+
+def rounded(x):
+    out = jax.ShapeDtypeStruct(x.shape, jnp.bfloat16)
+    return pl.pallas_call(
+        round_kernel,
+        in_specs=[VMEM],
+        out_specs=VMEM,
+        out_shape=out,
+        compiler_params=params(x, out),
+        cost_estimate=cost(x.size, 6 * x.size),
+    )(x)
+
+
+def join_kernel(*refs):
+    for i, ref in enumerate(refs[:-1]):
+        refs[-1][i] = ref[...]
+
+
+def join(arrays):
+    out = jax.ShapeDtypeStruct((len(arrays), *arrays[0].shape), arrays[0].dtype)
+    return pl.pallas_call(
+        join_kernel,
+        in_specs=[VMEM] * len(arrays),
+        out_specs=VMEM,
+        out_shape=out,
+        compiler_params=params(out, out),
+        cost_estimate=cost(out.size, 4 * out.size),
+    )(*arrays)
+
+
+def project_kernel(masks, last, n_f, me, core, *refs):
+    feats, pieces, out_ref = refs[:n_f], refs[n_f : n_f + 2], refs[-1]
     tokens = feats[0].shape[0]
+    region = pieces[0].shape[0]
+    weight = jnp.concatenate(
+        [pieces[0][...]] + [pieces[1][j] for j in range(pieces[1].shape[0])], axis=0
+    )
     for i, f_ref in enumerate(feats):
         mine = pl.ds(i * tokens, tokens)
-        total = old[0][mine, :] if old else None
-        for j in range(count):
-            cols = pl.ds(pl.multiple_of(at[j] * region, region), region)
-            part = jnp.dot(f_ref[:, cols], w_ref[j], preferred_element_type=jnp.float32)
-            total = part if total is None else total + part
+        part = [
+            f_ref[:, pl.ds(pl.multiple_of((me[0] ^ m) * region, region), region)] for m in masks
+        ]
+        total = jnp.dot(
+            jnp.concatenate(part, axis=1), weight, preferred_element_type=jnp.float32
+        )
+        if len(refs) > n_f + 3:
+            total = total + refs[n_f + 2][mine, :]
         if last:
-            place = lax.rem(at[count] + i, n_f) * tokens
+            place = lax.rem(core[0] + i, n_f) * tokens
             mine = pl.ds(pl.multiple_of(place, tokens), tokens)
         out_ref[mine, :] = total.astype(out_ref.dtype)
 
 
-def project(at, feats, pieces, total, last):
-    count, region, width = pieces.shape
+def project(masks, me, core, feats, pieces, total, last):
+    region, width = pieces[0].shape
     whole = len(feats) * feats[0].shape[0]
     old = [] if total is None else [total]
     out = jax.ShapeDtypeStruct((whole, width), jnp.bfloat16 if last else jnp.float32)
-    return pl.pallas_call(
-        functools.partial(project_kernel, last, len(feats)),
-        in_specs=[SMEM, VMEM] + [VMEM] * (len(feats) + len(old)),
+    depth = len(masks) * region
+    return pl.pallas_call(
+        functools.partial(project_kernel, masks, last, len(feats)),
+        in_specs=[SMEM, SMEM] + [VMEM] * (len(feats) + 2 + len(old)),
         out_specs=VMEM,
         out_shape=out,
-        compiler_params=params(pieces, out, *feats, *old),
-        cost_estimate=cost(
-            2 * whole * count * region * width, 2 * whole * count * region + 8 * whole * width
-        ),
-    )(at, pieces, *feats, *old)
+        compiler_params=params(*pieces, out, *feats, *old),
+        cost_estimate=cost(2 * whole * depth * width, 2 * whole * depth + 8 * whole * width),
+    )(me, core, *feats, *pieces, *old)
 
 
 def spans(mask_bits):
@@ -265,10 +330,8 @@
     width = key_grads.shape[1]
     region = rows // owners
     bins = bin_edges.shape[0] - 1
-    pad = (0, LANES - bins)
-    lo = jnp.pad(bin_edges[:-1], pad)[None]
-    hi = jnp.pad(bin_edges[1:], pad)[None]
     core1 = core.reshape(1).astype(jnp.int32)
+    me1 = me.reshape(1).astype(jnp.int32)
 
     [held] = load([features])
     n_chunks = 4 if cores == 2 else 1
@@ -282,29 +345,28 @@
     mine, _ = lax.optimization_barrier((key_grads, made[-1]))
     own = part_sum(core1, held, mine, 0, rows, error_in[0])
     later, _ = lax.optimization_barrier((features, [own] + got))
-    rest, outgoing = collect(selected[0, 0], lo, hi, own, got, n_chunks, owners, bins)
-    error_out = rest.astype(jnp.bfloat16)[None]
-    feats = [features] + [shift(later, "tensor", -s) for s in range(1, cores)]
+    rest, outgoing = collect(selected[0, 0], bin_edges, own, got, n_chunks, owners, bins)
+    error_out = rounded(rest)[None]
+    feats = [held] + [shift(later, "tensor", -s) for s in range(1, cores)]
 
     arrived = lax.all_to_all(
         outgoing.reshape(owners, SLOTS, width), "dp", split_axis=0, concat_axis=0, tiled=True
     )
-    info = jnp.stack([me.astype(jnp.int32), threshold[0]])
-    moment_new, second_new, master_new, weight = adam(
-        info, lo, hi, arrived, moment, second, master, bins
-    )
-
+    grad, weight = weigh(me1, threshold, bin_edges, arrived, moment, second, master)
     bits = [1 << i for i in range(owners.bit_length() - 1)]
     if 1 << len(bits) == owners and len(bits) > 2 and region % LANES == 0:
         plane, line = spans(bits[:2]), spans(bits[2:])
-        mine = jnp.stack([weight if m == 0 else swap(weight, "dp", m) for m in line])
-        feats = load(feats)
-        total = None
+        near = [swap(weight, "dp", b) for b in plane[1:]]
+        far = [swap(weight, "dp", m) for m in line[1:]]
+        near, far = lax.optimization_barrier((near, far))
+        rest = join(far)
+        groups = [[weight, rest]]
+        groups += [[own, swap(rest, "dp", b)] for own, b in zip(near, plane[1:])]
+        feats = [held, *load(feats[1:])]
+        keys = None
         for j, b in enumerate(plane):
-            here = mine if b == 0 else swap(mine, "dp", b)
-            at = jnp.stack([me ^ (b ^ m) for m in line] + [core]).astype(jnp.int32)
-            total = project(at, feats, here, total, j == len(plane) - 1)
-        keys = total
+            masks = tuple(b ^ m for m in line)
+            keys = project(masks, me1, core1, feats, groups[j], keys, j == len(plane) - 1)
     else:
         whole = jnp.concatenate(feats, axis=0)
         whole = jnp.roll(whole, core * tokens, axis=0)
@@ -313,6 +375,7 @@
             lax.all_gather(weight, "dp", axis=0, tiled=True),
             preferred_element_type=jnp.float32,
         ).astype(jnp.bfloat16)
+    moment_new, second_new, master_new = state(grad, moment, second, master)
     return (keys, error_out, moment_new, second_new, master_new)
 
 

time: 51.6 us -> 52.6 us (1.019)
  Pallas kernels: 18.7 us -> 16.6 us
  starting transfers between devices: 18.1 us -> 20 us
  waiting for transfers between devices: 11.4 us -> 13.2 us
  other arithmetic: 1.18 us -> 0 us
  local copies, waits for them, and re-layouts: 0.45 us -> 1.12 us
    ppermute x6 -> x9, starting transfers between devices: 7.94 us -> 9.78 us  [swap(): lax.ppermute(x, axis, [(i, i ^ mask) for i in range(lax.axis_size(axis))])]
    ppermute x6 -> x9, waiting for transfers between devices: 4.53 us -> 6.23 us  [swap(): lax.ppermute(x, axis, [(i, i ^ mask) for i in range(lax.axis_size(axis))])]
    pallas_call x2, Pallas kernels: 5.72 us -> 4.58 us  [load(): pl.pallas_call(functools.partial(load_kernel, pieces), in_specs=[ANY] * l...]
    unnamed x14 -> x18, local copies, waits for them, and re-layouts: 0.04 us -> 1.12 us
    broadcast_in_dim x1 -> x0, other arithmetic: 1.07 us -> none  [shards(): error_out = rest.astype(jnp.bfloat16)[None]]
    pallas_call x5 -> x8, Pallas kernels: 7.43 us -> 6.45 us  [the longest x4 3.54 us: project(): pl.pallas_call(functools.partial(project_kernel, masks, last, len(feats))...]
  transfers between devices with their start and end apart: 13 -> 16, of which waited for: 5 -> 7; matrix products, arithmetic and copies ran while one was open for 3% -> 0% of each run, Pallas kernels for 32% -> 28%
where the time goes in v3:
time: 52.6 us; the launch traced here: 52.4 us
  starting transfers between devices  20 us (38%)
  Pallas kernels  16.6 us (32%)
  waiting for transfers between devices  13.2 us (25%)
  between operations  1.5 us (3%)
  local copies, waits for them, and re-layouts  1.12 us (2%)
    ppermute x9, starting transfers between devices, swap(): lax.ppermute(x, axis, [(i, i ^ mask) for i in range(lax.axis_size(axis))])  9.78 us
    all_to_all x1, starting transfers between devices, shards(): lax.all_to_all(outgoing.reshape(owners, SLOTS, width), 'dp', split_axis=0...  8.03 us
    all_to_all x1, waiting for transfers between devices, shards(): lax.all_to_all(outgoing.reshape(owners, SLOTS, width), 'dp', split_axis=0...  6.88 us
    ppermute x9, waiting for transfers between devices, swap(): lax.ppermute(x, axis, [(i, i ^ mask) for i in range(lax.axis_size(axis))])  6.23 us
    pallas_call x2, Pallas kernels, load(): pl.pallas_call(functools.partial(load_kernel, pieces), in_specs=[ANY] * l...  4.58 us
    pallas_call x4, Pallas kernels, project(): pl.pallas_call(functools.partial(project_kernel, masks, last, len(feats))...  3.54 us
    pallas_call x5, Pallas kernels, part_sum(): pl.pallas_call(functools.partial(part_kernel, first), in_specs=[SMEM, VME...  3.49 us
    ppermute x6, starting transfers between devices, shift(): return lax.ppermute(x, axis, [(i, (i + step) % n) for i in range(n)])  2.17 us
  transfers between devices with their start and end apart: 16, of which 7 were waited for; matrix products, arithmetic and copies ran while one was open for 0% of the time, Pallas kernels for 28%

profile of v3, /device:TPU:0, one launch (start us, length us, event | category | flops | bytes accessed | tf_op | source)
XLA Modules:
  0.0 52.4 jit_solution(10390451834070679234)
XLA Ops:
  0.6 0.5 collective-permute-start
  1.1 2.2 %shard_map.128.f_ref.refs_0_ = bf16[512,4096]{1,0:T(8,128)(2,1)S(1)} custom-call(bf16[512,4096]{1,0:T(8,128)(2,1)} %refs_0_.1), custom_call_target="tpu_custom_call" | custom-call | bytes 8388608 | tf_op jit(solution)/shard_map/pallas_call | solution.py:72
  3.4 0.5 %shard_map.131 = f32[1024,128]{1,0:T(8,128)S(1)} custom-call(s32[1]{0:T(128)} %bitcast.1.core, bf16[512,4096]{1,0:T(8,128)(2,1)S(1)} %shard_map.128.f_ref.refs_0_, bf16[1024,128]{1,0:T(8,128)(2,1)S(1)} %collective-permute-done.g_ref), custom_call_target="tpu_custom_call" | custom-call | flops 134217728 | bytes 1572864 | tf_op jit(solution)/shard_map/pallas_call | solution.py:104
  4.0 0.5 shard_map.132
  4.6 0.5 collective-permute-start.2
  5.1 0.5 shard_map.133
  5.8 0.5 shard_map.129
  6.9 1.4 %shard_map.130.own_ref = f32[4096,128]{1,0:T(8,128)S(1)} custom-call(s32[1]{0:T(128)} %bitcast.1.core, bf16[512,4096]{1,0:T(8,128)(2,1)S(1)} %shard_map.128.f_ref.refs_0_, bf16[1024,128]{1,0:T(8,128)(2,1)S(1)} %copy-done.6, bf16[4096,128]{1,0:T(8,128)(2,1)S(1)} %bitcast.6), custom_call_target="tpu_custom_call" | custom-call | flops 536870912 | bytes 6291456 | tf_op jit(solution)/shard_map/pallas_call | solution.py:104
  8.8 2.1 %shard_map.135 = (f32[4096,128]{1,0:T(8,128)S(1)}, f32[128,128]{1,0:T(8,128)}) custom-call(s32[32]{0:T(128)S(1)} %bitcast.7, s32[17]{0:T(128)S(1)} %copy-done.7, f32[4096,128]{1,0:T(8,128)S(1)} %shard_map.130.own_ref, f32[1024,128]{1,0:T(8,128)S(1)} %collective-permute-done.1.refs_0_, f32[1024,128]{1,0:T(8,128)S(1)} %collective-permute-done.2.refs_1_, ...), custom_call_target="tpu_custom_call" | custom-call | flops 4194304 | bytes 6291456 | tf_op jit(solution)/shard_map/pallas_call | solution.py:157
  10.8 8.0 %all-to-all-start = ((f32[16,8,128]{2,1,0:T(8,128)}), f32[16,8,128]{2,1,0:T(8,128)S(1)}, u32[]{:S(2)}, u32[]{:S(2)}) async-start(f32[16,8,128]{2,1,0:T(8,128)} %bitcast.4), calls=%async_computation | async-start | bytes 131072 | tf_op jit(solution)/shard_map/all_to_all | solution.py:352
  19.5 6.9 %all-to-all-done.arr_ref = f32[16,8,128]{2,1,0:T(8,128)S(1)} async-done(((f32[16,8,128]{2,1,0:T(8,128)}), f32[16,8,128]{2,1,0:T(8,128)S(1)}, u32[]{:S(2)}, u32[]{:S(2)}) %all-to-all-start) | async-done | bytes 65568 | tf_op jit(solution)/shard_map/all_to_all | solution.py:352
  26.4 1.0 %shard_map.136 = (f32[256,128]{1,0:T(8,128)S(1)}, bf16[256,128]{1,0:T(8,128)(2,1)S(1)}) custom-call(s32[1]{0:T(128)} %bitcast.me, s32[1]{0:T(128)S(6)} %copy.14.least, s32[17]{0:T(128)S(1)} %copy-done.7, f32[16,8,128]{2,1,0:T(8,128)S(1)} %all-to-all-done.arr_ref, f32[256,128]{1,0:T(8,128)S(1)} %copy-done.3, f32[256,128]{1,0:T(8,128)S(1)} %copy-done.4, ...), custom_call_target="tpu_custom_call" | custom-call | flops 50331648 | bytes 983040 | tf_op jit(solution)/shard_map/pallas_call | solution.py:220
  27.4 1.0 %collective-permute-start.11 = (bf16[256,128]{1,0:T(8,128)(2,1)S(1)}, bf16[256,128]{1,0:T(8,128)(2,1)S(1)}, u32[]{:S(2)}, u32[]{:S(2)}) collective-permute-start(bf16[256,128]{1,0:T(8,128)(2,1)S(1)} %get-tuple-element.23.refs_2_), channel_id=1, source_target_pairs={{0,24},{2,26},{4,28},{6,30},{8,16},{10,18},{12,20},{14,22},{16,8},... | collective-permute-start | bytes 196616 | tf_op jit(solution)/shard_map/ppermute | solution.py:33
  28.4 1.2 %collective-permute-start.10 = (bf16[256,128]{1,0:T(8,128)(2,1)S(1)}, bf16[256,128]{1,0:T(8,128)(2,1)S(1)}, u32[]{:S(2)}, u32[]{:S(2)}) collective-permute-start(bf16[256,128]{1,0:T(8,128)(2,1)S(1)} %get-tuple-element.23.refs_2_), channel_id=1, source_target_pairs={{0,16},{2,18},{4,20},{6,22},{8,24},{10,26},{12,28},{14,30},{16,0},... | collective-permute-start | bytes 196616 | tf_op jit(solution)/shard_map/ppermute | solution.py:33
  29.6 2.3 %collective-permute-start.9 = (bf16[256,128]{1,0:T(8,128)(2,1)S(1)}, bf16[256,128]{1,0:T(8,128)(2,1)S(1)}, u32[]{:S(2)}, u32[]{:S(2)}) collective-permute-start(bf16[256,128]{1,0:T(8,128)(2,1)S(1)} %get-tuple-element.23.refs_2_), channel_id=1, source_target_pairs={{0,8},{2,10},{4,12},{6,14},{8,0},{10,2},{12,4},{14,6},{16,24},{18,... | collective-permute-start | bytes 196616 | tf_op jit(solution)/shard_map/ppermute | solution.py:33
  31.9 0.7 %collective-permute-start.8 = (bf16[256,128]{1,0:T(8,128)(2,1)S(1)}, bf16[256,128]{1,0:T(8,128)(2,1)S(1)}, u32[]{:S(2)}, u32[]{:S(2)}) collective-permute-start(bf16[256,128]{1,0:T(8,128)(2,1)S(1)} %get-tuple-element.23.refs_2_), channel_id=1, source_target_pairs={{0,6},{2,4},{4,2},{6,0},{8,14},{10,12},{12,10},{14,8},{16,22},{18,... | collective-permute-start | bytes 196616 | tf_op jit(solution)/shard_map/ppermute | solution.py:33
  32.5 1.3 %collective-permute-done.11.refs_2_ = bf16[256,128]{1,0:T(8,128)(2,1)S(1)} collective-permute-done((bf16[256,128]{1,0:T(8,128)(2,1)S(1)}, bf16[256,128]{1,0:T(8,128)(2,1)S(1)}, u32[]{:S(2)}, u32[]{:S(2)}) %collective-permute-start.11) | collective-permute-done | bytes 65568 | tf_op jit(solution)/shard_map/ppermute | solution.py:33
  33.8 0.7 %collective-permute-start.7 = (bf16[256,128]{1,0:T(8,128)(2,1)S(1)}, bf16[256,128]{1,0:T(8,128)(2,1)S(1)}, u32[]{:S(2)}, u32[]{:S(2)}) collective-permute-start(bf16[256,128]{1,0:T(8,128)(2,1)S(1)} %get-tuple-element.23.refs_2_), channel_id=1, source_target_pairs={{0,4},{2,6},{4,0},{6,2},{8,12},{10,14},{12,8},{14,10},{16,20},{18,... | collective-permute-start | bytes 196616 | tf_op jit(solution)/shard_map/ppermute | solution.py:33
  34.5 1.1 %collective-permute-done.10.refs_1_ = bf16[256,128]{1,0:T(8,128)(2,1)S(1)} collective-permute-done((bf16[256,128]{1,0:T(8,128)(2,1)S(1)}, bf16[256,128]{1,0:T(8,128)(2,1)S(1)}, u32[]{:S(2)}, u32[]{:S(2)}) %collective-permute-start.10) | collective-permute-done | bytes 65568 | tf_op jit(solution)/shard_map/ppermute | solution.py:33
  36.1 1.0 %collective-permute-done.8.refs_2_ = bf16[256,128]{1,0:T(8,128)(2,1)S(1)} collective-permute-done((bf16[256,128]{1,0:T(8,128)(2,1)S(1)}, bf16[256,128]{1,0:T(8,128)(2,1)S(1)}, u32[]{:S(2)}, u32[]{:S(2)}) %collective-permute-start.8) | collective-permute-done | bytes 65568 | tf_op jit(solution)/shard_map/ppermute | solution.py:33
  37.1 1.0 %collective-permute-done.7.refs_2_ = bf16[256,128]{1,0:T(8,128)(2,1)S(1)} collective-permute-done((bf16[256,128]{1,0:T(8,128)(2,1)S(1)}, bf16[256,128]{1,0:T(8,128)(2,1)S(1)}, u32[]{:S(2)}, u32[]{:S(2)}) %collective-permute-start.7) | collective-permute-done | bytes 65568 | tf_op jit(solution)/shard_map/ppermute | solution.py:33
  38.1 1.8 %collective-permute-done.6.refs_2_ = bf16[256,128]{1,0:T(8,128)(2,1)S(1)} collective-permute-done((bf16[256,128]{1,0:T(8,128)(2,1)S(1)}, bf16[256,128]{1,0:T(8,128)(2,1)S(1)}, u32[]{:S(2)}, u32[]{:S(2)}) %collective-permute-start.6) | collective-permute-done | bytes 65568 | tf_op jit(solution)/shard_map/ppermute | solution.py:33
  40.4 0.9 %collective-permute-start.13 = (bf16[3,256,128]{2,1,0:T(8,128)(2,1)S(1)}, bf16[3,256,128]{2,1,0:T(8,128)(2,1)S(1)}, u32[]{:S(2)}, u32[]{:S(2)}) collective-permute-start(bf16[3,256,128]{2,1,0:T(8,128)(2,1)S(1)} %shard_map.137.refs_3_), channel_id=1, source_target_pairs={{0,4},{2,6},{4,0},{6,2},{8,12},{10,14},{12,8},{14,10},{16,20},{18,... | collective-permute-start | bytes 589832 | tf_op jit(solution)/shard_map/ppermute | solution.py:33
  41.3 2.2 %collective-permute-start.12 = (bf16[3,256,128]{2,1,0:T(8,128)(2,1)S(1)}, bf16[3,256,128]{2,1,0:T(8,128)(2,1)S(1)}, u32[]{:S(2)}, u32[]{:S(2)}) collective-permute-start(bf16[3,256,128]{2,1,0:T(8,128)(2,1)S(1)} %shard_map.137.refs_3_), channel_id=1, source_target_pairs={{0,6},{2,4},{4,2},{6,0},{8,14},{10,12},{12,10},{14,8},{16,22},{18,... | collective-permute-start | bytes 589832 | tf_op jit(solution)/shard_map/ppermute | solution.py:33
  43.5 1.1 %shard_map.142 = bf16[4096,128]{1,0:T(8,128)(2,1)} custom-call(f32[4096,128]{1,0:T(8,128)S(1)} %get-tuple-element.30.x_ref), custom_call_target="tpu_custom_call" | custom-call | flops 524288 | bytes 3145728 | tf_op jit(solution)/shard_map/pallas_call | solution.py:253
  44.5 0.8 %shard_map.143 = (f32[256,128]{1,0:T(8,128)}, f32[256,128]{1,0:T(8,128)}, f32[256,128]{1,0:T(8,128)}) custom-call(f32[256,128]{1,0:T(8,128)S(1)} %get-tuple-element.31.g_ref, f32[256,128]{1,0:T(8,128)S(1)} %copy-done.3, f32[256,128]{1,0:T(8,128)S(1)} %copy-done.4, f32[256,128]{1,0:T(8,128)S(1)} %copy-done.5), custom_call_target="tpu_custom_call" | custom-call | flops 655360 | bytes 917504 | tf_op jit(solution)/shard_map/pallas_call | solution.py:237
  45.3 2.4 %shard_map.134.refs_1_ = bf16[512,4096]{1,0:T(8,128)(2,1)S(1)} custom-call(bf16[512,4096]{1,0:T(8,128)(2,1)} %collective-permute-done.5.refs_0_), custom_call_target="tpu_custom_call" | custom-call | bytes 8388608 | tf_op jit(solution)/shard_map/pallas_call | solution.py:72
  47.7 1.1 %copy-done.1 = bf16[512,4096]{1,0:T(8,128)(2,1)S(1)} copy-done((bf16[512,4096]{1,0:T(8,128)(2,1)S(1)}, bf16[512,4096]{1,0:T(8,128)(2,1)}, u32[]{:S(2)}) %copy-start.1) | copy-done | bytes 4194328
  48.8 0.7 %shard_map.138.refs_4_ = f32[1024,128]{1,0:T(8,128)S(1)} custom-call(s32[1]{0:T(128)} %bitcast.me, s32[1]{0:T(128)} %bitcast.1.core, bf16[512,4096]{1,0:T(8,128)(2,1)S(1)} %copy-done.1, bf16[512,4096]{1,0:T(8,128)(2,1)S(1)} %shard_map.134.refs_1_, bf16[256,128]{1,0:T(8,128)(2,1)S(1)} %get-tuple-element.23.refs_2_, bf16[3,256,128]{2,1,0:T(8,128)(2,1)S(1)} %shard_map.137.refs_3_), custom_call_target="tpu_custom_call" | custom-call | flops 268435456 | bytes 3145728 | tf_op jit(solution)/shard_map/pallas_call | solution.py:309
  49.5 0.7 %shard_map.139.refs_4_ = f32[1024,128]{1,0:T(8,128)S(1)} custom-call(s32[1]{0:T(128)} %bitcast.me, s32[1]{0:T(128)} %bitcast.1.core, bf16[512,4096]{1,0:T(8,128)(2,1)S(1)} %copy-done.1, bf16[512,4096]{1,0:T(8,128)(2,1)S(1)} %shard_map.134.refs_1_, bf16[256,128]{1,0:T(8,128)(2,1)S(1)} %collective-permute-done.6.refs_2_, ...), custom_call_target="tpu_custom_call" | custom-call | flops 268435456 | bytes 3145728 | tf_op jit(solution)/shard_map/pallas_call | solution.py:309
  50.2 0.7 %shard_map.140.refs_4_ = f32[1024,128]{1,0:T(8,128)S(1)} custom-call(s32[1]{0:T(128)} %bitcast.me, s32[1]{0:T(128)} %bitcast.1.core, bf16[512,4096]{1,0:T(8,128)(2,1)S(1)} %copy-done.1, bf16[512,4096]{1,0:T(8,128)(2,1)S(1)} %shard_map.134.refs_1_, bf16[256,128]{1,0:T(8,128)(2,1)S(1)} %collective-permute-done.7.refs_2_, ...), custom_call_target="tpu_custom_call" | custom-call | flops 268435456 | bytes 3145728 | tf_op jit(solution)/shard_map/pallas_call | solution.py:309
  50.9 1.4 %shard_map.141 = bf16[1024,128]{1,0:T(8,128)(2,1)} custom-call(s32[1]{0:T(128)} %bitcast.me, s32[1]{0:T(128)} %bitcast.1.core, bf16[512,4096]{1,0:T(8,128)(2,1)S(1)} %copy-done.1, bf16[512,4096]{1,0:T(8,128)(2,1)S(1)} %shard_map.134.refs_1_, bf16[256,128]{1,0:T(8,128)(2,1)S(1)} %collective-permute-done.8.refs_2_, ...), custom_call_target="tpu_custom_call" | custom-call | flops 268435456 | bytes 3145728 | tf_op jit(solution)/shard_map/pallas_call | solution.py:309
  (34 shorter events, 2.2 us)
Async XLA Ops:
  0.6 2.8 %collective-permute-start = (bf16[1024,128]{1,0:T(8,128)(2,1)}, bf16[1024,128]{1,0:T(8,128)(2,1)S(1)}, u32[]{:S(2)}, u32[]{:S(2)}) collective-permute-start(bf16[1024,128]{1,0:T(8,128)(2,1)} %g_ref), channel_id=1, source_target_pairs={{0,1},{1,0},{2,3},{3,2},{4,5},{5,4},{6,7},{7,6},{8,9},{9,8},{10,11... | collective-permute-start | bytes 786440 | tf_op jit(solution)/shard_map/ppermute | solution.py:29
  3.4 3.5 %copy-start = (bf16[512,4096]{1,0:T(8,128)(2,1)}, bf16[512,4096]{1,0:T(8,128)(2,1)S(1)}, u32[]{:S(2)}) copy-start(bf16[512,4096]{1,0:T(8,128)(2,1)S(1)} %shard_map.128.f_ref.refs_0_) | copy-start | bytes 12582916
  3.9 4.4 %collective-permute-start.1 = (f32[1024,128]{1,0:T(8,128)S(1)}, f32[1024,128]{1,0:T(8,128)S(1)}, u32[]{:S(2)}, u32[]{:S(2)}) collective-permute-start(f32[1024,128]{1,0:T(8,128)S(1)} %shard_map.131), channel_id=1, source_target_pairs={{0,1},{1,0},{2,3},{3,2},{4,5},{5,4},{6,7},{7,6},{8,9},{9,8},{10,11... | collective-permute-start | bytes 1572872 | tf_op jit(solution)/shard_map/ppermute | solution.py:29
  4.6 2.3 %copy-start.2 = (bf16[1,4096,128]{2,1,0:T(8,128)(2,1)S(1)}, bf16[1,4096,128]{2,1,0:T(8,128)(2,1)}, u32[]{:S(2)}) copy-start(bf16[1,4096,128]{2,1,0:T(8,128)(2,1)} %param.11) | copy-start | bytes 3145732
  4.6 2.3 %copy-start.6 = (bf16[1024,128]{1,0:T(8,128)(2,1)S(1)}, bf16[1024,128]{1,0:T(8,128)(2,1)}, u32[]{:S(2)}) copy-start(bf16[1024,128]{1,0:T(8,128)(2,1)} %g_ref) | copy-start | bytes 786436
  4.6 3.7 %collective-permute-start.2 = (f32[1024,128]{1,0:T(8,128)S(1)}, f32[1024,128]{1,0:T(8,128)S(1)}, u32[]{:S(2)}, u32[]{:S(2)}) collective-permute-start(f32[1024,128]{1,0:T(8,128)S(1)} %shard_map.132), channel_id=1, source_target_pairs={{0,1},{1,0},{2,3},{3,2},{4,5},{5,4},{6,7},{7,6},{8,9},{9,8},{10,11... | collective-permute-start | bytes 1572872 | tf_op jit(solution)/shard_map/ppermute | solution.py:29
  5.6 2.7 %collective-permute-start.3 = (f32[1024,128]{1,0:T(8,128)S(1)}, f32[1024,128]{1,0:T(8,128)S(1)}, u32[]{:S(2)}, u32[]{:S(2)}) collective-permute-start(f32[1024,128]{1,0:T(8,128)S(1)} %shard_map.133), channel_id=1, source_target_pairs={{0,1},{1,0},{2,3},{3,2},{4,5},{5,4},{6,7},{7,6},{8,9},{9,8},{10,11... | collective-permute-start | bytes 1572872 | tf_op jit(solution)/shard_map/ppermute | solution.py:29
  6.3 2.5 %copy-start.7 = (s32[17]{0:T(128)S(1)}, s32[17]{0:T(128)}, u32[]{:S(2)}) copy-start(s32[17]{0:T(128)} %edges.3) | copy-start | bytes 208
  6.3 2.4 %copy-start.8 = (s32[1,1,32]{2,1,0:T(1,128)S(1)}, s32[1,1,32]{2,1,0:T(1,128)}, u32[]{:S(2)}) copy-start(s32[1,1,32]{2,1,0:T(1,128)} %param.12) | copy-start | bytes 388
  6.3 2.0 %collective-permute-start.4 = (f32[1024,128]{1,0:T(8,128)S(1)}, f32[1024,128]{1,0:T(8,128)S(1)}, u32[]{:S(2)}, u32[]{:S(2)}) collective-permute-start(f32[1024,128]{1,0:T(8,128)S(1)} %shard_map.129), channel_id=1, source_target_pairs={{0,1},{1,0},{2,3},{3,2},{4,5},{5,4},{6,7},{7,6},{8,9},{9,8},{10,11... | collective-permute-start | bytes 1572872 | tf_op jit(solution)/shard_map/ppermute | solution.py:29
  6.8 19.5 %copy-start.3 = (f32[256,128]{1,0:T(8,128)S(1)}, f32[256,128]{1,0:T(8,128)}, u32[]{:S(2)}) copy-start(f32[256,128]{1,0:T(8,128)} %m_ref.3) | copy-start | bytes 393220
  6.9 19.5 %copy-start.4 = (f32[256,128]{1,0:T(8,128)S(1)}, f32[256,128]{1,0:T(8,128)}, u32[]{:S(2)}) copy-start(f32[256,128]{1,0:T(8,128)} %v_ref.3) | copy-start | bytes 393220
  6.9 19.5 %copy-start.5 = (f32[256,128]{1,0:T(8,128)S(1)}, f32[256,128]{1,0:T(8,128)}, u32[]{:S(2)}) copy-start(f32[256,128]{1,0:T(8,128)} %w_ref.3) | copy-start | bytes 393220
  8.4 37.0 %collective-permute-start.5 = (bf16[512,4096]{1,0:T(8,128)(2,1)}, bf16[512,4096]{1,0:T(8,128)(2,1)}, u32[]{:S(2)}, u32[]{:S(2)}) collective-permute-start(bf16[512,4096]{1,0:T(8,128)(2,1)} %refs_0_.1), channel_id=1, source_target_pairs={{0,1},{1,0},{2,3},{3,2},{4,5},{5,4},{6,7},{7,6},{8,9},{9,8},{10,11... | collective-permute-start | bytes 12582920 | tf_op jit(solution)/shard_map/ppermute | solution.py:29
  10.8 15.6 %all-to-all-start = ((f32[16,8,128]{2,1,0:T(8,128)}), f32[16,8,128]{2,1,0:T(8,128)S(1)}, u32[]{:S(2)}, u32[]{:S(2)}) async-start(f32[16,8,128]{2,1,0:T(8,128)} %bitcast.4), calls=%async_computation | async-start | bytes 131072 | tf_op jit(solution)/shard_map/all_to_all | solution.py:352
  27.4 6.4 %collective-permute-start.11 = (bf16[256,128]{1,0:T(8,128)(2,1)S(1)}, bf16[256,128]{1,0:T(8,128)(2,1)S(1)}, u32[]{:S(2)}, u32[]{:S(2)}) collective-permute-start(bf16[256,128]{1,0:T(8,128)(2,1)S(1)} %get-tuple-element.23.refs_2_), channel_id=1, source_target_pairs={{0,24},{2,26},{4,28},{6,30},{8,16},{10,18},{12,20},{14,22},{16,8},... | collective-permute-start | bytes 196616 | tf_op jit(solution)/shard_map/ppermute | solution.py:33
  28.4 7.2 %collective-permute-start.10 = (bf16[256,128]{1,0:T(8,128)(2,1)S(1)}, bf16[256,128]{1,0:T(8,128)(2,1)S(1)}, u32[]{:S(2)}, u32[]{:S(2)}) collective-permute-start(bf16[256,128]{1,0:T(8,128)(2,1)S(1)} %get-tuple-element.23.refs_2_), channel_id=1, source_target_pairs={{0,16},{2,18},{4,20},{6,22},{8,24},{10,26},{12,28},{14,30},{16,0},... | collective-permute-start | bytes 196616 | tf_op jit(solution)/shard_map/ppermute | solution.py:33
  29.6 6.4 %collective-permute-start.9 = (bf16[256,128]{1,0:T(8,128)(2,1)S(1)}, bf16[256,128]{1,0:T(8,128)(2,1)S(1)}, u32[]{:S(2)}, u32[]{:S(2)}) collective-permute-start(bf16[256,128]{1,0:T(8,128)(2,1)S(1)} %get-tuple-element.23.refs_2_), channel_id=1, source_target_pairs={{0,8},{2,10},{4,12},{6,14},{8,0},{10,2},{12,4},{14,6},{16,24},{18,... | collective-permute-start | bytes 196616 | tf_op jit(solution)/shard_map/ppermute | solution.py:33
  31.9 5.2 %collective-permute-start.8 = (bf16[256,128]{1,0:T(8,128)(2,1)S(1)}, bf16[256,128]{1,0:T(8,128)(2,1)S(1)}, u32[]{:S(2)}, u32[]{:S(2)}) collective-permute-start(bf16[256,128]{1,0:T(8,128)(2,1)S(1)} %get-tuple-element.23.refs_2_), channel_id=1, source_target_pairs={{0,6},{2,4},{4,2},{6,0},{8,14},{10,12},{12,10},{14,8},{16,22},{18,... | collective-permute-start | bytes 196616 | tf_op jit(solution)/shard_map/ppermute | solution.py:33
  33.8 4.3 %collective-permute-start.7 = (bf16[256,128]{1,0:T(8,128)(2,1)S(1)}, bf16[256,128]{1,0:T(8,128)(2,1)S(1)}, u32[]{:S(2)}, u32[]{:S(2)}) collective-permute-start(bf16[256,128]{1,0:T(8,128)(2,1)S(1)} %get-tuple-element.23.refs_2_), channel_id=1, source_target_pairs={{0,4},{2,6},{4,0},{6,2},{8,12},{10,14},{12,8},{14,10},{16,20},{18,... | collective-permute-start | bytes 196616 | tf_op jit(solution)/shard_map/ppermute | solution.py:33
  35.6 4.3 %collective-permute-start.6 = (bf16[256,128]{1,0:T(8,128)(2,1)S(1)}, bf16[256,128]{1,0:T(8,128)(2,1)S(1)}, u32[]{:S(2)}, u32[]{:S(2)}) collective-permute-start(bf16[256,128]{1,0:T(8,128)(2,1)S(1)} %get-tuple-element.23.refs_2_), channel_id=1, source_target_pairs={{0,2},{2,0},{4,6},{6,4},{8,10},{10,8},{12,14},{14,12},{16,18},{18,... | collective-permute-start | bytes 196616 | tf_op jit(solution)/shard_map/ppermute | solution.py:33
  39.9 9.6 %collective-permute-start.14 = (bf16[3,256,128]{2,1,0:T(8,128)(2,1)S(1)}, bf16[3,256,128]{2,1,0:T(8,128)(2,1)S(1)}, u32[]{:S(2)}, u32[]{:S(2)}) collective-permute-start(bf16[3,256,128]{2,1,0:T(8,128)(2,1)S(1)} %shard_map.137.refs_3_), channel_id=1, source_target_pairs={{0,2},{2,0},{4,6},{6,4},{8,10},{10,8},{12,14},{14,12},{16,18},{18,... | collective-permute-start | bytes 589832 | tf_op jit(solution)/shard_map/ppermute | solution.py:33
  40.4 9.8 %collective-permute-start.13 = (bf16[3,256,128]{2,1,0:T(8,128)(2,1)S(1)}, bf16[3,256,128]{2,1,0:T(8,128)(2,1)S(1)}, u32[]{:S(2)}, u32[]{:S(2)}) collective-permute-start(bf16[3,256,128]{2,1,0:T(8,128)(2,1)S(1)} %shard_map.137.refs_3_), channel_id=1, source_target_pairs={{0,4},{2,6},{4,0},{6,2},{8,12},{10,14},{12,8},{14,10},{16,20},{18,... | collective-permute-start | bytes 589832 | tf_op jit(solution)/shard_map/ppermute | solution.py:33
  41.3 9.6 %collective-permute-start.12 = (bf16[3,256,128]{2,1,0:T(8,128)(2,1)S(1)}, bf16[3,256,128]{2,1,0:T(8,128)(2,1)S(1)}, u32[]{:S(2)}, u32[]{:S(2)}) collective-permute-start(bf16[3,256,128]{2,1,0:T(8,128)(2,1)S(1)} %shard_map.137.refs_3_), channel_id=1, source_target_pairs={{0,6},{2,4},{4,2},{6,0},{8,14},{10,12},{12,10},{14,8},{16,22},{18,... | collective-permute-start | bytes 589832 | tf_op jit(solution)/shard_map/ppermute | solution.py:33
  45.3 3.4 %copy-start.1 = (bf16[512,4096]{1,0:T(8,128)(2,1)S(1)}, bf16[512,4096]{1,0:T(8,128)(2,1)}, u32[]{:S(2)}) copy-start(bf16[512,4096]{1,0:T(8,128)(2,1)} %copy-done) | copy-start | bytes 12582916

commit v4 on v3

--- a/solution.py
+++ b/solution.py
@@ -278,12 +278,10 @@
 
 
 def project_kernel(masks, last, n_f, me, core, *refs):
-    feats, pieces, out_ref = refs[:n_f], refs[n_f : n_f + 2], refs[-1]
+    feats, w_ref, out_ref = refs[:n_f], refs[n_f], refs[-1]
     tokens = feats[0].shape[0]
-    region = pieces[0].shape[0]
-    weight = jnp.concatenate(
-        [pieces[0][...]] + [pieces[1][j] for j in range(pieces[1].shape[0])], axis=0
-    )
+    count, region, width = w_ref.shape
+    weight = w_ref[...].reshape(count * region, width)
     for i, f_ref in enumerate(feats):
         mine = pl.ds(i * tokens, tokens)
         part = [
@@ -292,8 +290,8 @@
         total = jnp.dot(
             jnp.concatenate(part, axis=1), weight, preferred_element_type=jnp.float32
         )
-        if len(refs) > n_f + 3:
-            total = total + refs[n_f + 2][mine, :]
+        if len(refs) > n_f + 2:
+            total = total + refs[n_f + 1][mine, :]
         if last:
             place = lax.rem(core[0] + i, n_f) * tokens
             mine = pl.ds(pl.multiple_of(place, tokens), tokens)
@@ -301,19 +299,19 @@
 
 
 def project(masks, me, core, feats, pieces, total, last):
-    region, width = pieces[0].shape
+    region, width = pieces.shape[1:]
     whole = len(feats) * feats[0].shape[0]
     old = [] if total is None else [total]
     out = jax.ShapeDtypeStruct((whole, width), jnp.bfloat16 if last else jnp.float32)
     depth = len(masks) * region
     return pl.pallas_call(
         functools.partial(project_kernel, masks, last, len(feats)),
-        in_specs=[SMEM, SMEM] + [VMEM] * (len(feats) + 2 + len(old)),
+        in_specs=[SMEM, SMEM] + [VMEM] * (len(feats) + 1 + len(old)),
         out_specs=VMEM,
         out_shape=out,
-        compiler_params=params(*pieces, out, *feats, *old),
+        compiler_params=params(pieces, out, *feats, *old),
         cost_estimate=cost(2 * whole * depth * width, 2 * whole * depth + 8 * whole * width),
-    )(me, core, *feats, *pieces, *old)
+    )(me, core, *feats, pieces, *old)
 
 
 def spans(mask_bits):
@@ -352,17 +350,17 @@
     arrived = lax.all_to_all(
         outgoing.reshape(owners, SLOTS, width), "dp", split_axis=0, concat_axis=0, tiled=True
     )
+    arrived, error_out = lax.optimization_barrier((arrived, error_out))
     grad, weight = weigh(me1, threshold, bin_edges, arrived, moment, second, master)
     bits = [1 << i for i in range(owners.bit_length() - 1)]
     if 1 << len(bits) == owners and len(bits) > 2 and region % LANES == 0:
         plane, line = spans(bits[:2]), spans(bits[2:])
-        near = [swap(weight, "dp", b) for b in plane[1:]]
         far = [swap(weight, "dp", m) for m in line[1:]]
-        near, far = lax.optimization_barrier((near, far))
-        rest = join(far)
-        groups = [[weight, rest]]
-        groups += [[own, swap(rest, "dp", b)] for own, b in zip(near, plane[1:])]
-        feats = [held, *load(feats[1:])]
+        others = load(feats[1:])
+        far, others = lax.optimization_barrier((far, others))
+        feats = [held, *others]
+        mine = join([weight] + far)
+        groups = [mine if b == 0 else swap(mine, "dp", b) for b in plane]
         keys = None
         for j, b in enumerate(plane):
             masks = tuple(b ^ m for m in line)

time: 52.6 us -> 49.7 us (0.945)
  starting transfers between devices: 20 us -> 18.2 us
  local copies, waits for them, and re-layouts: 1.12 us -> 0.05 us
    ppermute x9 -> x6, starting transfers between devices: 9.78 us -> 8.01 us  [swap(): lax.ppermute(x, axis, [(i, i ^ mask) for i in range(lax.axis_size(axis))])]
    ppermute x9 -> x6, waiting for transfers between devices: 6.23 us -> 7.47 us  [swap(): lax.ppermute(x, axis, [(i, i ^ mask) for i in range(lax.axis_size(axis))])]
    all_to_all x1, waiting for transfers between devices: 6.88 us -> 5.81 us  [shards(): lax.all_to_all(outgoing.reshape(owners, SLOTS, width), 'dp', split_axis=0...]
    unnamed x18, local copies, waits for them, and re-layouts: 1.12 us -> 0.05 us
  transfers between devices with their start and end apart: 16 -> 13, of which waited for: 7 -> 5; matrix products, arithmetic and copies ran while one was open for 0% -> 0% of each run, Pallas kernels for 28% -> 29%
where the time goes in v4:
time: 49.7 us; the launch traced here: 49.5 us
  starting transfers between devices  18.2 us (37%)
  Pallas kernels  16.4 us (33%)
  waiting for transfers between devices  13.3 us (27%)
  between operations  1.5 us (3%)
    all_to_all x1, starting transfers between devices, shards(): lax.all_to_all(outgoing.reshape(owners, SLOTS, width), 'dp', split_axis=0...  8.02 us
    ppermute x6, starting transfers between devices, swap(): lax.ppermute(x, axis, [(i, i ^ mask) for i in range(lax.axis_size(axis))])  8.01 us
    ppermute x6, waiting for transfers between devices, swap(): lax.ppermute(x, axis, [(i, i ^ mask) for i in range(lax.axis_size(axis))])  7.47 us
    all_to_all x1, waiting for transfers between devices, shards(): lax.all_to_all(outgoing.reshape(owners, SLOTS, width), 'dp', split_axis=0...  5.81 us
    pallas_call x2, Pallas kernels, load(): pl.pallas_call(functools.partial(load_kernel, pieces), in_specs=[ANY] * l...  4.43 us
    pallas_call x4, Pallas kernels, project(): pl.pallas_call(functools.partial(project_kernel, masks, last, len(feats))...  3.53 us
    pallas_call x5, Pallas kernels, part_sum(): pl.pallas_call(functools.partial(part_kernel, first), in_specs=[SMEM, VME...  3.49 us
    ppermute x6, starting transfers between devices, shift(): return lax.ppermute(x, axis, [(i, (i + step) % n) for i in range(n)])  2.17 us
  transfers between devices with their start and end apart: 13, of which 5 were waited for; matrix products, arithmetic and copies ran while one was open for 0% of the time, Pallas kernels for 29%

profile of v4, /device:TPU:0, one launch (start us, length us, event | category | flops | bytes accessed | tf_op | source)
XLA Modules:
  0.0 49.5 jit_solution(16097046816902302386)
XLA Ops:
  0.6 0.5 %collective-permute-start = (bf16[1024,128]{1,0:T(8,128)(2,1)}, bf16[1024,128]{1,0:T(8,128)(2,1)S(1)}, u32[]{:S(2)}, u32[]{:S(2)}) collective-permute-start(bf16[1024,128]{1,0:T(8,128)(2,1)} %g_ref), channel_id=1, source_target_pairs={{0,1},{1,0},{2,3},{3,2},{4,5},{5,4},{6,7},{7,6},{8,9},{9,8},{10,11... | collective-permute-start | bytes 786440 | tf_op jit(solution)/shard_map/ppermute | solution.py:29
  1.1 2.2 %shard_map.128.f_ref.refs_0_ = bf16[512,4096]{1,0:T(8,128)(2,1)S(1)} custom-call(bf16[512,4096]{1,0:T(8,128)(2,1)} %refs_0_.1), custom_call_target="tpu_custom_call" | custom-call | bytes 8388608 | tf_op jit(solution)/shard_map/pallas_call | solution.py:72
  3.4 0.5 %shard_map.131 = f32[1024,128]{1,0:T(8,128)S(1)} custom-call(s32[1]{0:T(128)} %bitcast.1.core, bf16[512,4096]{1,0:T(8,128)(2,1)S(1)} %shard_map.128.f_ref.refs_0_, bf16[1024,128]{1,0:T(8,128)(2,1)S(1)} %collective-permute-done.g_ref), custom_call_target="tpu_custom_call" | custom-call | flops 134217728 | bytes 1572864 | tf_op jit(solution)/shard_map/pallas_call | solution.py:104
  3.9 0.1 collective-permute-start.1
  4.0 0.5 %shard_map.132 = f32[1024,128]{1,0:T(8,128)S(1)} custom-call(s32[1]{0:T(128)} %bitcast.1.core, bf16[512,4096]{1,0:T(8,128)(2,1)S(1)} %shard_map.128.f_ref.refs_0_, bf16[1024,128]{1,0:T(8,128)(2,1)S(1)} %collective-permute-done.g_ref), custom_call_target="tpu_custom_call" | custom-call | flops 134217728 | bytes 1572864 | tf_op jit(solution)/shard_map/pallas_call | solution.py:104
  4.6 0.5 %collective-permute-start.2 = (f32[1024,128]{1,0:T(8,128)S(1)}, f32[1024,128]{1,0:T(8,128)S(1)}, u32[]{:S(2)}, u32[]{:S(2)}) collective-permute-start(f32[1024,128]{1,0:T(8,128)S(1)} %shard_map.132), channel_id=1, source_target_pairs={{0,1},{1,0},{2,3},{3,2},{4,5},{5,4},{6,7},{7,6},{8,9},{9,8},{10,11... | collective-permute-start | bytes 1572872 | tf_op jit(solution)/shard_map/ppermute | solution.py:29
  5.1 0.5 %shard_map.133 = f32[1024,128]{1,0:T(8,128)S(1)} custom-call(s32[1]{0:T(128)} %bitcast.1.core, bf16[512,4096]{1,0:T(8,128)(2,1)S(1)} %shard_map.128.f_ref.refs_0_, bf16[1024,128]{1,0:T(8,128)(2,1)S(1)} %collective-permute-done.g_ref), custom_call_target="tpu_custom_call" | custom-call | flops 134217728 | bytes 1572864 | tf_op jit(solution)/shard_map/pallas_call | solution.py:104
  5.6 0.1 collective-permute-start.3
  5.8 0.5 %shard_map.129 = f32[1024,128]{1,0:T(8,128)S(1)} custom-call(s32[1]{0:T(128)} %bitcast.1.core, bf16[512,4096]{1,0:T(8,128)(2,1)S(1)} %shard_map.128.f_ref.refs_0_, bf16[1024,128]{1,0:T(8,128)(2,1)S(1)} %collective-permute-done.g_ref), custom_call_target="tpu_custom_call" | custom-call | flops 134217728 | bytes 1572864 | tf_op jit(solution)/shard_map/pallas_call | solution.py:104
  6.3 0.5 %collective-permute-start.4 = (f32[1024,128]{1,0:T(8,128)S(1)}, f32[1024,128]{1,0:T(8,128)S(1)}, u32[]{:S(2)}, u32[]{:S(2)}) collective-permute-start(f32[1024,128]{1,0:T(8,128)S(1)} %shard_map.129), channel_id=1, source_target_pairs={{0,1},{1,0},{2,3},{3,2},{4,5},{5,4},{6,7},{7,6},{8,9},{9,8},{10,11... | collective-permute-start | bytes 1572872 | tf_op jit(solution)/shard_map/ppermute | solution.py:29
  6.8 1.4 %shard_map.130.own_ref = f32[4096,128]{1,0:T(8,128)S(1)} custom-call(s32[1]{0:T(128)} %bitcast.1.core, bf16[512,4096]{1,0:T(8,128)(2,1)S(1)} %shard_map.128.f_ref.refs_0_, bf16[1024,128]{1,0:T(8,128)(2,1)S(1)} %copy-done.6, bf16[4096,128]{1,0:T(8,128)(2,1)S(1)} %bitcast.6), custom_call_target="tpu_custom_call" | custom-call | flops 536870912 | bytes 6291456 | tf_op jit(solution)/shard_map/pallas_call | solution.py:104
  8.4 0.4 collective-permute-start.8
  8.8 2.1 %shard_map.134 = (f32[4096,128]{1,0:T(8,128)S(1)}, f32[128,128]{1,0:T(8,128)}) custom-call(s32[32]{0:T(128)S(1)} %bitcast.7, s32[17]{0:T(128)S(1)} %copy-done.7, f32[4096,128]{1,0:T(8,128)S(1)} %shard_map.130.own_ref, f32[1024,128]{1,0:T(8,128)S(1)} %collective-permute-done.1.refs_0_, f32[1024,128]{1,0:T(8,128)S(1)} %collective-permute-done.2.refs_1_, ...), custom_call_target="tpu_custom_call" | custom-call | flops 4194304 | bytes 6291456 | tf_op jit(solution)/shard_map/pallas_call | solution.py:157
  10.8 8.0 %all-to-all-start = ((f32[16,8,128]{2,1,0:T(8,128)}), f32[16,8,128]{2,1,0:T(8,128)S(1)}, u32[]{:S(2)}, u32[]{:S(2)}) async-start(f32[16,8,128]{2,1,0:T(8,128)} %bitcast.4), calls=%async_computation | async-start | bytes 131072 | tf_op jit(solution)/shard_map/all_to_all | solution.py:350
  19.5 1.1 %shard_map.135 = bf16[4096,128]{1,0:T(8,128)(2,1)} custom-call(f32[4096,128]{1,0:T(8,128)S(1)} %get-tuple-element.22.x_ref), custom_call_target="tpu_custom_call" | custom-call | flops 524288 | bytes 3145728 | tf_op jit(solution)/shard_map/pallas_call | solution.py:253
  20.6 5.8 %all-to-all-done.arr_ref = f32[16,8,128]{2,1,0:T(8,128)S(1)} async-done(((f32[16,8,128]{2,1,0:T(8,128)}), f32[16,8,128]{2,1,0:T(8,128)S(1)}, u32[]{:S(2)}, u32[]{:S(2)}) %all-to-all-start) | async-done | bytes 65568 | tf_op jit(solution)/shard_map/all_to_all | solution.py:350
  26.4 1.0 %shard_map.136 = (f32[256,128]{1,0:T(8,128)S(1)}, bf16[256,128]{1,0:T(8,128)(2,1)S(1)}) custom-call(s32[1]{0:T(128)} %bitcast.me, s32[1]{0:T(128)S(6)} %copy.14.least, s32[17]{0:T(128)S(1)} %copy-done.7, f32[16,8,128]{2,1,0:T(8,128)S(1)} %all-to-all-done.arr_ref, f32[256,128]{1,0:T(8,128)S(1)} %copy-done.3, f32[256,128]{1,0:T(8,128)S(1)} %copy-done.4, ...), custom_call_target="tpu_custom_call" | custom-call | flops 50331648 | bytes 983040 | tf_op jit(solution)/shard_map/pallas_call | solution.py:220
  27.4 0.7 %collective-permute-start.5 = (bf16[256,128]{1,0:T(8,128)(2,1)S(1)}, bf16[256,128]{1,0:T(8,128)(2,1)S(1)}, u32[]{:S(2)}, u32[]{:S(2)}) collective-permute-start(bf16[256,128]{1,0:T(8,128)(2,1)S(1)} %get-tuple-element.24.refs_0_), channel_id=1, source_target_pairs={{0,8},{2,10},{4,12},{6,14},{8,0},{10,2},{12,4},{14,6},{16,24},{18,... | collective-permute-start | bytes 196616 | tf_op jit(solution)/shard_map/ppermute | solution.py:33
  28.1 0.8 %collective-permute-start.6 = (bf16[256,128]{1,0:T(8,128)(2,1)S(1)}, bf16[256,128]{1,0:T(8,128)(2,1)S(1)}, u32[]{:S(2)}, u32[]{:S(2)}) collective-permute-start(bf16[256,128]{1,0:T(8,128)(2,1)S(1)} %get-tuple-element.24.refs_0_), channel_id=1, source_target_pairs={{0,16},{2,18},{4,20},{6,22},{8,24},{10,26},{12,28},{14,30},{16,0},... | collective-permute-start | bytes 196616 | tf_op jit(solution)/shard_map/ppermute | solution.py:33
  29.0 2.9 %collective-permute-start.7 = (bf16[256,128]{1,0:T(8,128)(2,1)S(1)}, bf16[256,128]{1,0:T(8,128)(2,1)S(1)}, u32[]{:S(2)}, u32[]{:S(2)}) collective-permute-start(bf16[256,128]{1,0:T(8,128)(2,1)S(1)} %get-tuple-element.24.refs_0_), channel_id=1, source_target_pairs={{0,24},{2,26},{4,28},{6,30},{8,16},{10,18},{12,20},{14,22},{16,8},... | collective-permute-start | bytes 196616 | tf_op jit(solution)/shard_map/ppermute | solution.py:33
  31.9 2.2 %shard_map.137.refs_1_ = bf16[512,4096]{1,0:T(8,128)(2,1)S(1)} custom-call(bf16[512,4096]{1,0:T(8,128)(2,1)} %collective-permute-done.8.refs_0_), custom_call_target="tpu_custom_call" | custom-call | bytes 8388608 | tf_op jit(solution)/shard_map/pallas_call | solution.py:72
  34.1 1.2 %collective-permute-done.6.refs_2_ = bf16[256,128]{1,0:T(8,128)(2,1)S(1)} collective-permute-done((bf16[256,128]{1,0:T(8,128)(2,1)S(1)}, bf16[256,128]{1,0:T(8,128)(2,1)S(1)}, u32[]{:S(2)}, u32[]{:S(2)}) %collective-permute-start.6) | collective-permute-done | bytes 65568 | tf_op jit(solution)/shard_map/ppermute | solution.py:33
  35.3 0.8 %collective-permute-start.11 = (bf16[4,256,128]{2,1,0:T(8,128)(2,1)S(1)}, bf16[4,256,128]{2,1,0:T(8,128)(2,1)S(1)}, u32[]{:S(2)}, u32[]{:S(2)}) collective-permute-start(bf16[4,256,128]{2,1,0:T(8,128)(2,1)S(1)} %shard_map.138.refs_2_), channel_id=1, source_target_pairs={{0,2},{2,0},{4,6},{6,4},{8,10},{10,8},{12,14},{14,12},{16,18},{18,... | collective-permute-start | bytes 786440 | tf_op jit(solution)/shard_map/ppermute | solution.py:33
  36.1 0.5 %collective-permute-start.10 = (bf16[4,256,128]{2,1,0:T(8,128)(2,1)S(1)}, bf16[4,256,128]{2,1,0:T(8,128)(2,1)S(1)}, u32[]{:S(2)}, u32[]{:S(2)}) collective-permute-start(bf16[4,256,128]{2,1,0:T(8,128)(2,1)S(1)} %shard_map.138.refs_2_), channel_id=1, source_target_pairs={{0,4},{2,6},{4,0},{6,2},{8,12},{10,14},{12,8},{14,10},{16,20},{18,... | collective-permute-start | bytes 786440 | tf_op jit(solution)/shard_map/ppermute | solution.py:33
  36.6 2.3 %collective-permute-start.9 = (bf16[4,256,128]{2,1,0:T(8,128)(2,1)S(1)}, bf16[4,256,128]{2,1,0:T(8,128)(2,1)S(1)}, u32[]{:S(2)}, u32[]{:S(2)}) collective-permute-start(bf16[4,256,128]{2,1,0:T(8,128)(2,1)S(1)} %shard_map.138.refs_2_), channel_id=1, source_target_pairs={{0,6},{2,4},{4,2},{6,0},{8,14},{10,12},{12,10},{14,8},{16,22},{18,... | collective-permute-start | bytes 786440 | tf_op jit(solution)/shard_map/ppermute | solution.py:33
  38.9 0.8 %shard_map.143 = (f32[256,128]{1,0:T(8,128)}, f32[256,128]{1,0:T(8,128)}, f32[256,128]{1,0:T(8,128)}) custom-call(f32[256,128]{1,0:T(8,128)S(1)} %get-tuple-element.31.g_ref, f32[256,128]{1,0:T(8,128)S(1)} %copy-done.3, f32[256,128]{1,0:T(8,128)S(1)} %copy-done.4, f32[256,128]{1,0:T(8,128)S(1)} %copy-done.5), custom_call_target="tpu_custom_call" | custom-call | flops 655360 | bytes 917504 | tf_op jit(solution)/shard_map/pallas_call | solution.py:237
  39.7 0.7 %shard_map.139.refs_3_ = f32[1024,128]{1,0:T(8,128)S(1)} custom-call(s32[1]{0:T(128)} %bitcast.me, s32[1]{0:T(128)} %bitcast.1.core, bf16[512,4096]{1,0:T(8,128)(2,1)S(1)} %copy-done.1, bf16[512,4096]{1,0:T(8,128)(2,1)S(1)} %shard_map.137.refs_1_, bf16[4,256,128]{2,1,0:T(8,128)(2,1)S(1)} %shard_map.138.refs_2_), custom_call_target="tpu_custom_call" | custom-call | flops 268435456 | bytes 3145728 | tf_op jit(solution)/shard_map/pallas_call | solution.py:307
  40.4 3.7 %collective-permute-done.11.refs_2_ = bf16[4,256,128]{2,1,0:T(8,128)(2,1)S(1)} collective-permute-done((bf16[4,256,128]{2,1,0:T(8,128)(2,1)S(1)}, bf16[4,256,128]{2,1,0:T(8,128)(2,1)S(1)}, u32[]{:S(2)}, u32[]{:S(2)}) %collective-permute-start.11) | collective-permute-done | bytes 262176 | tf_op jit(solution)/shard_map/ppermute | solution.py:33
  44.1 0.7 %shard_map.140.refs_3_ = f32[1024,128]{1,0:T(8,128)S(1)} custom-call(s32[1]{0:T(128)} %bitcast.me, s32[1]{0:T(128)} %bitcast.1.core, bf16[512,4096]{1,0:T(8,128)(2,1)S(1)} %copy-done.1, bf16[512,4096]{1,0:T(8,128)(2,1)S(1)} %shard_map.137.refs_1_, bf16[4,256,128]{2,1,0:T(8,128)(2,1)S(1)} %collective-permute-done.11.refs_2_, f32[1024,128]{1,0:T(8,128)S(1)} %shard_map.139.refs_3_), custom_call_target="tpu_custom_call" | custom-call | flops 268435456 | bytes 3145728 | tf_op jit(solution)/shard_map/pallas_call | solution.py:307
  44.9 2.5 %collective-permute-done.10.refs_2_ = bf16[4,256,128]{2,1,0:T(8,128)(2,1)S(1)} collective-permute-done((bf16[4,256,128]{2,1,0:T(8,128)(2,1)S(1)}, bf16[4,256,128]{2,1,0:T(8,128)(2,1)S(1)}, u32[]{:S(2)}, u32[]{:S(2)}) %collective-permute-start.10) | collective-permute-done | bytes 262176 | tf_op jit(solution)/shard_map/ppermute | solution.py:33
  47.4 0.7 %shard_map.141.refs_3_ = f32[1024,128]{1,0:T(8,128)S(1)} custom-call(s32[1]{0:T(128)} %bitcast.me, s32[1]{0:T(128)} %bitcast.1.core, bf16[512,4096]{1,0:T(8,128)(2,1)S(1)} %copy-done.1, bf16[512,4096]{1,0:T(8,128)(2,1)S(1)} %shard_map.137.refs_1_, bf16[4,256,128]{2,1,0:T(8,128)(2,1)S(1)} %collective-permute-done.10.refs_2_, f32[1024,128]{1,0:T(8,128)S(1)} %shard_map.140.refs_3_), custom_call_target="tpu_custom_call" | custom-call | flops 268435456 | bytes 3145728 | tf_op jit(solution)/shard_map/pallas_call | solution.py:307
  48.1 1.4 %shard_map.142 = bf16[1024,128]{1,0:T(8,128)(2,1)} custom-call(s32[1]{0:T(128)} %bitcast.me, s32[1]{0:T(128)} %bitcast.1.core, bf16[512,4096]{1,0:T(8,128)(2,1)S(1)} %copy-done.1, bf16[512,4096]{1,0:T(8,128)(2,1)S(1)} %shard_map.137.refs_1_, bf16[4,256,128]{2,1,0:T(8,128)(2,1)S(1)} %collective-permute-done.9.refs_2_, f32[1024,128]{1,0:T(8,128)S(1)} %shard_map.141.refs_3_), custom_call_target="tpu_custom_call" | custom-call | flops 268435456 | bytes 3145728 | tf_op jit(solution)/shard_map/pallas_call | solution.py:307
  (28 shorter events, 0.1 us)
Async XLA Ops:
  0.6 2.8 %collective-permute-start = (bf16[1024,128]{1,0:T(8,128)(2,1)}, bf16[1024,128]{1,0:T(8,128)(2,1)S(1)}, u32[]{:S(2)}, u32[]{:S(2)}) collective-permute-start(bf16[1024,128]{1,0:T(8,128)(2,1)} %g_ref), channel_id=1, source_target_pairs={{0,1},{1,0},{2,3},{3,2},{4,5},{5,4},{6,7},{7,6},{8,9},{9,8},{10,11... | collective-permute-start | bytes 786440 | tf_op jit(solution)/shard_map/ppermute | solution.py:29
  3.4 3.5 %copy-start = (bf16[512,4096]{1,0:T(8,128)(2,1)}, bf16[512,4096]{1,0:T(8,128)(2,1)S(1)}, u32[]{:S(2)}) copy-start(bf16[512,4096]{1,0:T(8,128)(2,1)S(1)} %shard_map.128.f_ref.refs_0_) | copy-start | bytes 12582916
  3.9 4.4 %collective-permute-start.1 = (f32[1024,128]{1,0:T(8,128)S(1)}, f32[1024,128]{1,0:T(8,128)S(1)}, u32[]{:S(2)}, u32[]{:S(2)}) collective-permute-start(f32[1024,128]{1,0:T(8,128)S(1)} %shard_map.131), channel_id=1, source_target_pairs={{0,1},{1,0},{2,3},{3,2},{4,5},{5,4},{6,7},{7,6},{8,9},{9,8},{10,11... | collective-permute-start | bytes 1572872 | tf_op jit(solution)/shard_map/ppermute | solution.py:29
  4.6 2.3 %copy-start.2 = (bf16[1,4096,128]{2,1,0:T(8,128)(2,1)S(1)}, bf16[1,4096,128]{2,1,0:T(8,128)(2,1)}, u32[]{:S(2)}) copy-start(bf16[1,4096,128]{2,1,0:T(8,128)(2,1)} %param.11) | copy-start | bytes 3145732
  4.6 2.3 %copy-start.6 = (bf16[1024,128]{1,0:T(8,128)(2,1)S(1)}, bf16[1024,128]{1,0:T(8,128)(2,1)}, u32[]{:S(2)}) copy-start(bf16[1024,128]{1,0:T(8,128)(2,1)} %g_ref) | copy-start | bytes 786436
  4.6 3.7 %collective-permute-start.2 = (f32[1024,128]{1,0:T(8,128)S(1)}, f32[1024,128]{1,0:T(8,128)S(1)}, u32[]{:S(2)}, u32[]{:S(2)}) collective-permute-start(f32[1024,128]{1,0:T(8,128)S(1)} %shard_map.132), channel_id=1, source_target_pairs={{0,1},{1,0},{2,3},{3,2},{4,5},{5,4},{6,7},{7,6},{8,9},{9,8},{10,11... | collective-permute-start | bytes 1572872 | tf_op jit(solution)/shard_map/ppermute | solution.py:29
  5.6 2.7 %collective-permute-start.3 = (f32[1024,128]{1,0:T(8,128)S(1)}, f32[1024,128]{1,0:T(8,128)S(1)}, u32[]{:S(2)}, u32[]{:S(2)}) collective-permute-start(f32[1024,128]{1,0:T(8,128)S(1)} %shard_map.133), channel_id=1, source_target_pairs={{0,1},{1,0},{2,3},{3,2},{4,5},{5,4},{6,7},{7,6},{8,9},{9,8},{10,11... | collective-permute-start | bytes 1572872 | tf_op jit(solution)/shard_map/ppermute | solution.py:29
  6.3 2.5 %copy-start.7 = (s32[17]{0:T(128)S(1)}, s32[17]{0:T(128)}, u32[]{:S(2)}) copy-start(s32[17]{0:T(128)} %edges.3) | copy-start | bytes 208
  6.3 2.4 %copy-start.8 = (s32[1,1,32]{2,1,0:T(1,128)S(1)}, s32[1,1,32]{2,1,0:T(1,128)}, u32[]{:S(2)}) copy-start(s32[1,1,32]{2,1,0:T(1,128)} %param.12) | copy-start | bytes 388
  6.3 2.0 %collective-permute-start.4 = (f32[1024,128]{1,0:T(8,128)S(1)}, f32[1024,128]{1,0:T(8,128)S(1)}, u32[]{:S(2)}, u32[]{:S(2)}) collective-permute-start(f32[1024,128]{1,0:T(8,128)S(1)} %shard_map.129), channel_id=1, source_target_pairs={{0,1},{1,0},{2,3},{3,2},{4,5},{5,4},{6,7},{7,6},{8,9},{9,8},{10,11... | collective-permute-start | bytes 1572872 | tf_op jit(solution)/shard_map/ppermute | solution.py:29
  8.3 18.1 %copy-start.3 = (f32[256,128]{1,0:T(8,128)S(1)}, f32[256,128]{1,0:T(8,128)}, u32[]{:S(2)}) copy-start(f32[256,128]{1,0:T(8,128)} %m_ref.3) | copy-start | bytes 393220
  8.3 18.1 %copy-start.4 = (f32[256,128]{1,0:T(8,128)S(1)}, f32[256,128]{1,0:T(8,128)}, u32[]{:S(2)}) copy-start(f32[256,128]{1,0:T(8,128)} %v_ref.3) | copy-start | bytes 393220
  8.3 18.1 %copy-start.5 = (f32[256,128]{1,0:T(8,128)S(1)}, f32[256,128]{1,0:T(8,128)}, u32[]{:S(2)}) copy-start(f32[256,128]{1,0:T(8,128)} %w_ref.3) | copy-start | bytes 393220
  8.4 23.5 %collective-permute-start.8 = (bf16[512,4096]{1,0:T(8,128)(2,1)}, bf16[512,4096]{1,0:T(8,128)(2,1)}, u32[]{:S(2)}, u32[]{:S(2)}) collective-permute-start(bf16[512,4096]{1,0:T(8,128)(2,1)} %refs_0_.1), channel_id=1, source_target_pairs={{0,1},{1,0},{2,3},{3,2},{4,5},{5,4},{6,7},{7,6},{8,9},{9,8},{10,11... | collective-permute-start | bytes 12582920 | tf_op jit(solution)/shard_map/ppermute | solution.py:29
  10.8 15.6 %all-to-all-start = ((f32[16,8,128]{2,1,0:T(8,128)}), f32[16,8,128]{2,1,0:T(8,128)S(1)}, u32[]{:S(2)}, u32[]{:S(2)}) async-start(f32[16,8,128]{2,1,0:T(8,128)} %bitcast.4), calls=%async_computation | async-start | bytes 131072 | tf_op jit(solution)/shard_map/all_to_all | solution.py:350
  27.4 12.3 %copy-start.1 = (bf16[512,4096]{1,0:T(8,128)(2,1)S(1)}, bf16[512,4096]{1,0:T(8,128)(2,1)}, u32[]{:S(2)}) copy-start(bf16[512,4096]{1,0:T(8,128)(2,1)} %copy-done) | copy-start | bytes 12582916
  27.4 6.7 %collective-permute-start.5 = (bf16[256,128]{1,0:T(8,128)(2,1)S(1)}, bf16[256,128]{1,0:T(8,128)(2,1)S(1)}, u32[]{:S(2)}, u32[]{:S(2)}) collective-permute-start(bf16[256,128]{1,0:T(8,128)(2,1)S(1)} %get-tuple-element.24.refs_0_), channel_id=1, source_target_pairs={{0,8},{2,10},{4,12},{6,14},{8,0},{10,2},{12,4},{14,6},{16,24},{18,... | collective-permute-start | bytes 196616 | tf_op jit(solution)/shard_map/ppermute | solution.py:33
  28.1 7.2 %collective-permute-start.6 = (bf16[256,128]{1,0:T(8,128)(2,1)S(1)}, bf16[256,128]{1,0:T(8,128)(2,1)S(1)}, u32[]{:S(2)}, u32[]{:S(2)}) collective-permute-start(bf16[256,128]{1,0:T(8,128)(2,1)S(1)} %get-tuple-element.24.refs_0_), channel_id=1, source_target_pairs={{0,16},{2,18},{4,20},{6,22},{8,24},{10,26},{12,28},{14,30},{16,0},... | collective-permute-start | bytes 196616 | tf_op jit(solution)/shard_map/ppermute | solution.py:33
  29.0 6.3 %collective-permute-start.7 = (bf16[256,128]{1,0:T(8,128)(2,1)S(1)}, bf16[256,128]{1,0:T(8,128)(2,1)S(1)}, u32[]{:S(2)}, u32[]{:S(2)}) collective-permute-start(bf16[256,128]{1,0:T(8,128)(2,1)S(1)} %get-tuple-element.24.refs_0_), channel_id=1, source_target_pairs={{0,24},{2,26},{4,28},{6,30},{8,16},{10,18},{12,20},{14,22},{16,8},... | collective-permute-start | bytes 196616 | tf_op jit(solution)/shard_map/ppermute | solution.py:33
  35.3 8.8 %collective-permute-start.11 = (bf16[4,256,128]{2,1,0:T(8,128)(2,1)S(1)}, bf16[4,256,128]{2,1,0:T(8,128)(2,1)S(1)}, u32[]{:S(2)}, u32[]{:S(2)}) collective-permute-start(bf16[4,256,128]{2,1,0:T(8,128)(2,1)S(1)} %shard_map.138.refs_2_), channel_id=1, source_target_pairs={{0,2},{2,0},{4,6},{6,4},{8,10},{10,8},{12,14},{14,12},{16,18},{18,... | collective-permute-start | bytes 786440 | tf_op jit(solution)/shard_map/ppermute | solution.py:33
  36.1 11.3 %collective-permute-start.10 = (bf16[4,256,128]{2,1,0:T(8,128)(2,1)S(1)}, bf16[4,256,128]{2,1,0:T(8,128)(2,1)S(1)}, u32[]{:S(2)}, u32[]{:S(2)}) collective-permute-start(bf16[4,256,128]{2,1,0:T(8,128)(2,1)S(1)} %shard_map.138.refs_2_), channel_id=1, source_target_pairs={{0,4},{2,6},{4,0},{6,2},{8,12},{10,14},{12,8},{14,10},{16,20},{18,... | collective-permute-start | bytes 786440 | tf_op jit(solution)/shard_map/ppermute | solution.py:33
  36.6 11.5 %collective-permute-start.9 = (bf16[4,256,128]{2,1,0:T(8,128)(2,1)S(1)}, bf16[4,256,128]{2,1,0:T(8,128)(2,1)S(1)}, u32[]{:S(2)}, u32[]{:S(2)}) collective-permute-start(bf16[4,256,128]{2,1,0:T(8,128)(2,1)S(1)} %shard_map.138.refs_2_), channel_id=1, source_target_pairs={{0,6},{2,4},{4,2},{6,0},{8,14},{10,12},{12,10},{14,8},{16,22},{18,... | collective-permute-start | bytes 786440 | tf_op jit(solution)/shard_map/ppermute | solution.py:33

commit v5 on v4

--- a/solution.py
+++ b/solution.py
@@ -80,35 +80,75 @@
     )(*[pltpu.with_memory_space_constraint(a, pltpu.HBM) for a in arrays])
 
 
-def part_kernel(first, core, f_ref, g_ref, *rest):
-    tokens = f_ref.shape[0]
-    count = rest[-1].shape[0]
-    tile = min(1024, count)
-    g = g_ref[pl.ds(pl.multiple_of(core[0] * tokens, tokens), tokens), :]
-    for at in range(0, count, tile):
-        p = lax.dot_general(
-            f_ref[:, first + at : first + at + tile],
-            g,
-            (((0,), (0,)), ((), ())),
-            preferred_element_type=jnp.float32,
+def moves(f_any, first, next_ref, sem):
+    rows = next_ref.shape[0] // sem.shape[0]
+    return [
+        pltpu.make_async_copy(
+            f_any.at[j * rows : (j + 1) * rows, first : first + next_ref.shape[1]],
+            next_ref.at[j * rows : (j + 1) * rows],
+            sem.at[j],
         )
-        if len(rest) > 1:
-            p = p + rest[0][at : at + tile, :].astype(jnp.float32)
-        rest[-1][at : at + tile, :] = p
-
-
-def part_sum(core, features, grads, first, count, *error):
+        for j in range(sem.shape[0])
+    ]
+
+
+def part_kernel(following, n_f, core, *refs):
+    feats, refs = refs[:n_f], refs[n_f:]
+    coming = []
+    if following is not None:
+        f_any, *refs, next_ref, sem = refs
+        coming = moves(f_any, following, next_ref, sem)
+        for move in coming:
+            move.start()
+    if n_f:
+        g_ref, *error, out_ref = refs
+        tokens, count = feats[0].shape
+        g = g_ref[pl.ds(pl.multiple_of(core[0] * tokens, tokens), tokens), :]
+        tile = min(1024, count)
+        for i, f_ref in enumerate(feats):
+            for at in range(0, count, tile):
+                p = lax.dot_general(
+                    f_ref[:, at : at + tile],
+                    g,
+                    (((0,), (0,)), ((), ())),
+                    preferred_element_type=jnp.float32,
+                )
+                mine = slice(i * count + at, i * count + at + tile)
+                if error:
+                    p = p + error[0][mine, :].astype(jnp.float32)
+                out_ref[mine, :] = p
+    for move in coming:
+        move.wait()
+
+
+def part_sum(core, feats, grads, error, features, following, count):
     tokens = features.shape[0]
-    width = grads.shape[1]
-    part = jax.ShapeDtypeStruct((count, width), jnp.float32)
-    return pl.pallas_call(
-        functools.partial(part_kernel, first),
-        in_specs=[SMEM, VMEM, VMEM] + [VMEM] * len(error),
-        out_specs=VMEM,
-        out_shape=part,
-        compiler_params=params(features, grads, part, *error),
-        cost_estimate=cost(2 * tokens * count * width, 2 * tokens * count + 4 * count * width),
-    )(core, features, grads, *error)
+    ins, outs, scratch = list(feats), [], []
+    specs = [VMEM] * len(feats)
+    if following is not None:
+        ins.append(pltpu.with_memory_space_constraint(features, pltpu.HBM))
+        specs.append(ANY)
+        scratch = [pltpu.SemaphoreType.DMA((8,))]
+    width = 0
+    if feats:
+        width = grads.shape[1]
+        ins += [grads, *error]
+        specs += [VMEM] * (1 + len(error))
+        outs.append(jax.ShapeDtypeStruct((len(feats) * count, width), jnp.float32))
+    room = [*ins[: len(feats)], *outs, grads, *error]
+    if following is not None:
+        outs.append(pltpu.VMEM((tokens, count), features.dtype))
+        room.append(jax.ShapeDtypeStruct((tokens, count), features.dtype))
+    rows = max(1, len(feats)) * count
+    return pl.pallas_call(
+        functools.partial(part_kernel, following, len(feats)),
+        in_specs=[SMEM] + specs,
+        out_specs=[VMEM] * len(outs),
+        out_shape=outs,
+        scratch_shapes=scratch,
+        compiler_params=params(*room),
+        cost_estimate=cost(2 * tokens * rows * width, 2 * tokens * rows + 4 * rows * width),
+    )(core, *ins)
 
 
 def collect_kernel(n_chunks, owners, bins, sel, edges, own_ref, *refs):
@@ -331,21 +371,24 @@
     core1 = core.reshape(1).astype(jnp.int32)
     me1 = me.reshape(1).astype(jnp.int32)
 
-    [held] = load([features])
     n_chunks = 4 if cores == 2 else 1
     count = rows // n_chunks
+    blocks = [*part_sum(core1, [], key_grads, [], features, 0, count)]
     made, got = [], []
     for s in range(1, cores):
         theirs = shift(key_grads, "tensor", s)
         for j in range(n_chunks):
-            made.append(part_sum(core1, held, theirs, j * count, count))
-            got.append(shift(made[-1], "tensor", -s))
+            ahead = (j + 1) * count if len(blocks) == j + 1 < n_chunks else None
+            part, *more = part_sum(core1, [blocks[j]], theirs, [], features, ahead, count)
+            blocks += more
+            made.append(part)
+            got.append(shift(part, "tensor", -s))
     mine, _ = lax.optimization_barrier((key_grads, made[-1]))
-    own = part_sum(core1, held, mine, 0, rows, error_in[0])
+    [own] = part_sum(core1, blocks, mine, [error_in[0]], features, None, count)
     later, _ = lax.optimization_barrier((features, [own] + got))
     rest, outgoing = collect(selected[0, 0], bin_edges, own, got, n_chunks, owners, bins)
     error_out = rounded(rest)[None]
-    feats = [held] + [shift(later, "tensor", -s) for s in range(1, cores)]
+    feats = [features] + [shift(later, "tensor", -s) for s in range(1, cores)]
 
     arrived = lax.all_to_all(
         outgoing.reshape(owners, SLOTS, width), "dp", split_axis=0, concat_axis=0, tiled=True
@@ -358,7 +401,7 @@
         far = [swap(weight, "dp", m) for m in line[1:]]
         others = load(feats[1:])
         far, others = lax.optimization_barrier((far, others))
-        feats = [held, *others]
+        feats = [*load(feats[:1]), *others]
         mine = join([weight] + far)
         groups = [mine if b == 0 else swap(mine, "dp", b) for b in plane]
         keys = None

time: 49.7 us -> 53.6 us (1.078)
  Pallas kernels: 16.4 us -> 21 us
    pallas_call x5 -> x6, Pallas kernels: 3.49 us -> 8.04 us  [part_sum(): pl.pallas_call(functools.partial(part_kernel, following, len(feats)), in_...]
    ppermute x6, waiting for transfers between devices: 7.47 us -> 5.24 us  [swap(): lax.ppermute(x, axis, [(i, i ^ mask) for i in range(lax.axis_size(axis))])]
    ppermute x6, waiting for transfers between devices: 0.07 us -> 1.7 us  [shift(): return lax.ppermute(x, axis, [(i, (i + step) % n) for i in range(n)])]
  transfers between devices with their start and end apart: 13 -> 13, of which waited for: 5 -> 7; matrix products, arithmetic and copies ran while one was open for 0% -> 0% of each run, Pallas kernels for 29% -> 27%
where the time goes in v5:
time: 53.6 us; the launch traced here: 53.2 us
  Pallas kernels  21 us (39%)
  starting transfers between devices  18 us (34%)
  waiting for transfers between devices  12.8 us (24%)
  between operations  1.47 us (3%)
    pallas_call x6, Pallas kernels, part_sum(): pl.pallas_call(functools.partial(part_kernel, following, len(feats)), in_...  8.04 us
    all_to_all x1, starting transfers between devices, shards(): lax.all_to_all(outgoing.reshape(owners, SLOTS, width), 'dp', split_axis=0...  8.02 us
    ppermute x6, starting transfers between devices, swap(): lax.ppermute(x, axis, [(i, i ^ mask) for i in range(lax.axis_size(axis))])  8.01 us
    all_to_all x1, waiting for transfers between devices, shards(): lax.all_to_all(outgoing.reshape(owners, SLOTS, width), 'dp', split_axis=0...  5.81 us
    ppermute x6, waiting for transfers between devices, swap(): lax.ppermute(x, axis, [(i, i ^ mask) for i in range(lax.axis_size(axis))])  5.24 us
    pallas_call x2, Pallas kernels, load(): pl.pallas_call(functools.partial(load_kernel, pieces), in_specs=[ANY] * l...  4.43 us
    pallas_call x4, Pallas kernels, project(): pl.pallas_call(functools.partial(project_kernel, masks, last, len(feats))...  3.53 us
    pallas_call x1, Pallas kernels, collect(): pl.pallas_call(functools.partial(collect_kernel, n_chunks, owners, bins),...  2.07 us
  transfers between devices with their start and end apart: 13, of which 7 were waited for; matrix products, arithmetic and copies ran while one was open for 0% of the time, Pallas kernels for 27%

profile of v5, /device:TPU:0, one launch (start us, length us, event | category | flops | bytes accessed | tf_op | source)
XLA Modules:
  0.0 53.2 jit_solution(7168084851037058685)
XLA Ops:
  0.6 0.5 collective-permute-start
  1.1 1.4 %shard_map.129.refs_0_ = bf16[512,1024]{1,0:T(8,128)(2,1)S(1)} custom-call(s32[1]{0:T(128)} %bitcast.1.core, bf16[512,4096]{1,0:T(8,128)(2,1)} %refs_1_.5), custom_call_target="tpu_custom_call" | custom-call | bytes 1048576 | tf_op jit(solution)/shard_map/pallas_call | solution.py:143
  2.5 1.5 %shard_map.130 = (f32[1024,128]{1,0:T(8,128)S(1)}, bf16[512,1024]{1,0:T(8,128)(2,1)S(1)}) custom-call(s32[1]{0:T(128)} %bitcast.1.core, bf16[512,1024]{1,0:T(8,128)(2,1)S(1)} %shard_map.129.refs_0_, bf16[512,4096]{1,0:T(8,128)(2,1)} %refs_1_.5, bf16[1024,128]{1,0:T(8,128)(2,1)S(1)} %collective-permute-done.refs_2_.refs_1_), custom_call_target="tpu_custom_call" | custom-call | flops 134217728 | bytes 1572864 | tf_op jit(solution)/shard_map/pallas_call | solution.py:143
  4.1 1.5 %shard_map.131 = (f32[1024,128]{1,0:T(8,128)S(1)}, bf16[512,1024]{1,0:T(8,128)(2,1)S(1)}) custom-call(s32[1]{0:T(128)} %bitcast.1.core, bf16[512,1024]{1,0:T(8,128)(2,1)S(1)} %get-tuple-element.26.refs_0_.refs_1_, bf16[512,4096]{1,0:T(8,128)(2,1)} %refs_1_.5, bf16[1024,128]{1,0:T(8,128)(2,1)S(1)} %collective-permute-done.refs_2_.refs_1_), custom_call_target="tpu_custom_call" | custom-call | flops 134217728 | bytes 1572864 | tf_op jit(solution)/shard_map/pallas_call | solution.py:143
  5.6 1.7 %shard_map.132 = (f32[1024,128]{1,0:T(8,128)S(1)}, bf16[512,1024]{1,0:T(8,128)(2,1)S(1)}) custom-call(s32[1]{0:T(128)} %bitcast.1.core, bf16[512,1024]{1,0:T(8,128)(2,1)S(1)} %get-tuple-element.27.refs_0_.refs_2_, bf16[512,4096]{1,0:T(8,128)(2,1)} %refs_1_.5, bf16[1024,128]{1,0:T(8,128)(2,1)S(1)} %collective-permute-done.refs_2_.refs_1_), custom_call_target="tpu_custom_call" | custom-call | flops 134217728 | bytes 1572864 | tf_op jit(solution)/shard_map/pallas_call | solution.py:143
  7.3 0.5 shard_map.133
  7.9 0.4 collective-permute-start.4
  8.5 0.4 collective-permute-start.2
  9.0 1.4 %shard_map.134.own_ref = f32[4096,128]{1,0:T(8,128)S(1)} custom-call(s32[1]{0:T(128)} %bitcast.1.core, bf16[512,1024]{1,0:T(8,128)(2,1)S(1)} %shard_map.129.refs_0_, bf16[512,1024]{1,0:T(8,128)(2,1)S(1)} %get-tuple-element.26.refs_0_.refs_1_, bf16[512,1024]{1,0:T(8,128)(2,1)S(1)} %get-tuple-element.27.refs_0_.refs_2_, ...), custom_call_target="tpu_custom_call" | custom-call | flops 536870912 | bytes 6291456 | tf_op jit(solution)/shard_map/pallas_call | solution.py:143
  10.6 0.7 %collective-permute-done.2.refs_1_ = f32[1024,128]{1,0:T(8,128)S(1)} collective-permute-done((f32[1024,128]{1,0:T(8,128)S(1)}, f32[1024,128]{1,0:T(8,128)S(1)}, u32[]{:S(2)}, u32[]{:S(2)}) %collective-permute-start.2) | collective-permute-done | bytes 524320 | tf_op jit(solution)/shard_map/ppermute | solution.py:29
  11.4 0.7 %collective-permute-done.1.refs_0_ = f32[1024,128]{1,0:T(8,128)S(1)} collective-permute-done((f32[1024,128]{1,0:T(8,128)S(1)}, f32[1024,128]{1,0:T(8,128)S(1)}, u32[]{:S(2)}, u32[]{:S(2)}) %collective-permute-start.1) | collective-permute-done | bytes 524320 | tf_op jit(solution)/shard_map/ppermute | solution.py:29
  12.5 2.1 %shard_map.135 = (f32[4096,128]{1,0:T(8,128)S(1)}, f32[128,128]{1,0:T(8,128)}) custom-call(s32[32]{0:T(128)S(1)} %bitcast.7, s32[17]{0:T(128)S(1)} %copy-done.5, f32[4096,128]{1,0:T(8,128)S(1)} %shard_map.134.own_ref, f32[1024,128]{1,0:T(8,128)S(1)} %collective-permute-done.1.refs_0_, f32[1024,128]{1,0:T(8,128)S(1)} %collective-permute-done.2.refs_1_, ...), custom_call_target="tpu_custom_call" | custom-call | flops 4194304 | bytes 6291456 | tf_op jit(solution)/shard_map/pallas_call | solution.py:197
  14.6 8.0 %all-to-all-start = ((f32[16,8,128]{2,1,0:T(8,128)}), f32[16,8,128]{2,1,0:T(8,128)S(1)}, u32[]{:S(2)}, u32[]{:S(2)}) async-start(f32[16,8,128]{2,1,0:T(8,128)} %bitcast.4), calls=%async_computation | async-start | bytes 131072 | tf_op jit(solution)/shard_map/all_to_all | solution.py:393
  23.2 1.1 %shard_map.136 = bf16[4096,128]{1,0:T(8,128)(2,1)} custom-call(f32[4096,128]{1,0:T(8,128)S(1)} %get-tuple-element.34.x_ref), custom_call_target="tpu_custom_call" | custom-call | flops 524288 | bytes 3145728 | tf_op jit(solution)/shard_map/pallas_call | solution.py:293
  24.3 5.8 %all-to-all-done.arr_ref = f32[16,8,128]{2,1,0:T(8,128)S(1)} async-done(((f32[16,8,128]{2,1,0:T(8,128)}), f32[16,8,128]{2,1,0:T(8,128)S(1)}, u32[]{:S(2)}, u32[]{:S(2)}) %all-to-all-start) | async-done | bytes 65568 | tf_op jit(solution)/shard_map/all_to_all | solution.py:393
  30.1 1.0 %shard_map.137 = (f32[256,128]{1,0:T(8,128)S(1)}, bf16[256,128]{1,0:T(8,128)(2,1)S(1)}) custom-call(s32[1]{0:T(128)} %bitcast.me, s32[1]{0:T(128)S(6)} %copy.14.least, s32[17]{0:T(128)S(1)} %copy-done.5, f32[16,8,128]{2,1,0:T(8,128)S(1)} %all-to-all-done.arr_ref, f32[256,128]{1,0:T(8,128)S(1)} %copy-done.1, f32[256,128]{1,0:T(8,128)S(1)} %copy-done.2, ...), custom_call_target="tpu_custom_call" | custom-call | flops 50331648 | bytes 983040 | tf_op jit(solution)/shard_map/pallas_call | solution.py:260
  31.2 0.7 %collective-permute-start.5 = (bf16[256,128]{1,0:T(8,128)(2,1)S(1)}, bf16[256,128]{1,0:T(8,128)(2,1)S(1)}, u32[]{:S(2)}, u32[]{:S(2)}) collective-permute-start(bf16[256,128]{1,0:T(8,128)(2,1)S(1)} %get-tuple-element.36.refs_0_), channel_id=1, source_target_pairs={{0,8},{2,10},{4,12},{6,14},{8,0},{10,2},{12,4},{14,6},{16,24},{18,... | collective-permute-start | bytes 196616 | tf_op jit(solution)/shard_map/ppermute | solution.py:33
  31.9 0.8 %collective-permute-start.6 = (bf16[256,128]{1,0:T(8,128)(2,1)S(1)}, bf16[256,128]{1,0:T(8,128)(2,1)S(1)}, u32[]{:S(2)}, u32[]{:S(2)}) collective-permute-start(bf16[256,128]{1,0:T(8,128)(2,1)S(1)} %get-tuple-element.36.refs_0_), channel_id=1, source_target_pairs={{0,16},{2,18},{4,20},{6,22},{8,24},{10,26},{12,28},{14,30},{16,0},... | collective-permute-start | bytes 196616 | tf_op jit(solution)/shard_map/ppermute | solution.py:33
  32.7 2.9 %collective-permute-start.7 = (bf16[256,128]{1,0:T(8,128)(2,1)S(1)}, bf16[256,128]{1,0:T(8,128)(2,1)S(1)}, u32[]{:S(2)}, u32[]{:S(2)}) collective-permute-start(bf16[256,128]{1,0:T(8,128)(2,1)S(1)} %get-tuple-element.36.refs_0_), channel_id=1, source_target_pairs={{0,24},{2,26},{4,28},{6,30},{8,16},{10,18},{12,20},{14,22},{16,8},... | collective-permute-start | bytes 196616 | tf_op jit(solution)/shard_map/ppermute | solution.py:33
  35.6 2.2 %shard_map.138.refs_1_ = bf16[512,4096]{1,0:T(8,128)(2,1)S(1)} custom-call(bf16[512,4096]{1,0:T(8,128)(2,1)} %collective-permute-done.8.refs_0_), custom_call_target="tpu_custom_call" | custom-call | bytes 8388608 | tf_op jit(solution)/shard_map/pallas_call | solution.py:72
  37.9 1.2 %collective-permute-done.6.refs_2_ = bf16[256,128]{1,0:T(8,128)(2,1)S(1)} collective-permute-done((bf16[256,128]{1,0:T(8,128)(2,1)S(1)}, bf16[256,128]{1,0:T(8,128)(2,1)S(1)}, u32[]{:S(2)}, u32[]{:S(2)}) %collective-permute-start.6) | collective-permute-done | bytes 65568 | tf_op jit(solution)/shard_map/ppermute | solution.py:33
  39.0 0.8 %collective-permute-start.11 = (bf16[4,256,128]{2,1,0:T(8,128)(2,1)S(1)}, bf16[4,256,128]{2,1,0:T(8,128)(2,1)S(1)}, u32[]{:S(2)}, u32[]{:S(2)}) collective-permute-start(bf16[4,256,128]{2,1,0:T(8,128)(2,1)S(1)} %shard_map.139.refs_2_), channel_id=1, source_target_pairs={{0,2},{2,0},{4,6},{6,4},{8,10},{10,8},{12,14},{14,12},{16,18},{18,... | collective-permute-start | bytes 786440 | tf_op jit(solution)/shard_map/ppermute | solution.py:33
  39.8 0.5 collective-permute-start.10
  40.3 2.3 %collective-permute-start.9 = (bf16[4,256,128]{2,1,0:T(8,128)(2,1)S(1)}, bf16[4,256,128]{2,1,0:T(8,128)(2,1)S(1)}, u32[]{:S(2)}, u32[]{:S(2)}) collective-permute-start(bf16[4,256,128]{2,1,0:T(8,128)(2,1)S(1)} %shard_map.139.refs_2_), channel_id=1, source_target_pairs={{0,6},{2,4},{4,2},{6,0},{8,14},{10,12},{12,10},{14,8},{16,22},{18,... | collective-permute-start | bytes 786440 | tf_op jit(solution)/shard_map/ppermute | solution.py:33
  42.6 2.2 %shard_map.128.refs_0_ = bf16[512,4096]{1,0:T(8,128)(2,1)S(1)} custom-call(bf16[512,4096]{1,0:T(8,128)(2,1)} %refs_1_.5), custom_call_target="tpu_custom_call" | custom-call | bytes 8388608 | tf_op jit(solution)/shard_map/pallas_call | solution.py:72
  44.8 0.8 %shard_map.144 = (f32[256,128]{1,0:T(8,128)}, f32[256,128]{1,0:T(8,128)}, f32[256,128]{1,0:T(8,128)}) custom-call(f32[256,128]{1,0:T(8,128)S(1)} %get-tuple-element.43.g_ref, f32[256,128]{1,0:T(8,128)S(1)} %copy-done.1, f32[256,128]{1,0:T(8,128)S(1)} %copy-done.2, f32[256,128]{1,0:T(8,128)S(1)} %copy-done.3), custom_call_target="tpu_custom_call" | custom-call | flops 655360 | bytes 917504 | tf_op jit(solution)/shard_map/pallas_call | solution.py:277
  45.6 0.7 %shard_map.140.refs_3_ = f32[1024,128]{1,0:T(8,128)S(1)} custom-call(s32[1]{0:T(128)} %bitcast.me, s32[1]{0:T(128)} %bitcast.1.core, bf16[512,4096]{1,0:T(8,128)(2,1)S(1)} %shard_map.128.refs_0_, bf16[512,4096]{1,0:T(8,128)(2,1)S(1)} %shard_map.138.refs_1_, bf16[4,256,128]{2,1,0:T(8,128)(2,1)S(1)} %shard_map.139.refs_2_), custom_call_target="tpu_custom_call" | custom-call | flops 268435456 | bytes 3145728 | tf_op jit(solution)/shard_map/pallas_call | solution.py:347
  46.3 1.5 %collective-permute-done.11.refs_2_ = bf16[4,256,128]{2,1,0:T(8,128)(2,1)S(1)} collective-permute-done((bf16[4,256,128]{2,1,0:T(8,128)(2,1)S(1)}, bf16[4,256,128]{2,1,0:T(8,128)(2,1)S(1)}, u32[]{:S(2)}, u32[]{:S(2)}) %collective-permute-start.11) | collective-permute-done | bytes 262176 | tf_op jit(solution)/shard_map/ppermute | solution.py:33
  47.9 0.7 %shard_map.141.refs_3_ = f32[1024,128]{1,0:T(8,128)S(1)} custom-call(s32[1]{0:T(128)} %bitcast.me, s32[1]{0:T(128)} %bitcast.1.core, bf16[512,4096]{1,0:T(8,128)(2,1)S(1)} %shard_map.128.refs_0_, bf16[512,4096]{1,0:T(8,128)(2,1)S(1)} %shard_map.138.refs_1_, bf16[4,256,128]{2,1,0:T(8,128)(2,1)S(1)} %collective-permute-done.11.refs_2_, ...), custom_call_target="tpu_custom_call" | custom-call | flops 268435456 | bytes 3145728 | tf_op jit(solution)/shard_map/pallas_call | solution.py:347
  48.6 2.5 %collective-permute-done.10.refs_2_ = bf16[4,256,128]{2,1,0:T(8,128)(2,1)S(1)} collective-permute-done((bf16[4,256,128]{2,1,0:T(8,128)(2,1)S(1)}, bf16[4,256,128]{2,1,0:T(8,128)(2,1)S(1)}, u32[]{:S(2)}, u32[]{:S(2)}) %collective-permute-start.10) | collective-permute-done | bytes 262176 | tf_op jit(solution)/shard_map/ppermute | solution.py:33
  51.1 0.7 %shard_map.142.refs_3_ = f32[1024,128]{1,0:T(8,128)S(1)} custom-call(s32[1]{0:T(128)} %bitcast.me, s32[1]{0:T(128)} %bitcast.1.core, bf16[512,4096]{1,0:T(8,128)(2,1)S(1)} %shard_map.128.refs_0_, bf16[512,4096]{1,0:T(8,128)(2,1)S(1)} %shard_map.138.refs_1_, bf16[4,256,128]{2,1,0:T(8,128)(2,1)S(1)} %collective-permute-done.10.refs_2_, ...), custom_call_target="tpu_custom_call" | custom-call | flops 268435456 | bytes 3145728 | tf_op jit(solution)/shard_map/pallas_call | solution.py:347
  51.8 1.4 %shard_map.143 = bf16[1024,128]{1,0:T(8,128)(2,1)} custom-call(s32[1]{0:T(128)} %bitcast.me, s32[1]{0:T(128)} %bitcast.1.core, bf16[512,4096]{1,0:T(8,128)(2,1)S(1)} %shard_map.128.refs_0_, bf16[512,4096]{1,0:T(8,128)(2,1)S(1)} %shard_map.138.refs_1_, bf16[4,256,128]{2,1,0:T(8,128)(2,1)S(1)} %collective-permute-done.9.refs_2_, ...), custom_call_target="tpu_custom_call" | custom-call | flops 268435456 | bytes 3145728 | tf_op jit(solution)/shard_map/pallas_call | solution.py:347
  (25 shorter events, 0.9 us)
Async XLA Ops:
  0.6 1.9 %collective-permute-start = (bf16[1024,128]{1,0:T(8,128)(2,1)}, bf16[1024,128]{1,0:T(8,128)(2,1)S(1)}, u32[]{:S(2)}, u32[]{:S(2)}) collective-permute-start(bf16[1024,128]{1,0:T(8,128)(2,1)} %refs_4_), channel_id=1, source_target_pairs={{0,1},{1,0},{2,3},{3,2},{4,5},{5,4},{6,7},{7,6},{8,9},{9,8},{10,11... | collective-permute-start | bytes 786440 | tf_op jit(solution)/shard_map/ppermute | solution.py:29
  5.6 3.4 %copy-start = (bf16[1,4096,128]{2,1,0:T(8,128)(2,1)S(1)}, bf16[1,4096,128]{2,1,0:T(8,128)(2,1)}, u32[]{:S(2)}) copy-start(bf16[1,4096,128]{2,1,0:T(8,128)(2,1)} %param.11) | copy-start | bytes 3145732
  5.6 3.4 %copy-start.4 = (bf16[1024,128]{1,0:T(8,128)(2,1)S(1)}, bf16[1024,128]{1,0:T(8,128)(2,1)}, u32[]{:S(2)}) copy-start(bf16[1024,128]{1,0:T(8,128)(2,1)} %refs_4_) | copy-start | bytes 786436
  7.9 4.6 %copy-start.5 = (s32[17]{0:T(128)S(1)}, s32[17]{0:T(128)}, u32[]{:S(2)}) copy-start(s32[17]{0:T(128)} %edges.3) | copy-start | bytes 208
  7.9 4.6 %copy-start.6 = (s32[1,1,32]{2,1,0:T(1,128)S(1)}, s32[1,1,32]{2,1,0:T(1,128)}, u32[]{:S(2)}) copy-start(s32[1,1,32]{2,1,0:T(1,128)} %param.12) | copy-start | bytes 388
  7.9 2.5 %collective-permute-start.4 = (f32[1024,128]{1,0:T(8,128)S(1)}, f32[1024,128]{1,0:T(8,128)S(1)}, u32[]{:S(2)}, u32[]{:S(2)}) collective-permute-start(f32[1024,128]{1,0:T(8,128)S(1)} %shard_map.133), channel_id=1, source_target_pairs={{0,1},{1,0},{2,3},{3,2},{4,5},{5,4},{6,7},{7,6},{8,9},{9,8},{10,11... | collective-permute-start | bytes 1572872 | tf_op jit(solution)/shard_map/ppermute | solution.py:29
  8.3 2.3 %collective-permute-start.3 = (f32[1024,128]{1,0:T(8,128)S(1)}, f32[1024,128]{1,0:T(8,128)S(1)}, u32[]{:S(2)}, u32[]{:S(2)}) collective-permute-start(f32[1024,128]{1,0:T(8,128)S(1)} %get-tuple-element.32), channel_id=1, source_target_pairs={{0,1},{1,0},{2,3},{3,2},{4,5},{5,4},{6,7},{7,6},{8,9},{9,8},{10,11... | collective-permute-start | bytes 1572872 | tf_op jit(solution)/shard_map/ppermute | solution.py:29
  8.5 2.9 %collective-permute-start.2 = (f32[1024,128]{1,0:T(8,128)S(1)}, f32[1024,128]{1,0:T(8,128)S(1)}, u32[]{:S(2)}, u32[]{:S(2)}) collective-permute-start(f32[1024,128]{1,0:T(8,128)S(1)} %get-tuple-element.31), channel_id=1, source_target_pairs={{0,1},{1,0},{2,3},{3,2},{4,5},{5,4},{6,7},{7,6},{8,9},{9,8},{10,11... | collective-permute-start | bytes 1572872 | tf_op jit(solution)/shard_map/ppermute | solution.py:29
  8.8 3.3 %collective-permute-start.1 = (f32[1024,128]{1,0:T(8,128)S(1)}, f32[1024,128]{1,0:T(8,128)S(1)}, u32[]{:S(2)}, u32[]{:S(2)}) collective-permute-start(f32[1024,128]{1,0:T(8,128)S(1)} %get-tuple-element.30), channel_id=1, source_target_pairs={{0,1},{1,0},{2,3},{3,2},{4,5},{5,4},{6,7},{7,6},{8,9},{9,8},{10,11... | collective-permute-start | bytes 1572872 | tf_op jit(solution)/shard_map/ppermute | solution.py:29
  10.4 19.7 %copy-start.1 = (f32[256,128]{1,0:T(8,128)S(1)}, f32[256,128]{1,0:T(8,128)}, u32[]{:S(2)}) copy-start(f32[256,128]{1,0:T(8,128)} %m_ref.3) | copy-start | bytes 393220
  10.4 19.7 %copy-start.2 = (f32[256,128]{1,0:T(8,128)S(1)}, f32[256,128]{1,0:T(8,128)}, u32[]{:S(2)}) copy-start(f32[256,128]{1,0:T(8,128)} %v_ref.3) | copy-start | bytes 393220
  10.4 19.7 %copy-start.3 = (f32[256,128]{1,0:T(8,128)S(1)}, f32[256,128]{1,0:T(8,128)}, u32[]{:S(2)}) copy-start(f32[256,128]{1,0:T(8,128)} %w_ref.3) | copy-start | bytes 393220
  12.1 23.5 %collective-permute-start.8 = (bf16[512,4096]{1,0:T(8,128)(2,1)}, bf16[512,4096]{1,0:T(8,128)(2,1)}, u32[]{:S(2)}, u32[]{:S(2)}) collective-permute-start(bf16[512,4096]{1,0:T(8,128)(2,1)} %refs_1_.5), channel_id=1, source_target_pairs={{0,1},{1,0},{2,3},{3,2},{4,5},{5,4},{6,7},{7,6},{8,9},{9,8},{10,11... | collective-permute-start | bytes 12582920 | tf_op jit(solution)/shard_map/ppermute | solution.py:29
  14.6 15.6 %all-to-all-start = ((f32[16,8,128]{2,1,0:T(8,128)}), f32[16,8,128]{2,1,0:T(8,128)S(1)}, u32[]{:S(2)}, u32[]{:S(2)}) async-start(f32[16,8,128]{2,1,0:T(8,128)} %bitcast.4), calls=%async_computation | async-start | bytes 131072 | tf_op jit(solution)/shard_map/all_to_all | solution.py:393
  31.2 6.7 %collective-permute-start.5 = (bf16[256,128]{1,0:T(8,128)(2,1)S(1)}, bf16[256,128]{1,0:T(8,128)(2,1)S(1)}, u32[]{:S(2)}, u32[]{:S(2)}) collective-permute-start(bf16[256,128]{1,0:T(8,128)(2,1)S(1)} %get-tuple-element.36.refs_0_), channel_id=1, source_target_pairs={{0,8},{2,10},{4,12},{6,14},{8,0},{10,2},{12,4},{14,6},{16,24},{18,... | collective-permute-start | bytes 196616 | tf_op jit(solution)/shard_map/ppermute | solution.py:33
  31.9 7.1 %collective-permute-start.6 = (bf16[256,128]{1,0:T(8,128)(2,1)S(1)}, bf16[256,128]{1,0:T(8,128)(2,1)S(1)}, u32[]{:S(2)}, u32[]{:S(2)}) collective-permute-start(bf16[256,128]{1,0:T(8,128)(2,1)S(1)} %get-tuple-element.36.refs_0_), channel_id=1, source_target_pairs={{0,16},{2,18},{4,20},{6,22},{8,24},{10,26},{12,28},{14,30},{16,0},... | collective-permute-start | bytes 196616 | tf_op jit(solution)/shard_map/ppermute | solution.py:33
  32.7 6.3 %collective-permute-start.7 = (bf16[256,128]{1,0:T(8,128)(2,1)S(1)}, bf16[256,128]{1,0:T(8,128)(2,1)S(1)}, u32[]{:S(2)}, u32[]{:S(2)}) collective-permute-start(bf16[256,128]{1,0:T(8,128)(2,1)S(1)} %get-tuple-element.36.refs_0_), channel_id=1, source_target_pairs={{0,24},{2,26},{4,28},{6,30},{8,16},{10,18},{12,20},{14,22},{16,8},... | collective-permute-start | bytes 196616 | tf_op jit(solution)/shard_map/ppermute | solution.py:33
  39.0 8.8 %collective-permute-start.11 = (bf16[4,256,128]{2,1,0:T(8,128)(2,1)S(1)}, bf16[4,256,128]{2,1,0:T(8,128)(2,1)S(1)}, u32[]{:S(2)}, u32[]{:S(2)}) collective-permute-start(bf16[4,256,128]{2,1,0:T(8,128)(2,1)S(1)} %shard_map.139.refs_2_), channel_id=1, source_target_pairs={{0,2},{2,0},{4,6},{6,4},{8,10},{10,8},{12,14},{14,12},{16,18},{18,... | collective-permute-start | bytes 786440 | tf_op jit(solution)/shard_map/ppermute | solution.py:33
  39.8 11.3 %collective-permute-start.10 = (bf16[4,256,128]{2,1,0:T(8,128)(2,1)S(1)}, bf16[4,256,128]{2,1,0:T(8,128)(2,1)S(1)}, u32[]{:S(2)}, u32[]{:S(2)}) collective-permute-start(bf16[4,256,128]{2,1,0:T(8,128)(2,1)S(1)} %shard_map.139.refs_2_), channel_id=1, source_target_pairs={{0,4},{2,6},{4,0},{6,2},{8,12},{10,14},{12,8},{14,10},{16,20},{18,... | collective-permute-start | bytes 786440 | tf_op jit(solution)/shard_map/ppermute | solution.py:33
  40.3 11.5 %collective-permute-start.9 = (bf16[4,256,128]{2,1,0:T(8,128)(2,1)S(1)}, bf16[4,256,128]{2,1,0:T(8,128)(2,1)S(1)}, u32[]{:S(2)}, u32[]{:S(2)}) collective-permute-start(bf16[4,256,128]{2,1,0:T(8,128)(2,1)S(1)} %shard_map.139.refs_2_), channel_id=1, source_target_pairs={{0,6},{2,4},{4,2},{6,0},{8,14},{10,12},{12,10},{14,8},{16,22},{18,... | collective-permute-start | bytes 786440 | tf_op jit(solution)/shard_map/ppermute | solution.py:33

commit v6 on v4

--- a/solution.py
+++ b/solution.py
@@ -29,8 +29,14 @@
     return lax.ppermute(x, axis, [(i, (i + step) % n) for i in range(n)])
 
 
-def swap(x, axis, mask):
-    return lax.ppermute(x, axis, [(i, i ^ mask) for i in range(lax.axis_size(axis))])
+def swap(x, masks):
+    n, cores = lax.axis_size("dp"), lax.axis_size("tensor")
+    pairs = [
+        (i * cores + c, (i ^ masks[c % len(masks)]) * cores + c)
+        for i in range(n)
+        for c in range(cores)
+    ]
+    return lax.ppermute(x, ("dp", "tensor"), pairs)
 
 
 def params(*arrays):
@@ -282,10 +288,12 @@
     tokens = feats[0].shape[0]
     count, region, width = w_ref.shape
     weight = w_ref[...].reshape(count * region, width)
+    odd = lax.rem(core[0], 2) == 1
+    mine_of = [jnp.where(odd, m[1], m[0]) for m in masks]
     for i, f_ref in enumerate(feats):
         mine = pl.ds(i * tokens, tokens)
         part = [
-            f_ref[:, pl.ds(pl.multiple_of((me[0] ^ m) * region, region), region)] for m in masks
+            f_ref[:, pl.ds(pl.multiple_of((me[0] ^ m) * region, region), region)] for m in mine_of
         ]
         total = jnp.dot(
             jnp.concatenate(part, axis=1), weight, preferred_element_type=jnp.float32
@@ -355,15 +363,17 @@
     bits = [1 << i for i in range(owners.bit_length() - 1)]
     if 1 << len(bits) == owners and len(bits) > 2 and region % LANES == 0:
         plane, line = spans(bits[:2]), spans(bits[2:])
-        far = [swap(weight, "dp", m) for m in line[1:]]
+        plane = list(zip(plane, [plane[0], plane[2], plane[1], *plane[3:]]))
+        line = list(zip(line, [line[0], *line[2:], line[1]]))
+        far = [swap(weight, m) for m in line[1:]]
         others = load(feats[1:])
         far, others = lax.optimization_barrier((far, others))
         feats = [held, *others]
         mine = join([weight] + far)
-        groups = [mine if b == 0 else swap(mine, "dp", b) for b in plane]
+        groups = [mine if j == 0 else swap(mine, b) for j, b in enumerate(plane)]
         keys = None
         for j, b in enumerate(plane):
-            masks = tuple(b ^ m for m in line)
+            masks = tuple((b[0] ^ m[0], b[1] ^ m[1]) for m in line)
             keys = project(masks, me1, core1, feats, groups[j], keys, j == len(plane) - 1)
     else:
         whole = jnp.concatenate(feats, axis=0)

time: 49.7 us -> 51 us (1.026)
  waiting for transfers between devices: 13.3 us -> 14.6 us
    ppermute x6, waiting for transfers between devices: 7.47 us -> 8.71 us  [swap(): return lax.ppermute(x, ('dp', 'tensor'), pairs)]
  transfers between devices with their start and end apart: 13 -> 13, of which waited for: 5 -> 5; matrix products, arithmetic and copies ran while one was open for 0% -> 0% of each run, Pallas kernels for 29% -> 28%
where the time goes in v6:
time: 51 us; the launch traced here: 50.8 us
  starting transfers between devices  18.2 us (36%)
  Pallas kernels  16.4 us (32%)
  waiting for transfers between devices  14.6 us (29%)
  between operations  1.51 us (3%)
    ppermute x6, waiting for transfers between devices, swap(): return lax.ppermute(x, ('dp', 'tensor'), pairs)  8.71 us
    all_to_all x1, starting transfers between devices, shards(): lax.all_to_all(outgoing.reshape(owners, SLOTS, width), 'dp', split_axis=0...  8.02 us
    ppermute x6, starting transfers between devices, swap(): return lax.ppermute(x, ('dp', 'tensor'), pairs)  8.01 us
    all_to_all x1, waiting for transfers between devices, shards(): lax.all_to_all(outgoing.reshape(owners, SLOTS, width), 'dp', split_axis=0...  5.81 us
    pallas_call x2, Pallas kernels, load(): pl.pallas_call(functools.partial(load_kernel, pieces), in_specs=[ANY] * l...  4.43 us
    pallas_call x4, Pallas kernels, project(): pl.pallas_call(functools.partial(project_kernel, masks, last, len(feats))...  3.53 us
    pallas_call x5, Pallas kernels, part_sum(): pl.pallas_call(functools.partial(part_kernel, first), in_specs=[SMEM, VME...  3.49 us
    ppermute x6, starting transfers between devices, shift(): return lax.ppermute(x, axis, [(i, (i + step) % n) for i in range(n)])  2.17 us
  transfers between devices with their start and end apart: 13, of which 5 were waited for; matrix products, arithmetic and copies ran while one was open for 0% of the time, Pallas kernels for 28%

profile of v6, /device:TPU:0, one launch (start us, length us, event | category | flops | bytes accessed | tf_op | source)
XLA Modules:
  0.0 50.8 jit_solution(17923782408221192142)
XLA Ops:
  0.6 0.5 %collective-permute-start = (bf16[1024,128]{1,0:T(8,128)(2,1)}, bf16[1024,128]{1,0:T(8,128)(2,1)S(1)}, u32[]{:S(2)}, u32[]{:S(2)}) collective-permute-start(bf16[1024,128]{1,0:T(8,128)(2,1)} %g_ref), channel_id=1, source_target_pairs={{0,1},{1,0},{2,3},{3,2},{4,5},{5,4},{6,7},{7,6},{8,9},{9,8},{10,11... | collective-permute-start | bytes 786440 | tf_op jit(solution)/shard_map/ppermute | solution.py:29
  1.1 2.2 %shard_map.128.f_ref.refs_0_ = bf16[512,4096]{1,0:T(8,128)(2,1)S(1)} custom-call(bf16[512,4096]{1,0:T(8,128)(2,1)} %refs_0_.1), custom_call_target="tpu_custom_call" | custom-call | bytes 8388608 | tf_op jit(solution)/shard_map/pallas_call | solution.py:78
  3.4 0.5 %shard_map.131 = f32[1024,128]{1,0:T(8,128)S(1)} custom-call(s32[1]{0:T(128)} %bitcast.1.core, bf16[512,4096]{1,0:T(8,128)(2,1)S(1)} %shard_map.128.f_ref.refs_0_, bf16[1024,128]{1,0:T(8,128)(2,1)S(1)} %collective-permute-done.g_ref), custom_call_target="tpu_custom_call" | custom-call | flops 134217728 | bytes 1572864 | tf_op jit(solution)/shard_map/pallas_call | solution.py:110
  3.9 0.1 collective-permute-start.1
  4.0 0.5 %shard_map.132 = f32[1024,128]{1,0:T(8,128)S(1)} custom-call(s32[1]{0:T(128)} %bitcast.1.core, bf16[512,4096]{1,0:T(8,128)(2,1)S(1)} %shard_map.128.f_ref.refs_0_, bf16[1024,128]{1,0:T(8,128)(2,1)S(1)} %collective-permute-done.g_ref), custom_call_target="tpu_custom_call" | custom-call | flops 134217728 | bytes 1572864 | tf_op jit(solution)/shard_map/pallas_call | solution.py:110
  4.6 0.5 %collective-permute-start.2 = (f32[1024,128]{1,0:T(8,128)S(1)}, f32[1024,128]{1,0:T(8,128)S(1)}, u32[]{:S(2)}, u32[]{:S(2)}) collective-permute-start(f32[1024,128]{1,0:T(8,128)S(1)} %shard_map.132), channel_id=1, source_target_pairs={{0,1},{1,0},{2,3},{3,2},{4,5},{5,4},{6,7},{7,6},{8,9},{9,8},{10,11... | collective-permute-start | bytes 1572872 | tf_op jit(solution)/shard_map/ppermute | solution.py:29
  5.1 0.5 %shard_map.133 = f32[1024,128]{1,0:T(8,128)S(1)} custom-call(s32[1]{0:T(128)} %bitcast.1.core, bf16[512,4096]{1,0:T(8,128)(2,1)S(1)} %shard_map.128.f_ref.refs_0_, bf16[1024,128]{1,0:T(8,128)(2,1)S(1)} %collective-permute-done.g_ref), custom_call_target="tpu_custom_call" | custom-call | flops 134217728 | bytes 1572864 | tf_op jit(solution)/shard_map/pallas_call | solution.py:110
  5.6 0.1 collective-permute-start.3
  5.8 0.5 %shard_map.129 = f32[1024,128]{1,0:T(8,128)S(1)} custom-call(s32[1]{0:T(128)} %bitcast.1.core, bf16[512,4096]{1,0:T(8,128)(2,1)S(1)} %shard_map.128.f_ref.refs_0_, bf16[1024,128]{1,0:T(8,128)(2,1)S(1)} %collective-permute-done.g_ref), custom_call_target="tpu_custom_call" | custom-call | flops 134217728 | bytes 1572864 | tf_op jit(solution)/shard_map/pallas_call | solution.py:110
  6.3 0.5 %collective-permute-start.4 = (f32[1024,128]{1,0:T(8,128)S(1)}, f32[1024,128]{1,0:T(8,128)S(1)}, u32[]{:S(2)}, u32[]{:S(2)}) collective-permute-start(f32[1024,128]{1,0:T(8,128)S(1)} %shard_map.129), channel_id=1, source_target_pairs={{0,1},{1,0},{2,3},{3,2},{4,5},{5,4},{6,7},{7,6},{8,9},{9,8},{10,11... | collective-permute-start | bytes 1572872 | tf_op jit(solution)/shard_map/ppermute | solution.py:29
  6.8 1.4 %shard_map.130.own_ref = f32[4096,128]{1,0:T(8,128)S(1)} custom-call(s32[1]{0:T(128)} %bitcast.1.core, bf16[512,4096]{1,0:T(8,128)(2,1)S(1)} %shard_map.128.f_ref.refs_0_, bf16[1024,128]{1,0:T(8,128)(2,1)S(1)} %copy-done.6, bf16[4096,128]{1,0:T(8,128)(2,1)S(1)} %bitcast.6), custom_call_target="tpu_custom_call" | custom-call | flops 536870912 | bytes 6291456 | tf_op jit(solution)/shard_map/pallas_call | solution.py:110
  8.4 0.4 collective-permute-start.8
  8.8 2.1 %shard_map.134 = (f32[4096,128]{1,0:T(8,128)S(1)}, f32[128,128]{1,0:T(8,128)}) custom-call(s32[32]{0:T(128)S(1)} %bitcast.7, s32[17]{0:T(128)S(1)} %copy-done.7, f32[4096,128]{1,0:T(8,128)S(1)} %shard_map.130.own_ref, f32[1024,128]{1,0:T(8,128)S(1)} %collective-permute-done.1.refs_0_, f32[1024,128]{1,0:T(8,128)S(1)} %collective-permute-done.2.refs_1_, ...), custom_call_target="tpu_custom_call" | custom-call | flops 4194304 | bytes 6291456 | tf_op jit(solution)/shard_map/pallas_call | solution.py:163
  10.8 8.0 %all-to-all-start = ((f32[16,8,128]{2,1,0:T(8,128)}), f32[16,8,128]{2,1,0:T(8,128)S(1)}, u32[]{:S(2)}, u32[]{:S(2)}) async-start(f32[16,8,128]{2,1,0:T(8,128)} %bitcast.4), calls=%async_computation | async-start | bytes 131072 | tf_op jit(solution)/shard_map/all_to_all | solution.py:358
  19.5 1.1 %shard_map.135 = bf16[4096,128]{1,0:T(8,128)(2,1)} custom-call(f32[4096,128]{1,0:T(8,128)S(1)} %get-tuple-element.22.x_ref), custom_call_target="tpu_custom_call" | custom-call | flops 524288 | bytes 3145728 | tf_op jit(solution)/shard_map/pallas_call | solution.py:259
  20.6 5.8 %all-to-all-done.arr_ref = f32[16,8,128]{2,1,0:T(8,128)S(1)} async-done(((f32[16,8,128]{2,1,0:T(8,128)}), f32[16,8,128]{2,1,0:T(8,128)S(1)}, u32[]{:S(2)}, u32[]{:S(2)}) %all-to-all-start) | async-done | bytes 65568 | tf_op jit(solution)/shard_map/all_to_all | solution.py:358
  26.4 1.0 %shard_map.136 = (f32[256,128]{1,0:T(8,128)S(1)}, bf16[256,128]{1,0:T(8,128)(2,1)S(1)}) custom-call(s32[1]{0:T(128)} %bitcast.me, s32[1]{0:T(128)S(6)} %copy.14.least, s32[17]{0:T(128)S(1)} %copy-done.7, f32[16,8,128]{2,1,0:T(8,128)S(1)} %all-to-all-done.arr_ref, f32[256,128]{1,0:T(8,128)S(1)} %copy-done.3, f32[256,128]{1,0:T(8,128)S(1)} %copy-done.4, ...), custom_call_target="tpu_custom_call" | custom-call | flops 50331648 | bytes 983040 | tf_op jit(solution)/shard_map/pallas_call | solution.py:226
  27.4 0.7 %collective-permute-start.5 = (bf16[256,128]{1,0:T(8,128)(2,1)S(1)}, bf16[256,128]{1,0:T(8,128)(2,1)S(1)}, u32[]{:S(2)}, u32[]{:S(2)}) collective-permute-start(bf16[256,128]{1,0:T(8,128)(2,1)S(1)} %get-tuple-element.24.refs_0_), channel_id=1, source_target_pairs={{0,8},{1,17},{2,10},{3,19},{4,12},{5,21},{6,14},{7,23},{8,0},{9,25... | collective-permute-start | bytes 196616 | tf_op jit(solution)/shard_map/ppermute | solution.py:39
  28.1 0.8 %collective-permute-start.6 = (bf16[256,128]{1,0:T(8,128)(2,1)S(1)}, bf16[256,128]{1,0:T(8,128)(2,1)S(1)}, u32[]{:S(2)}, u32[]{:S(2)}) collective-permute-start(bf16[256,128]{1,0:T(8,128)(2,1)S(1)} %get-tuple-element.24.refs_0_), channel_id=1, source_target_pairs={{0,16},{1,25},{2,18},{3,27},{4,20},{5,29},{6,22},{7,31},{8,24},{9,... | collective-permute-start | bytes 196616 | tf_op jit(solution)/shard_map/ppermute | solution.py:39
  29.0 2.9 %collective-permute-start.7 = (bf16[256,128]{1,0:T(8,128)(2,1)S(1)}, bf16[256,128]{1,0:T(8,128)(2,1)S(1)}, u32[]{:S(2)}, u32[]{:S(2)}) collective-permute-start(bf16[256,128]{1,0:T(8,128)(2,1)S(1)} %get-tuple-element.24.refs_0_), channel_id=1, source_target_pairs={{0,24},{1,9},{2,26},{3,11},{4,28},{5,13},{6,30},{7,15},{8,16},{9,1... | collective-permute-start | bytes 196616 | tf_op jit(solution)/shard_map/ppermute | solution.py:39
  31.9 2.2 %shard_map.137.refs_1_ = bf16[512,4096]{1,0:T(8,128)(2,1)S(1)} custom-call(bf16[512,4096]{1,0:T(8,128)(2,1)} %collective-permute-done.8.refs_0_), custom_call_target="tpu_custom_call" | custom-call | bytes 8388608 | tf_op jit(solution)/shard_map/pallas_call | solution.py:78
  34.1 1.0 %collective-permute-done.7.refs_3_ = bf16[256,128]{1,0:T(8,128)(2,1)S(1)} collective-permute-done((bf16[256,128]{1,0:T(8,128)(2,1)S(1)}, bf16[256,128]{1,0:T(8,128)(2,1)S(1)}, u32[]{:S(2)}, u32[]{:S(2)}) %collective-permute-start.7) | collective-permute-done | bytes 65568 | tf_op jit(solution)/shard_map/ppermute | solution.py:39
  35.1 0.7 %collective-permute-start.11 = (bf16[4,256,128]{2,1,0:T(8,128)(2,1)S(1)}, bf16[4,256,128]{2,1,0:T(8,128)(2,1)S(1)}, u32[]{:S(2)}, u32[]{:S(2)}) collective-permute-start(bf16[4,256,128]{2,1,0:T(8,128)(2,1)S(1)} %shard_map.138.refs_2_), channel_id=1, source_target_pairs={{0,2},{1,5},{2,0},{3,7},{4,6},{5,1},{6,4},{7,3},{8,10},{9,13},{10,... | collective-permute-start | bytes 786440 | tf_op jit(solution)/shard_map/ppermute | solution.py:39
  35.8 0.5 collective-permute-start.10
  36.4 2.3 %collective-permute-start.9 = (bf16[4,256,128]{2,1,0:T(8,128)(2,1)S(1)}, bf16[4,256,128]{2,1,0:T(8,128)(2,1)S(1)}, u32[]{:S(2)}, u32[]{:S(2)}) collective-permute-start(bf16[4,256,128]{2,1,0:T(8,128)(2,1)S(1)} %shard_map.138.refs_2_), channel_id=1, source_target_pairs={{0,6},{1,7},{2,4},{3,5},{4,2},{5,3},{6,0},{7,1},{8,14},{9,15},{10,... | collective-permute-start | bytes 786440 | tf_op jit(solution)/shard_map/ppermute | solution.py:39
  38.7 0.8 %shard_map.143 = (f32[256,128]{1,0:T(8,128)}, f32[256,128]{1,0:T(8,128)}, f32[256,128]{1,0:T(8,128)}) custom-call(f32[256,128]{1,0:T(8,128)S(1)} %get-tuple-element.31.g_ref, f32[256,128]{1,0:T(8,128)S(1)} %copy-done.3, f32[256,128]{1,0:T(8,128)S(1)} %copy-done.4, f32[256,128]{1,0:T(8,128)S(1)} %copy-done.5), custom_call_target="tpu_custom_call" | custom-call | flops 655360 | bytes 917504 | tf_op jit(solution)/shard_map/pallas_call | solution.py:243
  39.5 0.7 %shard_map.139.refs_3_ = f32[1024,128]{1,0:T(8,128)S(1)} custom-call(s32[1]{0:T(128)} %bitcast.me, s32[1]{0:T(128)} %bitcast.1.core, bf16[512,4096]{1,0:T(8,128)(2,1)S(1)} %copy-done.1, bf16[512,4096]{1,0:T(8,128)(2,1)S(1)} %shard_map.137.refs_1_, bf16[4,256,128]{2,1,0:T(8,128)(2,1)S(1)} %shard_map.138.refs_2_), custom_call_target="tpu_custom_call" | custom-call | flops 268435456 | bytes 3145728 | tf_op jit(solution)/shard_map/pallas_call | solution.py:315
  40.2 4.2 %collective-permute-done.11.refs_2_ = bf16[4,256,128]{2,1,0:T(8,128)(2,1)S(1)} collective-permute-done((bf16[4,256,128]{2,1,0:T(8,128)(2,1)S(1)}, bf16[4,256,128]{2,1,0:T(8,128)(2,1)S(1)}, u32[]{:S(2)}, u32[]{:S(2)}) %collective-permute-start.11) | collective-permute-done | bytes 262176 | tf_op jit(solution)/shard_map/ppermute | solution.py:39
  44.4 0.7 %shard_map.140.refs_3_ = f32[1024,128]{1,0:T(8,128)S(1)} custom-call(s32[1]{0:T(128)} %bitcast.me, s32[1]{0:T(128)} %bitcast.1.core, bf16[512,4096]{1,0:T(8,128)(2,1)S(1)} %copy-done.1, bf16[512,4096]{1,0:T(8,128)(2,1)S(1)} %shard_map.137.refs_1_, bf16[4,256,128]{2,1,0:T(8,128)(2,1)S(1)} %collective-permute-done.11.refs_2_, f32[1024,128]{1,0:T(8,128)S(1)} %shard_map.139.refs_3_), custom_call_target="tpu_custom_call" | custom-call | flops 268435456 | bytes 3145728 | tf_op jit(solution)/shard_map/pallas_call | solution.py:315
  45.1 0.7 %shard_map.141.refs_3_ = f32[1024,128]{1,0:T(8,128)S(1)} custom-call(s32[1]{0:T(128)} %bitcast.me, s32[1]{0:T(128)} %bitcast.1.core, bf16[512,4096]{1,0:T(8,128)(2,1)S(1)} %copy-done.1, bf16[512,4096]{1,0:T(8,128)(2,1)S(1)} %shard_map.137.refs_1_, bf16[4,256,128]{2,1,0:T(8,128)(2,1)S(1)} %collective-permute-done.10.refs_2_, f32[1024,128]{1,0:T(8,128)S(1)} %shard_map.140.refs_3_), custom_call_target="tpu_custom_call" | custom-call | flops 268435456 | bytes 3145728 | tf_op jit(solution)/shard_map/pallas_call | solution.py:315
  45.8 3.5 %collective-permute-done.9.refs_2_ = bf16[4,256,128]{2,1,0:T(8,128)(2,1)S(1)} collective-permute-done((bf16[4,256,128]{2,1,0:T(8,128)(2,1)S(1)}, bf16[4,256,128]{2,1,0:T(8,128)(2,1)S(1)}, u32[]{:S(2)}, u32[]{:S(2)}) %collective-permute-start.9) | collective-permute-done | bytes 262176 | tf_op jit(solution)/shard_map/ppermute | solution.py:39
  49.4 1.4 %shard_map.142 = bf16[1024,128]{1,0:T(8,128)(2,1)} custom-call(s32[1]{0:T(128)} %bitcast.me, s32[1]{0:T(128)} %bitcast.1.core, bf16[512,4096]{1,0:T(8,128)(2,1)S(1)} %copy-done.1, bf16[512,4096]{1,0:T(8,128)(2,1)S(1)} %shard_map.137.refs_1_, bf16[4,256,128]{2,1,0:T(8,128)(2,1)S(1)} %collective-permute-done.9.refs_2_, f32[1024,128]{1,0:T(8,128)S(1)} %shard_map.141.refs_3_), custom_call_target="tpu_custom_call" | custom-call | flops 268435456 | bytes 3145728 | tf_op jit(solution)/shard_map/pallas_call | solution.py:315
  (28 shorter events, 0.1 us)
Async XLA Ops:
  0.6 2.8 %collective-permute-start = (bf16[1024,128]{1,0:T(8,128)(2,1)}, bf16[1024,128]{1,0:T(8,128)(2,1)S(1)}, u32[]{:S(2)}, u32[]{:S(2)}) collective-permute-start(bf16[1024,128]{1,0:T(8,128)(2,1)} %g_ref), channel_id=1, source_target_pairs={{0,1},{1,0},{2,3},{3,2},{4,5},{5,4},{6,7},{7,6},{8,9},{9,8},{10,11... | collective-permute-start | bytes 786440 | tf_op jit(solution)/shard_map/ppermute | solution.py:29
  3.4 3.5 %copy-start = (bf16[512,4096]{1,0:T(8,128)(2,1)}, bf16[512,4096]{1,0:T(8,128)(2,1)S(1)}, u32[]{:S(2)}) copy-start(bf16[512,4096]{1,0:T(8,128)(2,1)S(1)} %shard_map.128.f_ref.refs_0_) | copy-start | bytes 12582916
  3.9 4.4 %collective-permute-start.1 = (f32[1024,128]{1,0:T(8,128)S(1)}, f32[1024,128]{1,0:T(8,128)S(1)}, u32[]{:S(2)}, u32[]{:S(2)}) collective-permute-start(f32[1024,128]{1,0:T(8,128)S(1)} %shard_map.131), channel_id=1, source_target_pairs={{0,1},{1,0},{2,3},{3,2},{4,5},{5,4},{6,7},{7,6},{8,9},{9,8},{10,11... | collective-permute-start | bytes 1572872 | tf_op jit(solution)/shard_map/ppermute | solution.py:29
  4.6 2.3 %copy-start.2 = (bf16[1,4096,128]{2,1,0:T(8,128)(2,1)S(1)}, bf16[1,4096,128]{2,1,0:T(8,128)(2,1)}, u32[]{:S(2)}) copy-start(bf16[1,4096,128]{2,1,0:T(8,128)(2,1)} %param.11) | copy-start | bytes 3145732
  4.6 2.3 %copy-start.6 = (bf16[1024,128]{1,0:T(8,128)(2,1)S(1)}, bf16[1024,128]{1,0:T(8,128)(2,1)}, u32[]{:S(2)}) copy-start(bf16[1024,128]{1,0:T(8,128)(2,1)} %g_ref) | copy-start | bytes 786436
  4.6 3.7 %collective-permute-start.2 = (f32[1024,128]{1,0:T(8,128)S(1)}, f32[1024,128]{1,0:T(8,128)S(1)}, u32[]{:S(2)}, u32[]{:S(2)}) collective-permute-start(f32[1024,128]{1,0:T(8,128)S(1)} %shard_map.132), channel_id=1, source_target_pairs={{0,1},{1,0},{2,3},{3,2},{4,5},{5,4},{6,7},{7,6},{8,9},{9,8},{10,11... | collective-permute-start | bytes 1572872 | tf_op jit(solution)/shard_map/ppermute | solution.py:29
  5.6 2.7 %collective-permute-start.3 = (f32[1024,128]{1,0:T(8,128)S(1)}, f32[1024,128]{1,0:T(8,128)S(1)}, u32[]{:S(2)}, u32[]{:S(2)}) collective-permute-start(f32[1024,128]{1,0:T(8,128)S(1)} %shard_map.133), channel_id=1, source_target_pairs={{0,1},{1,0},{2,3},{3,2},{4,5},{5,4},{6,7},{7,6},{8,9},{9,8},{10,11... | collective-permute-start | bytes 1572872 | tf_op jit(solution)/shard_map/ppermute | solution.py:29
  6.3 2.5 %copy-start.7 = (s32[17]{0:T(128)S(1)}, s32[17]{0:T(128)}, u32[]{:S(2)}) copy-start(s32[17]{0:T(128)} %edges.3) | copy-start | bytes 208
  6.3 2.4 %copy-start.8 = (s32[1,1,32]{2,1,0:T(1,128)S(1)}, s32[1,1,32]{2,1,0:T(1,128)}, u32[]{:S(2)}) copy-start(s32[1,1,32]{2,1,0:T(1,128)} %param.12) | copy-start | bytes 388
  6.3 2.0 %collective-permute-start.4 = (f32[1024,128]{1,0:T(8,128)S(1)}, f32[1024,128]{1,0:T(8,128)S(1)}, u32[]{:S(2)}, u32[]{:S(2)}) collective-permute-start(f32[1024,128]{1,0:T(8,128)S(1)} %shard_map.129), channel_id=1, source_target_pairs={{0,1},{1,0},{2,3},{3,2},{4,5},{5,4},{6,7},{7,6},{8,9},{9,8},{10,11... | collective-permute-start | bytes 1572872 | tf_op jit(solution)/shard_map/ppermute | solution.py:29
  8.3 18.1 %copy-start.3 = (f32[256,128]{1,0:T(8,128)S(1)}, f32[256,128]{1,0:T(8,128)}, u32[]{:S(2)}) copy-start(f32[256,128]{1,0:T(8,128)} %m_ref.3) | copy-start | bytes 393220
  8.3 18.1 %copy-start.4 = (f32[256,128]{1,0:T(8,128)S(1)}, f32[256,128]{1,0:T(8,128)}, u32[]{:S(2)}) copy-start(f32[256,128]{1,0:T(8,128)} %v_ref.3) | copy-start | bytes 393220
  8.3 18.1 %copy-start.5 = (f32[256,128]{1,0:T(8,128)S(1)}, f32[256,128]{1,0:T(8,128)}, u32[]{:S(2)}) copy-start(f32[256,128]{1,0:T(8,128)} %w_ref.3) | copy-start | bytes 393220
  8.4 23.5 %collective-permute-start.8 = (bf16[512,4096]{1,0:T(8,128)(2,1)}, bf16[512,4096]{1,0:T(8,128)(2,1)}, u32[]{:S(2)}, u32[]{:S(2)}) collective-permute-start(bf16[512,4096]{1,0:T(8,128)(2,1)} %refs_0_.1), channel_id=1, source_target_pairs={{0,1},{1,0},{2,3},{3,2},{4,5},{5,4},{6,7},{7,6},{8,9},{9,8},{10,11... | collective-permute-start | bytes 12582920 | tf_op jit(solution)/shard_map/ppermute | solution.py:29
  10.8 15.6 %all-to-all-start = ((f32[16,8,128]{2,1,0:T(8,128)}), f32[16,8,128]{2,1,0:T(8,128)S(1)}, u32[]{:S(2)}, u32[]{:S(2)}) async-start(f32[16,8,128]{2,1,0:T(8,128)} %bitcast.4), calls=%async_computation | async-start | bytes 131072 | tf_op jit(solution)/shard_map/all_to_all | solution.py:358
  27.4 12.1 %copy-start.1 = (bf16[512,4096]{1,0:T(8,128)(2,1)S(1)}, bf16[512,4096]{1,0:T(8,128)(2,1)}, u32[]{:S(2)}) copy-start(bf16[512,4096]{1,0:T(8,128)(2,1)} %copy-done) | copy-start | bytes 12582916
  27.4 6.7 %collective-permute-start.5 = (bf16[256,128]{1,0:T(8,128)(2,1)S(1)}, bf16[256,128]{1,0:T(8,128)(2,1)S(1)}, u32[]{:S(2)}, u32[]{:S(2)}) collective-permute-start(bf16[256,128]{1,0:T(8,128)(2,1)S(1)} %get-tuple-element.24.refs_0_), channel_id=1, source_target_pairs={{0,8},{1,17},{2,10},{3,19},{4,12},{5,21},{6,14},{7,23},{8,0},{9,25... | collective-permute-start | bytes 196616 | tf_op jit(solution)/shard_map/ppermute | solution.py:39
  28.1 6.0 %collective-permute-start.6 = (bf16[256,128]{1,0:T(8,128)(2,1)S(1)}, bf16[256,128]{1,0:T(8,128)(2,1)S(1)}, u32[]{:S(2)}, u32[]{:S(2)}) collective-permute-start(bf16[256,128]{1,0:T(8,128)(2,1)S(1)} %get-tuple-element.24.refs_0_), channel_id=1, source_target_pairs={{0,16},{1,25},{2,18},{3,27},{4,20},{5,29},{6,22},{7,31},{8,24},{9,... | collective-permute-start | bytes 196616 | tf_op jit(solution)/shard_map/ppermute | solution.py:39
  29.0 6.1 %collective-permute-start.7 = (bf16[256,128]{1,0:T(8,128)(2,1)S(1)}, bf16[256,128]{1,0:T(8,128)(2,1)S(1)}, u32[]{:S(2)}, u32[]{:S(2)}) collective-permute-start(bf16[256,128]{1,0:T(8,128)(2,1)S(1)} %get-tuple-element.24.refs_0_), channel_id=1, source_target_pairs={{0,24},{1,9},{2,26},{3,11},{4,28},{5,13},{6,30},{7,15},{8,16},{9,1... | collective-permute-start | bytes 196616 | tf_op jit(solution)/shard_map/ppermute | solution.py:39
  35.1 9.3 %collective-permute-start.11 = (bf16[4,256,128]{2,1,0:T(8,128)(2,1)S(1)}, bf16[4,256,128]{2,1,0:T(8,128)(2,1)S(1)}, u32[]{:S(2)}, u32[]{:S(2)}) collective-permute-start(bf16[4,256,128]{2,1,0:T(8,128)(2,1)S(1)} %shard_map.138.refs_2_), channel_id=1, source_target_pairs={{0,2},{1,5},{2,0},{3,7},{4,6},{5,1},{6,4},{7,3},{8,10},{9,13},{10,... | collective-permute-start | bytes 786440 | tf_op jit(solution)/shard_map/ppermute | solution.py:39
  35.8 9.3 %collective-permute-start.10 = (bf16[4,256,128]{2,1,0:T(8,128)(2,1)S(1)}, bf16[4,256,128]{2,1,0:T(8,128)(2,1)S(1)}, u32[]{:S(2)}, u32[]{:S(2)}) collective-permute-start(bf16[4,256,128]{2,1,0:T(8,128)(2,1)S(1)} %shard_map.138.refs_2_), channel_id=1, source_target_pairs={{0,4},{1,3},{2,6},{3,1},{4,0},{5,7},{6,2},{7,5},{8,12},{9,11},{10,... | collective-permute-start | bytes 786440 | tf_op jit(solution)/shard_map/ppermute | solution.py:39
  36.4 13.0 %collective-permute-start.9 = (bf16[4,256,128]{2,1,0:T(8,128)(2,1)S(1)}, bf16[4,256,128]{2,1,0:T(8,128)(2,1)S(1)}, u32[]{:S(2)}, u32[]{:S(2)}) collective-permute-start(bf16[4,256,128]{2,1,0:T(8,128)(2,1)S(1)} %shard_map.138.refs_2_), channel_id=1, source_target_pairs={{0,6},{1,7},{2,4},{3,5},{4,2},{5,3},{6,0},{7,1},{8,14},{9,15},{10,... | collective-permute-start | bytes 786440 | tf_op jit(solution)/shard_map/ppermute | solution.py:39

commit v7 on v3

--- a/solution.py
+++ b/solution.py
@@ -278,12 +278,12 @@
 
 
 def project_kernel(masks, last, n_f, me, core, *refs):
-    feats, pieces, out_ref = refs[:n_f], refs[n_f : n_f + 2], refs[-1]
+    feats, pieces, out_ref = refs[:n_f], refs[n_f:-1], refs[-1]
+    old = [ref for ref in pieces if ref.dtype == jnp.float32]
+    pieces = pieces[: len(pieces) - len(old)]
     tokens = feats[0].shape[0]
-    region = pieces[0].shape[0]
-    weight = jnp.concatenate(
-        [pieces[0][...]] + [pieces[1][j] for j in range(pieces[1].shape[0])], axis=0
-    )
+    region, width = pieces[0].shape[-2:]
+    weight = jnp.concatenate([ref[...].reshape(-1, width) for ref in pieces], axis=0)
     for i, f_ref in enumerate(feats):
         mine = pl.ds(i * tokens, tokens)
         part = [
@@ -292,8 +292,8 @@
         total = jnp.dot(
             jnp.concatenate(part, axis=1), weight, preferred_element_type=jnp.float32
         )
-        if len(refs) > n_f + 3:
-            total = total + refs[n_f + 2][mine, :]
+        if old:
+            total = total + old[0][mine, :]
         if last:
             place = lax.rem(core[0] + i, n_f) * tokens
             mine = pl.ds(pl.multiple_of(place, tokens), tokens)
@@ -301,14 +301,14 @@
 
 
 def project(masks, me, core, feats, pieces, total, last):
-    region, width = pieces[0].shape
+    region, width = pieces[0].shape[-2:]
     whole = len(feats) * feats[0].shape[0]
     old = [] if total is None else [total]
     out = jax.ShapeDtypeStruct((whole, width), jnp.bfloat16 if last else jnp.float32)
     depth = len(masks) * region
     return pl.pallas_call(
         functools.partial(project_kernel, masks, last, len(feats)),
-        in_specs=[SMEM, SMEM] + [VMEM] * (len(feats) + 2 + len(old)),
+        in_specs=[SMEM, SMEM] + [VMEM] * (len(feats) + len(pieces) + len(old)),
         out_specs=VMEM,
         out_shape=out,
         compiler_params=params(*pieces, out, *feats, *old),
@@ -352,16 +352,18 @@
     arrived = lax.all_to_all(
         outgoing.reshape(owners, SLOTS, width), "dp", split_axis=0, concat_axis=0, tiled=True
     )
+    arrived, error_out = lax.optimization_barrier((arrived, error_out))
     grad, weight = weigh(me1, threshold, bin_edges, arrived, moment, second, master)
     bits = [1 << i for i in range(owners.bit_length() - 1)]
     if 1 << len(bits) == owners and len(bits) > 2 and region % LANES == 0:
         plane, line = spans(bits[:2]), spans(bits[2:])
+        far = [swap(weight, "dp", m) for m in line[1:]]
         near = [swap(weight, "dp", b) for b in plane[1:]]
-        far = [swap(weight, "dp", m) for m in line[1:]]
-        near, far = lax.optimization_barrier((near, far))
         rest = join(far)
         groups = [[weight, rest]]
-        groups += [[own, swap(rest, "dp", b)] for own, b in zip(near, plane[1:])]
+        groups += [[own, swap(rest, "dp", b)] for own, b in zip(near[:-1], plane[1:-1])]
+        final, near = lax.optimization_barrier((rest, near))
+        groups.append([near[-1], swap(final, "dp", plane[-1])])
         feats = [held, *load(feats[1:])]
         keys = None
         for j, b in enumerate(plane):

time: 52.6 us -> 49.9 us (0.949)
  waiting for transfers between devices: 13.2 us -> 10.4 us
    ppermute x9, waiting for transfers between devices: 6.23 us -> 4.57 us  [swap(): lax.ppermute(x, axis, [(i, i ^ mask) for i in range(lax.axis_size(axis))])]
    all_to_all x1, waiting for transfers between devices: 6.88 us -> 5.81 us  [shards(): lax.all_to_all(outgoing.reshape(owners, SLOTS, width), 'dp', split_axis=0...]
  transfers between devices with their start and end apart: 16 -> 16, of which waited for: 7 -> 4; matrix products, arithmetic and copies ran while one was open for 0% -> 0% of each run, Pallas kernels for 28% -> 29%
where the time goes in v7:
time: 49.9 us; the launch traced here: 49.7 us
  starting transfers between devices  20 us (40%)
  Pallas kernels  16.6 us (33%)
  waiting for transfers between devices  10.4 us (21%)
  between operations  1.5 us (3%)
  local copies, waits for them, and re-layouts  1.12 us (2%)
    ppermute x9, starting transfers between devices, swap(): lax.ppermute(x, axis, [(i, i ^ mask) for i in range(lax.axis_size(axis))])  9.82 us
    all_to_all x1, starting transfers between devices, shards(): lax.all_to_all(outgoing.reshape(owners, SLOTS, width), 'dp', split_axis=0...  8.02 us
    all_to_all x1, waiting for transfers between devices, shards(): lax.all_to_all(outgoing.reshape(owners, SLOTS, width), 'dp', split_axis=0...  5.81 us
    pallas_call x2, Pallas kernels, load(): pl.pallas_call(functools.partial(load_kernel, pieces), in_specs=[ANY] * l...  4.58 us
    ppermute x9, waiting for transfers between devices, swap(): lax.ppermute(x, axis, [(i, i ^ mask) for i in range(lax.axis_size(axis))])  4.57 us
    pallas_call x4, Pallas kernels, project(): pl.pallas_call(functools.partial(project_kernel, masks, last, len(feats))...  3.54 us
    pallas_call x5, Pallas kernels, part_sum(): pl.pallas_call(functools.partial(part_kernel, first), in_specs=[SMEM, VME...  3.49 us
    ppermute x6, starting transfers between devices, shift(): return lax.ppermute(x, axis, [(i, (i + step) % n) for i in range(n)])  2.17 us
  transfers between devices with their start and end apart: 16, of which 4 were waited for; matrix products, arithmetic and copies ran while one was open for 0% of the time, Pallas kernels for 29%

profile of v7, /device:TPU:0, one launch (start us, length us, event | category | flops | bytes accessed | tf_op | source)
XLA Modules:
  0.0 49.7 jit_solution(10048538030339832355)
XLA Ops:
  0.6 0.5 %collective-permute-start = (bf16[1024,128]{1,0:T(8,128)(2,1)}, bf16[1024,128]{1,0:T(8,128)(2,1)S(1)}, u32[]{:S(2)}, u32[]{:S(2)}) collective-permute-start(bf16[1024,128]{1,0:T(8,128)(2,1)} %g_ref), channel_id=1, source_target_pairs={{0,1},{1,0},{2,3},{3,2},{4,5},{5,4},{6,7},{7,6},{8,9},{9,8},{10,11... | collective-permute-start | bytes 786440 | tf_op jit(solution)/shard_map/ppermute | solution.py:29
  1.1 2.2 %shard_map.128.f_ref.refs_0_ = bf16[512,4096]{1,0:T(8,128)(2,1)S(1)} custom-call(bf16[512,4096]{1,0:T(8,128)(2,1)} %refs_0_.1), custom_call_target="tpu_custom_call" | custom-call | bytes 8388608 | tf_op jit(solution)/shard_map/pallas_call | solution.py:72
  3.4 0.5 %shard_map.129 = f32[1024,128]{1,0:T(8,128)S(1)} custom-call(s32[1]{0:T(128)} %bitcast.1.core, bf16[512,4096]{1,0:T(8,128)(2,1)S(1)} %shard_map.128.f_ref.refs_0_, bf16[1024,128]{1,0:T(8,128)(2,1)S(1)} %collective-permute-done.g_ref), custom_call_target="tpu_custom_call" | custom-call | flops 134217728 | bytes 1572864 | tf_op jit(solution)/shard_map/pallas_call | solution.py:104
  4.0 0.5 %shard_map.131 = f32[1024,128]{1,0:T(8,128)S(1)} custom-call(s32[1]{0:T(128)} %bitcast.1.core, bf16[512,4096]{1,0:T(8,128)(2,1)S(1)} %shard_map.128.f_ref.refs_0_, bf16[1024,128]{1,0:T(8,128)(2,1)S(1)} %collective-permute-done.g_ref), custom_call_target="tpu_custom_call" | custom-call | flops 134217728 | bytes 1572864 | tf_op jit(solution)/shard_map/pallas_call | solution.py:104
  4.6 0.5 %collective-permute-start.1 = (f32[1024,128]{1,0:T(8,128)S(1)}, f32[1024,128]{1,0:T(8,128)S(1)}, u32[]{:S(2)}, u32[]{:S(2)}) collective-permute-start(f32[1024,128]{1,0:T(8,128)S(1)} %shard_map.131), channel_id=1, source_target_pairs={{0,1},{1,0},{2,3},{3,2},{4,5},{5,4},{6,7},{7,6},{8,9},{9,8},{10,11... | collective-permute-start | bytes 1572872 | tf_op jit(solution)/shard_map/ppermute | solution.py:29
  5.1 0.5 %shard_map.132 = f32[1024,128]{1,0:T(8,128)S(1)} custom-call(s32[1]{0:T(128)} %bitcast.1.core, bf16[512,4096]{1,0:T(8,128)(2,1)S(1)} %shard_map.128.f_ref.refs_0_, bf16[1024,128]{1,0:T(8,128)(2,1)S(1)} %collective-permute-done.g_ref), custom_call_target="tpu_custom_call" | custom-call | flops 134217728 | bytes 1572864 | tf_op jit(solution)/shard_map/pallas_call | solution.py:104
  5.8 0.5 %shard_map.133 = f32[1024,128]{1,0:T(8,128)S(1)} custom-call(s32[1]{0:T(128)} %bitcast.1.core, bf16[512,4096]{1,0:T(8,128)(2,1)S(1)} %shard_map.128.f_ref.refs_0_, bf16[1024,128]{1,0:T(8,128)(2,1)S(1)} %collective-permute-done.g_ref), custom_call_target="tpu_custom_call" | custom-call | flops 134217728 | bytes 1572864 | tf_op jit(solution)/shard_map/pallas_call | solution.py:104
  6.3 0.5 %collective-permute-start.3 = (f32[1024,128]{1,0:T(8,128)S(1)}, f32[1024,128]{1,0:T(8,128)S(1)}, u32[]{:S(2)}, u32[]{:S(2)}) collective-permute-start(f32[1024,128]{1,0:T(8,128)S(1)} %shard_map.133), channel_id=1, source_target_pairs={{0,1},{1,0},{2,3},{3,2},{4,5},{5,4},{6,7},{7,6},{8,9},{9,8},{10,11... | collective-permute-start | bytes 1572872 | tf_op jit(solution)/shard_map/ppermute | solution.py:29
  6.8 1.4 %shard_map.130.own_ref = f32[4096,128]{1,0:T(8,128)S(1)} custom-call(s32[1]{0:T(128)} %bitcast.1.core, bf16[512,4096]{1,0:T(8,128)(2,1)S(1)} %shard_map.128.f_ref.refs_0_, bf16[1024,128]{1,0:T(8,128)(2,1)S(1)} %copy-done.6, bf16[4096,128]{1,0:T(8,128)(2,1)S(1)} %bitcast.6), custom_call_target="tpu_custom_call" | custom-call | flops 536870912 | bytes 6291456 | tf_op jit(solution)/shard_map/pallas_call | solution.py:104
  8.8 2.1 %shard_map.135 = (f32[4096,128]{1,0:T(8,128)S(1)}, f32[128,128]{1,0:T(8,128)}) custom-call(s32[32]{0:T(128)S(1)} %bitcast.7, s32[17]{0:T(128)S(1)} %copy-done.7, f32[4096,128]{1,0:T(8,128)S(1)} %shard_map.130.own_ref, f32[1024,128]{1,0:T(8,128)S(1)} %collective-permute-done.1.refs_0_, f32[1024,128]{1,0:T(8,128)S(1)} %collective-permute-done.2.refs_1_, ...), custom_call_target="tpu_custom_call" | custom-call | flops 4194304 | bytes 6291456 | tf_op jit(solution)/shard_map/pallas_call | solution.py:157
  10.8 8.0 %all-to-all-start = ((f32[16,8,128]{2,1,0:T(8,128)}), f32[16,8,128]{2,1,0:T(8,128)S(1)}, u32[]{:S(2)}, u32[]{:S(2)}) async-start(f32[16,8,128]{2,1,0:T(8,128)} %bitcast.4), calls=%async_computation | async-start | bytes 131072 | tf_op jit(solution)/shard_map/all_to_all | solution.py:352
  19.5 1.1 %shard_map.136 = bf16[4096,128]{1,0:T(8,128)(2,1)} custom-call(f32[4096,128]{1,0:T(8,128)S(1)} %get-tuple-element.21.x_ref), custom_call_target="tpu_custom_call" | custom-call | flops 524288 | bytes 3145728 | tf_op jit(solution)/shard_map/pallas_call | solution.py:253
  20.6 5.8 %all-to-all-done.arr_ref = f32[16,8,128]{2,1,0:T(8,128)S(1)} async-done(((f32[16,8,128]{2,1,0:T(8,128)}), f32[16,8,128]{2,1,0:T(8,128)S(1)}, u32[]{:S(2)}, u32[]{:S(2)}) %all-to-all-start) | async-done | bytes 65568 | tf_op jit(solution)/shard_map/all_to_all | solution.py:352
  26.4 1.0 %shard_map.137 = (f32[256,128]{1,0:T(8,128)S(1)}, bf16[256,128]{1,0:T(8,128)(2,1)S(1)}) custom-call(s32[1]{0:T(128)} %bitcast.me, s32[1]{0:T(128)S(6)} %copy.14.least, s32[17]{0:T(128)S(1)} %copy-done.7, f32[16,8,128]{2,1,0:T(8,128)S(1)} %all-to-all-done.arr_ref, f32[256,128]{1,0:T(8,128)S(1)} %copy-done.3, f32[256,128]{1,0:T(8,128)S(1)} %copy-done.4, ...), custom_call_target="tpu_custom_call" | custom-call | flops 50331648 | bytes 983040 | tf_op jit(solution)/shard_map/pallas_call | solution.py:220
  27.4 0.7 %collective-permute-start.6 = (bf16[256,128]{1,0:T(8,128)(2,1)S(1)}, bf16[256,128]{1,0:T(8,128)(2,1)S(1)}, u32[]{:S(2)}, u32[]{:S(2)}) collective-permute-start(bf16[256,128]{1,0:T(8,128)(2,1)S(1)} %get-tuple-element.23.refs_2_), channel_id=1, source_target_pairs={{0,8},{2,10},{4,12},{6,14},{8,0},{10,2},{12,4},{14,6},{16,24},{18,... | collective-permute-start | bytes 196616 | tf_op jit(solution)/shard_map/ppermute | solution.py:33
  28.1 0.8 %collective-permute-start.7 = (bf16[256,128]{1,0:T(8,128)(2,1)S(1)}, bf16[256,128]{1,0:T(8,128)(2,1)S(1)}, u32[]{:S(2)}, u32[]{:S(2)}) collective-permute-start(bf16[256,128]{1,0:T(8,128)(2,1)S(1)} %get-tuple-element.23.refs_2_), channel_id=1, source_target_pairs={{0,16},{2,18},{4,20},{6,22},{8,24},{10,26},{12,28},{14,30},{16,0},... | collective-permute-start | bytes 196616 | tf_op jit(solution)/shard_map/ppermute | solution.py:33
  29.0 2.9 %collective-permute-start.8 = (bf16[256,128]{1,0:T(8,128)(2,1)S(1)}, bf16[256,128]{1,0:T(8,128)(2,1)S(1)}, u32[]{:S(2)}, u32[]{:S(2)}) collective-permute-start(bf16[256,128]{1,0:T(8,128)(2,1)S(1)} %get-tuple-element.23.refs_2_), channel_id=1, source_target_pairs={{0,24},{2,26},{4,28},{6,30},{8,16},{10,18},{12,20},{14,22},{16,8},... | collective-permute-start | bytes 196616 | tf_op jit(solution)/shard_map/ppermute | solution.py:33
  31.9 0.8 %collective-permute-start.9 = (bf16[256,128]{1,0:T(8,128)(2,1)S(1)}, bf16[256,128]{1,0:T(8,128)(2,1)S(1)}, u32[]{:S(2)}, u32[]{:S(2)}) collective-permute-start(bf16[256,128]{1,0:T(8,128)(2,1)S(1)} %get-tuple-element.23.refs_2_), channel_id=1, source_target_pairs={{0,2},{2,0},{4,6},{6,4},{8,10},{10,8},{12,14},{14,12},{16,18},{18,... | collective-permute-start | bytes 196616 | tf_op jit(solution)/shard_map/ppermute | solution.py:33
  32.7 0.4 collective-permute-start.10
  33.1 2.2 %collective-permute-done.7.refs_1_ = bf16[256,128]{1,0:T(8,128)(2,1)S(1)} collective-permute-done((bf16[256,128]{1,0:T(8,128)(2,1)S(1)}, bf16[256,128]{1,0:T(8,128)(2,1)S(1)}, u32[]{:S(2)}, u32[]{:S(2)}) %collective-permute-start.7) | collective-permute-done | bytes 65568 | tf_op jit(solution)/shard_map/ppermute | solution.py:33
  35.3 0.7 %collective-permute-start.11 = (bf16[256,128]{1,0:T(8,128)(2,1)S(1)}, bf16[256,128]{1,0:T(8,128)(2,1)S(1)}, u32[]{:S(2)}, u32[]{:S(2)}) collective-permute-start(bf16[256,128]{1,0:T(8,128)(2,1)S(1)} %get-tuple-element.23.refs_2_), channel_id=1, source_target_pairs={{0,6},{2,4},{4,2},{6,0},{8,14},{10,12},{12,10},{14,8},{16,22},{18,... | collective-permute-start | bytes 196616 | tf_op jit(solution)/shard_map/ppermute | solution.py:33
  36.0 1.5 %collective-permute-start.14 = (bf16[3,256,128]{2,1,0:T(8,128)(2,1)S(1)}, bf16[3,256,128]{2,1,0:T(8,128)(2,1)S(1)}, u32[]{:S(2)}, u32[]{:S(2)}) collective-permute-start(bf16[3,256,128]{2,1,0:T(8,128)(2,1)S(1)} %shard_map.138.refs_3_), channel_id=1, source_target_pairs={{0,2},{2,0},{4,6},{6,4},{8,10},{10,8},{12,14},{14,12},{16,18},{18,... | collective-permute-start | bytes 589832 | tf_op jit(solution)/shard_map/ppermute | solution.py:33
  37.5 1.4 %collective-permute-start.13 = (bf16[3,256,128]{2,1,0:T(8,128)(2,1)S(1)}, bf16[3,256,128]{2,1,0:T(8,128)(2,1)S(1)}, u32[]{:S(2)}, u32[]{:S(2)}) collective-permute-start(bf16[3,256,128]{2,1,0:T(8,128)(2,1)S(1)} %shard_map.138.refs_3_), channel_id=1, source_target_pairs={{0,4},{2,6},{4,0},{6,2},{8,12},{10,14},{12,8},{14,10},{16,20},{18,... | collective-permute-start | bytes 589832 | tf_op jit(solution)/shard_map/ppermute | solution.py:33
  38.9 2.3 %collective-permute-done.11.refs_2_ = bf16[256,128]{1,0:T(8,128)(2,1)S(1)} collective-permute-done((bf16[256,128]{1,0:T(8,128)(2,1)S(1)}, bf16[256,128]{1,0:T(8,128)(2,1)S(1)}, u32[]{:S(2)}, u32[]{:S(2)}) %collective-permute-start.11) | collective-permute-done | bytes 65568 | tf_op jit(solution)/shard_map/ppermute | solution.py:33
  41.2 0.6 %collective-permute-start.12 = (bf16[3,256,128]{2,1,0:T(8,128)(2,1)S(1)}, bf16[3,256,128]{2,1,0:T(8,128)(2,1)S(1)}, u32[]{:S(2)}, u32[]{:S(2)}) collective-permute-start(bf16[3,256,128]{2,1,0:T(8,128)(2,1)S(1)} %shard_map.138.refs_3_), channel_id=1, source_target_pairs={{0,6},{2,4},{4,2},{6,0},{8,14},{10,12},{12,10},{14,8},{16,22},{18,... | collective-permute-start | bytes 589832 | tf_op jit(solution)/shard_map/ppermute | solution.py:33
  41.8 0.8 %shard_map.143 = (f32[256,128]{1,0:T(8,128)}, f32[256,128]{1,0:T(8,128)}, f32[256,128]{1,0:T(8,128)}) custom-call(f32[256,128]{1,0:T(8,128)S(1)} %get-tuple-element.27.g_ref, f32[256,128]{1,0:T(8,128)S(1)} %copy-done.3, f32[256,128]{1,0:T(8,128)S(1)} %copy-done.4, f32[256,128]{1,0:T(8,128)S(1)} %copy-done.5), custom_call_target="tpu_custom_call" | custom-call | flops 655360 | bytes 917504 | tf_op jit(solution)/shard_map/pallas_call | solution.py:237
  42.6 2.4 %shard_map.134.refs_1_ = bf16[512,4096]{1,0:T(8,128)(2,1)S(1)} custom-call(bf16[512,4096]{1,0:T(8,128)(2,1)} %collective-permute-done.5.refs_0_), custom_call_target="tpu_custom_call" | custom-call | bytes 8388608 | tf_op jit(solution)/shard_map/pallas_call | solution.py:72
  45.0 1.1 %copy-done.1 = bf16[512,4096]{1,0:T(8,128)(2,1)S(1)} copy-done((bf16[512,4096]{1,0:T(8,128)(2,1)S(1)}, bf16[512,4096]{1,0:T(8,128)(2,1)}, u32[]{:S(2)}) %copy-start.1) | copy-done | bytes 4194328
  46.1 0.7 %shard_map.139.refs_4_ = f32[1024,128]{1,0:T(8,128)S(1)} custom-call(s32[1]{0:T(128)} %bitcast.me, s32[1]{0:T(128)} %bitcast.1.core, bf16[512,4096]{1,0:T(8,128)(2,1)S(1)} %copy-done.1, bf16[512,4096]{1,0:T(8,128)(2,1)S(1)} %shard_map.134.refs_1_, bf16[256,128]{1,0:T(8,128)(2,1)S(1)} %get-tuple-element.23.refs_2_, bf16[3,256,128]{2,1,0:T(8,128)(2,1)S(1)} %shard_map.138.refs_3_), custom_call_target="tpu_custom_call" | custom-call | flops 268435456 | bytes 3145728 | tf_op jit(solution)/shard_map/pallas_call | solution.py:309
  46.8 0.7 %shard_map.140.refs_4_ = f32[1024,128]{1,0:T(8,128)S(1)} custom-call(s32[1]{0:T(128)} %bitcast.me, s32[1]{0:T(128)} %bitcast.1.core, bf16[512,4096]{1,0:T(8,128)(2,1)S(1)} %copy-done.1, bf16[512,4096]{1,0:T(8,128)(2,1)S(1)} %shard_map.134.refs_1_, bf16[256,128]{1,0:T(8,128)(2,1)S(1)} %collective-permute-done.9.refs_2_, ...), custom_call_target="tpu_custom_call" | custom-call | flops 268435456 | bytes 3145728 | tf_op jit(solution)/shard_map/pallas_call | solution.py:309
  47.5 0.7 %shard_map.141.refs_4_ = f32[1024,128]{1,0:T(8,128)S(1)} custom-call(s32[1]{0:T(128)} %bitcast.me, s32[1]{0:T(128)} %bitcast.1.core, bf16[512,4096]{1,0:T(8,128)(2,1)S(1)} %copy-done.1, bf16[512,4096]{1,0:T(8,128)(2,1)S(1)} %shard_map.134.refs_1_, bf16[256,128]{1,0:T(8,128)(2,1)S(1)} %collective-permute-done.10.refs_2_, ...), custom_call_target="tpu_custom_call" | custom-call | flops 268435456 | bytes 3145728 | tf_op jit(solution)/shard_map/pallas_call | solution.py:309
  48.2 1.4 %shard_map.142 = bf16[1024,128]{1,0:T(8,128)(2,1)} custom-call(s32[1]{0:T(128)} %bitcast.me, s32[1]{0:T(128)} %bitcast.1.core, bf16[512,4096]{1,0:T(8,128)(2,1)S(1)} %copy-done.1, bf16[512,4096]{1,0:T(8,128)(2,1)S(1)} %shard_map.134.refs_1_, bf16[256,128]{1,0:T(8,128)(2,1)S(1)} %collective-permute-done.11.refs_2_, ...), custom_call_target="tpu_custom_call" | custom-call | flops 268435456 | bytes 3145728 | tf_op jit(solution)/shard_map/pallas_call | solution.py:309
  (34 shorter events, 0.8 us)
Async XLA Ops:
  0.6 2.8 %collective-permute-start = (bf16[1024,128]{1,0:T(8,128)(2,1)}, bf16[1024,128]{1,0:T(8,128)(2,1)S(1)}, u32[]{:S(2)}, u32[]{:S(2)}) collective-permute-start(bf16[1024,128]{1,0:T(8,128)(2,1)} %g_ref), channel_id=1, source_target_pairs={{0,1},{1,0},{2,3},{3,2},{4,5},{5,4},{6,7},{7,6},{8,9},{9,8},{10,11... | collective-permute-start | bytes 786440 | tf_op jit(solution)/shard_map/ppermute | solution.py:29
  3.4 3.5 %copy-start = (bf16[512,4096]{1,0:T(8,128)(2,1)}, bf16[512,4096]{1,0:T(8,128)(2,1)S(1)}, u32[]{:S(2)}) copy-start(bf16[512,4096]{1,0:T(8,128)(2,1)S(1)} %shard_map.128.f_ref.refs_0_) | copy-start | bytes 12582916
  3.9 4.4 %collective-permute-start.4 = (f32[1024,128]{1,0:T(8,128)S(1)}, f32[1024,128]{1,0:T(8,128)S(1)}, u32[]{:S(2)}, u32[]{:S(2)}) collective-permute-start(f32[1024,128]{1,0:T(8,128)S(1)} %shard_map.129), channel_id=1, source_target_pairs={{0,1},{1,0},{2,3},{3,2},{4,5},{5,4},{6,7},{7,6},{8,9},{9,8},{10,11... | collective-permute-start | bytes 1572872 | tf_op jit(solution)/shard_map/ppermute | solution.py:29
  4.6 2.3 %copy-start.2 = (bf16[1,4096,128]{2,1,0:T(8,128)(2,1)S(1)}, bf16[1,4096,128]{2,1,0:T(8,128)(2,1)}, u32[]{:S(2)}) copy-start(bf16[1,4096,128]{2,1,0:T(8,128)(2,1)} %param.11) | copy-start | bytes 3145732
  4.6 2.3 %copy-start.6 = (bf16[1024,128]{1,0:T(8,128)(2,1)S(1)}, bf16[1024,128]{1,0:T(8,128)(2,1)}, u32[]{:S(2)}) copy-start(bf16[1024,128]{1,0:T(8,128)(2,1)} %g_ref) | copy-start | bytes 786436
  4.6 3.7 %collective-permute-start.1 = (f32[1024,128]{1,0:T(8,128)S(1)}, f32[1024,128]{1,0:T(8,128)S(1)}, u32[]{:S(2)}, u32[]{:S(2)}) collective-permute-start(f32[1024,128]{1,0:T(8,128)S(1)} %shard_map.131), channel_id=1, source_target_pairs={{0,1},{1,0},{2,3},{3,2},{4,5},{5,4},{6,7},{7,6},{8,9},{9,8},{10,11... | collective-permute-start | bytes 1572872 | tf_op jit(solution)/shard_map/ppermute | solution.py:29
  5.6 2.7 %collective-permute-start.2 = (f32[1024,128]{1,0:T(8,128)S(1)}, f32[1024,128]{1,0:T(8,128)S(1)}, u32[]{:S(2)}, u32[]{:S(2)}) collective-permute-start(f32[1024,128]{1,0:T(8,128)S(1)} %shard_map.132), channel_id=1, source_target_pairs={{0,1},{1,0},{2,3},{3,2},{4,5},{5,4},{6,7},{7,6},{8,9},{9,8},{10,11... | collective-permute-start | bytes 1572872 | tf_op jit(solution)/shard_map/ppermute | solution.py:29
  6.3 2.4 %copy-start.7 = (s32[17]{0:T(128)S(1)}, s32[17]{0:T(128)}, u32[]{:S(2)}) copy-start(s32[17]{0:T(128)} %edges.3) | copy-start | bytes 208
  6.3 2.4 %copy-start.8 = (s32[1,1,32]{2,1,0:T(1,128)S(1)}, s32[1,1,32]{2,1,0:T(1,128)}, u32[]{:S(2)}) copy-start(s32[1,1,32]{2,1,0:T(1,128)} %param.12) | copy-start | bytes 388
  6.3 2.0 %collective-permute-start.3 = (f32[1024,128]{1,0:T(8,128)S(1)}, f32[1024,128]{1,0:T(8,128)S(1)}, u32[]{:S(2)}, u32[]{:S(2)}) collective-permute-start(f32[1024,128]{1,0:T(8,128)S(1)} %shard_map.133), channel_id=1, source_target_pairs={{0,1},{1,0},{2,3},{3,2},{4,5},{5,4},{6,7},{7,6},{8,9},{9,8},{10,11... | collective-permute-start | bytes 1572872 | tf_op jit(solution)/shard_map/ppermute | solution.py:29
  8.3 18.1 %copy-start.3 = (f32[256,128]{1,0:T(8,128)S(1)}, f32[256,128]{1,0:T(8,128)}, u32[]{:S(2)}) copy-start(f32[256,128]{1,0:T(8,128)} %m_ref.3) | copy-start | bytes 393220
  8.3 18.1 %copy-start.4 = (f32[256,128]{1,0:T(8,128)S(1)}, f32[256,128]{1,0:T(8,128)}, u32[]{:S(2)}) copy-start(f32[256,128]{1,0:T(8,128)} %v_ref.3) | copy-start | bytes 393220
  8.3 18.1 %copy-start.5 = (f32[256,128]{1,0:T(8,128)S(1)}, f32[256,128]{1,0:T(8,128)}, u32[]{:S(2)}) copy-start(f32[256,128]{1,0:T(8,128)} %w_ref.3) | copy-start | bytes 393220
  8.4 34.3 %collective-permute-start.5 = (bf16[512,4096]{1,0:T(8,128)(2,1)}, bf16[512,4096]{1,0:T(8,128)(2,1)}, u32[]{:S(2)}, u32[]{:S(2)}) collective-permute-start(bf16[512,4096]{1,0:T(8,128)(2,1)} %refs_0_.1), channel_id=1, source_target_pairs={{0,1},{1,0},{2,3},{3,2},{4,5},{5,4},{6,7},{7,6},{8,9},{9,8},{10,11... | collective-permute-start | bytes 12582920 | tf_op jit(solution)/shard_map/ppermute | solution.py:29
  10.8 15.6 %all-to-all-start = ((f32[16,8,128]{2,1,0:T(8,128)}), f32[16,8,128]{2,1,0:T(8,128)S(1)}, u32[]{:S(2)}, u32[]{:S(2)}) async-start(f32[16,8,128]{2,1,0:T(8,128)} %bitcast.4), calls=%async_computation | async-start | bytes 131072 | tf_op jit(solution)/shard_map/all_to_all | solution.py:352
  27.4 5.3 %collective-permute-start.6 = (bf16[256,128]{1,0:T(8,128)(2,1)S(1)}, bf16[256,128]{1,0:T(8,128)(2,1)S(1)}, u32[]{:S(2)}, u32[]{:S(2)}) collective-permute-start(bf16[256,128]{1,0:T(8,128)(2,1)S(1)} %get-tuple-element.23.refs_2_), channel_id=1, source_target_pairs={{0,8},{2,10},{4,12},{6,14},{8,0},{10,2},{12,4},{14,6},{16,24},{18,... | collective-permute-start | bytes 196616 | tf_op jit(solution)/shard_map/ppermute | solution.py:33
  28.1 7.2 %collective-permute-start.7 = (bf16[256,128]{1,0:T(8,128)(2,1)S(1)}, bf16[256,128]{1,0:T(8,128)(2,1)S(1)}, u32[]{:S(2)}, u32[]{:S(2)}) collective-permute-start(bf16[256,128]{1,0:T(8,128)(2,1)S(1)} %get-tuple-element.23.refs_2_), channel_id=1, source_target_pairs={{0,16},{2,18},{4,20},{6,22},{8,24},{10,26},{12,28},{14,30},{16,0},... | collective-permute-start | bytes 196616 | tf_op jit(solution)/shard_map/ppermute | solution.py:33
  29.0 7.0 %collective-permute-start.8 = (bf16[256,128]{1,0:T(8,128)(2,1)S(1)}, bf16[256,128]{1,0:T(8,128)(2,1)S(1)}, u32[]{:S(2)}, u32[]{:S(2)}) collective-permute-start(bf16[256,128]{1,0:T(8,128)(2,1)S(1)} %get-tuple-element.23.refs_2_), channel_id=1, source_target_pairs={{0,24},{2,26},{4,28},{6,30},{8,16},{10,18},{12,20},{14,22},{16,8},... | collective-permute-start | bytes 196616 | tf_op jit(solution)/shard_map/ppermute | solution.py:33
  31.9 5.6 %collective-permute-start.9 = (bf16[256,128]{1,0:T(8,128)(2,1)S(1)}, bf16[256,128]{1,0:T(8,128)(2,1)S(1)}, u32[]{:S(2)}, u32[]{:S(2)}) collective-permute-start(bf16[256,128]{1,0:T(8,128)(2,1)S(1)} %get-tuple-element.23.refs_2_), channel_id=1, source_target_pairs={{0,2},{2,0},{4,6},{6,4},{8,10},{10,8},{12,14},{14,12},{16,18},{18,... | collective-permute-start | bytes 196616 | tf_op jit(solution)/shard_map/ppermute | solution.py:33
  32.7 6.2 %collective-permute-start.10 = (bf16[256,128]{1,0:T(8,128)(2,1)S(1)}, bf16[256,128]{1,0:T(8,128)(2,1)S(1)}, u32[]{:S(2)}, u32[]{:S(2)}) collective-permute-start(bf16[256,128]{1,0:T(8,128)(2,1)S(1)} %get-tuple-element.23.refs_2_), channel_id=1, source_target_pairs={{0,4},{2,6},{4,0},{6,2},{8,12},{10,14},{12,8},{14,10},{16,20},{18,... | collective-permute-start | bytes 196616 | tf_op jit(solution)/shard_map/ppermute | solution.py:33
  35.3 5.9 %collective-permute-start.11 = (bf16[256,128]{1,0:T(8,128)(2,1)S(1)}, bf16[256,128]{1,0:T(8,128)(2,1)S(1)}, u32[]{:S(2)}, u32[]{:S(2)}) collective-permute-start(bf16[256,128]{1,0:T(8,128)(2,1)S(1)} %get-tuple-element.23.refs_2_), channel_id=1, source_target_pairs={{0,6},{2,4},{4,2},{6,0},{8,14},{10,12},{12,10},{14,8},{16,22},{18,... | collective-permute-start | bytes 196616 | tf_op jit(solution)/shard_map/ppermute | solution.py:33
  36.0 10.8 %collective-permute-start.14 = (bf16[3,256,128]{2,1,0:T(8,128)(2,1)S(1)}, bf16[3,256,128]{2,1,0:T(8,128)(2,1)S(1)}, u32[]{:S(2)}, u32[]{:S(2)}) collective-permute-start(bf16[3,256,128]{2,1,0:T(8,128)(2,1)S(1)} %shard_map.138.refs_3_), channel_id=1, source_target_pairs={{0,2},{2,0},{4,6},{6,4},{8,10},{10,8},{12,14},{14,12},{16,18},{18,... | collective-permute-start | bytes 589832 | tf_op jit(solution)/shard_map/ppermute | solution.py:33
  37.5 10.0 %collective-permute-start.13 = (bf16[3,256,128]{2,1,0:T(8,128)(2,1)S(1)}, bf16[3,256,128]{2,1,0:T(8,128)(2,1)S(1)}, u32[]{:S(2)}, u32[]{:S(2)}) collective-permute-start(bf16[3,256,128]{2,1,0:T(8,128)(2,1)S(1)} %shard_map.138.refs_3_), channel_id=1, source_target_pairs={{0,4},{2,6},{4,0},{6,2},{8,12},{10,14},{12,8},{14,10},{16,20},{18,... | collective-permute-start | bytes 589832 | tf_op jit(solution)/shard_map/ppermute | solution.py:33
  41.2 7.0 %collective-permute-start.12 = (bf16[3,256,128]{2,1,0:T(8,128)(2,1)S(1)}, bf16[3,256,128]{2,1,0:T(8,128)(2,1)S(1)}, u32[]{:S(2)}, u32[]{:S(2)}) collective-permute-start(bf16[3,256,128]{2,1,0:T(8,128)(2,1)S(1)} %shard_map.138.refs_3_), channel_id=1, source_target_pairs={{0,6},{2,4},{4,2},{6,0},{8,14},{10,12},{12,10},{14,8},{16,22},{18,... | collective-permute-start | bytes 589832 | tf_op jit(solution)/shard_map/ppermute | solution.py:33
  42.6 3.4 %copy-start.1 = (bf16[512,4096]{1,0:T(8,128)(2,1)S(1)}, bf16[512,4096]{1,0:T(8,128)(2,1)}, u32[]{:S(2)}) copy-start(bf16[512,4096]{1,0:T(8,128)(2,1)} %copy-done) | copy-start | bytes 12582916

commit v8 on v7

--- a/solution.py
+++ b/solution.py
@@ -362,9 +362,9 @@
         rest = join(far)
         groups = [[weight, rest]]
         groups += [[own, swap(rest, "dp", b)] for own, b in zip(near[:-1], plane[1:-1])]
-        final, near = lax.optimization_barrier((rest, near))
+        final, near, others = lax.optimization_barrier((rest, near, load(feats[1:])))
         groups.append([near[-1], swap(final, "dp", plane[-1])])
-        feats = [held, *load(feats[1:])]
+        feats = [held, *others]
         keys = None
         for j, b in enumerate(plane):
             masks = tuple(b ^ m for m in line)

time: 49.9 us -> 49.4 us (0.990)
  local copies, waits for them, and re-layouts: 1.12 us -> 0.05 us
  waiting for transfers between devices: 10.4 us -> 11.1 us
    unnamed x18, local copies, waits for them, and re-layouts: 1.12 us -> 0.05 us
    ppermute x9, waiting for transfers between devices: 4.57 us -> 5.2 us  [swap(): lax.ppermute(x, axis, [(i, i ^ mask) for i in range(lax.axis_size(axis))])]
  transfers between devices with their start and end apart: 16 -> 16, of which waited for: 4 -> 6; matrix products, arithmetic and copies ran while one was open for 0% -> 0% of each run, Pallas kernels for 29% -> 29%
where the time goes in v8:
time: 49.4 us; the launch traced here: 49.2 us
  starting transfers between devices  20.1 us (41%)
  Pallas kernels  16.4 us (33%)
  waiting for transfers between devices  11.1 us (22%)
  between operations  1.51 us (3%)
    ppermute x9, starting transfers between devices, swap(): lax.ppermute(x, axis, [(i, i ^ mask) for i in range(lax.axis_size(axis))])  9.95 us
    all_to_all x1, starting transfers between devices, shards(): lax.all_to_all(outgoing.reshape(owners, SLOTS, width), 'dp', split_axis=0...  8.02 us
    all_to_all x1, waiting for transfers between devices, shards(): lax.all_to_all(outgoing.reshape(owners, SLOTS, width), 'dp', split_axis=0...  5.81 us
    ppermute x9, waiting for transfers between devices, swap(): lax.ppermute(x, axis, [(i, i ^ mask) for i in range(lax.axis_size(axis))])  5.2 us
    pallas_call x2, Pallas kernels, load(): pl.pallas_call(functools.partial(load_kernel, pieces), in_specs=[ANY] * l...  4.43 us
    pallas_call x4, Pallas kernels, project(): pl.pallas_call(functools.partial(project_kernel, masks, last, len(feats))...  3.53 us
    pallas_call x5, Pallas kernels, part_sum(): pl.pallas_call(functools.partial(part_kernel, first), in_specs=[SMEM, VME...  3.49 us
    ppermute x6, starting transfers between devices, shift(): return lax.ppermute(x, axis, [(i, (i + step) % n) for i in range(n)])  2.17 us
  transfers between devices with their start and end apart: 16, of which 6 were waited for; matrix products, arithmetic and copies ran while one was open for 0% of the time, Pallas kernels for 29%

profile of v8, /device:TPU:0, one launch (start us, length us, event | category | flops | bytes accessed | tf_op | source)
XLA Modules:
  0.0 49.2 jit_solution(11157610554043368093)
XLA Ops:
  0.6 0.5 %collective-permute-start = (bf16[1024,128]{1,0:T(8,128)(2,1)}, bf16[1024,128]{1,0:T(8,128)(2,1)S(1)}, u32[]{:S(2)}, u32[]{:S(2)}) collective-permute-start(bf16[1024,128]{1,0:T(8,128)(2,1)} %g_ref), channel_id=1, source_target_pairs={{0,1},{1,0},{2,3},{3,2},{4,5},{5,4},{6,7},{7,6},{8,9},{9,8},{10,11... | collective-permute-start | bytes 786440 | tf_op jit(solution)/shard_map/ppermute | solution.py:29
  1.1 2.2 %shard_map.128.f_ref.refs_0_ = bf16[512,4096]{1,0:T(8,128)(2,1)S(1)} custom-call(bf16[512,4096]{1,0:T(8,128)(2,1)} %refs_0_.1), custom_call_target="tpu_custom_call" | custom-call | bytes 8388608 | tf_op jit(solution)/shard_map/pallas_call | solution.py:72
  3.4 0.5 %shard_map.131 = f32[1024,128]{1,0:T(8,128)S(1)} custom-call(s32[1]{0:T(128)} %bitcast.1.core, bf16[512,4096]{1,0:T(8,128)(2,1)S(1)} %shard_map.128.f_ref.refs_0_, bf16[1024,128]{1,0:T(8,128)(2,1)S(1)} %collective-permute-done.g_ref), custom_call_target="tpu_custom_call" | custom-call | flops 134217728 | bytes 1572864 | tf_op jit(solution)/shard_map/pallas_call | solution.py:104
  4.0 0.5 %shard_map.132 = f32[1024,128]{1,0:T(8,128)S(1)} custom-call(s32[1]{0:T(128)} %bitcast.1.core, bf16[512,4096]{1,0:T(8,128)(2,1)S(1)} %shard_map.128.f_ref.refs_0_, bf16[1024,128]{1,0:T(8,128)(2,1)S(1)} %collective-permute-done.g_ref), custom_call_target="tpu_custom_call" | custom-call | flops 134217728 | bytes 1572864 | tf_op jit(solution)/shard_map/pallas_call | solution.py:104
  4.6 0.5 %collective-permute-start.2 = (f32[1024,128]{1,0:T(8,128)S(1)}, f32[1024,128]{1,0:T(8,128)S(1)}, u32[]{:S(2)}, u32[]{:S(2)}) collective-permute-start(f32[1024,128]{1,0:T(8,128)S(1)} %shard_map.132), channel_id=1, source_target_pairs={{0,1},{1,0},{2,3},{3,2},{4,5},{5,4},{6,7},{7,6},{8,9},{9,8},{10,11... | collective-permute-start | bytes 1572872 | tf_op jit(solution)/shard_map/ppermute | solution.py:29
  5.1 0.5 %shard_map.133 = f32[1024,128]{1,0:T(8,128)S(1)} custom-call(s32[1]{0:T(128)} %bitcast.1.core, bf16[512,4096]{1,0:T(8,128)(2,1)S(1)} %shard_map.128.f_ref.refs_0_, bf16[1024,128]{1,0:T(8,128)(2,1)S(1)} %collective-permute-done.g_ref), custom_call_target="tpu_custom_call" | custom-call | flops 134217728 | bytes 1572864 | tf_op jit(solution)/shard_map/pallas_call | solution.py:104
  5.8 0.5 %shard_map.129 = f32[1024,128]{1,0:T(8,128)S(1)} custom-call(s32[1]{0:T(128)} %bitcast.1.core, bf16[512,4096]{1,0:T(8,128)(2,1)S(1)} %shard_map.128.f_ref.refs_0_, bf16[1024,128]{1,0:T(8,128)(2,1)S(1)} %collective-permute-done.g_ref), custom_call_target="tpu_custom_call" | custom-call | flops 134217728 | bytes 1572864 | tf_op jit(solution)/shard_map/pallas_call | solution.py:104
  6.3 0.5 %collective-permute-start.4 = (f32[1024,128]{1,0:T(8,128)S(1)}, f32[1024,128]{1,0:T(8,128)S(1)}, u32[]{:S(2)}, u32[]{:S(2)}) collective-permute-start(f32[1024,128]{1,0:T(8,128)S(1)} %shard_map.129), channel_id=1, source_target_pairs={{0,1},{1,0},{2,3},{3,2},{4,5},{5,4},{6,7},{7,6},{8,9},{9,8},{10,11... | collective-permute-start | bytes 1572872 | tf_op jit(solution)/shard_map/ppermute | solution.py:29
  6.8 1.4 %shard_map.130.own_ref = f32[4096,128]{1,0:T(8,128)S(1)} custom-call(s32[1]{0:T(128)} %bitcast.1.core, bf16[512,4096]{1,0:T(8,128)(2,1)S(1)} %shard_map.128.f_ref.refs_0_, bf16[1024,128]{1,0:T(8,128)(2,1)S(1)} %copy-done.6, bf16[4096,128]{1,0:T(8,128)(2,1)S(1)} %bitcast.6), custom_call_target="tpu_custom_call" | custom-call | flops 536870912 | bytes 6291456 | tf_op jit(solution)/shard_map/pallas_call | solution.py:104
  8.8 2.1 %shard_map.134 = (f32[4096,128]{1,0:T(8,128)S(1)}, f32[128,128]{1,0:T(8,128)}) custom-call(s32[32]{0:T(128)S(1)} %bitcast.7, s32[17]{0:T(128)S(1)} %copy-done.7, f32[4096,128]{1,0:T(8,128)S(1)} %shard_map.130.own_ref, f32[1024,128]{1,0:T(8,128)S(1)} %collective-permute-done.1.refs_0_, f32[1024,128]{1,0:T(8,128)S(1)} %collective-permute-done.2.refs_1_, ...), custom_call_target="tpu_custom_call" | custom-call | flops 4194304 | bytes 6291456 | tf_op jit(solution)/shard_map/pallas_call | solution.py:157
  10.8 8.0 %all-to-all-start = ((f32[16,8,128]{2,1,0:T(8,128)}), f32[16,8,128]{2,1,0:T(8,128)S(1)}, u32[]{:S(2)}, u32[]{:S(2)}) async-start(f32[16,8,128]{2,1,0:T(8,128)} %bitcast.4), calls=%async_computation | async-start | bytes 131072 | tf_op jit(solution)/shard_map/all_to_all | solution.py:352
  19.5 1.1 %shard_map.135 = bf16[4096,128]{1,0:T(8,128)(2,1)} custom-call(f32[4096,128]{1,0:T(8,128)S(1)} %get-tuple-element.21.x_ref), custom_call_target="tpu_custom_call" | custom-call | flops 524288 | bytes 3145728 | tf_op jit(solution)/shard_map/pallas_call | solution.py:253
  20.6 5.8 %all-to-all-done.arr_ref = f32[16,8,128]{2,1,0:T(8,128)S(1)} async-done(((f32[16,8,128]{2,1,0:T(8,128)}), f32[16,8,128]{2,1,0:T(8,128)S(1)}, u32[]{:S(2)}, u32[]{:S(2)}) %all-to-all-start) | async-done | bytes 65568 | tf_op jit(solution)/shard_map/all_to_all | solution.py:352
  26.4 1.0 %shard_map.136 = (f32[256,128]{1,0:T(8,128)S(1)}, bf16[256,128]{1,0:T(8,128)(2,1)S(1)}) custom-call(s32[1]{0:T(128)} %bitcast.me, s32[1]{0:T(128)S(6)} %copy.14.least, s32[17]{0:T(128)S(1)} %copy-done.7, f32[16,8,128]{2,1,0:T(8,128)S(1)} %all-to-all-done.arr_ref, f32[256,128]{1,0:T(8,128)S(1)} %copy-done.3, f32[256,128]{1,0:T(8,128)S(1)} %copy-done.4, ...), custom_call_target="tpu_custom_call" | custom-call | flops 50331648 | bytes 983040 | tf_op jit(solution)/shard_map/pallas_call | solution.py:220
  27.4 0.7 %collective-permute-start.5 = (bf16[256,128]{1,0:T(8,128)(2,1)S(1)}, bf16[256,128]{1,0:T(8,128)(2,1)S(1)}, u32[]{:S(2)}, u32[]{:S(2)}) collective-permute-start(bf16[256,128]{1,0:T(8,128)(2,1)S(1)} %get-tuple-element.23.refs_2_), channel_id=1, source_target_pairs={{0,8},{2,10},{4,12},{6,14},{8,0},{10,2},{12,4},{14,6},{16,24},{18,... | collective-permute-start | bytes 196616 | tf_op jit(solution)/shard_map/ppermute | solution.py:33
  28.1 0.8 %collective-permute-start.6 = (bf16[256,128]{1,0:T(8,128)(2,1)S(1)}, bf16[256,128]{1,0:T(8,128)(2,1)S(1)}, u32[]{:S(2)}, u32[]{:S(2)}) collective-permute-start(bf16[256,128]{1,0:T(8,128)(2,1)S(1)} %get-tuple-element.23.refs_2_), channel_id=1, source_target_pairs={{0,16},{2,18},{4,20},{6,22},{8,24},{10,26},{12,28},{14,30},{16,0},... | collective-permute-start | bytes 196616 | tf_op jit(solution)/shard_map/ppermute | solution.py:33
  29.0 2.9 %collective-permute-start.7 = (bf16[256,128]{1,0:T(8,128)(2,1)S(1)}, bf16[256,128]{1,0:T(8,128)(2,1)S(1)}, u32[]{:S(2)}, u32[]{:S(2)}) collective-permute-start(bf16[256,128]{1,0:T(8,128)(2,1)S(1)} %get-tuple-element.23.refs_2_), channel_id=1, source_target_pairs={{0,24},{2,26},{4,28},{6,30},{8,16},{10,18},{12,20},{14,22},{16,8},... | collective-permute-start | bytes 196616 | tf_op jit(solution)/shard_map/ppermute | solution.py:33
  31.9 0.8 %collective-permute-start.8 = (bf16[256,128]{1,0:T(8,128)(2,1)S(1)}, bf16[256,128]{1,0:T(8,128)(2,1)S(1)}, u32[]{:S(2)}, u32[]{:S(2)}) collective-permute-start(bf16[256,128]{1,0:T(8,128)(2,1)S(1)} %get-tuple-element.23.refs_2_), channel_id=1, source_target_pairs={{0,2},{2,0},{4,6},{6,4},{8,10},{10,8},{12,14},{14,12},{16,18},{18,... | collective-permute-start | bytes 196616 | tf_op jit(solution)/shard_map/ppermute | solution.py:33
  32.7 0.4 collective-permute-start.9
  33.1 2.2 %collective-permute-done.6.refs_1_ = bf16[256,128]{1,0:T(8,128)(2,1)S(1)} collective-permute-done((bf16[256,128]{1,0:T(8,128)(2,1)S(1)}, bf16[256,128]{1,0:T(8,128)(2,1)S(1)}, u32[]{:S(2)}, u32[]{:S(2)}) %collective-permute-start.6) | collective-permute-done | bytes 65568 | tf_op jit(solution)/shard_map/ppermute | solution.py:33
  35.3 0.7 %collective-permute-start.10 = (bf16[256,128]{1,0:T(8,128)(2,1)S(1)}, bf16[256,128]{1,0:T(8,128)(2,1)S(1)}, u32[]{:S(2)}, u32[]{:S(2)}) collective-permute-start(bf16[256,128]{1,0:T(8,128)(2,1)S(1)} %get-tuple-element.23.refs_2_), channel_id=1, source_target_pairs={{0,6},{2,4},{4,2},{6,0},{8,14},{10,12},{12,10},{14,8},{16,22},{18,... | collective-permute-start | bytes 196616 | tf_op jit(solution)/shard_map/ppermute | solution.py:33
  36.0 1.5 %collective-permute-start.14 = (bf16[3,256,128]{2,1,0:T(8,128)(2,1)S(1)}, bf16[3,256,128]{2,1,0:T(8,128)(2,1)S(1)}, u32[]{:S(2)}, u32[]{:S(2)}) collective-permute-start(bf16[3,256,128]{2,1,0:T(8,128)(2,1)S(1)} %shard_map.137.refs_3_), channel_id=1, source_target_pairs={{0,2},{2,0},{4,6},{6,4},{8,10},{10,8},{12,14},{14,12},{16,18},{18,... | collective-permute-start | bytes 589832 | tf_op jit(solution)/shard_map/ppermute | solution.py:33
  37.5 1.4 %collective-permute-start.13 = (bf16[3,256,128]{2,1,0:T(8,128)(2,1)S(1)}, bf16[3,256,128]{2,1,0:T(8,128)(2,1)S(1)}, u32[]{:S(2)}, u32[]{:S(2)}) collective-permute-start(bf16[3,256,128]{2,1,0:T(8,128)(2,1)S(1)} %shard_map.137.refs_3_), channel_id=1, source_target_pairs={{0,4},{2,6},{4,0},{6,2},{8,12},{10,14},{12,8},{14,10},{16,20},{18,... | collective-permute-start | bytes 589832 | tf_op jit(solution)/shard_map/ppermute | solution.py:33
  38.9 2.2 %shard_map.138.refs_1_ = bf16[512,4096]{1,0:T(8,128)(2,1)S(1)} custom-call(bf16[512,4096]{1,0:T(8,128)(2,1)} %collective-permute-done.11.refs_0_), custom_call_target="tpu_custom_call" | custom-call | bytes 8388608 | tf_op jit(solution)/shard_map/pallas_call | solution.py:72
  41.1 0.7 %collective-permute-start.12 = (bf16[3,256,128]{2,1,0:T(8,128)(2,1)S(1)}, bf16[3,256,128]{2,1,0:T(8,128)(2,1)S(1)}, u32[]{:S(2)}, u32[]{:S(2)}) collective-permute-start(bf16[3,256,128]{2,1,0:T(8,128)(2,1)S(1)} %shard_map.137.refs_3_), channel_id=1, source_target_pairs={{0,6},{2,4},{4,2},{6,0},{8,14},{10,12},{12,10},{14,8},{16,22},{18,... | collective-permute-start | bytes 589832 | tf_op jit(solution)/shard_map/ppermute | solution.py:33
  41.9 0.8 %shard_map.143 = (f32[256,128]{1,0:T(8,128)}, f32[256,128]{1,0:T(8,128)}, f32[256,128]{1,0:T(8,128)}) custom-call(f32[256,128]{1,0:T(8,128)S(1)} %get-tuple-element.29.g_ref, f32[256,128]{1,0:T(8,128)S(1)} %copy-done.3, f32[256,128]{1,0:T(8,128)S(1)} %copy-done.4, f32[256,128]{1,0:T(8,128)S(1)} %copy-done.5), custom_call_target="tpu_custom_call" | custom-call | flops 655360 | bytes 917504 | tf_op jit(solution)/shard_map/pallas_call | solution.py:237
  42.7 0.7 %shard_map.139.refs_4_ = f32[1024,128]{1,0:T(8,128)S(1)} custom-call(s32[1]{0:T(128)} %bitcast.me, s32[1]{0:T(128)} %bitcast.1.core, bf16[512,4096]{1,0:T(8,128)(2,1)S(1)} %copy-done.1, bf16[512,4096]{1,0:T(8,128)(2,1)S(1)} %shard_map.138.refs_1_, bf16[256,128]{1,0:T(8,128)(2,1)S(1)} %get-tuple-element.23.refs_2_, bf16[3,256,128]{2,1,0:T(8,128)(2,1)S(1)} %shard_map.137.refs_3_), custom_call_target="tpu_custom_call" | custom-call | flops 268435456 | bytes 3145728 | tf_op jit(solution)/shard_map/pallas_call | solution.py:309
  43.4 0.5 %collective-permute-done.14.refs_3_ = bf16[3,256,128]{2,1,0:T(8,128)(2,1)S(1)} collective-permute-done((bf16[3,256,128]{2,1,0:T(8,128)(2,1)S(1)}, bf16[3,256,128]{2,1,0:T(8,128)(2,1)S(1)}, u32[]{:S(2)}, u32[]{:S(2)}) %collective-permute-start.14) | collective-permute-done | bytes 196640 | tf_op jit(solution)/shard_map/ppermute | solution.py:33
  43.9 0.7 %shard_map.140.refs_4_ = f32[1024,128]{1,0:T(8,128)S(1)} custom-call(s32[1]{0:T(128)} %bitcast.me, s32[1]{0:T(128)} %bitcast.1.core, bf16[512,4096]{1,0:T(8,128)(2,1)S(1)} %copy-done.1, bf16[512,4096]{1,0:T(8,128)(2,1)S(1)} %shard_map.138.refs_1_, bf16[256,128]{1,0:T(8,128)(2,1)S(1)} %collective-permute-done.8.refs_2_, ...), custom_call_target="tpu_custom_call" | custom-call | flops 268435456 | bytes 3145728 | tf_op jit(solution)/shard_map/pallas_call | solution.py:309
  44.7 0.7 %shard_map.141.refs_4_ = f32[1024,128]{1,0:T(8,128)S(1)} custom-call(s32[1]{0:T(128)} %bitcast.me, s32[1]{0:T(128)} %bitcast.1.core, bf16[512,4096]{1,0:T(8,128)(2,1)S(1)} %copy-done.1, bf16[512,4096]{1,0:T(8,128)(2,1)S(1)} %shard_map.138.refs_1_, bf16[256,128]{1,0:T(8,128)(2,1)S(1)} %collective-permute-done.9.refs_2_, ...), custom_call_target="tpu_custom_call" | custom-call | flops 268435456 | bytes 3145728 | tf_op jit(solution)/shard_map/pallas_call | solution.py:309
  45.4 2.3 %collective-permute-done.12.refs_3_ = bf16[3,256,128]{2,1,0:T(8,128)(2,1)S(1)} collective-permute-done((bf16[3,256,128]{2,1,0:T(8,128)(2,1)S(1)}, bf16[3,256,128]{2,1,0:T(8,128)(2,1)S(1)}, u32[]{:S(2)}, u32[]{:S(2)}) %collective-permute-start.12) | collective-permute-done | bytes 196640 | tf_op jit(solution)/shard_map/ppermute | solution.py:33
  47.8 1.4 %shard_map.142 = bf16[1024,128]{1,0:T(8,128)(2,1)} custom-call(s32[1]{0:T(128)} %bitcast.me, s32[1]{0:T(128)} %bitcast.1.core, bf16[512,4096]{1,0:T(8,128)(2,1)S(1)} %copy-done.1, bf16[512,4096]{1,0:T(8,128)(2,1)S(1)} %shard_map.138.refs_1_, bf16[256,128]{1,0:T(8,128)(2,1)S(1)} %collective-permute-done.10.refs_2_, ...), custom_call_target="tpu_custom_call" | custom-call | flops 268435456 | bytes 3145728 | tf_op jit(solution)/shard_map/pallas_call | solution.py:309
  (34 shorter events, 0.9 us)
Async XLA Ops:
  0.6 2.8 %collective-permute-start = (bf16[1024,128]{1,0:T(8,128)(2,1)}, bf16[1024,128]{1,0:T(8,128)(2,1)S(1)}, u32[]{:S(2)}, u32[]{:S(2)}) collective-permute-start(bf16[1024,128]{1,0:T(8,128)(2,1)} %g_ref), channel_id=1, source_target_pairs={{0,1},{1,0},{2,3},{3,2},{4,5},{5,4},{6,7},{7,6},{8,9},{9,8},{10,11... | collective-permute-start | bytes 786440 | tf_op jit(solution)/shard_map/ppermute | solution.py:29
  3.4 3.5 %copy-start = (bf16[512,4096]{1,0:T(8,128)(2,1)}, bf16[512,4096]{1,0:T(8,128)(2,1)S(1)}, u32[]{:S(2)}) copy-start(bf16[512,4096]{1,0:T(8,128)(2,1)S(1)} %shard_map.128.f_ref.refs_0_) | copy-start | bytes 12582916
  3.9 4.4 %collective-permute-start.1 = (f32[1024,128]{1,0:T(8,128)S(1)}, f32[1024,128]{1,0:T(8,128)S(1)}, u32[]{:S(2)}, u32[]{:S(2)}) collective-permute-start(f32[1024,128]{1,0:T(8,128)S(1)} %shard_map.131), channel_id=1, source_target_pairs={{0,1},{1,0},{2,3},{3,2},{4,5},{5,4},{6,7},{7,6},{8,9},{9,8},{10,11... | collective-permute-start | bytes 1572872 | tf_op jit(solution)/shard_map/ppermute | solution.py:29
  4.6 2.3 %copy-start.2 = (bf16[1,4096,128]{2,1,0:T(8,128)(2,1)S(1)}, bf16[1,4096,128]{2,1,0:T(8,128)(2,1)}, u32[]{:S(2)}) copy-start(bf16[1,4096,128]{2,1,0:T(8,128)(2,1)} %param.11) | copy-start | bytes 3145732
  4.6 2.3 %copy-start.6 = (bf16[1024,128]{1,0:T(8,128)(2,1)S(1)}, bf16[1024,128]{1,0:T(8,128)(2,1)}, u32[]{:S(2)}) copy-start(bf16[1024,128]{1,0:T(8,128)(2,1)} %g_ref) | copy-start | bytes 786436
  4.6 3.7 %collective-permute-start.2 = (f32[1024,128]{1,0:T(8,128)S(1)}, f32[1024,128]{1,0:T(8,128)S(1)}, u32[]{:S(2)}, u32[]{:S(2)}) collective-permute-start(f32[1024,128]{1,0:T(8,128)S(1)} %shard_map.132), channel_id=1, source_target_pairs={{0,1},{1,0},{2,3},{3,2},{4,5},{5,4},{6,7},{7,6},{8,9},{9,8},{10,11... | collective-permute-start | bytes 1572872 | tf_op jit(solution)/shard_map/ppermute | solution.py:29
  5.6 2.7 %collective-permute-start.3 = (f32[1024,128]{1,0:T(8,128)S(1)}, f32[1024,128]{1,0:T(8,128)S(1)}, u32[]{:S(2)}, u32[]{:S(2)}) collective-permute-start(f32[1024,128]{1,0:T(8,128)S(1)} %shard_map.133), channel_id=1, source_target_pairs={{0,1},{1,0},{2,3},{3,2},{4,5},{5,4},{6,7},{7,6},{8,9},{9,8},{10,11... | collective-permute-start | bytes 1572872 | tf_op jit(solution)/shard_map/ppermute | solution.py:29
  6.3 2.5 %copy-start.7 = (s32[17]{0:T(128)S(1)}, s32[17]{0:T(128)}, u32[]{:S(2)}) copy-start(s32[17]{0:T(128)} %edges.3) | copy-start | bytes 208
  6.3 2.4 %copy-start.8 = (s32[1,1,32]{2,1,0:T(1,128)S(1)}, s32[1,1,32]{2,1,0:T(1,128)}, u32[]{:S(2)}) copy-start(s32[1,1,32]{2,1,0:T(1,128)} %param.12) | copy-start | bytes 388
  6.3 2.0 %collective-permute-start.4 = (f32[1024,128]{1,0:T(8,128)S(1)}, f32[1024,128]{1,0:T(8,128)S(1)}, u32[]{:S(2)}, u32[]{:S(2)}) collective-permute-start(f32[1024,128]{1,0:T(8,128)S(1)} %shard_map.129), channel_id=1, source_target_pairs={{0,1},{1,0},{2,3},{3,2},{4,5},{5,4},{6,7},{7,6},{8,9},{9,8},{10,11... | collective-permute-start | bytes 1572872 | tf_op jit(solution)/shard_map/ppermute | solution.py:29
  8.3 18.1 %copy-start.3 = (f32[256,128]{1,0:T(8,128)S(1)}, f32[256,128]{1,0:T(8,128)}, u32[]{:S(2)}) copy-start(f32[256,128]{1,0:T(8,128)} %m_ref.3) | copy-start | bytes 393220
  8.3 18.1 %copy-start.4 = (f32[256,128]{1,0:T(8,128)S(1)}, f32[256,128]{1,0:T(8,128)}, u32[]{:S(2)}) copy-start(f32[256,128]{1,0:T(8,128)} %v_ref.3) | copy-start | bytes 393220
  8.3 18.1 %copy-start.5 = (f32[256,128]{1,0:T(8,128)S(1)}, f32[256,128]{1,0:T(8,128)}, u32[]{:S(2)}) copy-start(f32[256,128]{1,0:T(8,128)} %w_ref.3) | copy-start | bytes 393220
  8.4 29.1 %collective-permute-start.11 = (bf16[512,4096]{1,0:T(8,128)(2,1)}, bf16[512,4096]{1,0:T(8,128)(2,1)}, u32[]{:S(2)}, u32[]{:S(2)}) collective-permute-start(bf16[512,4096]{1,0:T(8,128)(2,1)} %refs_0_.1), channel_id=1, source_target_pairs={{0,1},{1,0},{2,3},{3,2},{4,5},{5,4},{6,7},{7,6},{8,9},{9,8},{10,11... | collective-permute-start | bytes 12582920 | tf_op jit(solution)/shard_map/ppermute | solution.py:29
  10.8 15.6 %all-to-all-start = ((f32[16,8,128]{2,1,0:T(8,128)}), f32[16,8,128]{2,1,0:T(8,128)S(1)}, u32[]{:S(2)}, u32[]{:S(2)}) async-start(f32[16,8,128]{2,1,0:T(8,128)} %bitcast.4), calls=%async_computation | async-start | bytes 131072 | tf_op jit(solution)/shard_map/all_to_all | solution.py:352
  27.4 5.3 %collective-permute-start.5 = (bf16[256,128]{1,0:T(8,128)(2,1)S(1)}, bf16[256,128]{1,0:T(8,128)(2,1)S(1)}, u32[]{:S(2)}, u32[]{:S(2)}) collective-permute-start(bf16[256,128]{1,0:T(8,128)(2,1)S(1)} %get-tuple-element.23.refs_2_), channel_id=1, source_target_pairs={{0,8},{2,10},{4,12},{6,14},{8,0},{10,2},{12,4},{14,6},{16,24},{18,... | collective-permute-start | bytes 196616 | tf_op jit(solution)/shard_map/ppermute | solution.py:33
  28.1 7.2 %collective-permute-start.6 = (bf16[256,128]{1,0:T(8,128)(2,1)S(1)}, bf16[256,128]{1,0:T(8,128)(2,1)S(1)}, u32[]{:S(2)}, u32[]{:S(2)}) collective-permute-start(bf16[256,128]{1,0:T(8,128)(2,1)S(1)} %get-tuple-element.23.refs_2_), channel_id=1, source_target_pairs={{0,16},{2,18},{4,20},{6,22},{8,24},{10,26},{12,28},{14,30},{16,0},... | collective-permute-start | bytes 196616 | tf_op jit(solution)/shard_map/ppermute | solution.py:33
  29.0 7.0 %collective-permute-start.7 = (bf16[256,128]{1,0:T(8,128)(2,1)S(1)}, bf16[256,128]{1,0:T(8,128)(2,1)S(1)}, u32[]{:S(2)}, u32[]{:S(2)}) collective-permute-start(bf16[256,128]{1,0:T(8,128)(2,1)S(1)} %get-tuple-element.23.refs_2_), channel_id=1, source_target_pairs={{0,24},{2,26},{4,28},{6,30},{8,16},{10,18},{12,20},{14,22},{16,8},... | collective-permute-start | bytes 196616 | tf_op jit(solution)/shard_map/ppermute | solution.py:33
  31.9 9.2 %collective-permute-start.8 = (bf16[256,128]{1,0:T(8,128)(2,1)S(1)}, bf16[256,128]{1,0:T(8,128)(2,1)S(1)}, u32[]{:S(2)}, u32[]{:S(2)}) collective-permute-start(bf16[256,128]{1,0:T(8,128)(2,1)S(1)} %get-tuple-element.23.refs_2_), channel_id=1, source_target_pairs={{0,2},{2,0},{4,6},{6,4},{8,10},{10,8},{12,14},{14,12},{16,18},{18,... | collective-permute-start | bytes 196616 | tf_op jit(solution)/shard_map/ppermute | solution.py:33
  32.7 8.4 %collective-permute-start.9 = (bf16[256,128]{1,0:T(8,128)(2,1)S(1)}, bf16[256,128]{1,0:T(8,128)(2,1)S(1)}, u32[]{:S(2)}, u32[]{:S(2)}) collective-permute-start(bf16[256,128]{1,0:T(8,128)(2,1)S(1)} %get-tuple-element.23.refs_2_), channel_id=1, source_target_pairs={{0,4},{2,6},{4,0},{6,2},{8,12},{10,14},{12,8},{14,10},{16,20},{18,... | collective-permute-start | bytes 196616 | tf_op jit(solution)/shard_map/ppermute | solution.py:33
  35.3 5.8 %collective-permute-start.10 = (bf16[256,128]{1,0:T(8,128)(2,1)S(1)}, bf16[256,128]{1,0:T(8,128)(2,1)S(1)}, u32[]{:S(2)}, u32[]{:S(2)}) collective-permute-start(bf16[256,128]{1,0:T(8,128)(2,1)S(1)} %get-tuple-element.23.refs_2_), channel_id=1, source_target_pairs={{0,6},{2,4},{4,2},{6,0},{8,14},{10,12},{12,10},{14,8},{16,22},{18,... | collective-permute-start | bytes 196616 | tf_op jit(solution)/shard_map/ppermute | solution.py:33
  36.0 6.7 %copy-start.1 = (bf16[512,4096]{1,0:T(8,128)(2,1)S(1)}, bf16[512,4096]{1,0:T(8,128)(2,1)}, u32[]{:S(2)}) copy-start(bf16[512,4096]{1,0:T(8,128)(2,1)} %copy-done) | copy-start | bytes 12582916
  36.0 7.9 %collective-permute-start.14 = (bf16[3,256,128]{2,1,0:T(8,128)(2,1)S(1)}, bf16[3,256,128]{2,1,0:T(8,128)(2,1)S(1)}, u32[]{:S(2)}, u32[]{:S(2)}) collective-permute-start(bf16[3,256,128]{2,1,0:T(8,128)(2,1)S(1)} %shard_map.137.refs_3_), channel_id=1, source_target_pairs={{0,2},{2,0},{4,6},{6,4},{8,10},{10,8},{12,14},{14,12},{16,18},{18,... | collective-permute-start | bytes 589832 | tf_op jit(solution)/shard_map/ppermute | solution.py:33
  37.5 7.2 %collective-permute-start.13 = (bf16[3,256,128]{2,1,0:T(8,128)(2,1)S(1)}, bf16[3,256,128]{2,1,0:T(8,128)(2,1)S(1)}, u32[]{:S(2)}, u32[]{:S(2)}) collective-permute-start(bf16[3,256,128]{2,1,0:T(8,128)(2,1)S(1)} %shard_map.137.refs_3_), channel_id=1, source_target_pairs={{0,4},{2,6},{4,0},{6,2},{8,12},{10,14},{12,8},{14,10},{16,20},{18,... | collective-permute-start | bytes 589832 | tf_op jit(solution)/shard_map/ppermute | solution.py:33
  41.1 6.6 %collective-permute-start.12 = (bf16[3,256,128]{2,1,0:T(8,128)(2,1)S(1)}, bf16[3,256,128]{2,1,0:T(8,128)(2,1)S(1)}, u32[]{:S(2)}, u32[]{:S(2)}) collective-permute-start(bf16[3,256,128]{2,1,0:T(8,128)(2,1)S(1)} %shard_map.137.refs_3_), channel_id=1, source_target_pairs={{0,6},{2,4},{4,2},{6,0},{8,14},{10,12},{12,10},{14,8},{16,22},{18,... | collective-permute-start | bytes 589832 | tf_op jit(solution)/shard_map/ppermute | solution.py:33

commit v9 on v8

--- a/solution.py
+++ b/solution.py
@@ -354,6 +354,8 @@
     )
     arrived, error_out = lax.optimization_barrier((arrived, error_out))
     grad, weight = weigh(me1, threshold, bin_edges, arrived, moment, second, master)
+    states = state(grad, moment, second, master)
+
     bits = [1 << i for i in range(owners.bit_length() - 1)]
     if 1 << len(bits) == owners and len(bits) > 2 and region % LANES == 0:
         plane, line = spans(bits[:2]), spans(bits[2:])
@@ -362,7 +364,8 @@
         rest = join(far)
         groups = [[weight, rest]]
         groups += [[own, swap(rest, "dp", b)] for own, b in zip(near[:-1], plane[1:-1])]
-        final, near, others = lax.optimization_barrier((rest, near, load(feats[1:])))
+        final, near, states = lax.optimization_barrier((rest, near, states))
+        others = load(feats[1:])
         groups.append([near[-1], swap(final, "dp", plane[-1])])
         feats = [held, *others]
         keys = None
@@ -377,7 +380,7 @@
             lax.all_gather(weight, "dp", axis=0, tiled=True),
             preferred_element_type=jnp.float32,
         ).astype(jnp.bfloat16)
-    moment_new, second_new, master_new = state(grad, moment, second, master)
+    moment_new, second_new, master_new = states
     return (keys, error_out, moment_new, second_new, master_new)
 
 

time: 49.4 us -> 49.4 us (level)
  waiting for transfers between devices: 11.1 us -> 10.6 us
  transfers between devices with their start and end apart: 16 -> 16, of which waited for: 6 -> 5; matrix products, arithmetic and copies ran while one was open for 0% -> 0% of each run, Pallas kernels for 29% -> 30%
where the time goes in v9:
time: 49.4 us; the launch traced here: 49.2 us
  starting transfers between devices  20 us (40%)
  Pallas kernels  16.7 us (34%)
  waiting for transfers between devices  10.6 us (21%)
  between operations  1.5 us (3%)
    ppermute x9, starting transfers between devices, swap(): lax.ppermute(x, axis, [(i, i ^ mask) for i in range(lax.axis_size(axis))])  9.81 us
    all_to_all x1, starting transfers between devices, shards(): lax.all_to_all(outgoing.reshape(owners, SLOTS, width), 'dp', split_axis=0...  8.02 us
    all_to_all x1, waiting for transfers between devices, shards(): lax.all_to_all(outgoing.reshape(owners, SLOTS, width), 'dp', split_axis=0...  5.81 us
    ppermute x9, waiting for transfers between devices, swap(): lax.ppermute(x, axis, [(i, i ^ mask) for i in range(lax.axis_size(axis))])  4.75 us
    pallas_call x2, Pallas kernels, load(): pl.pallas_call(functools.partial(load_kernel, pieces), in_specs=[ANY] * l...  4.72 us
    pallas_call x4, Pallas kernels, project(): pl.pallas_call(functools.partial(project_kernel, masks, last, len(feats))...  3.54 us
    pallas_call x5, Pallas kernels, part_sum(): pl.pallas_call(functools.partial(part_kernel, first), in_specs=[SMEM, VME...  3.49 us
    ppermute x6, starting transfers between devices, shift(): return lax.ppermute(x, axis, [(i, (i + step) % n) for i in range(n)])  2.17 us
  transfers between devices with their start and end apart: 16, of which 5 were waited for; matrix products, arithmetic and copies ran while one was open for 0% of the time, Pallas kernels for 30%

profile of v9, /device:TPU:0, one launch (start us, length us, event | category | flops | bytes accessed | tf_op | source)
XLA Modules:
  0.0 49.2 jit_solution(2038839016026874181)
XLA Ops:
  0.6 0.5 %collective-permute-start = (bf16[1024,128]{1,0:T(8,128)(2,1)}, bf16[1024,128]{1,0:T(8,128)(2,1)S(1)}, u32[]{:S(2)}, u32[]{:S(2)}) collective-permute-start(bf16[1024,128]{1,0:T(8,128)(2,1)} %g_ref), channel_id=1, source_target_pairs={{0,1},{1,0},{2,3},{3,2},{4,5},{5,4},{6,7},{7,6},{8,9},{9,8},{10,11... | collective-permute-start | bytes 786440 | tf_op jit(solution)/shard_map/ppermute | solution.py:29
  1.1 2.2 %shard_map.128.f_ref.refs_0_ = bf16[512,4096]{1,0:T(8,128)(2,1)S(1)} custom-call(bf16[512,4096]{1,0:T(8,128)(2,1)} %refs_0_.1), custom_call_target="tpu_custom_call" | custom-call | bytes 8388608 | tf_op jit(solution)/shard_map/pallas_call | solution.py:72
  3.4 0.5 %shard_map.129 = f32[1024,128]{1,0:T(8,128)S(1)} custom-call(s32[1]{0:T(128)} %bitcast.1.core, bf16[512,4096]{1,0:T(8,128)(2,1)S(1)} %shard_map.128.f_ref.refs_0_, bf16[1024,128]{1,0:T(8,128)(2,1)S(1)} %collective-permute-done.g_ref), custom_call_target="tpu_custom_call" | custom-call | flops 134217728 | bytes 1572864 | tf_op jit(solution)/shard_map/pallas_call | solution.py:104
  4.0 0.5 %shard_map.131 = f32[1024,128]{1,0:T(8,128)S(1)} custom-call(s32[1]{0:T(128)} %bitcast.1.core, bf16[512,4096]{1,0:T(8,128)(2,1)S(1)} %shard_map.128.f_ref.refs_0_, bf16[1024,128]{1,0:T(8,128)(2,1)S(1)} %collective-permute-done.g_ref), custom_call_target="tpu_custom_call" | custom-call | flops 134217728 | bytes 1572864 | tf_op jit(solution)/shard_map/pallas_call | solution.py:104
  4.6 0.5 %collective-permute-start.1 = (f32[1024,128]{1,0:T(8,128)S(1)}, f32[1024,128]{1,0:T(8,128)S(1)}, u32[]{:S(2)}, u32[]{:S(2)}) collective-permute-start(f32[1024,128]{1,0:T(8,128)S(1)} %shard_map.131), channel_id=1, source_target_pairs={{0,1},{1,0},{2,3},{3,2},{4,5},{5,4},{6,7},{7,6},{8,9},{9,8},{10,11... | collective-permute-start | bytes 1572872 | tf_op jit(solution)/shard_map/ppermute | solution.py:29
  5.1 0.5 %shard_map.132 = f32[1024,128]{1,0:T(8,128)S(1)} custom-call(s32[1]{0:T(128)} %bitcast.1.core, bf16[512,4096]{1,0:T(8,128)(2,1)S(1)} %shard_map.128.f_ref.refs_0_, bf16[1024,128]{1,0:T(8,128)(2,1)S(1)} %collective-permute-done.g_ref), custom_call_target="tpu_custom_call" | custom-call | flops 134217728 | bytes 1572864 | tf_op jit(solution)/shard_map/pallas_call | solution.py:104
  5.8 0.5 %shard_map.133 = f32[1024,128]{1,0:T(8,128)S(1)} custom-call(s32[1]{0:T(128)} %bitcast.1.core, bf16[512,4096]{1,0:T(8,128)(2,1)S(1)} %shard_map.128.f_ref.refs_0_, bf16[1024,128]{1,0:T(8,128)(2,1)S(1)} %collective-permute-done.g_ref), custom_call_target="tpu_custom_call" | custom-call | flops 134217728 | bytes 1572864 | tf_op jit(solution)/shard_map/pallas_call | solution.py:104
  6.3 0.5 %collective-permute-start.3 = (f32[1024,128]{1,0:T(8,128)S(1)}, f32[1024,128]{1,0:T(8,128)S(1)}, u32[]{:S(2)}, u32[]{:S(2)}) collective-permute-start(f32[1024,128]{1,0:T(8,128)S(1)} %shard_map.133), channel_id=1, source_target_pairs={{0,1},{1,0},{2,3},{3,2},{4,5},{5,4},{6,7},{7,6},{8,9},{9,8},{10,11... | collective-permute-start | bytes 1572872 | tf_op jit(solution)/shard_map/ppermute | solution.py:29
  6.8 1.4 %shard_map.130.own_ref = f32[4096,128]{1,0:T(8,128)S(1)} custom-call(s32[1]{0:T(128)} %bitcast.1.core, bf16[512,4096]{1,0:T(8,128)(2,1)S(1)} %shard_map.128.f_ref.refs_0_, bf16[1024,128]{1,0:T(8,128)(2,1)S(1)} %copy-done.6, bf16[4096,128]{1,0:T(8,128)(2,1)S(1)} %bitcast.6), custom_call_target="tpu_custom_call" | custom-call | flops 536870912 | bytes 6291456 | tf_op jit(solution)/shard_map/pallas_call | solution.py:104
  8.8 2.1 %shard_map.135 = (f32[4096,128]{1,0:T(8,128)S(1)}, f32[128,128]{1,0:T(8,128)}) custom-call(s32[32]{0:T(128)S(1)} %bitcast.7, s32[17]{0:T(128)S(1)} %copy-done.7, f32[4096,128]{1,0:T(8,128)S(1)} %shard_map.130.own_ref, f32[1024,128]{1,0:T(8,128)S(1)} %collective-permute-done.1.refs_0_, f32[1024,128]{1,0:T(8,128)S(1)} %collective-permute-done.2.refs_1_, ...), custom_call_target="tpu_custom_call" | custom-call | flops 4194304 | bytes 6291456 | tf_op jit(solution)/shard_map/pallas_call | solution.py:157
  10.8 8.0 %all-to-all-start = ((f32[16,8,128]{2,1,0:T(8,128)}), f32[16,8,128]{2,1,0:T(8,128)S(1)}, u32[]{:S(2)}, u32[]{:S(2)}) async-start(f32[16,8,128]{2,1,0:T(8,128)} %bitcast.4), calls=%async_computation | async-start | bytes 131072 | tf_op jit(solution)/shard_map/all_to_all | solution.py:352
  19.5 1.1 %shard_map.136 = bf16[4096,128]{1,0:T(8,128)(2,1)} custom-call(f32[4096,128]{1,0:T(8,128)S(1)} %get-tuple-element.24.x_ref), custom_call_target="tpu_custom_call" | custom-call | flops 524288 | bytes 3145728 | tf_op jit(solution)/shard_map/pallas_call | solution.py:253
  20.6 5.8 %all-to-all-done.arr_ref = f32[16,8,128]{2,1,0:T(8,128)S(1)} async-done(((f32[16,8,128]{2,1,0:T(8,128)}), f32[16,8,128]{2,1,0:T(8,128)S(1)}, u32[]{:S(2)}, u32[]{:S(2)}) %all-to-all-start) | async-done | bytes 65568 | tf_op jit(solution)/shard_map/all_to_all | solution.py:352
  26.4 1.0 %shard_map.137 = (f32[256,128]{1,0:T(8,128)S(1)}, bf16[256,128]{1,0:T(8,128)(2,1)S(1)}) custom-call(s32[1]{0:T(128)} %bitcast.me, s32[1]{0:T(128)S(6)} %copy.14.least, s32[17]{0:T(128)S(1)} %copy-done.7, f32[16,8,128]{2,1,0:T(8,128)S(1)} %all-to-all-done.arr_ref, f32[256,128]{1,0:T(8,128)S(1)} %copy-done.3, f32[256,128]{1,0:T(8,128)S(1)} %copy-done.4, ...), custom_call_target="tpu_custom_call" | custom-call | flops 50331648 | bytes 983040 | tf_op jit(solution)/shard_map/pallas_call | solution.py:220
  27.4 0.7 %collective-permute-start.6 = (bf16[256,128]{1,0:T(8,128)(2,1)S(1)}, bf16[256,128]{1,0:T(8,128)(2,1)S(1)}, u32[]{:S(2)}, u32[]{:S(2)}) collective-permute-start(bf16[256,128]{1,0:T(8,128)(2,1)S(1)} %get-tuple-element.26.refs_2_), channel_id=1, source_target_pairs={{0,8},{2,10},{4,12},{6,14},{8,0},{10,2},{12,4},{14,6},{16,24},{18,... | collective-permute-start | bytes 196616 | tf_op jit(solution)/shard_map/ppermute | solution.py:33
  28.1 0.8 %collective-permute-start.7 = (bf16[256,128]{1,0:T(8,128)(2,1)S(1)}, bf16[256,128]{1,0:T(8,128)(2,1)S(1)}, u32[]{:S(2)}, u32[]{:S(2)}) collective-permute-start(bf16[256,128]{1,0:T(8,128)(2,1)S(1)} %get-tuple-element.26.refs_2_), channel_id=1, source_target_pairs={{0,16},{2,18},{4,20},{6,22},{8,24},{10,26},{12,28},{14,30},{16,0},... | collective-permute-start | bytes 196616 | tf_op jit(solution)/shard_map/ppermute | solution.py:33
  29.0 2.9 %collective-permute-start.8 = (bf16[256,128]{1,0:T(8,128)(2,1)S(1)}, bf16[256,128]{1,0:T(8,128)(2,1)S(1)}, u32[]{:S(2)}, u32[]{:S(2)}) collective-permute-start(bf16[256,128]{1,0:T(8,128)(2,1)S(1)} %get-tuple-element.26.refs_2_), channel_id=1, source_target_pairs={{0,24},{2,26},{4,28},{6,30},{8,16},{10,18},{12,20},{14,22},{16,8},... | collective-permute-start | bytes 196616 | tf_op jit(solution)/shard_map/ppermute | solution.py:33
  31.9 0.8 %collective-permute-start.9 = (bf16[256,128]{1,0:T(8,128)(2,1)S(1)}, bf16[256,128]{1,0:T(8,128)(2,1)S(1)}, u32[]{:S(2)}, u32[]{:S(2)}) collective-permute-start(bf16[256,128]{1,0:T(8,128)(2,1)S(1)} %get-tuple-element.26.refs_2_), channel_id=1, source_target_pairs={{0,2},{2,0},{4,6},{6,4},{8,10},{10,8},{12,14},{14,12},{16,18},{18,... | collective-permute-start | bytes 196616 | tf_op jit(solution)/shard_map/ppermute | solution.py:33
  32.7 0.4 collective-permute-start.10
  33.1 2.2 %collective-permute-done.7.refs_1_ = bf16[256,128]{1,0:T(8,128)(2,1)S(1)} collective-permute-done((bf16[256,128]{1,0:T(8,128)(2,1)S(1)}, bf16[256,128]{1,0:T(8,128)(2,1)S(1)}, u32[]{:S(2)}, u32[]{:S(2)}) %collective-permute-start.7) | collective-permute-done | bytes 65568 | tf_op jit(solution)/shard_map/ppermute | solution.py:33
  35.3 0.7 %collective-permute-start.11 = (bf16[256,128]{1,0:T(8,128)(2,1)S(1)}, bf16[256,128]{1,0:T(8,128)(2,1)S(1)}, u32[]{:S(2)}, u32[]{:S(2)}) collective-permute-start(bf16[256,128]{1,0:T(8,128)(2,1)S(1)} %get-tuple-element.26.refs_2_), channel_id=1, source_target_pairs={{0,6},{2,4},{4,2},{6,0},{8,14},{10,12},{12,10},{14,8},{16,22},{18,... | collective-permute-start | bytes 196616 | tf_op jit(solution)/shard_map/ppermute | solution.py:33
  36.0 1.5 %collective-permute-start.14 = (bf16[3,256,128]{2,1,0:T(8,128)(2,1)S(1)}, bf16[3,256,128]{2,1,0:T(8,128)(2,1)S(1)}, u32[]{:S(2)}, u32[]{:S(2)}) collective-permute-start(bf16[3,256,128]{2,1,0:T(8,128)(2,1)S(1)} %shard_map.138.refs_3_), channel_id=1, source_target_pairs={{0,2},{2,0},{4,6},{6,4},{8,10},{10,8},{12,14},{14,12},{16,18},{18,... | collective-permute-start | bytes 589832 | tf_op jit(solution)/shard_map/ppermute | solution.py:33
  37.5 1.4 %collective-permute-start.13 = (bf16[3,256,128]{2,1,0:T(8,128)(2,1)S(1)}, bf16[3,256,128]{2,1,0:T(8,128)(2,1)S(1)}, u32[]{:S(2)}, u32[]{:S(2)}) collective-permute-start(bf16[3,256,128]{2,1,0:T(8,128)(2,1)S(1)} %shard_map.138.refs_3_), channel_id=1, source_target_pairs={{0,4},{2,6},{4,0},{6,2},{8,12},{10,14},{12,8},{14,10},{16,20},{18,... | collective-permute-start | bytes 589832 | tf_op jit(solution)/shard_map/ppermute | solution.py:33
  38.9 0.8 %shard_map.139 = (f32[256,128]{1,0:T(8,128)}, f32[256,128]{1,0:T(8,128)}, f32[256,128]{1,0:T(8,128)}) custom-call(f32[256,128]{1,0:T(8,128)S(1)} %get-tuple-element.27.g_ref, f32[256,128]{1,0:T(8,128)S(1)} %copy-done.3, f32[256,128]{1,0:T(8,128)S(1)} %copy-done.4, f32[256,128]{1,0:T(8,128)S(1)} %copy-done.5), custom_call_target="tpu_custom_call" | custom-call | flops 655360 | bytes 917504 | tf_op jit(solution)/shard_map/pallas_call | solution.py:237
  39.7 1.5 %collective-permute-done.11.refs_2_ = bf16[256,128]{1,0:T(8,128)(2,1)S(1)} collective-permute-done((bf16[256,128]{1,0:T(8,128)(2,1)S(1)}, bf16[256,128]{1,0:T(8,128)(2,1)S(1)}, u32[]{:S(2)}, u32[]{:S(2)}) %collective-permute-start.11) | collective-permute-done | bytes 65568 | tf_op jit(solution)/shard_map/ppermute | solution.py:33
  41.2 0.6 %collective-permute-start.12 = (bf16[3,256,128]{2,1,0:T(8,128)(2,1)S(1)}, bf16[3,256,128]{2,1,0:T(8,128)(2,1)S(1)}, u32[]{:S(2)}, u32[]{:S(2)}) collective-permute-start(bf16[3,256,128]{2,1,0:T(8,128)(2,1)S(1)} %shard_map.138.refs_3_), channel_id=1, source_target_pairs={{0,6},{2,4},{4,2},{6,0},{8,14},{10,12},{12,10},{14,8},{16,22},{18,... | collective-permute-start | bytes 589832 | tf_op jit(solution)/shard_map/ppermute | solution.py:33
  41.8 2.5 %shard_map.134.refs_1_ = bf16[512,4096]{1,0:T(8,128)(2,1)S(1)} custom-call(bf16[512,4096]{1,0:T(8,128)(2,1)} %collective-permute-done.5.refs_0_), custom_call_target="tpu_custom_call" | custom-call | bytes 8388608 | tf_op jit(solution)/shard_map/pallas_call | solution.py:72
  44.7 0.7 %shard_map.140.refs_4_ = f32[1024,128]{1,0:T(8,128)S(1)} custom-call(s32[1]{0:T(128)} %bitcast.me, s32[1]{0:T(128)} %bitcast.1.core, bf16[512,4096]{1,0:T(8,128)(2,1)S(1)} %copy-done.1, bf16[512,4096]{1,0:T(8,128)(2,1)S(1)} %shard_map.134.refs_1_, bf16[256,128]{1,0:T(8,128)(2,1)S(1)} %get-tuple-element.26.refs_2_, bf16[3,256,128]{2,1,0:T(8,128)(2,1)S(1)} %shard_map.138.refs_3_), custom_call_target="tpu_custom_call" | custom-call | flops 268435456 | bytes 3145728 | tf_op jit(solution)/shard_map/pallas_call | solution.py:309
  45.4 0.7 %shard_map.141.refs_4_ = f32[1024,128]{1,0:T(8,128)S(1)} custom-call(s32[1]{0:T(128)} %bitcast.me, s32[1]{0:T(128)} %bitcast.1.core, bf16[512,4096]{1,0:T(8,128)(2,1)S(1)} %copy-done.1, bf16[512,4096]{1,0:T(8,128)(2,1)S(1)} %shard_map.134.refs_1_, bf16[256,128]{1,0:T(8,128)(2,1)S(1)} %collective-permute-done.9.refs_2_, ...), custom_call_target="tpu_custom_call" | custom-call | flops 268435456 | bytes 3145728 | tf_op jit(solution)/shard_map/pallas_call | solution.py:309
  46.1 0.7 %shard_map.142.refs_4_ = f32[1024,128]{1,0:T(8,128)S(1)} custom-call(s32[1]{0:T(128)} %bitcast.me, s32[1]{0:T(128)} %bitcast.1.core, bf16[512,4096]{1,0:T(8,128)(2,1)S(1)} %copy-done.1, bf16[512,4096]{1,0:T(8,128)(2,1)S(1)} %shard_map.134.refs_1_, bf16[256,128]{1,0:T(8,128)(2,1)S(1)} %collective-permute-done.10.refs_2_, ...), custom_call_target="tpu_custom_call" | custom-call | flops 268435456 | bytes 3145728 | tf_op jit(solution)/shard_map/pallas_call | solution.py:309
  46.8 1.0 %collective-permute-done.12.refs_3_ = bf16[3,256,128]{2,1,0:T(8,128)(2,1)S(1)} collective-permute-done((bf16[3,256,128]{2,1,0:T(8,128)(2,1)S(1)}, bf16[3,256,128]{2,1,0:T(8,128)(2,1)S(1)}, u32[]{:S(2)}, u32[]{:S(2)}) %collective-permute-start.12) | collective-permute-done | bytes 196640 | tf_op jit(solution)/shard_map/ppermute | solution.py:33
  47.8 1.4 %shard_map.143 = bf16[1024,128]{1,0:T(8,128)(2,1)} custom-call(s32[1]{0:T(128)} %bitcast.me, s32[1]{0:T(128)} %bitcast.1.core, bf16[512,4096]{1,0:T(8,128)(2,1)S(1)} %copy-done.1, bf16[512,4096]{1,0:T(8,128)(2,1)S(1)} %shard_map.134.refs_1_, bf16[256,128]{1,0:T(8,128)(2,1)S(1)} %collective-permute-done.11.refs_2_, ...), custom_call_target="tpu_custom_call" | custom-call | flops 268435456 | bytes 3145728 | tf_op jit(solution)/shard_map/pallas_call | solution.py:309
  (34 shorter events, 1.1 us)
Async XLA Ops:
  0.6 2.8 %collective-permute-start = (bf16[1024,128]{1,0:T(8,128)(2,1)}, bf16[1024,128]{1,0:T(8,128)(2,1)S(1)}, u32[]{:S(2)}, u32[]{:S(2)}) collective-permute-start(bf16[1024,128]{1,0:T(8,128)(2,1)} %g_ref), channel_id=1, source_target_pairs={{0,1},{1,0},{2,3},{3,2},{4,5},{5,4},{6,7},{7,6},{8,9},{9,8},{10,11... | collective-permute-start | bytes 786440 | tf_op jit(solution)/shard_map/ppermute | solution.py:29
  3.4 3.5 %copy-start = (bf16[512,4096]{1,0:T(8,128)(2,1)}, bf16[512,4096]{1,0:T(8,128)(2,1)S(1)}, u32[]{:S(2)}) copy-start(bf16[512,4096]{1,0:T(8,128)(2,1)S(1)} %shard_map.128.f_ref.refs_0_) | copy-start | bytes 12582916
  3.9 4.4 %collective-permute-start.4 = (f32[1024,128]{1,0:T(8,128)S(1)}, f32[1024,128]{1,0:T(8,128)S(1)}, u32[]{:S(2)}, u32[]{:S(2)}) collective-permute-start(f32[1024,128]{1,0:T(8,128)S(1)} %shard_map.129), channel_id=1, source_target_pairs={{0,1},{1,0},{2,3},{3,2},{4,5},{5,4},{6,7},{7,6},{8,9},{9,8},{10,11... | collective-permute-start | bytes 1572872 | tf_op jit(solution)/shard_map/ppermute | solution.py:29
  4.6 2.3 %copy-start.2 = (bf16[1,4096,128]{2,1,0:T(8,128)(2,1)S(1)}, bf16[1,4096,128]{2,1,0:T(8,128)(2,1)}, u32[]{:S(2)}) copy-start(bf16[1,4096,128]{2,1,0:T(8,128)(2,1)} %param.11) | copy-start | bytes 3145732
  4.6 2.3 %copy-start.6 = (bf16[1024,128]{1,0:T(8,128)(2,1)S(1)}, bf16[1024,128]{1,0:T(8,128)(2,1)}, u32[]{:S(2)}) copy-start(bf16[1024,128]{1,0:T(8,128)(2,1)} %g_ref) | copy-start | bytes 786436
  4.6 3.7 %collective-permute-start.1 = (f32[1024,128]{1,0:T(8,128)S(1)}, f32[1024,128]{1,0:T(8,128)S(1)}, u32[]{:S(2)}, u32[]{:S(2)}) collective-permute-start(f32[1024,128]{1,0:T(8,128)S(1)} %shard_map.131), channel_id=1, source_target_pairs={{0,1},{1,0},{2,3},{3,2},{4,5},{5,4},{6,7},{7,6},{8,9},{9,8},{10,11... | collective-permute-start | bytes 1572872 | tf_op jit(solution)/shard_map/ppermute | solution.py:29
  5.6 2.7 %collective-permute-start.2 = (f32[1024,128]{1,0:T(8,128)S(1)}, f32[1024,128]{1,0:T(8,128)S(1)}, u32[]{:S(2)}, u32[]{:S(2)}) collective-permute-start(f32[1024,128]{1,0:T(8,128)S(1)} %shard_map.132), channel_id=1, source_target_pairs={{0,1},{1,0},{2,3},{3,2},{4,5},{5,4},{6,7},{7,6},{8,9},{9,8},{10,11... | collective-permute-start | bytes 1572872 | tf_op jit(solution)/shard_map/ppermute | solution.py:29
  6.3 2.4 %copy-start.7 = (s32[17]{0:T(128)S(1)}, s32[17]{0:T(128)}, u32[]{:S(2)}) copy-start(s32[17]{0:T(128)} %edges.3) | copy-start | bytes 208
  6.3 2.4 %copy-start.8 = (s32[1,1,32]{2,1,0:T(1,128)S(1)}, s32[1,1,32]{2,1,0:T(1,128)}, u32[]{:S(2)}) copy-start(s32[1,1,32]{2,1,0:T(1,128)} %param.12) | copy-start | bytes 388
  6.3 2.0 %collective-permute-start.3 = (f32[1024,128]{1,0:T(8,128)S(1)}, f32[1024,128]{1,0:T(8,128)S(1)}, u32[]{:S(2)}, u32[]{:S(2)}) collective-permute-start(f32[1024,128]{1,0:T(8,128)S(1)} %shard_map.133), channel_id=1, source_target_pairs={{0,1},{1,0},{2,3},{3,2},{4,5},{5,4},{6,7},{7,6},{8,9},{9,8},{10,11... | collective-permute-start | bytes 1572872 | tf_op jit(solution)/shard_map/ppermute | solution.py:29
  8.3 18.1 %copy-start.3 = (f32[256,128]{1,0:T(8,128)S(1)}, f32[256,128]{1,0:T(8,128)}, u32[]{:S(2)}) copy-start(f32[256,128]{1,0:T(8,128)} %m_ref.3) | copy-start | bytes 393220
  8.3 18.1 %copy-start.4 = (f32[256,128]{1,0:T(8,128)S(1)}, f32[256,128]{1,0:T(8,128)}, u32[]{:S(2)}) copy-start(f32[256,128]{1,0:T(8,128)} %v_ref.3) | copy-start | bytes 393220
  8.3 18.1 %copy-start.5 = (f32[256,128]{1,0:T(8,128)S(1)}, f32[256,128]{1,0:T(8,128)}, u32[]{:S(2)}) copy-start(f32[256,128]{1,0:T(8,128)} %w_ref.3) | copy-start | bytes 393220
  8.4 33.5 %collective-permute-start.5 = (bf16[512,4096]{1,0:T(8,128)(2,1)}, bf16[512,4096]{1,0:T(8,128)(2,1)}, u32[]{:S(2)}, u32[]{:S(2)}) collective-permute-start(bf16[512,4096]{1,0:T(8,128)(2,1)} %refs_0_.1), channel_id=1, source_target_pairs={{0,1},{1,0},{2,3},{3,2},{4,5},{5,4},{6,7},{7,6},{8,9},{9,8},{10,11... | collective-permute-start | bytes 12582920 | tf_op jit(solution)/shard_map/ppermute | solution.py:29
  10.8 15.6 %all-to-all-start = ((f32[16,8,128]{2,1,0:T(8,128)}), f32[16,8,128]{2,1,0:T(8,128)S(1)}, u32[]{:S(2)}, u32[]{:S(2)}) async-start(f32[16,8,128]{2,1,0:T(8,128)} %bitcast.4), calls=%async_computation | async-start | bytes 131072 | tf_op jit(solution)/shard_map/all_to_all | solution.py:352
  27.4 5.3 %collective-permute-start.6 = (bf16[256,128]{1,0:T(8,128)(2,1)S(1)}, bf16[256,128]{1,0:T(8,128)(2,1)S(1)}, u32[]{:S(2)}, u32[]{:S(2)}) collective-permute-start(bf16[256,128]{1,0:T(8,128)(2,1)S(1)} %get-tuple-element.26.refs_2_), channel_id=1, source_target_pairs={{0,8},{2,10},{4,12},{6,14},{8,0},{10,2},{12,4},{14,6},{16,24},{18,... | collective-permute-start | bytes 196616 | tf_op jit(solution)/shard_map/ppermute | solution.py:33
  28.1 7.2 %collective-permute-start.7 = (bf16[256,128]{1,0:T(8,128)(2,1)S(1)}, bf16[256,128]{1,0:T(8,128)(2,1)S(1)}, u32[]{:S(2)}, u32[]{:S(2)}) collective-permute-start(bf16[256,128]{1,0:T(8,128)(2,1)S(1)} %get-tuple-element.26.refs_2_), channel_id=1, source_target_pairs={{0,16},{2,18},{4,20},{6,22},{8,24},{10,26},{12,28},{14,30},{16,0},... | collective-permute-start | bytes 196616 | tf_op jit(solution)/shard_map/ppermute | solution.py:33
  29.0 7.0 %collective-permute-start.8 = (bf16[256,128]{1,0:T(8,128)(2,1)S(1)}, bf16[256,128]{1,0:T(8,128)(2,1)S(1)}, u32[]{:S(2)}, u32[]{:S(2)}) collective-permute-start(bf16[256,128]{1,0:T(8,128)(2,1)S(1)} %get-tuple-element.26.refs_2_), channel_id=1, source_target_pairs={{0,24},{2,26},{4,28},{6,30},{8,16},{10,18},{12,20},{14,22},{16,8},... | collective-permute-start | bytes 196616 | tf_op jit(solution)/shard_map/ppermute | solution.py:33
  31.9 5.6 %collective-permute-start.9 = (bf16[256,128]{1,0:T(8,128)(2,1)S(1)}, bf16[256,128]{1,0:T(8,128)(2,1)S(1)}, u32[]{:S(2)}, u32[]{:S(2)}) collective-permute-start(bf16[256,128]{1,0:T(8,128)(2,1)S(1)} %get-tuple-element.26.refs_2_), channel_id=1, source_target_pairs={{0,2},{2,0},{4,6},{6,4},{8,10},{10,8},{12,14},{14,12},{16,18},{18,... | collective-permute-start | bytes 196616 | tf_op jit(solution)/shard_map/ppermute | solution.py:33
  32.7 7.0 %collective-permute-start.10 = (bf16[256,128]{1,0:T(8,128)(2,1)S(1)}, bf16[256,128]{1,0:T(8,128)(2,1)S(1)}, u32[]{:S(2)}, u32[]{:S(2)}) collective-permute-start(bf16[256,128]{1,0:T(8,128)(2,1)S(1)} %get-tuple-element.26.refs_2_), channel_id=1, source_target_pairs={{0,4},{2,6},{4,0},{6,2},{8,12},{10,14},{12,8},{14,10},{16,20},{18,... | collective-permute-start | bytes 196616 | tf_op jit(solution)/shard_map/ppermute | solution.py:33
  35.3 5.9 %collective-permute-start.11 = (bf16[256,128]{1,0:T(8,128)(2,1)S(1)}, bf16[256,128]{1,0:T(8,128)(2,1)S(1)}, u32[]{:S(2)}, u32[]{:S(2)}) collective-permute-start(bf16[256,128]{1,0:T(8,128)(2,1)S(1)} %get-tuple-element.26.refs_2_), channel_id=1, source_target_pairs={{0,6},{2,4},{4,2},{6,0},{8,14},{10,12},{12,10},{14,8},{16,22},{18,... | collective-permute-start | bytes 196616 | tf_op jit(solution)/shard_map/ppermute | solution.py:33
  36.0 9.4 %collective-permute-start.14 = (bf16[3,256,128]{2,1,0:T(8,128)(2,1)S(1)}, bf16[3,256,128]{2,1,0:T(8,128)(2,1)S(1)}, u32[]{:S(2)}, u32[]{:S(2)}) collective-permute-start(bf16[3,256,128]{2,1,0:T(8,128)(2,1)S(1)} %shard_map.138.refs_3_), channel_id=1, source_target_pairs={{0,2},{2,0},{4,6},{6,4},{8,10},{10,8},{12,14},{14,12},{16,18},{18,... | collective-permute-start | bytes 589832 | tf_op jit(solution)/shard_map/ppermute | solution.py:33
  37.5 8.6 %collective-permute-start.13 = (bf16[3,256,128]{2,1,0:T(8,128)(2,1)S(1)}, bf16[3,256,128]{2,1,0:T(8,128)(2,1)S(1)}, u32[]{:S(2)}, u32[]{:S(2)}) collective-permute-start(bf16[3,256,128]{2,1,0:T(8,128)(2,1)S(1)} %shard_map.138.refs_3_), channel_id=1, source_target_pairs={{0,4},{2,6},{4,0},{6,2},{8,12},{10,14},{12,8},{14,10},{16,20},{18,... | collective-permute-start | bytes 589832 | tf_op jit(solution)/shard_map/ppermute | solution.py:33
  41.2 3.4 %copy-start.1 = (bf16[512,4096]{1,0:T(8,128)(2,1)S(1)}, bf16[512,4096]{1,0:T(8,128)(2,1)}, u32[]{:S(2)}) copy-start(bf16[512,4096]{1,0:T(8,128)(2,1)} %copy-done) | copy-start | bytes 12582916
  41.2 6.6 %collective-permute-start.12 = (bf16[3,256,128]{2,1,0:T(8,128)(2,1)S(1)}, bf16[3,256,128]{2,1,0:T(8,128)(2,1)S(1)}, u32[]{:S(2)}, u32[]{:S(2)}) collective-permute-start(bf16[3,256,128]{2,1,0:T(8,128)(2,1)S(1)} %shard_map.138.refs_3_), channel_id=1, source_target_pairs={{0,6},{2,4},{4,2},{6,0},{8,14},{10,12},{12,10},{14,8},{16,22},{18,... | collective-permute-start | bytes 589832 | tf_op jit(solution)/shard_map/ppermute | solution.py:33

commit v10 on v8

--- a/solution.py
+++ b/solution.py
@@ -357,6 +357,7 @@
     bits = [1 << i for i in range(owners.bit_length() - 1)]
     if 1 << len(bits) == owners and len(bits) > 2 and region % LANES == 0:
         plane, line = spans(bits[:2]), spans(bits[2:])
+        plane = [plane[0], *plane[:0:-1]]
         far = [swap(weight, "dp", m) for m in line[1:]]
         near = [swap(weight, "dp", b) for b in plane[1:]]
         rest = join(far)

time: 49.4 us -> 48.5 us (0.982)
  waiting for transfers between devices: 11.1 us -> 9.04 us
  starting transfers between devices: 20.1 us -> 21.3 us
    ppermute x9, waiting for transfers between devices: 5.2 us -> 3.16 us  [swap(): lax.ppermute(x, axis, [(i, i ^ mask) for i in range(lax.axis_size(axis))])]
    ppermute x9, starting transfers between devices: 9.95 us -> 11.1 us  [swap(): lax.ppermute(x, axis, [(i, i ^ mask) for i in range(lax.axis_size(axis))])]
  transfers between devices with their start and end apart: 16 -> 16, of which waited for: 6 -> 6; matrix products, arithmetic and copies ran while one was open for 0% -> 0% of each run, Pallas kernels for 29% -> 30%
where the time goes in v10:
time: 48.5 us; the launch traced here: 48.3 us
  starting transfers between devices  21.3 us (44%)
  Pallas kernels  16.4 us (34%)
  waiting for transfers between devices  9.04 us (19%)
  between operations  1.51 us (3%)
    ppermute x9, starting transfers between devices, swap(): lax.ppermute(x, axis, [(i, i ^ mask) for i in range(lax.axis_size(axis))])  11.1 us
    all_to_all x1, starting transfers between devices, shards(): lax.all_to_all(outgoing.reshape(owners, SLOTS, width), 'dp', split_axis=0...  8.02 us
    all_to_all x1, waiting for transfers between devices, shards(): lax.all_to_all(outgoing.reshape(owners, SLOTS, width), 'dp', split_axis=0...  5.81 us
    pallas_call x2, Pallas kernels, load(): pl.pallas_call(functools.partial(load_kernel, pieces), in_specs=[ANY] * l...  4.43 us
    pallas_call x4, Pallas kernels, project(): pl.pallas_call(functools.partial(project_kernel, masks, last, len(feats))...  3.52 us
    pallas_call x5, Pallas kernels, part_sum(): pl.pallas_call(functools.partial(part_kernel, first), in_specs=[SMEM, VME...  3.49 us
    ppermute x9, waiting for transfers between devices, swap(): lax.ppermute(x, axis, [(i, i ^ mask) for i in range(lax.axis_size(axis))])  3.16 us
    ppermute x6, starting transfers between devices, shift(): return lax.ppermute(x, axis, [(i, (i + step) % n) for i in range(n)])  2.17 us
  transfers between devices with their start and end apart: 16, of which 6 were waited for; matrix products, arithmetic and copies ran while one was open for 0% of the time, Pallas kernels for 30%

profile of v10, /device:TPU:0, one launch (start us, length us, event | category | flops | bytes accessed | tf_op | source)
XLA Modules:
  0.0 48.3 jit_solution(1262050906652465720)
XLA Ops:
  0.6 0.5 %collective-permute-start = (bf16[1024,128]{1,0:T(8,128)(2,1)}, bf16[1024,128]{1,0:T(8,128)(2,1)S(1)}, u32[]{:S(2)}, u32[]{:S(2)}) collective-permute-start(bf16[1024,128]{1,0:T(8,128)(2,1)} %g_ref), channel_id=1, source_target_pairs={{0,1},{1,0},{2,3},{3,2},{4,5},{5,4},{6,7},{7,6},{8,9},{9,8},{10,11... | collective-permute-start | bytes 786440 | tf_op jit(solution)/shard_map/ppermute | solution.py:29
  1.1 2.2 %shard_map.128.f_ref.refs_0_ = bf16[512,4096]{1,0:T(8,128)(2,1)S(1)} custom-call(bf16[512,4096]{1,0:T(8,128)(2,1)} %refs_0_.1), custom_call_target="tpu_custom_call" | custom-call | bytes 8388608 | tf_op jit(solution)/shard_map/pallas_call | solution.py:72
  3.4 0.5 %shard_map.131 = f32[1024,128]{1,0:T(8,128)S(1)} custom-call(s32[1]{0:T(128)} %bitcast.1.core, bf16[512,4096]{1,0:T(8,128)(2,1)S(1)} %shard_map.128.f_ref.refs_0_, bf16[1024,128]{1,0:T(8,128)(2,1)S(1)} %collective-permute-done.g_ref), custom_call_target="tpu_custom_call" | custom-call | flops 134217728 | bytes 1572864 | tf_op jit(solution)/shard_map/pallas_call | solution.py:104
  4.0 0.5 %shard_map.132 = f32[1024,128]{1,0:T(8,128)S(1)} custom-call(s32[1]{0:T(128)} %bitcast.1.core, bf16[512,4096]{1,0:T(8,128)(2,1)S(1)} %shard_map.128.f_ref.refs_0_, bf16[1024,128]{1,0:T(8,128)(2,1)S(1)} %collective-permute-done.g_ref), custom_call_target="tpu_custom_call" | custom-call | flops 134217728 | bytes 1572864 | tf_op jit(solution)/shard_map/pallas_call | solution.py:104
  4.6 0.5 %collective-permute-start.2 = (f32[1024,128]{1,0:T(8,128)S(1)}, f32[1024,128]{1,0:T(8,128)S(1)}, u32[]{:S(2)}, u32[]{:S(2)}) collective-permute-start(f32[1024,128]{1,0:T(8,128)S(1)} %shard_map.132), channel_id=1, source_target_pairs={{0,1},{1,0},{2,3},{3,2},{4,5},{5,4},{6,7},{7,6},{8,9},{9,8},{10,11... | collective-permute-start | bytes 1572872 | tf_op jit(solution)/shard_map/ppermute | solution.py:29
  5.1 0.5 %shard_map.133 = f32[1024,128]{1,0:T(8,128)S(1)} custom-call(s32[1]{0:T(128)} %bitcast.1.core, bf16[512,4096]{1,0:T(8,128)(2,1)S(1)} %shard_map.128.f_ref.refs_0_, bf16[1024,128]{1,0:T(8,128)(2,1)S(1)} %collective-permute-done.g_ref), custom_call_target="tpu_custom_call" | custom-call | flops 134217728 | bytes 1572864 | tf_op jit(solution)/shard_map/pallas_call | solution.py:104
  5.8 0.5 %shard_map.129 = f32[1024,128]{1,0:T(8,128)S(1)} custom-call(s32[1]{0:T(128)} %bitcast.1.core, bf16[512,4096]{1,0:T(8,128)(2,1)S(1)} %shard_map.128.f_ref.refs_0_, bf16[1024,128]{1,0:T(8,128)(2,1)S(1)} %collective-permute-done.g_ref), custom_call_target="tpu_custom_call" | custom-call | flops 134217728 | bytes 1572864 | tf_op jit(solution)/shard_map/pallas_call | solution.py:104
  6.3 0.5 %collective-permute-start.4 = (f32[1024,128]{1,0:T(8,128)S(1)}, f32[1024,128]{1,0:T(8,128)S(1)}, u32[]{:S(2)}, u32[]{:S(2)}) collective-permute-start(f32[1024,128]{1,0:T(8,128)S(1)} %shard_map.129), channel_id=1, source_target_pairs={{0,1},{1,0},{2,3},{3,2},{4,5},{5,4},{6,7},{7,6},{8,9},{9,8},{10,11... | collective-permute-start | bytes 1572872 | tf_op jit(solution)/shard_map/ppermute | solution.py:29
  6.8 1.4 %shard_map.130.own_ref = f32[4096,128]{1,0:T(8,128)S(1)} custom-call(s32[1]{0:T(128)} %bitcast.1.core, bf16[512,4096]{1,0:T(8,128)(2,1)S(1)} %shard_map.128.f_ref.refs_0_, bf16[1024,128]{1,0:T(8,128)(2,1)S(1)} %copy-done.6, bf16[4096,128]{1,0:T(8,128)(2,1)S(1)} %bitcast.6), custom_call_target="tpu_custom_call" | custom-call | flops 536870912 | bytes 6291456 | tf_op jit(solution)/shard_map/pallas_call | solution.py:104
  8.8 2.1 %shard_map.134 = (f32[4096,128]{1,0:T(8,128)S(1)}, f32[128,128]{1,0:T(8,128)}) custom-call(s32[32]{0:T(128)S(1)} %bitcast.7, s32[17]{0:T(128)S(1)} %copy-done.7, f32[4096,128]{1,0:T(8,128)S(1)} %shard_map.130.own_ref, f32[1024,128]{1,0:T(8,128)S(1)} %collective-permute-done.1.refs_0_, f32[1024,128]{1,0:T(8,128)S(1)} %collective-permute-done.2.refs_1_, ...), custom_call_target="tpu_custom_call" | custom-call | flops 4194304 | bytes 6291456 | tf_op jit(solution)/shard_map/pallas_call | solution.py:157
  10.8 8.0 %all-to-all-start = ((f32[16,8,128]{2,1,0:T(8,128)}), f32[16,8,128]{2,1,0:T(8,128)S(1)}, u32[]{:S(2)}, u32[]{:S(2)}) async-start(f32[16,8,128]{2,1,0:T(8,128)} %bitcast.4), calls=%async_computation | async-start | bytes 131072 | tf_op jit(solution)/shard_map/all_to_all | solution.py:352
  19.5 1.1 %shard_map.135 = bf16[4096,128]{1,0:T(8,128)(2,1)} custom-call(f32[4096,128]{1,0:T(8,128)S(1)} %get-tuple-element.21.x_ref), custom_call_target="tpu_custom_call" | custom-call | flops 524288 | bytes 3145728 | tf_op jit(solution)/shard_map/pallas_call | solution.py:253
  20.6 5.8 %all-to-all-done.arr_ref = f32[16,8,128]{2,1,0:T(8,128)S(1)} async-done(((f32[16,8,128]{2,1,0:T(8,128)}), f32[16,8,128]{2,1,0:T(8,128)S(1)}, u32[]{:S(2)}, u32[]{:S(2)}) %all-to-all-start) | async-done | bytes 65568 | tf_op jit(solution)/shard_map/all_to_all | solution.py:352
  26.4 1.0 %shard_map.136 = (f32[256,128]{1,0:T(8,128)S(1)}, bf16[256,128]{1,0:T(8,128)(2,1)S(1)}) custom-call(s32[1]{0:T(128)} %bitcast.me, s32[1]{0:T(128)S(6)} %copy.14.least, s32[17]{0:T(128)S(1)} %copy-done.7, f32[16,8,128]{2,1,0:T(8,128)S(1)} %all-to-all-done.arr_ref, f32[256,128]{1,0:T(8,128)S(1)} %copy-done.3, f32[256,128]{1,0:T(8,128)S(1)} %copy-done.4, ...), custom_call_target="tpu_custom_call" | custom-call | flops 50331648 | bytes 983040 | tf_op jit(solution)/shard_map/pallas_call | solution.py:220
  27.4 0.7 %collective-permute-start.5 = (bf16[256,128]{1,0:T(8,128)(2,1)S(1)}, bf16[256,128]{1,0:T(8,128)(2,1)S(1)}, u32[]{:S(2)}, u32[]{:S(2)}) collective-permute-start(bf16[256,128]{1,0:T(8,128)(2,1)S(1)} %get-tuple-element.23.refs_2_), channel_id=1, source_target_pairs={{0,8},{2,10},{4,12},{6,14},{8,0},{10,2},{12,4},{14,6},{16,24},{18,... | collective-permute-start | bytes 196616 | tf_op jit(solution)/shard_map/ppermute | solution.py:33
  28.1 0.8 %collective-permute-start.6 = (bf16[256,128]{1,0:T(8,128)(2,1)S(1)}, bf16[256,128]{1,0:T(8,128)(2,1)S(1)}, u32[]{:S(2)}, u32[]{:S(2)}) collective-permute-start(bf16[256,128]{1,0:T(8,128)(2,1)S(1)} %get-tuple-element.23.refs_2_), channel_id=1, source_target_pairs={{0,16},{2,18},{4,20},{6,22},{8,24},{10,26},{12,28},{14,30},{16,0},... | collective-permute-start | bytes 196616 | tf_op jit(solution)/shard_map/ppermute | solution.py:33
  29.0 2.9 %collective-permute-start.7 = (bf16[256,128]{1,0:T(8,128)(2,1)S(1)}, bf16[256,128]{1,0:T(8,128)(2,1)S(1)}, u32[]{:S(2)}, u32[]{:S(2)}) collective-permute-start(bf16[256,128]{1,0:T(8,128)(2,1)S(1)} %get-tuple-element.23.refs_2_), channel_id=1, source_target_pairs={{0,24},{2,26},{4,28},{6,30},{8,16},{10,18},{12,20},{14,22},{16,8},... | collective-permute-start | bytes 196616 | tf_op jit(solution)/shard_map/ppermute | solution.py:33
  31.9 0.7 %collective-permute-start.8 = (bf16[256,128]{1,0:T(8,128)(2,1)S(1)}, bf16[256,128]{1,0:T(8,128)(2,1)S(1)}, u32[]{:S(2)}, u32[]{:S(2)}) collective-permute-start(bf16[256,128]{1,0:T(8,128)(2,1)S(1)} %get-tuple-element.23.refs_2_), channel_id=1, source_target_pairs={{0,6},{2,4},{4,2},{6,0},{8,14},{10,12},{12,10},{14,8},{16,22},{18,... | collective-permute-start | bytes 196616 | tf_op jit(solution)/shard_map/ppermute | solution.py:33
  32.5 1.6 %collective-permute-start.9 = (bf16[256,128]{1,0:T(8,128)(2,1)S(1)}, bf16[256,128]{1,0:T(8,128)(2,1)S(1)}, u32[]{:S(2)}, u32[]{:S(2)}) collective-permute-start(bf16[256,128]{1,0:T(8,128)(2,1)S(1)} %get-tuple-element.23.refs_2_), channel_id=1, source_target_pairs={{0,4},{2,6},{4,0},{6,2},{8,12},{10,14},{12,8},{14,10},{16,20},{18,... | collective-permute-start | bytes 196616 | tf_op jit(solution)/shard_map/ppermute | solution.py:33
  34.2 1.1 %collective-permute-done.6.refs_1_ = bf16[256,128]{1,0:T(8,128)(2,1)S(1)} collective-permute-done((bf16[256,128]{1,0:T(8,128)(2,1)S(1)}, bf16[256,128]{1,0:T(8,128)(2,1)S(1)}, u32[]{:S(2)}, u32[]{:S(2)}) %collective-permute-start.6) | collective-permute-done | bytes 65568 | tf_op jit(solution)/shard_map/ppermute | solution.py:33
  35.3 0.7 %collective-permute-start.10 = (bf16[256,128]{1,0:T(8,128)(2,1)S(1)}, bf16[256,128]{1,0:T(8,128)(2,1)S(1)}, u32[]{:S(2)}, u32[]{:S(2)}) collective-permute-start(bf16[256,128]{1,0:T(8,128)(2,1)S(1)} %get-tuple-element.23.refs_2_), channel_id=1, source_target_pairs={{0,2},{2,0},{4,6},{6,4},{8,10},{10,8},{12,14},{14,12},{16,18},{18,... | collective-permute-start | bytes 196616 | tf_op jit(solution)/shard_map/ppermute | solution.py:33
  36.0 1.5 %collective-permute-start.14 = (bf16[3,256,128]{2,1,0:T(8,128)(2,1)S(1)}, bf16[3,256,128]{2,1,0:T(8,128)(2,1)S(1)}, u32[]{:S(2)}, u32[]{:S(2)}) collective-permute-start(bf16[3,256,128]{2,1,0:T(8,128)(2,1)S(1)} %shard_map.137.refs_3_), channel_id=1, source_target_pairs={{0,6},{2,4},{4,2},{6,0},{8,14},{10,12},{12,10},{14,8},{16,22},{18,... | collective-permute-start | bytes 589832 | tf_op jit(solution)/shard_map/ppermute | solution.py:33
  37.5 1.4 %collective-permute-start.13 = (bf16[3,256,128]{2,1,0:T(8,128)(2,1)S(1)}, bf16[3,256,128]{2,1,0:T(8,128)(2,1)S(1)}, u32[]{:S(2)}, u32[]{:S(2)}) collective-permute-start(bf16[3,256,128]{2,1,0:T(8,128)(2,1)S(1)} %shard_map.137.refs_3_), channel_id=1, source_target_pairs={{0,4},{2,6},{4,0},{6,2},{8,12},{10,14},{12,8},{14,10},{16,20},{18,... | collective-permute-start | bytes 589832 | tf_op jit(solution)/shard_map/ppermute | solution.py:33
  38.9 2.2 %shard_map.138.refs_1_ = bf16[512,4096]{1,0:T(8,128)(2,1)S(1)} custom-call(bf16[512,4096]{1,0:T(8,128)(2,1)} %collective-permute-done.11.refs_0_), custom_call_target="tpu_custom_call" | custom-call | bytes 8388608 | tf_op jit(solution)/shard_map/pallas_call | solution.py:72
  41.1 0.8 %collective-permute-start.12 = (bf16[3,256,128]{2,1,0:T(8,128)(2,1)S(1)}, bf16[3,256,128]{2,1,0:T(8,128)(2,1)S(1)}, u32[]{:S(2)}, u32[]{:S(2)}) collective-permute-start(bf16[3,256,128]{2,1,0:T(8,128)(2,1)S(1)} %shard_map.137.refs_3_), channel_id=1, source_target_pairs={{0,2},{2,0},{4,6},{6,4},{8,10},{10,8},{12,14},{14,12},{16,18},{18,... | collective-permute-start | bytes 589832 | tf_op jit(solution)/shard_map/ppermute | solution.py:33
  41.9 0.8 %shard_map.143 = (f32[256,128]{1,0:T(8,128)}, f32[256,128]{1,0:T(8,128)}, f32[256,128]{1,0:T(8,128)}) custom-call(f32[256,128]{1,0:T(8,128)S(1)} %get-tuple-element.29.g_ref, f32[256,128]{1,0:T(8,128)S(1)} %copy-done.3, f32[256,128]{1,0:T(8,128)S(1)} %copy-done.4, f32[256,128]{1,0:T(8,128)S(1)} %copy-done.5), custom_call_target="tpu_custom_call" | custom-call | flops 655360 | bytes 917504 | tf_op jit(solution)/shard_map/pallas_call | solution.py:237
  42.7 0.7 %shard_map.139.refs_4_ = f32[1024,128]{1,0:T(8,128)S(1)} custom-call(s32[1]{0:T(128)} %bitcast.me, s32[1]{0:T(128)} %bitcast.1.core, bf16[512,4096]{1,0:T(8,128)(2,1)S(1)} %copy-done.1, bf16[512,4096]{1,0:T(8,128)(2,1)S(1)} %shard_map.138.refs_1_, bf16[256,128]{1,0:T(8,128)(2,1)S(1)} %get-tuple-element.23.refs_2_, bf16[3,256,128]{2,1,0:T(8,128)(2,1)S(1)} %shard_map.137.refs_3_), custom_call_target="tpu_custom_call" | custom-call | flops 268435456 | bytes 3145728 | tf_op jit(solution)/shard_map/pallas_call | solution.py:309
  43.4 0.7 %collective-permute-done.14.refs_3_ = bf16[3,256,128]{2,1,0:T(8,128)(2,1)S(1)} collective-permute-done((bf16[3,256,128]{2,1,0:T(8,128)(2,1)S(1)}, bf16[3,256,128]{2,1,0:T(8,128)(2,1)S(1)}, u32[]{:S(2)}, u32[]{:S(2)}) %collective-permute-start.14) | collective-permute-done | bytes 196640 | tf_op jit(solution)/shard_map/ppermute | solution.py:33
  44.2 0.7 %shard_map.140.refs_4_ = f32[1024,128]{1,0:T(8,128)S(1)} custom-call(s32[1]{0:T(128)} %bitcast.me, s32[1]{0:T(128)} %bitcast.1.core, bf16[512,4096]{1,0:T(8,128)(2,1)S(1)} %copy-done.1, bf16[512,4096]{1,0:T(8,128)(2,1)S(1)} %shard_map.138.refs_1_, bf16[256,128]{1,0:T(8,128)(2,1)S(1)} %collective-permute-done.8.refs_2_, ...), custom_call_target="tpu_custom_call" | custom-call | flops 268435456 | bytes 3145728 | tf_op jit(solution)/shard_map/pallas_call | solution.py:309
  44.9 1.1 %collective-permute-done.13.refs_3_ = bf16[3,256,128]{2,1,0:T(8,128)(2,1)S(1)} collective-permute-done((bf16[3,256,128]{2,1,0:T(8,128)(2,1)S(1)}, bf16[3,256,128]{2,1,0:T(8,128)(2,1)S(1)}, u32[]{:S(2)}, u32[]{:S(2)}) %collective-permute-start.13) | collective-permute-done | bytes 196640 | tf_op jit(solution)/shard_map/ppermute | solution.py:33
  45.9 0.7 %shard_map.141.refs_4_ = f32[1024,128]{1,0:T(8,128)S(1)} custom-call(s32[1]{0:T(128)} %bitcast.me, s32[1]{0:T(128)} %bitcast.1.core, bf16[512,4096]{1,0:T(8,128)(2,1)S(1)} %copy-done.1, bf16[512,4096]{1,0:T(8,128)(2,1)S(1)} %shard_map.138.refs_1_, bf16[256,128]{1,0:T(8,128)(2,1)S(1)} %collective-permute-done.9.refs_2_, ...), custom_call_target="tpu_custom_call" | custom-call | flops 268435456 | bytes 3145728 | tf_op jit(solution)/shard_map/pallas_call | solution.py:309
  46.9 1.4 %shard_map.142 = bf16[1024,128]{1,0:T(8,128)(2,1)} custom-call(s32[1]{0:T(128)} %bitcast.me, s32[1]{0:T(128)} %bitcast.1.core, bf16[512,4096]{1,0:T(8,128)(2,1)S(1)} %copy-done.1, bf16[512,4096]{1,0:T(8,128)(2,1)S(1)} %shard_map.138.refs_1_, bf16[256,128]{1,0:T(8,128)(2,1)S(1)} %collective-permute-done.10.refs_2_, ...), custom_call_target="tpu_custom_call" | custom-call | flops 268435456 | bytes 3145728 | tf_op jit(solution)/shard_map/pallas_call | solution.py:309
  (34 shorter events, 1.0 us)
Async XLA Ops:
  0.6 2.8 %collective-permute-start = (bf16[1024,128]{1,0:T(8,128)(2,1)}, bf16[1024,128]{1,0:T(8,128)(2,1)S(1)}, u32[]{:S(2)}, u32[]{:S(2)}) collective-permute-start(bf16[1024,128]{1,0:T(8,128)(2,1)} %g_ref), channel_id=1, source_target_pairs={{0,1},{1,0},{2,3},{3,2},{4,5},{5,4},{6,7},{7,6},{8,9},{9,8},{10,11... | collective-permute-start | bytes 786440 | tf_op jit(solution)/shard_map/ppermute | solution.py:29
  3.4 3.5 %copy-start = (bf16[512,4096]{1,0:T(8,128)(2,1)}, bf16[512,4096]{1,0:T(8,128)(2,1)S(1)}, u32[]{:S(2)}) copy-start(bf16[512,4096]{1,0:T(8,128)(2,1)S(1)} %shard_map.128.f_ref.refs_0_) | copy-start | bytes 12582916
  3.9 4.4 %collective-permute-start.1 = (f32[1024,128]{1,0:T(8,128)S(1)}, f32[1024,128]{1,0:T(8,128)S(1)}, u32[]{:S(2)}, u32[]{:S(2)}) collective-permute-start(f32[1024,128]{1,0:T(8,128)S(1)} %shard_map.131), channel_id=1, source_target_pairs={{0,1},{1,0},{2,3},{3,2},{4,5},{5,4},{6,7},{7,6},{8,9},{9,8},{10,11... | collective-permute-start | bytes 1572872 | tf_op jit(solution)/shard_map/ppermute | solution.py:29
  4.6 2.3 %copy-start.2 = (bf16[1,4096,128]{2,1,0:T(8,128)(2,1)S(1)}, bf16[1,4096,128]{2,1,0:T(8,128)(2,1)}, u32[]{:S(2)}) copy-start(bf16[1,4096,128]{2,1,0:T(8,128)(2,1)} %param.11) | copy-start | bytes 3145732
  4.6 2.3 %copy-start.6 = (bf16[1024,128]{1,0:T(8,128)(2,1)S(1)}, bf16[1024,128]{1,0:T(8,128)(2,1)}, u32[]{:S(2)}) copy-start(bf16[1024,128]{1,0:T(8,128)(2,1)} %g_ref) | copy-start | bytes 786436
  4.6 3.7 %collective-permute-start.2 = (f32[1024,128]{1,0:T(8,128)S(1)}, f32[1024,128]{1,0:T(8,128)S(1)}, u32[]{:S(2)}, u32[]{:S(2)}) collective-permute-start(f32[1024,128]{1,0:T(8,128)S(1)} %shard_map.132), channel_id=1, source_target_pairs={{0,1},{1,0},{2,3},{3,2},{4,5},{5,4},{6,7},{7,6},{8,9},{9,8},{10,11... | collective-permute-start | bytes 1572872 | tf_op jit(solution)/shard_map/ppermute | solution.py:29
  5.6 2.7 %collective-permute-start.3 = (f32[1024,128]{1,0:T(8,128)S(1)}, f32[1024,128]{1,0:T(8,128)S(1)}, u32[]{:S(2)}, u32[]{:S(2)}) collective-permute-start(f32[1024,128]{1,0:T(8,128)S(1)} %shard_map.133), channel_id=1, source_target_pairs={{0,1},{1,0},{2,3},{3,2},{4,5},{5,4},{6,7},{7,6},{8,9},{9,8},{10,11... | collective-permute-start | bytes 1572872 | tf_op jit(solution)/shard_map/ppermute | solution.py:29
  6.3 2.5 %copy-start.7 = (s32[17]{0:T(128)S(1)}, s32[17]{0:T(128)}, u32[]{:S(2)}) copy-start(s32[17]{0:T(128)} %edges.3) | copy-start | bytes 208
  6.3 2.4 %copy-start.8 = (s32[1,1,32]{2,1,0:T(1,128)S(1)}, s32[1,1,32]{2,1,0:T(1,128)}, u32[]{:S(2)}) copy-start(s32[1,1,32]{2,1,0:T(1,128)} %param.12) | copy-start | bytes 388
  6.3 2.0 %collective-permute-start.4 = (f32[1024,128]{1,0:T(8,128)S(1)}, f32[1024,128]{1,0:T(8,128)S(1)}, u32[]{:S(2)}, u32[]{:S(2)}) collective-permute-start(f32[1024,128]{1,0:T(8,128)S(1)} %shard_map.129), channel_id=1, source_target_pairs={{0,1},{1,0},{2,3},{3,2},{4,5},{5,4},{6,7},{7,6},{8,9},{9,8},{10,11... | collective-permute-start | bytes 1572872 | tf_op jit(solution)/shard_map/ppermute | solution.py:29
  8.3 18.1 %copy-start.3 = (f32[256,128]{1,0:T(8,128)S(1)}, f32[256,128]{1,0:T(8,128)}, u32[]{:S(2)}) copy-start(f32[256,128]{1,0:T(8,128)} %m_ref.3) | copy-start | bytes 393220
  8.3 18.1 %copy-start.4 = (f32[256,128]{1,0:T(8,128)S(1)}, f32[256,128]{1,0:T(8,128)}, u32[]{:S(2)}) copy-start(f32[256,128]{1,0:T(8,128)} %v_ref.3) | copy-start | bytes 393220
  8.3 18.1 %copy-start.5 = (f32[256,128]{1,0:T(8,128)S(1)}, f32[256,128]{1,0:T(8,128)}, u32[]{:S(2)}) copy-start(f32[256,128]{1,0:T(8,128)} %w_ref.3) | copy-start | bytes 393220
  8.4 29.2 %collective-permute-start.11 = (bf16[512,4096]{1,0:T(8,128)(2,1)}, bf16[512,4096]{1,0:T(8,128)(2,1)}, u32[]{:S(2)}, u32[]{:S(2)}) collective-permute-start(bf16[512,4096]{1,0:T(8,128)(2,1)} %refs_0_.1), channel_id=1, source_target_pairs={{0,1},{1,0},{2,3},{3,2},{4,5},{5,4},{6,7},{7,6},{8,9},{9,8},{10,11... | collective-permute-start | bytes 12582920 | tf_op jit(solution)/shard_map/ppermute | solution.py:29
  10.8 15.6 %all-to-all-start = ((f32[16,8,128]{2,1,0:T(8,128)}), f32[16,8,128]{2,1,0:T(8,128)S(1)}, u32[]{:S(2)}, u32[]{:S(2)}) async-start(f32[16,8,128]{2,1,0:T(8,128)} %bitcast.4), calls=%async_computation | async-start | bytes 131072 | tf_op jit(solution)/shard_map/all_to_all | solution.py:352
  27.4 5.1 %collective-permute-start.5 = (bf16[256,128]{1,0:T(8,128)(2,1)S(1)}, bf16[256,128]{1,0:T(8,128)(2,1)S(1)}, u32[]{:S(2)}, u32[]{:S(2)}) collective-permute-start(bf16[256,128]{1,0:T(8,128)(2,1)S(1)} %get-tuple-element.23.refs_2_), channel_id=1, source_target_pairs={{0,8},{2,10},{4,12},{6,14},{8,0},{10,2},{12,4},{14,6},{16,24},{18,... | collective-permute-start | bytes 196616 | tf_op jit(solution)/shard_map/ppermute | solution.py:33
  28.1 7.2 %collective-permute-start.6 = (bf16[256,128]{1,0:T(8,128)(2,1)S(1)}, bf16[256,128]{1,0:T(8,128)(2,1)S(1)}, u32[]{:S(2)}, u32[]{:S(2)}) collective-permute-start(bf16[256,128]{1,0:T(8,128)(2,1)S(1)} %get-tuple-element.23.refs_2_), channel_id=1, source_target_pairs={{0,16},{2,18},{4,20},{6,22},{8,24},{10,26},{12,28},{14,30},{16,0},... | collective-permute-start | bytes 196616 | tf_op jit(solution)/shard_map/ppermute | solution.py:33
  29.0 7.1 %collective-permute-start.7 = (bf16[256,128]{1,0:T(8,128)(2,1)S(1)}, bf16[256,128]{1,0:T(8,128)(2,1)S(1)}, u32[]{:S(2)}, u32[]{:S(2)}) collective-permute-start(bf16[256,128]{1,0:T(8,128)(2,1)S(1)} %get-tuple-element.23.refs_2_), channel_id=1, source_target_pairs={{0,24},{2,26},{4,28},{6,30},{8,16},{10,18},{12,20},{14,22},{16,8},... | collective-permute-start | bytes 196616 | tf_op jit(solution)/shard_map/ppermute | solution.py:33
  31.9 9.2 %collective-permute-start.8 = (bf16[256,128]{1,0:T(8,128)(2,1)S(1)}, bf16[256,128]{1,0:T(8,128)(2,1)S(1)}, u32[]{:S(2)}, u32[]{:S(2)}) collective-permute-start(bf16[256,128]{1,0:T(8,128)(2,1)S(1)} %get-tuple-element.23.refs_2_), channel_id=1, source_target_pairs={{0,6},{2,4},{4,2},{6,0},{8,14},{10,12},{12,10},{14,8},{16,22},{18,... | collective-permute-start | bytes 196616 | tf_op jit(solution)/shard_map/ppermute | solution.py:33
  32.5 8.6 %collective-permute-start.9 = (bf16[256,128]{1,0:T(8,128)(2,1)S(1)}, bf16[256,128]{1,0:T(8,128)(2,1)S(1)}, u32[]{:S(2)}, u32[]{:S(2)}) collective-permute-start(bf16[256,128]{1,0:T(8,128)(2,1)S(1)} %get-tuple-element.23.refs_2_), channel_id=1, source_target_pairs={{0,4},{2,6},{4,0},{6,2},{8,12},{10,14},{12,8},{14,10},{16,20},{18,... | collective-permute-start | bytes 196616 | tf_op jit(solution)/shard_map/ppermute | solution.py:33
  35.3 5.8 %collective-permute-start.10 = (bf16[256,128]{1,0:T(8,128)(2,1)S(1)}, bf16[256,128]{1,0:T(8,128)(2,1)S(1)}, u32[]{:S(2)}, u32[]{:S(2)}) collective-permute-start(bf16[256,128]{1,0:T(8,128)(2,1)S(1)} %get-tuple-element.23.refs_2_), channel_id=1, source_target_pairs={{0,2},{2,0},{4,6},{6,4},{8,10},{10,8},{12,14},{14,12},{16,18},{18,... | collective-permute-start | bytes 196616 | tf_op jit(solution)/shard_map/ppermute | solution.py:33
  36.0 6.7 %copy-start.1 = (bf16[512,4096]{1,0:T(8,128)(2,1)S(1)}, bf16[512,4096]{1,0:T(8,128)(2,1)}, u32[]{:S(2)}) copy-start(bf16[512,4096]{1,0:T(8,128)(2,1)} %copy-done) | copy-start | bytes 12582916
  36.0 8.1 %collective-permute-start.14 = (bf16[3,256,128]{2,1,0:T(8,128)(2,1)S(1)}, bf16[3,256,128]{2,1,0:T(8,128)(2,1)S(1)}, u32[]{:S(2)}, u32[]{:S(2)}) collective-permute-start(bf16[3,256,128]{2,1,0:T(8,128)(2,1)S(1)} %shard_map.137.refs_3_), channel_id=1, source_target_pairs={{0,6},{2,4},{4,2},{6,0},{8,14},{10,12},{12,10},{14,8},{16,22},{18,... | collective-permute-start | bytes 589832 | tf_op jit(solution)/shard_map/ppermute | solution.py:33
  37.5 8.4 %collective-permute-start.13 = (bf16[3,256,128]{2,1,0:T(8,128)(2,1)S(1)}, bf16[3,256,128]{2,1,0:T(8,128)(2,1)S(1)}, u32[]{:S(2)}, u32[]{:S(2)}) collective-permute-start(bf16[3,256,128]{2,1,0:T(8,128)(2,1)S(1)} %shard_map.137.refs_3_), channel_id=1, source_target_pairs={{0,4},{2,6},{4,0},{6,2},{8,12},{10,14},{12,8},{14,10},{16,20},{18,... | collective-permute-start | bytes 589832 | tf_op jit(solution)/shard_map/ppermute | solution.py:33
  41.1 5.7 %collective-permute-start.12 = (bf16[3,256,128]{2,1,0:T(8,128)(2,1)S(1)}, bf16[3,256,128]{2,1,0:T(8,128)(2,1)S(1)}, u32[]{:S(2)}, u32[]{:S(2)}) collective-permute-start(bf16[3,256,128]{2,1,0:T(8,128)(2,1)S(1)} %shard_map.137.refs_3_), channel_id=1, source_target_pairs={{0,2},{2,0},{4,6},{6,4},{8,10},{10,8},{12,14},{14,12},{16,18},{18,... | collective-permute-start | bytes 589832 | tf_op jit(solution)/shard_map/ppermute | solution.py:33
